TPU v7x, 32 devices: a whole 2x2x4 slice. The times are simulated.
32 devices in a mesh: ctx: 8 (over y, x, core), head: 4 (over z).
Axes of the slice: x: 2, y: 2, z: 4, core: 2. Of those that a mesh axis runs over, the one named last changes fastest.
Arguments:
- query_rows: bfloat16 [4096, 2048], P('ctx', 'head'), may hold values from -12 to 12
- key_rows: bfloat16 [4096, 2048], P('ctx', 'head'), may hold values from -12 to 12
- value_rows: bfloat16 [4096, 2048], P('ctx', 'head'), may hold values from -6 to 6
- grad_out: bfloat16 [4096, 2048], P('ctx', 'head'), may hold values from -6 to 6
- house_dirs: float32 [32, 2048], P('ctx', 'head'), may hold values from -6 to 6
- owners: int32 [32, 2], P('ctx'), may hold values from 0 to 7, all different within a row; in each aligned block of 4 rows (0 to 3, 4 to 7, ...) at most 2 rows name the same one
- offsets: int32 [32, 2], P('ctx'), may hold values from 0 to 3
- w_query: bfloat16 [4096, 2048], P(None, 'head'), may hold values from -0.09375 to 0.09375
- w_key: bfloat16 [4096, 2048], P(None, 'head'), may hold values from -0.09375 to 0.09375
- w_value: bfloat16 [4096, 2048], P(None, 'head'), may hold values from -0.09375 to 0.09375
Outputs:
- input_grad: bfloat16 [4096, 4096], P('ctx', 'head')
- house_grad: float32 [32, 2048], P('ctx', 'head')
Inputs may be any that keep to these rules, and one draw needn't show every extreme that they name: `owners`: each query block names 2 different ctx indices; the query blocks of one ctx index name any one ctx index at most 2 times, and exactly 2 times for some.
All inputs are finite; a program needn't handle non-finite values.
Results may differ from a plain program's by a relative error of at most 0.025.
Values may be sent and summed in bfloat16 or wider, within the bound.
No kernel may reach another device: no remote copies, remote signals or barrier semaphores. Data moves between devices by JAX's collectives and lax.ppermute only.
A program may use at most 128 MiB of HBM per device.

v0:
```python
import functools
import math

import jax
import jax.numpy as jnp
from jax import lax
from jax.experimental import pallas as pl
from jax.experimental.pallas import tpu as pltpu
from jax.sharding import PartitionSpec as P

DH = 128
BLK = 128
MAXL = 2
HIGH = lax.Precision.HIGHEST
F32 = jnp.float32
BF16 = jnp.bfloat16


def nn(a, b):
    return lax.dot_general(a, b, (((1,), (0,)), ((), ())), preferred_element_type=F32)


def nt(a, b):
    return lax.dot_general(a, b, (((1,), (1,)), ((), ())), preferred_element_type=F32)


def tn(a, b):
    return lax.dot_general(a, b, (((0,), (0,)), ((), ())), preferred_element_type=F32)


def nn_high(a, b):
    return lax.dot_general(
        a, b, (((1,), (0,)), ((), ())), precision=HIGH, preferred_element_type=F32
    )


def nt_high(a, b):
    return lax.dot_general(
        a, b, (((1,), (1,)), ((), ())), precision=HIGH, preferred_element_type=F32
    )


def split(value):
    top = value.astype(BF16)
    return top, (value - top.astype(F32)).astype(BF16)


def iota(shape, dim):
    return lax.broadcasted_iota(jnp.int32, shape, dim)


def head(h):
    return slice(h * DH, (h + 1) * DH)


def listed(ints_ref, entry, entries):
    return ints_ref[1 + entry], ints_ref[1 + entries + entry]


def grant(mebibytes):
    return pltpu.CompilerParams(vmem_limit_bytes=mebibytes * 1024 * 1024)


def cost(microseconds):
    return pl.CostEstimate(
        flops=int(microseconds * 1.15e9), bytes_accessed=1 << 20, transcendentals=0
    )


def in_smem(count):
    return [pl.BlockSpec(memory_space=pltpu.SMEM)] * count


def in_vmem(count):
    return [pl.BlockSpec(memory_space=pltpu.VMEM)] * count


def chain_kernel(heads, parts, ints_ref, *refs):
    house_refs = refs[:parts]
    unit_ref, rows_ref, inv_ref, unit_t_ref, unit_h, house_all = refs[parts:]
    count = unit_ref.shape[0]
    span = count // parts
    for t, ref in enumerate(house_refs):
        place = (ints_ref[0] // (8 // parts)) ^ t if parts > 1 else 0
        house_all[pl.ds(pl.multiple_of(place * span, span), span), :] = ref[...]
    eye = (iota((count, count), 0) == iota((count, count), 1)).astype(F32)
    for h in range(heads):
        house = house_all[:, head(h)]
        lengths = jnp.sqrt(jnp.sum(house * house, axis=1, keepdims=True) + 1e-06)
        unit_ref[:, head(h)] = house / lengths
        unit_h[h] = house / lengths
        inv_ref[h] = eye

    def eliminate(step, carry):
        below = iota((count, 1), 0) > step
        for h in range(heads):
            pivot = unit_h[h, pl.ds(step, 1), :]
            overlap = jnp.sum(unit_h[h] * pivot, axis=1, keepdims=True)
            factor = jnp.where(below, 2.0 * overlap, 0.0)
            inv_ref[h] = inv_ref[h] - factor * inv_ref[h, pl.ds(step, 1), :]
        return carry

    lax.fori_loop(0, count, eliminate, 0)
    eye_wide = (iota((DH, DH), 0) == iota((DH, DH), 1)).astype(F32)
    for h in range(heads):
        units = unit_ref[:, head(h)]
        rows_ref[:, head(h)] = nn_high(inv_ref[h], units)
        unit_t_ref[h] = nt_high(eye_wide, units)


def run_chain(ints, house_parts, heads):
    span, width = house_parts[0].shape
    parts = len(house_parts)
    count = span * parts
    return pl.pallas_call(
        functools.partial(chain_kernel, heads, parts),
        out_shape=[
            jax.ShapeDtypeStruct((count, width), F32),
            jax.ShapeDtypeStruct((count, width), F32),
            jax.ShapeDtypeStruct((heads, count, count), F32),
            jax.ShapeDtypeStruct((heads, DH, count), F32),
        ],
        in_specs=in_smem(1) + in_vmem(parts),
        out_specs=in_vmem(4),
        scratch_shapes=[pltpu.VMEM((heads, count, DH), F32), pltpu.VMEM((count, width), F32)],
        compiler_params=grant(60),
        cost_estimate=cost(6),
        name="house_chain",
    )(ints, *house_parts)


def rotate_kernel(
    heads,
    blocks,
    ints_ref,
    rows_ref,
    unit_t_ref,
    query_ref,
    key_ref,
    qrot_ref,
    krot_ref,
    local_ref,
    listed_ref,
):
    count = rows_ref.shape[0]
    entries = blocks * MAXL
    eye = (iota((DH, DH), 0) == iota((DH, DH), 1)).astype(F32)

    def cumulative(h, block):
        kept = jnp.where(iota((DH, count), 1) <= block, unit_t_ref[h], 0.0)
        return split(eye - 2.0 * nn_high(kept, rows_ref[:, head(h)]))

    base = ints_ref[0] * blocks

    def local_block(b, carry):
        here = pl.ds(pl.multiple_of(b * BLK, BLK), BLK)
        for h in range(heads):
            hi, lo = cumulative(h, base + b)
            local_ref[b, h] = hi
            query, key = query_ref[here, head(h)], key_ref[here, head(h)]
            qrot_ref[here, head(h)] = (nn(query, hi) + nn(query, lo)).astype(BF16)
            krot_ref[here, head(h)] = (nn(key, hi) + nn(key, lo)).astype(BF16)
        return carry

    lax.fori_loop(0, blocks, local_block, 0)

    def listed_block(e, carry):
        owner, offset = listed(ints_ref, e, entries)
        for h in range(heads):
            hi, lo = cumulative(h, owner * blocks + offset)
            listed_ref[e, h, :DH] = hi
            listed_ref[e, h, DH:] = lo
        return carry

    lax.fori_loop(0, entries, listed_block, 0)


def run_rotate(ints, house_rows, unit_t, query_rows, key_rows, heads, blocks):
    rows, width = query_rows.shape
    entries = blocks * MAXL
    return pl.pallas_call(
        functools.partial(rotate_kernel, heads, blocks),
        out_shape=[
            jax.ShapeDtypeStruct((rows, width), BF16),
            jax.ShapeDtypeStruct((rows, width), BF16),
            jax.ShapeDtypeStruct((blocks, heads, DH, DH), BF16),
            jax.ShapeDtypeStruct((entries, heads, 2 * DH, DH), BF16),
        ],
        in_specs=in_smem(1) + in_vmem(4),
        out_specs=in_vmem(4),
        compiler_params=grant(60),
        cost_estimate=cost(9),
        name="rotate",
    )(ints, house_rows, unit_t, query_rows, key_rows)


def attend_kernel(heads, blocks, places, pieces, *refs):
    ints_ref = refs[0]
    source_count = 1 + max(place[0] for pair in places for place in pair)
    sources = refs[1 : 1 + source_count]
    refs = refs[1 + source_count :]
    (query_ref, qrot_ref, krot_ref, value_ref, grad_ref, local_ref, listed_ref) = refs[:7]
    dq_ref, dcum_ref, dk_ref, dv_ref = refs[7:11]
    outs = refs[11 : 11 + max(len(pieces), 1)]
    refs = refs[11 + max(len(pieces), 1) :]
    far_keys, far_values, sems = refs[:3]
    entries = blocks * MAXL
    scaling = DH ** (-0.5)
    log_scale = scaling * math.log2(math.e)

    def start(e, src, kind, slot, where):
        pltpu.make_async_copy(src.at[where], slot.at[e], sems.at[kind, e]).start()

    for e in range(entries):
        owner, offset = listed(ints_ref, e, entries)
        row = pl.multiple_of(offset * BLK, BLK)
        if len(places) == 1:
            start(e, sources[0], 0, far_keys, (owner, pl.ds(row, BLK)))
            start(e, sources[1], 1, far_values, (owner, pl.ds(row, BLK)))
        else:
            distance = owner ^ ints_ref[0]
            for r, (key_place, value_place) in enumerate(places):

                @pl.when(distance == r)
                def _():
                    source, first = key_place
                    start(e, sources[source], 0, far_keys, pl.ds(first + row, BLK))
                    source, first = value_place
                    start(e, sources[source], 1, far_values, pl.ds(first + row, BLK))

    out_copies = []
    if pieces:
        payloads, out_sems = refs[3 : 3 + heads], refs[3 + heads]
        for payload in payloads:
            payload[...] = jnp.zeros_like(payload)
    for kind, slots in ((0, far_keys), (1, far_values)):
        for e in range(entries):
            pltpu.make_async_copy(slots.at[e], slots.at[e], sems.at[kind, e]).wait()

    later = iota((BLK, BLK), 0) > iota((BLK, BLK), 1)
    empty = jnp.zeros((BLK, DH), BF16)
    steps = range(blocks)
    for h in range(heads):
        lanes = head(h)
        spans = [slice(a * BLK, (a + 1) * BLK) for a in steps]
        both, keys, values = [], [], []
        for a in steps:
            qrot, grad = qrot_ref[spans[a], lanes], grad_ref[spans[a], lanes]
            upper = jnp.concatenate([qrot, empty], axis=1)
            lower = jnp.concatenate([empty, grad], axis=1)
            both.append(jnp.concatenate([upper, lower], axis=0))
            keys.append([krot_ref[spans[b], lanes] for b in range(a + 1)])
            values.append([value_ref[spans[b], lanes] for b in range(a + 1)])
            for l in range(MAXL):
                e = a * MAXL + l
                raw = far_keys[e, :, lanes]
                raw = jnp.concatenate([raw, raw], axis=1)
                keys[a].append(nn(raw, listed_ref[e, h]).astype(BF16))
                values[a].append(far_values[e, :, lanes])
        scores, dprobs, tops = [], [], []
        for a in steps:
            scores.append([])
            dprobs.append([])
            top = None
            for b in range(a + 1 + MAXL):
                pair = nt(jnp.concatenate([keys[a][b], values[a][b]], axis=1), both[a])
                part = pair[:, :BLK] * log_scale
                if b == a:
                    part = jnp.where(later, -jnp.inf, part)
                scores[a].append(part)
                dprobs[a].append(pair[:, BLK:])
                top = part if top is None else jnp.maximum(top, part)
            tops.append(jnp.max(top, axis=0, keepdims=True))
        weights, inverses, deltas = [], [], []
        for a in steps:
            weights.append([])
            total, inner = None, None
            for part, dprob in zip(scores[a], dprobs[a]):
                weight = jnp.exp2(part - tops[a])
                weights[a].append(weight)
                product = weight * dprob
                total = weight if total is None else total + weight
                inner = product if inner is None else inner + product
            inverses.append(1.0 / jnp.sum(total, axis=0, keepdims=True))
            deltas.append(jnp.sum(inner, axis=0, keepdims=True) * inverses[a])
        dscores, pairs = [], []
        for a in steps:
            dscores.append([])
            pairs.append([])
            for b in range(a + 1 + MAXL):
                probs = weights[a][b] * inverses[a]
                dscore = (probs * (dprobs[a][b] - deltas[a])).astype(BF16)
                dscores[a].append(dscore)
                wide = jnp.concatenate([dscore, probs.astype(BF16)], axis=1)
                pairs[a].append(nn(wide, both[a]))
        for b in steps:
            total = pairs[b][b]
            for a in range(b + 1, blocks):
                total = total + pairs[a][b]
            dk_ref[spans[b], lanes] = total[:, :DH] * scaling
            dv_ref[spans[b], lanes] = total[:, DH:]
        for e in range(entries):
            pair = pairs[e // MAXL][e // MAXL + 1 + e % MAXL]
            dkey, dvalue = (pair[:, :DH] * scaling).astype(BF16), pair[:, DH:].astype(BF16)
            if pieces:
                owner, offset = listed(ints_ref, e, entries)
                distance = owner ^ ints_ref[0]
                at = (distance & 1) * blocks + offset
                payloads[h][at, distance >> 1, :, :DH] += dkey
                payloads[h][at, distance >> 1, :, DH:] += dvalue
            else:
                outs[0][e, :, 2 * h * DH : (2 * h + 1) * DH] = dkey
                outs[0][e, :, (2 * h + 1) * DH : (2 * h + 2) * DH] = dvalue
        halves = []
        for a in steps:
            wide, tall = jnp.concatenate(dscores[a], axis=0), jnp.concatenate(keys[a], axis=0)
            halves.append(split(tn(wide, tall) * scaling))
        for a in steps:
            dq_top, dq_low = halves[a]
            dq_ref[spans[a], lanes] = nt(dq_top, local_ref[a, h]).astype(BF16)
            query = query_ref[spans[a], lanes]
            query = jnp.concatenate([query, query], axis=0)
            dcum_ref[a, h] = tn(query, jnp.concatenate([dq_top, dq_low], axis=0))
        for i, (first, size) in enumerate(pieces):
            where = outs[i].at[:, :, :, 2 * h * DH : (2 * h + 2) * DH]
            source = payloads[h].at[pl.ds(first, size)]
            copy = pltpu.make_async_copy(source, where, out_sems.at[i, h])
            copy.start()
            out_copies.append(copy)
    for copy in out_copies:
        copy.wait()


def run_attend(ints, sources, places, arrays, heads, blocks, pieces):
    rows, width = arrays[0].shape
    entries = blocks * MAXL
    any_spec = pl.BlockSpec(memory_space=pl.ANY)
    scratch = [
        pltpu.VMEM((entries, BLK, width), BF16),
        pltpu.VMEM((entries, BLK, width), BF16),
        pltpu.SemaphoreType.DMA((2, entries)),
    ]
    if pieces:
        chips = len(places) // 2
        out_parts = [
            jax.ShapeDtypeStruct((size, chips, BLK, 2 * width), BF16) for _, size in pieces
        ]
        part_specs = [any_spec] * len(pieces)
        scratch += [pltpu.VMEM((2 * blocks, chips, BLK, 2 * DH), BF16)] * heads
        scratch += [pltpu.SemaphoreType.DMA((len(pieces), heads))]
    else:
        out_parts = [jax.ShapeDtypeStruct((entries, BLK, 2 * width), BF16)]
        part_specs = in_vmem(1)
    return pl.pallas_call(
        functools.partial(attend_kernel, heads, blocks, places, pieces),
        out_shape=[
            jax.ShapeDtypeStruct((rows, width), BF16),
            jax.ShapeDtypeStruct((blocks, heads, DH, DH), F32),
            jax.ShapeDtypeStruct((rows, width), F32),
            jax.ShapeDtypeStruct((rows, width), F32),
        ]
        + out_parts,
        in_specs=in_smem(1) + [any_spec] * len(sources) + in_vmem(7),
        out_specs=in_vmem(4) + part_specs,
        scratch_shapes=scratch,
        compiler_params=grant(60),
        cost_estimate=cost(15),
        name="attend",
    )(ints, *sources, *arrays)


def merge_kernel(own_ref, got_ref, *refs):
    for i, ref in enumerate(refs[-3:]):
        total = own_ref[0, i + 1].astype(F32) + got_ref[0, i + 1].astype(F32)
        ref[0] = total.astype(BF16)


def run_merge(own, got, first, size, afters):
    _, chips, rows, width = own.shape
    cut = 2
    lanes = width // cut
    whole = pl.BlockSpec((1, chips, rows, lanes), lambda j, c: (first + j, 0, 0, c))
    return pl.pallas_call(
        merge_kernel,
        grid=(size, cut),
        out_shape=[jax.ShapeDtypeStruct((size, rows, width), BF16)] * (chips - 1),
        in_specs=[whole] * 2 + [pl.BlockSpec((16, 128), lambda j, c: (0, 0))] * len(afters),
        out_specs=[pl.BlockSpec((1, rows, lanes), lambda j, c: (j, 0, c))] * (chips - 1),
        compiler_params=grant(60),
        cost_estimate=cost(2),
        name="merge",
    )(own, got, *afters)


def project_kernel(heads, parts, size, layout, flip_ref, after_ref, *refs):
    groups = sum(layout)
    part_refs = refs[: size * parts]
    dk_loc, dv_loc, dq_ref, key_ref, dcum_in, cum_ref = refs[size * parts : size * parts + 6]
    weight_refs = refs[size * parts + 6 : size * parts + 9]
    out_refs = refs[size * parts + 9 : -3]
    dcum_out, tiles, sems = refs[-3:]
    count, _, tile, _ = tiles.shape
    per = count // groups
    copies = []
    for t in range(count):
        m = t // per
        row = ((m + flip_ref[0] * (groups - 1 - 2 * m)) * per + t % per) * tile
        rows = pl.ds(pl.multiple_of(row, tile), tile)
        for w, ref in enumerate(weight_refs):
            copy = pltpu.make_async_copy(ref.at[rows], tiles.at[t, w], sems.at[t, w])
            copy.start()
            copies.append(copy)

    dk_rows, dv_rows = [], []
    for j in range(size):
        here = slice(j * BLK, (j + 1) * BLK)
        dk, dv = [], []
        for h in range(heads):
            both = slice(2 * h * DH, (2 * h + 2) * DH)
            total = part_refs[j * parts][0, :, both].astype(F32)
            for ref in part_refs[j * parts + 1 : (j + 1) * parts]:
                total = total + ref[0, :, both].astype(F32)
            dv.append((dv_loc[here, head(h)] + total[:, DH:]).astype(BF16))
            dk_top, dk_low = split(dk_loc[here, head(h)] + total[:, :DH])
            dk.append(nt(dk_top, cum_ref[j, h]).astype(BF16))
            key = key_ref[here, head(h)]
            key = jnp.concatenate([key, key], axis=0)
            dcum = tn(key, jnp.concatenate([dk_top, dk_low], axis=0))
            dcum_out[j, h] = dcum_in[j, h] + dcum
        dk_rows.append(jnp.concatenate(dk, axis=1))
        dv_rows.append(jnp.concatenate(dv, axis=1))
    grads = (dq_ref[...], jnp.concatenate(dk_rows, axis=0), jnp.concatenate(dv_rows, axis=0))

    for t in range(count):
        term = None
        for w, grad in enumerate(grads):
            copies[3 * t + w].wait()
            part = nt(tiles[t, w], grad)
            term = part if term is None else term + part
        term = term.T.astype(BF16)
        m, spot = t // per, slice(t % per * tile, (t % per + 1) * tile)
        ends = [sum(layout[: i + 1]) for i in range(len(layout))]
        at = next(i for i, end in enumerate(ends) if m < end)
        out_refs[at][m - ends[at] + layout[at], :, spot] = term


def run_project(
    block, layout, flip, after, parts, dk_loc, dv_loc, dq, key_rows, dcum, cum, weights
):
    size, groups = len(parts), sum(layout)
    width = dq.shape[1]
    heads = width // DH
    model = weights[0].shape[0]
    chunk = model // groups
    tile = min(512, chunk)

    def part_spec(index):
        return pl.BlockSpec((1, BLK, 2 * width), lambda t: (index, 0, 0))

    def whole(*shape):
        return pl.BlockSpec(shape, lambda t: (0,) * len(shape))

    rows_spec = pl.BlockSpec((size * BLK, width), lambda t: (block // size, 0))
    head_spec = pl.BlockSpec((size, heads, DH, DH), lambda t: (block // size, 0, 0, 0))
    flat = [part for row in parts for part in row]
    rows = size * BLK
    return pl.pallas_call(
        functools.partial(project_kernel, heads, len(parts[0]), size, layout),
        grid=(1,),
        in_specs=in_smem(1)
        + [whole(16, 128)]
        + [part_spec(index) for _, index in flat]
        + [rows_spec] * 4
        + [head_spec] * 2
        + [pl.BlockSpec(memory_space=pl.ANY)] * 3,
        out_specs=[whole(count, rows, chunk) for count in layout] + [whole(size, heads, DH, DH)],
        scratch_shapes=[
            pltpu.VMEM((model // tile, 3, tile, width), BF16),
            pltpu.SemaphoreType.DMA((model // tile, 3)),
        ],
        out_shape=[jax.ShapeDtypeStruct((count, rows, chunk), BF16) for count in layout]
        + [jax.ShapeDtypeStruct((size, heads, DH, DH), F32)],
        compiler_params=grant(60),
        cost_estimate=cost(12),
        name="project",
    )(
        flip,
        after,
        *[part for part, _ in flat],
        dk_loc,
        dv_loc,
        dq,
        key_rows,
        dcum,
        cum,
        *weights,
    )


def adjoint_kernel(heads, blocks, ints_ref, after_ref, *refs):
    dcums = [ref.at[j] for ref in refs[:-4] for j in range(ref.shape[0])]
    unit_ref, rows_ref, inv_ref, out_ref = refs[-4:]
    count, width = unit_ref.shape
    stacked = (blocks * count, count)
    eye = (iota((count, count), 0) == iota((count, count), 1)).astype(F32)
    base = ints_ref[0] * blocks
    level, col = iota(stacked, 0), iota(stacked, 1)
    row = level % count
    mine = base + level // count
    alive = row[:, :1] <= mine[:, :1]
    for h in range(heads):
        units, rows, inverse = unit_ref[:, head(h)], rows_ref[:, head(h)], inv_ref[h]
        inverse_t = nt_high(eye, inverse)
        moved = jnp.concatenate([nt_high(rows, dcum[h]) for dcum in dcums], axis=0)
        overlap = jnp.where(col <= mine, nt_high(moved, units), 0.0)
        gamma = nn_high(overlap, inverse)
        gamma = jnp.where((row < col) & (col <= mine), gamma, 0.0)
        beta = jnp.concatenate([eye - inverse_t] * blocks, axis=0)
        beta = jnp.where(col <= mine, beta, 0.0)
        x_all = jnp.where(alive, moved - 2.0 * nn_high(gamma, units), 0.0)
        turned = jnp.concatenate([units] * blocks, axis=0) - nn_high(beta, units)
        turned = jnp.where(alive, turned, 0.0)
        x_total, y_total = None, None
        for j, dcum in enumerate(dcums):
            here = slice(j * count, (j + 1) * count)
            y_part = nn_high(turned[here], dcum[h])
            x_total = x_all[here] if j == 0 else x_total + x_all[here]
            y_total = y_part if j == 0 else y_total + y_part
        out_ref[:, head(h)] = x_total
        out_ref[:, slice(width + h * DH, width + (h + 1) * DH)] = y_total


def run_adjoint(ints, after, dcums, unit, rows, inverse, heads, blocks):
    count, width = unit.shape
    return pl.pallas_call(
        functools.partial(adjoint_kernel, heads, blocks),
        out_shape=jax.ShapeDtypeStruct((count, 2 * width), F32),
        in_specs=in_smem(1) + [pl.BlockSpec(memory_space=pl.ANY)] + in_vmem(len(dcums) + 3),
        out_specs=pl.BlockSpec(memory_space=pltpu.VMEM),
        compiler_params=grant(60),
        cost_estimate=cost(2),
        name="adjoint",
    )(ints, after, *dcums, unit, rows, inverse)


def house_kernel(heads, blocks, base_ref, got_ref, unit_ref, rows_ref, house_ref, out_ref):
    count, width = unit_ref.shape
    total = jnp.sum(got_ref[...], axis=0)
    for h in range(heads):
        x_part = total[:, head(h)]
        y_part = total[:, slice(width + h * DH, width + (h + 1) * DH)]
        along = nt_high(y_part, rows_ref[:, head(h)])
        spot = iota((blocks, count), 0) + base_ref[0] * blocks
        along = jnp.where(iota((blocks, count), 1) < spot, along, 0.0)
        turned = y_part - 2.0 * nn_high(along, unit_ref[:, head(h)])
        dunit = -2.0 * (x_part + turned)
        house = house_ref[:, head(h)]
        lengths = jnp.sqrt(jnp.sum(house * house, axis=1, keepdims=True) + 1e-06)
        unit = house / lengths
        inner = jnp.sum(unit * dunit, axis=1, keepdims=True)
        out_ref[:, head(h)] = (dunit - unit * inner) / lengths


def run_house(ints, got, unit, rows, house_dirs, heads, blocks):
    return pl.pallas_call(
        functools.partial(house_kernel, heads, blocks),
        out_shape=jax.ShapeDtypeStruct(house_dirs.shape, F32),
        in_specs=[pl.BlockSpec(memory_space=pltpu.SMEM)] + in_vmem(4),
        out_specs=pl.BlockSpec(memory_space=pltpu.VMEM),
        compiler_params=grant(60),
        cost_estimate=cost(2),
        name="house_grad",
    )(ints, got, unit, rows, house_dirs)


def hop(value, distance, count):
    return lax.ppermute(value, "ctx", [(i, i ^ distance) for i in range(count)])


def slide(value, pairs):
    return lax.ppermute(value, "head", pairs)


def fold_kernel(rest_ref, inward_ref, after_ref, out_ref):
    out_ref[...] = (rest_ref[...].astype(F32) + inward_ref[...].astype(F32)).astype(BF16)


def run_fold(rest, inward, after):
    count, rows, width = rest.shape
    later = pl.BlockSpec((1, rows, width), lambda t: (t + 1, 0, 0))
    return pl.pallas_call(
        fold_kernel,
        grid=(count - 1,),
        out_shape=jax.ShapeDtypeStruct((count - 1, rows, width), BF16),
        in_specs=[later, later, pl.BlockSpec((16, 128), lambda t: (0, 0))],
        out_specs=pl.BlockSpec((1, rows, width), lambda t: (t, 0, 0)),
        compiler_params=grant(60),
        cost_estimate=cost(2),
        name="fold",
    )(rest, inward, after)


INWARD = [(0, 1), (3, 2)]
MIDDLE = [(1, 2), (2, 1)]
OUTWARD = [(1, 0), (2, 3)]


def line_scatter(first, rest, inward, after):
    place = lax.axis_index("head")
    ends = (place == 0) | (place == 3)
    swapped = slide(run_fold(rest, inward, after), MIDDLE)
    outward = slide(first + swapped[1:], OUTWARD)
    total = jnp.where(ends, first, rest[:1]).astype(F32) + inward[:1].astype(F32)
    total = total + swapped[:1].astype(F32) + outward.astype(F32)
    return total[0].astype(BF16), swapped


def line_scatter_apart(first, near, far, last):
    place = lax.axis_index("head")
    ends = (place == 0) | (place == 3)
    in_last, in_far, in_near = slide(last, INWARD), slide(far, INWARD), slide(near, INWARD)
    swap_last, swap_far = slide(last + in_last, MIDDLE), slide(far + in_far, MIDDLE)
    outward = slide(first + swap_last, OUTWARD)
    total = jnp.where(ends, first, near).astype(F32) + in_near.astype(F32)
    total = total + swap_far.astype(F32) + outward.astype(F32)
    return total[0].astype(BF16)


def shards(
    query_rows, key_rows, value_rows, grad_out, house_dirs, owners, offsets, w_query, w_key, w_value
):
    tok_rows, width = query_rows.shape
    heads, blocks = width // DH, tok_rows // BLK
    ctx_count, groups = lax.axis_size("ctx"), lax.axis_size("head")
    my_index = lax.axis_index("ctx").astype(jnp.int32)
    ints = jnp.concatenate([my_index.reshape(1), owners.reshape(-1), offsets.reshape(-1)])
    by_hand = ctx_count == 8 and groups == 4 and blocks == 4
    core, across, along = 1, 2, 4

    if by_hand:
        other = hop(house_dirs, core, 8)
        upper = (my_index & core) != 0
        low, high = jnp.where(upper, other, house_dirs), jnp.where(upper, house_dirs, other)
        house_pair = jnp.concatenate([low, high], axis=0)
        house_parts = [house_pair] + [hop(house_pair, t, 8) for t in (2, 4, 6)]
        value_x, key_y = hop(value_rows, across, 8), hop(key_rows, along, 8)
        key_late, value_late, *_ = lax.optimization_barrier((key_rows, value_rows, *house_parts))
        key_x, value_y = hop(key_late, across, 8), hop(value_late, along, 8)
        key_d, value_d = hop(key_y, across, 8), hop(value_x, along, 8)
    else:
        house_parts = [lax.all_gather(house_dirs, "ctx", axis=0, tiled=True)]

    unit, rows, inverse, unit_t = run_chain(ints, house_parts, heads)
    qrot, krot, local, listed_cum = run_rotate(
        ints, rows, unit_t, query_rows, key_rows, heads, blocks
    )
    if by_hand:
        late = lax.optimization_barrier((key_x, value_y, key_d, value_d, qrot))
        siblings = (key_late, value_late, late[0], value_x, key_y, late[1], late[2], late[3])
        siblings = [hop(part, core, 8) for part in siblings]
        own = (key_rows, value_rows, key_x, value_x, key_y, value_y, key_d, value_d)
        sources, places = [], []
        for t in range(4):
            for pair in (own[2 * t : 2 * t + 2], siblings[2 * t : 2 * t + 2]):
                places.append(((len(sources), 0), (len(sources) + 1, 0)))
                sources += pair
    else:
        sources = [lax.all_gather(key_rows, "ctx"), lax.all_gather(value_rows, "ctx")]
        places = [((0, 0), (1, 0))]

    rounds = ((0, 1), (1, blocks - 1), (blocks, 1), (blocks + 1, blocks - 1))
    dq, dcum, dk_loc, dv_loc, *outs = run_attend(
        ints,
        sources,
        places,
        (query_rows, qrot, krot, value_rows, grad_out, local, listed_cum),
        heads,
        blocks,
        rounds if by_hand else (),
    )
    weights = (w_query, w_key, w_value)
    flip = jnp.where(by_hand & (lax.axis_index("head") >= 2), 1, 0).astype(jnp.int32).reshape(1)

    def project(block, layout, after, parts):
        return run_project(
            block, layout, flip, after, parts, dk_loc, dv_loc, dq, key_rows, dcum, local, weights
        )

    share = jnp.zeros((tok_rows, w_query.shape[0] // groups), BF16)
    if by_hand:
        got = hop(outs[2], core, 8)
        got = [got, hop(lax.optimization_barrier((outs[3], got))[0], core, 8)]

        def give_back(j, afters):
            source, first = min(j, 1), max(j - 1, 0)
            sent = run_merge(outs[source], got[source], first, 1, [part[0] for part in afters])
            back = [hop(part, t, 8) for part, t in zip(sent, (across, along, across + along))]
            near = [part.reshape(-1, BLK, 2 * width) for part in (outs[source], got[source])]
            return [(part, 4 * first) for part in near] + [(part, 0) for part in back], sent, back

        joint, apart = (1, groups - 1), (1,) * groups
        parts_0, _, back_0 = give_back(0, [])
        parts_1, sent_1, back_1 = give_back(1, back_0)
        *terms_0, dcum_0 = project(0, joint, sent_1[2][0], [parts_0])
        inward_0 = slide(terms_0[1], INWARD)
        parts_2, sent_2, back_2 = give_back(2, back_1 + [terms_0[1]])
        *terms_1, dcum_1 = project(1, joint, sent_2[2][0], [parts_1])
        inward_1 = slide(terms_1[1], INWARD)
        parts_3, _, back_3 = give_back(3, back_2 + [terms_1[1], inward_0])
        *terms_2, dcum_2 = project(2, apart, inward_1[0], [parts_2, parts_3])
        done_0, _ = line_scatter(*terms_0, inward_0, back_3[2][0])
        done_1, swapped = line_scatter(*terms_1, inward_1, back_3[2][0])
        done_2 = line_scatter_apart(*terms_2)
        late = swapped[0]
        dcums = [dcum_0, dcum_1, dcum_2]
        for j, done in enumerate((done_0, done_1, done_2)):
            share = lax.dynamic_update_slice(share, done, (j * BLK, 0))
    else:
        spots = (owners * blocks + offsets).reshape(-1)
        empty = jnp.zeros((ctx_count * blocks, BLK, 2 * width), BF16)
        filled = empty.at[spots].add(outs[0])
        back = lax.psum_scatter(filled, "ctx", scatter_dimension=0, tiled=True)
        late, dcums = key_rows, []
        for j in range(blocks):
            *terms, dcum_out = project(j, (groups,), key_rows, [[(back, j)]])
            dcums.append(dcum_out)
            done = lax.psum_scatter(terms[0], "head", scatter_dimension=0, tiled=False)
            share = lax.dynamic_update_slice(share, done, (j * BLK, 0))

    sums = run_adjoint(ints, late, dcums, unit, rows, inverse, heads, blocks)
    sums = sums.reshape(ctx_count, blocks, 2 * width)
    got = lax.all_to_all(sums, "ctx", split_axis=0, concat_axis=0, tiled=True)
    house_grad = run_house(ints, got, unit, rows, house_dirs, heads, blocks)
    return (share, house_grad)


def solution(mesh):
    placed = (
        P("ctx", "head"),
        P("ctx", "head"),
        P("ctx", "head"),
        P("ctx", "head"),
        P("ctx", "head"),
        P("ctx", None),
        P("ctx", None),
        P(None, "head"),
        P(None, "head"),
        P(None, "head"),
    )
    return jax.shard_map(
        shards,
        mesh=mesh,
        in_specs=placed,
        out_specs=(P("ctx", "head"), P("ctx", "head")),
        check_vma=False,
    )
```

profile of v0, /device:TPU:0, one launch (start us, length us, event | category | flops | bytes accessed | tf_op | source)
XLA Modules:
  0.0 248.3 jit_solution(6574887500165210365)
XLA Ops:
  1.1 2.6 %collective-permute-start.9 = (bf16[512,512]{1,0:T(8,128)(2,1)}, bf16[512,512]{1,0:T(8,128)(2,1)S(1)}, u32[]{:S(2)}, u32[]{:S(2)}) collective-permute-start(bf16[512,512]{1,0:T(8,128)(2,1)} %refs_13_.5), channel_id=1, source_target_pairs={{0,16},{4,20},{8,24},{12,28},{16,0},{20,4},{24,8},{28,12},{1,17},{... | collective-permute-start | bytes 1572872 | tf_op jit(solution)/shard_map/ppermute | solution.py:577
  8.3 2.9 %collective-permute-start.3 = (f32[8,512]{1,0:T(8,128)S(1)}, f32[8,512]{1,0:T(8,128)S(1)}, u32[]{:S(2)}, u32[]{:S(2)}) collective-permute-start(f32[8,512]{1,0:T(8,128)S(1)} %pad_maximum_fusion.refs_0_), channel_id=1, source_target_pairs={{0,24},{4,28},{8,16},{12,20},{16,8},{20,12},{24,0},{28,4},{1,25},{... | collective-permute-start | bytes 49160 | tf_op jit(solution)/shard_map/ppermute | solution.py:577
  11.9 6.6 %collective-permute-done.1.refs_1_ = f32[8,512]{1,0:T(8,128)S(1)} collective-permute-done((f32[8,512]{1,0:T(8,128)S(1)}, f32[8,512]{1,0:T(8,128)S(1)}, u32[]{:S(2)}, u32[]{:S(2)}) %collective-permute-start.1) | collective-permute-done | bytes 16416 | tf_op jit(solution)/shard_map/ppermute | solution.py:577
  21.6 5.4 %house_chain.1 = (f32[32,512]{1,0:T(8,128)}, f32[32,512]{1,0:T(8,128)}, f32[4,32,32]{2,1,0:T(8,128)}, f32[4,128,32]{2,1,0:T(8,128)}) custom-call(s32[17]{0:T(128)} %pad_add_fusion.ints_ref.refs_0_.base_ref, f32[8,512]{1,0:T(8,128)} %copy-done.10, f32[8,512]{1,0:T(8,128)} %copy-done.37, f32[8,512]{1,0:T(8,128)} %copy-done.38, f32[8,512]{1,0:T(8,128)} %copy-done.39), custom_call_target="tpu_custom_call" | custom-call | flops 6899999744 | bytes 1048576 | tf_op jit(solution)/shard_map/house_chain/pallas_call | solution.py:115
  27.8 3.9 %collective-permute-done.6.refs_5_ = bf16[512,512]{1,0:T(8,128)(2,1)S(1)} collective-permute-done((bf16[512,512]{1,0:T(8,128)(2,1)}, bf16[512,512]{1,0:T(8,128)(2,1)S(1)}, u32[]{:S(2)}, u32[]{:S(2)}) %collective-permute-start.6) | collective-permute-done | bytes 524320 | tf_op jit(solution)/shard_map/ppermute | solution.py:577
  31.8 3.3 %collective-permute-done.8.refs_10_ = bf16[512,512]{1,0:T(8,128)(2,1)S(1)} collective-permute-done((bf16[512,512]{1,0:T(8,128)(2,1)}, bf16[512,512]{1,0:T(8,128)(2,1)S(1)}, u32[]{:S(2)}, u32[]{:S(2)}) %collective-permute-start.8) | collective-permute-done | bytes 524320 | tf_op jit(solution)/shard_map/ppermute | solution.py:577
  35.5 11.0 %rotate.1 = (bf16[512,512]{1,0:T(8,128)(2,1)}, bf16[512,512]{1,0:T(8,128)(2,1)}, bf16[4,4,128,128]{3,2,1,0:T(8,128)(2,1)}, bf16[8,4,256,128]{3,2,1,0:T(8,128)(2,1)}) custom-call(s32[17]{0:T(128)} %pad_add_fusion.ints_ref.refs_0_.base_ref, f32[32,512]{1,0:T(8,128)} %get-tuple-element.50.rows_ref.refs_4_, f32[4,128,32]{2,1,0:T(8,128)} %get-tuple-element.51.unit_t_ref, ...), custom_call_target="tpu_custom_call" | custom-call | flops 10350000128 | bytes 1048576 | tf_op jit(solution)/shard_map/rotate/pallas_call | solution.py:181
  54.8 16.1 %attend.1 = (bf16[512,512]{1,0:T(8,128)(2,1)}, f32[4,4,128,128]{3,2,1,0:T(8,128)}, f32[512,512]{1,0:T(8,128)}, f32[512,512]{1,0:T(8,128)}, bf16[1,4,128,1024]{3,...) custom-call(s32[17]{0:T(128)} %pad_add_fusion.ints_ref.refs_0_.base_, ...), custom_call_target="tpu_custom_call" | custom-call | flops 17250000896 | bytes 1048576 | tf_op jit(solution)/shard_map/attend/pallas_call | solution.py:354
  71.2 2.7 %collective-permute-done.18.got_ref = bf16[1,4,128,1024]{3,2,1,0:T(8,128)(2,1)S(1)} collective-permute-done((bf16[1,4,128,1024]{3,2,1,0:T(8,128)(2,1)}, bf16[1,4,128,1024]{3,2,1,0:T(8,128)(2,1)S(1)}, u32[]{:S(2)}, u32[]{:S(2)}) %collective-permute-start.18) | collective-permute-done | bytes 1048608 | tf_op jit(solution)/shard_map/ppermute | solution.py:577
  81.0 6.0 %collective-permute-done.20.refs_2_ = bf16[1,128,1024]{2,1,0:T(8,128)(2,1)} collective-permute-done((bf16[1,128,1024]{2,1,0:T(8,128)(2,1)}, bf16[1,128,1024]{2,1,0:T(8,128)(2,1)}, u32[]{:S(2)}, u32[]{:S(2)}) %collective-permute-start.20) | collective-permute-done | bytes 262176 | tf_op jit(solution)/shard_map/ppermute | solution.py:577
  86.9 4.4 %collective-permute-done.21.refs_3_ = bf16[1,128,1024]{2,1,0:T(8,128)(2,1)} collective-permute-done((bf16[1,128,1024]{2,1,0:T(8,128)(2,1)}, bf16[1,128,1024]{2,1,0:T(8,128)(2,1)}, u32[]{:S(2)}, u32[]{:S(2)}) %collective-permute-start.21) | collective-permute-done | bytes 262176 | tf_op jit(solution)/shard_map/ppermute | solution.py:577
  100.4 12.8 %project.3 = (bf16[1,128,1024]{2,1,0:T(8,128)(2,1)}, bf16[3,128,1024]{2,1,0:T(8,128)(2,1)}, f32[1,4,128,128]{3,2,1,0:T(8,128)}) custom-call(s32[1]{0:T(128)} %bitcast.flip_ref, bf16[128,1024]{1,0:T(8,128)(2,1)} %bitcast.51, bf16[4,128,1024]{2,1,0:T(8,128)(2,1)} %bitcast.55, bf16[4,128,1024]{2,1,0:T(8,128)(2,1)} %bitcast.41, ...), custom_call_target="tpu_custom_call" | custom-call | flops 13799999488 | bytes 1048576 | tf_op jit(solution)/shard_map/project/pallas_call | solution.py:467
  113.2 3.5 %collective-permute-start.23 = (bf16[3,128,1024]{2,1,0:T(8,128)(2,1)}, bf16[3,128,1024]{2,1,0:T(8,128)(2,1)S(1)}, u32[]{:S(2)}, u32[]{:S(2)}) collective-permute-start(bf16[3,128,1024]{2,1,0:T(8,128)(2,1)} %get-tuple-element.74.rest_ref), channel_id=1, source_target_pairs={{0,1},{3,2},{4,5},{7,6},{8,9},{11,10},{12,13},{15,14},{16,17},{19,... | collective-permute-start | bytes 2359304 | tf_op jit(solution)/shard_map/ppermute | solution.py:581
  121.7 12.9 %project.4 = (bf16[1,128,1024]{2,1,0:T(8,128)(2,1)}, bf16[3,128,1024]{2,1,0:T(8,128)(2,1)}, f32[1,4,128,128]{3,2,1,0:T(8,128)}) custom-call(s32[1]{0:T(128)} %bitcast.flip_ref, bf16[128,1024]{1,0:T(8,128)(2,1)} %bitcast.50, bf16[12,128,1024]{2,1,0:T(8,128)(2,1)} %bitcast.52, bf16[12,128,1024]{2,1,0:T(8,128)(2,1)} %bitcast.38, ...), custom_call_target="tpu_custom_call" | custom-call | flops 13799999488 | bytes 1048576 | tf_op jit(solution)/shard_map/project/pallas_call | solution.py:467
  142.0 6.3 %collective-permute-done.27.refs_2_ = bf16[1,128,1024]{2,1,0:T(8,128)(2,1)S(1)} collective-permute-done((bf16[1,128,1024]{2,1,0:T(8,128)(2,1)S(1)}, bf16[1,128,1024]{2,1,0:T(8,128)(2,1)S(1)}, u32[]{:S(2)}, u32[]{:S(2)}) %collective-permute-start.27) | collective-permute-done | bytes 262176 | tf_op jit(solution)/shard_map/ppermute | solution.py:577
  156.9 6.1 %collective-permute-done.30.refs_9_ = bf16[1,128,1024]{2,1,0:T(8,128)(2,1)S(1)} collective-permute-done((bf16[1,128,1024]{2,1,0:T(8,128)(2,1)}, bf16[1,128,1024]{2,1,0:T(8,128)(2,1)S(1)}, u32[]{:S(2)}, u32[]{:S(2)}) %collective-permute-start.30) | collective-permute-done | bytes 262176 | tf_op jit(solution)/shard_map/ppermute | solution.py:577
  163.0 2.8 %collective-permute-done.36.refs_7_ = bf16[1,128,1024]{2,1,0:T(8,128)(2,1)S(1)} collective-permute-done((bf16[1,128,1024]{2,1,0:T(8,128)(2,1)}, bf16[1,128,1024]{2,1,0:T(8,128)(2,1)S(1)}, u32[]{:S(2)}, u32[]{:S(2)}) %collective-permute-start.36) | collective-permute-done | bytes 262176 | tf_op jit(solution)/shard_map/ppermute | solution.py:577
  167.8 14.1 %project.5 = (bf16[1,256,1024]{2,1,0:T(8,128)(2,1)}, bf16[1,256,1024]{2,1,0:T(8,128)(2,1)}, bf16[1,256,1024]{2,1,0:T(8,128)(2,1)}, bf16[1,256,1024]{2,1,0:T(8,128)(2,1)}, f32[2,4,128,128]{3,2,1,0:T(8,128)}) custom-call(s32[1]{0:T(128)} %bitcast.flip_ref, bf16[128,1024]{1,0:T(8,128)(2,1)} %slice_bitcast_fusion.1.after_ref, bf16[12,128,1024]{2,1,0:T(8,128)(2,1)} %bitcast.53, ...), custom_call_target="tpu_custom_call" | custom-call | flops 13799999488 | bytes 1048576 | tf_op jit(solution)/shard_map/project/pallas_call | solution.py:467
  190.0 5.0 %collective-permute-start.39 = (bf16[1,256,1024]{2,1,0:T(8,128)(2,1)S(1)}, bf16[1,256,1024]{2,1,0:T(8,128)(2,1)S(1)}, u32[]{:S(2)}, u32[]{:S(2)}) collective-permute-start(bf16[1,256,1024]{2,1,0:T(8,128)(2,1)S(1)} %copy-done.4), channel_id=1, source_target_pairs={{0,1},{3,2},{4,5},{7,6},{8,9},{11,10},{12,13},{15,14},{16,17},{19,... | collective-permute-start | bytes 1572872 | tf_op jit(solution)/shard_map/ppermute | solution.py:581
  197.7 7.3 %adjoint.1 = f32[32,1024]{1,0:T(8,128)} custom-call(s32[17]{0:T(128)} %pad_add_fusion.ints_ref.refs_0_.base_ref, bf16[128,1024]{1,0:T(8,128)(2,1)} %get-tuple-element.94.after_ref, f32[1,4,128,128]{3,2,1,0:T(8,128)} %get-tuple-element.89.refs_0_, f32[1,4,128,128]{3,2,1,0:T(8,128)} %get-tuple-element.90.refs_1_, ...), custom_call_target="tpu_custom_call" | custom-call | flops 2300000000 | bytes 1048576 | tf_op jit(solution)/shard_map/adjoint/pallas_call | solution.py:535
  206.6 3.4 %all-to-all-start = ((f32[8,4,1024]{2,1,0:T(4,128)}), f32[8,4,1024]{2,1,0:T(4,128)S(1)}, u32[]{:S(2)}, u32[]{:S(2)}) async-start(f32[8,4,1024]{2,1,0:T(4,128)} %reshape.46), calls=%async_computation | async-start | bytes 262144 | tf_op jit(solution)/shard_map/all_to_all | solution.py:732
  213.0 8.6 %collective-permute-start.38 = (bf16[1,256,1024]{2,1,0:T(8,128)(2,1)}, bf16[1,256,1024]{2,1,0:T(8,128)(2,1)}, u32[]{:S(2)}, u32[]{:S(2)}) collective-permute-start(bf16[1,256,1024]{2,1,0:T(8,128)(2,1)} %get-tuple-element.86), channel_id=1, source_target_pairs={{0,1},{3,2},{4,5},{7,6},{8,9},{11,10},{12,13},{15,14},{16,17},{19,... | collective-permute-start | bytes 1572872 | tf_op jit(solution)/shard_map/ppermute | solution.py:581
  231.8 2.8 %collective-permute-done.35 = bf16[1,128,1024]{2,1,0:T(8,128)(2,1)} collective-permute-done((bf16[1,128,1024]{2,1,0:T(8,128)(2,1)S(1)}, bf16[1,128,1024]{2,1,0:T(8,128)(2,1)}, u32[]{:S(2)}, u32[]{:S(2)}) %collective-permute-start.35) | collective-permute-done | bytes 262176 | tf_op jit(solution)/shard_map/ppermute | solution.py:581
  236.0 9.7 %collective-permute-done.43 = bf16[1,256,1024]{2,1,0:T(8,128)(2,1)S(1)} collective-permute-done((bf16[1,256,1024]{2,1,0:T(8,128)(2,1)S(1)}, bf16[1,256,1024]{2,1,0:T(8,128)(2,1)S(1)}, u32[]{:S(2)}, u32[]{:S(2)}) %collective-permute-start.43) | collective-permute-done | bytes 524320 | tf_op jit(solution)/shard_map/ppermute | solution.py:581
  (181 shorter events, 87.2 us)
Async XLA Ops:
  1.1 25.9 %collective-permute-start.9 = (bf16[512,512]{1,0:T(8,128)(2,1)}, bf16[512,512]{1,0:T(8,128)(2,1)S(1)}, u32[]{:S(2)}, u32[]{:S(2)}) collective-permute-start(bf16[512,512]{1,0:T(8,128)(2,1)} %refs_13_.5), channel_id=1, source_target_pairs={{0,16},{4,20},{8,24},{12,28},{16,0},{20,4},{24,8},{28,12},{1,17},{... | collective-permute-start | bytes 1572872 | tf_op jit(solution)/shard_map/ppermute | solution.py:577
  3.7 23.6 %collective-permute-start.7 = (bf16[512,512]{1,0:T(8,128)(2,1)}, bf16[512,512]{1,0:T(8,128)(2,1)S(1)}, u32[]{:S(2)}, u32[]{:S(2)}) collective-permute-start(bf16[512,512]{1,0:T(8,128)(2,1)} %refs_20_.1), channel_id=1, source_target_pairs={{0,8},{4,12},{8,0},{12,4},{16,24},{20,28},{24,16},{28,20},{1,9},{5... | collective-permute-start | bytes 1572872 | tf_op jit(solution)/shard_map/ppermute | solution.py:577
  20.1 28.7 %collective-permute-start.4 = (bf16[512,512]{1,0:T(8,128)(2,1)}, bf16[512,512]{1,0:T(8,128)(2,1)S(1)}, u32[]{:S(2)}, u32[]{:S(2)}) collective-permute-start(bf16[512,512]{1,0:T(8,128)(2,1)} %refs_13_.5), channel_id=1, source_target_pairs={{0,4},{4,0},{8,12},{12,8},{16,20},{20,16},{24,28},{28,24},{1,5},{5... | collective-permute-start | bytes 1572872 | tf_op jit(solution)/shard_map/ppermute | solution.py:577
  20.1 14.9 %collective-permute-start.8 = (bf16[512,512]{1,0:T(8,128)(2,1)}, bf16[512,512]{1,0:T(8,128)(2,1)S(1)}, u32[]{:S(2)}, u32[]{:S(2)}) collective-permute-start(bf16[512,512]{1,0:T(8,128)(2,1)} %refs_20_.1), channel_id=1, source_target_pairs={{0,16},{4,20},{8,24},{12,28},{16,0},{20,4},{24,8},{28,12},{1,17},{... | collective-permute-start | bytes 1572872 | tf_op jit(solution)/shard_map/ppermute | solution.py:577
  27.0 21.9 %collective-permute-start.5 = (bf16[512,512]{1,0:T(8,128)(2,1)S(1)}, bf16[512,512]{1,0:T(8,128)(2,1)S(1)}, u32[]{:S(2)}, u32[]{:S(2)}) collective-permute-start(bf16[512,512]{1,0:T(8,128)(2,1)S(1)} %copy-done.13), channel_id=1, source_target_pairs={{0,4},{4,0},{8,12},{12,8},{16,20},{20,16},{24,28},{28,24},{1,5},{5... | collective-permute-start | bytes 1572872 | tf_op jit(solution)/shard_map/ppermute | solution.py:577
  27.3 21.0 %collective-permute-start.11 = (bf16[512,512]{1,0:T(8,128)(2,1)S(1)}, bf16[512,512]{1,0:T(8,128)(2,1)}, u32[]{:S(2)}, u32[]{:S(2)}) collective-permute-start(bf16[512,512]{1,0:T(8,128)(2,1)S(1)} %collective-permute-done.7.refs_6_), channel_id=1, source_target_pairs={{0,16},{4,20},{8,24},{12,28},{16,0},{20,4},{24,8},{28,12},{1,17},{... | collective-permute-start | bytes 1572872 | tf_op jit(solution)/shard_map/ppermute | solution.py:577
  31.8 17.6 %collective-permute-start.13 = (bf16[512,512]{1,0:T(8,128)(2,1)S(1)}, bf16[512,512]{1,0:T(8,128)(2,1)}, u32[]{:S(2)}, u32[]{:S(2)}) collective-permute-start(bf16[512,512]{1,0:T(8,128)(2,1)S(1)} %collective-permute-done.7.refs_6_), channel_id=1, source_target_pairs={{0,4},{4,0},{8,12},{12,8},{16,20},{20,16},{24,28},{28,24},{1,5},{5... | collective-permute-start | bytes 1572872 | tf_op jit(solution)/shard_map/ppermute | solution.py:577
  75.0 17.9 %collective-permute-start.19 = (bf16[3,4,128,1024]{3,2,1,0:T(8,128)(2,1)}, bf16[3,4,128,1024]{3,2,1,0:T(8,128)(2,1)S(1)}, u32[]{:S(2)}, u32[]{:S(2)}) collective-permute-start(bf16[3,4,128,1024]{3,2,1,0:T(8,128)(2,1)} %get-tuple-element.63), channel_id=1, source_target_pairs={{0,4},{4,0},{8,12},{12,8},{16,20},{20,16},{24,28},{28,24},{1,5},{5... | collective-permute-start | bytes 9437192 | tf_op jit(solution)/shard_map/ppermute | solution.py:577
  78.0 13.3 %collective-permute-start.21 = (bf16[1,128,1024]{2,1,0:T(8,128)(2,1)}, bf16[1,128,1024]{2,1,0:T(8,128)(2,1)}, u32[]{:S(2)}, u32[]{:S(2)}) collective-permute-start(bf16[1,128,1024]{2,1,0:T(8,128)(2,1)} %get-tuple-element.66), channel_id=1, source_target_pairs={{0,16},{4,20},{8,24},{12,28},{16,0},{20,4},{24,8},{28,12},{1,17},{... | collective-permute-start | bytes 786440 | tf_op jit(solution)/shard_map/ppermute | solution.py:577
  79.5 13.4 %collective-permute-start.22 = (bf16[1,128,1024]{2,1,0:T(8,128)(2,1)}, bf16[1,128,1024]{2,1,0:T(8,128)(2,1)}, u32[]{:S(2)}, u32[]{:S(2)}) collective-permute-start(bf16[1,128,1024]{2,1,0:T(8,128)(2,1)} %get-tuple-element.67), channel_id=1, source_target_pairs={{0,24},{4,28},{8,16},{12,20},{16,8},{20,12},{24,0},{28,4},{1,25},{... | collective-permute-start | bytes 786440 | tf_op jit(solution)/shard_map/ppermute | solution.py:577
  96.9 21.5 %collective-permute-start.26 = (bf16[1,128,1024]{2,1,0:T(8,128)(2,1)}, bf16[1,128,1024]{2,1,0:T(8,128)(2,1)S(1)}, u32[]{:S(2)}, u32[]{:S(2)}) collective-permute-start(bf16[1,128,1024]{2,1,0:T(8,128)(2,1)} %get-tuple-element.68), channel_id=1, source_target_pairs={{0,24},{4,28},{8,16},{12,20},{16,8},{20,12},{24,0},{28,4},{1,25},{... | collective-permute-start | bytes 786440 | tf_op jit(solution)/shard_map/ppermute | solution.py:577
  98.7 19.7 %collective-permute-start.24 = (bf16[1,128,1024]{2,1,0:T(8,128)(2,1)}, bf16[1,128,1024]{2,1,0:T(8,128)(2,1)S(1)}, u32[]{:S(2)}, u32[]{:S(2)}) collective-permute-start(bf16[1,128,1024]{2,1,0:T(8,128)(2,1)} %get-tuple-element.75), channel_id=1, source_target_pairs={{0,8},{4,12},{8,0},{12,4},{16,24},{20,28},{24,16},{28,20},{1,9},{5... | collective-permute-start | bytes 786440 | tf_op jit(solution)/shard_map/ppermute | solution.py:577
  99.2 19.2 %collective-permute-start.25 = (bf16[1,128,1024]{2,1,0:T(8,128)(2,1)}, bf16[1,128,1024]{2,1,0:T(8,128)(2,1)S(1)}, u32[]{:S(2)}, u32[]{:S(2)}) collective-permute-start(bf16[1,128,1024]{2,1,0:T(8,128)(2,1)} %get-tuple-element.76), channel_id=1, source_target_pairs={{0,16},{4,20},{8,24},{12,28},{16,0},{20,4},{24,8},{28,12},{1,17},{... | collective-permute-start | bytes 786440 | tf_op jit(solution)/shard_map/ppermute | solution.py:577
  113.2 28.0 %collective-permute-start.23 = (bf16[3,128,1024]{2,1,0:T(8,128)(2,1)}, bf16[3,128,1024]{2,1,0:T(8,128)(2,1)S(1)}, u32[]{:S(2)}, u32[]{:S(2)}) collective-permute-start(bf16[3,128,1024]{2,1,0:T(8,128)(2,1)} %get-tuple-element.74.rest_ref), channel_id=1, source_target_pairs={{0,1},{3,2},{4,5},{7,6},{8,9},{11,10},{12,13},{15,14},{16,17},{19,... | collective-permute-start | bytes 2359304 | tf_op jit(solution)/shard_map/ppermute | solution.py:581
  134.6 21.5 %collective-permute-start.33 = (bf16[3,128,1024]{2,1,0:T(8,128)(2,1)}, bf16[3,128,1024]{2,1,0:T(8,128)(2,1)S(1)}, u32[]{:S(2)}, u32[]{:S(2)}) collective-permute-start(bf16[3,128,1024]{2,1,0:T(8,128)(2,1)} %get-tuple-element.80.rest_ref), channel_id=1, source_target_pairs={{0,1},{3,2},{4,5},{7,6},{8,9},{11,10},{12,13},{15,14},{16,17},{19,... | collective-permute-start | bytes 2359304 | tf_op jit(solution)/shard_map/ppermute | solution.py:581
  181.9 14.1 %collective-permute-start.41 = (bf16[1,256,1024]{2,1,0:T(8,128)(2,1)}, bf16[1,256,1024]{2,1,0:T(8,128)(2,1)S(1)}, u32[]{:S(2)}, u32[]{:S(2)}) collective-permute-start(bf16[1,256,1024]{2,1,0:T(8,128)(2,1)} %get-tuple-element.88), channel_id=1, source_target_pairs={{0,1},{3,2},{4,5},{7,6},{8,9},{11,10},{12,13},{15,14},{16,17},{19,... | collective-permute-start | bytes 1572872 | tf_op jit(solution)/shard_map/ppermute | solution.py:581
  188.6 21.4 %collective-permute-start.31 = (bf16[2,128,1024]{2,1,0:T(8,128)(2,1)}, bf16[2,128,1024]{2,1,0:T(8,128)(2,1)}, u32[]{:S(2)}, u32[]{:S(2)}) collective-permute-start(bf16[2,128,1024]{2,1,0:T(8,128)(2,1)} %fold.2), channel_id=1, source_target_pairs={{1,2},{2,1},{5,6},{6,5},{9,10},{10,9},{13,14},{14,13},{17,18},{18,... | collective-permute-start | bytes 1572872 | tf_op jit(solution)/shard_map/ppermute | solution.py:581
  190.0 31.6 %collective-permute-start.39 = (bf16[1,256,1024]{2,1,0:T(8,128)(2,1)S(1)}, bf16[1,256,1024]{2,1,0:T(8,128)(2,1)S(1)}, u32[]{:S(2)}, u32[]{:S(2)}) collective-permute-start(bf16[1,256,1024]{2,1,0:T(8,128)(2,1)S(1)} %copy-done.4), channel_id=1, source_target_pairs={{0,1},{3,2},{4,5},{7,6},{8,9},{11,10},{12,13},{15,14},{16,17},{19,... | collective-permute-start | bytes 1572872 | tf_op jit(solution)/shard_map/ppermute | solution.py:581
  196.3 32.5 %collective-permute-start.42 = (bf16[1,256,1024]{2,1,0:T(8,128)(2,1)S(1)}, bf16[1,256,1024]{2,1,0:T(8,128)(2,1)S(1)}, u32[]{:S(2)}, u32[]{:S(2)}) collective-permute-start(bf16[1,256,1024]{2,1,0:T(8,128)(2,1)S(1)} %add.55), channel_id=1, source_target_pairs={{1,2},{2,1},{5,6},{6,5},{9,10},{10,9},{13,14},{14,13},{17,18},{18,... | collective-permute-start | bytes 1572872 | tf_op jit(solution)/shard_map/ppermute | solution.py:581
  206.6 18.9 %all-to-all-start = ((f32[8,4,1024]{2,1,0:T(4,128)}), f32[8,4,1024]{2,1,0:T(4,128)S(1)}, u32[]{:S(2)}, u32[]{:S(2)}) async-start(f32[8,4,1024]{2,1,0:T(4,128)} %reshape.46), calls=%async_computation | async-start | bytes 262144 | tf_op jit(solution)/shard_map/all_to_all | solution.py:732
  211.7 18.5 %collective-permute-start.32 = (bf16[1,128,1024]{2,1,0:T(8,128)(2,1)}, bf16[1,128,1024]{2,1,0:T(8,128)(2,1)}, u32[]{:S(2)}, u32[]{:S(2)}) collective-permute-start(bf16[1,128,1024]{2,1,0:T(8,128)(2,1)} %slice_add_fusion.1), channel_id=1, source_target_pairs={{1,0},{2,3},{5,4},{6,7},{9,8},{10,11},{13,12},{14,15},{17,16},{18,... | collective-permute-start | bytes 786440 | tf_op jit(solution)/shard_map/ppermute | solution.py:581
  213.0 22.9 %collective-permute-start.38 = (bf16[1,256,1024]{2,1,0:T(8,128)(2,1)}, bf16[1,256,1024]{2,1,0:T(8,128)(2,1)}, u32[]{:S(2)}, u32[]{:S(2)}) collective-permute-start(bf16[1,256,1024]{2,1,0:T(8,128)(2,1)} %get-tuple-element.86), channel_id=1, source_target_pairs={{0,1},{3,2},{4,5},{7,6},{8,9},{11,10},{12,13},{15,14},{16,17},{19,... | collective-permute-start | bytes 1572872 | tf_op jit(solution)/shard_map/ppermute | solution.py:581
  222.6 13.4 %collective-permute-start.40 = (bf16[1,256,1024]{2,1,0:T(8,128)(2,1)}, bf16[1,256,1024]{2,1,0:T(8,128)(2,1)}, u32[]{:S(2)}, u32[]{:S(2)}) collective-permute-start(bf16[1,256,1024]{2,1,0:T(8,128)(2,1)} %add.53), channel_id=1, source_target_pairs={{1,2},{2,1},{5,6},{6,5},{9,10},{10,9},{13,14},{14,13},{17,18},{18,... | collective-permute-start | bytes 1572872 | tf_op jit(solution)/shard_map/ppermute | solution.py:581
  229.0 16.7 %collective-permute-start.43 = (bf16[1,256,1024]{2,1,0:T(8,128)(2,1)S(1)}, bf16[1,256,1024]{2,1,0:T(8,128)(2,1)S(1)}, u32[]{:S(2)}, u32[]{:S(2)}) collective-permute-start(bf16[1,256,1024]{2,1,0:T(8,128)(2,1)S(1)} %add.56), channel_id=1, source_target_pairs={{1,0},{2,3},{5,4},{6,7},{9,8},{10,11},{13,12},{14,15},{17,16},{18,... | collective-permute-start | bytes 1572872 | tf_op jit(solution)/shard_map/ppermute | solution.py:581
  (61 other events, 471.2 us)
where the time goes:
time: 249 us; the launch traced here: 248 us
  Pallas kernels  95.6 us (38%)
  waiting for transfers between devices  65.2 us (26%)
  starting transfers between devices  60.3 us (24%)
  local copies, waits for them, and re-layouts  16.6 us (7%)
  other arithmetic  9.61 us (4%)
    ppermute x32, waiting for transfers between devices, hop(): return lax.ppermute(value, 'ctx', [(i, i ^ distance) for i in range(count)])  51.6 us
    pallas_call x3, Pallas kernels, run_project(): pl.pallas_call(functools.partial(project_kernel, heads, len(parts[0]), si...  39.7 us
    ppermute x12, starting transfers between devices, slide(): return lax.ppermute(value, 'head', pairs)  28.7 us
    ppermute x32, starting transfers between devices, hop(): return lax.ppermute(value, 'ctx', [(i, i ^ distance) for i in range(count)])  28.2 us
    pallas_call x1, Pallas kernels, run_attend(): pl.pallas_call(functools.partial(attend_kernel, heads, blocks, places, pi...  16.1 us
    ppermute x12, waiting for transfers between devices, slide(): return lax.ppermute(value, 'head', pairs)  13.5 us
    pallas_call x1, Pallas kernels, run_rotate(): pl.pallas_call(functools.partial(rotate_kernel, heads, blocks), out_shape...  11 us
    unnamed x82, local copies, waits for them, and re-layouts  9.79 us
  transfers between devices with their start and end apart: 45, of which 20 were waited for; matrix products, arithmetic and copies ran while one was open for 7% of the time, Pallas kernels for 25%

commit v1 on v0

--- a/solution.py
+++ b/solution.py
@@ -384,7 +384,8 @@
         merge_kernel,
         grid=(size, cut),
         out_shape=[jax.ShapeDtypeStruct((size, rows, width), BF16)] * (chips - 1),
-        in_specs=[whole] * 2 + [pl.BlockSpec((16, 128), lambda j, c: (0, 0))] * len(afters),
+        in_specs=[whole] * 2
+        + [pl.BlockSpec((1, 16, 128), lambda j, c: (0, 0, 0))] * len(afters),
         out_specs=[pl.BlockSpec((1, rows, lanes), lambda j, c: (j, 0, c))] * (chips - 1),
         compiler_params=grant(60),
         cost_estimate=cost(2),
@@ -392,18 +393,22 @@
     )(own, got, *afters)
 
 
-def project_kernel(heads, parts, size, layout, flip_ref, after_ref, *refs):
-    groups = sum(layout)
-    part_refs = refs[: size * parts]
-    dk_loc, dv_loc, dq_ref, key_ref, dcum_in, cum_ref = refs[size * parts : size * parts + 6]
-    weight_refs = refs[size * parts + 6 : size * parts + 9]
-    out_refs = refs[size * parts + 9 : -3]
-    dcum_out, tiles, sems = refs[-3:]
-    count, _, tile, _ = tiles.shape
-    per = count // groups
+def project_kernel(heads, parts, size, groups, chunks, flip_ref, after_ref, *refs):
+    outs = len(chunks)
+    tiles, sems = refs[-2:]
+    per = tiles.shape[0] // outs
+    tile = tiles.shape[2]
+    if parts:
+        part_refs, refs = refs[: size * parts], refs[size * parts :]
+        dk_loc, dv_loc, dq_ref, key_ref, dcum_in, cum_ref = refs[:6]
+        weight_refs, out_refs = refs[6:9], refs[9 : 9 + outs]
+        dcum_out, dk_out, dv_out = refs[9 + outs : 12 + outs]
+    else:
+        dq_ref, dk_ref, dv_ref = refs[:3]
+        weight_refs, out_refs = refs[3:6], refs[6 : 6 + outs]
     copies = []
-    for t in range(count):
-        m = t // per
+    for t in range(outs * per):
+        m = chunks[t // per]
         row = ((m + flip_ref[0] * (groups - 1 - 2 * m)) * per + t % per) * tile
         rows = pl.ds(pl.multiple_of(row, tile), tile)
         for w, ref in enumerate(weight_refs):
@@ -411,48 +416,51 @@
             copy.start()
             copies.append(copy)
 
-    dk_rows, dv_rows = [], []
-    for j in range(size):
-        here = slice(j * BLK, (j + 1) * BLK)
-        dk, dv = [], []
-        for h in range(heads):
-            both = slice(2 * h * DH, (2 * h + 2) * DH)
-            total = part_refs[j * parts][0, :, both].astype(F32)
-            for ref in part_refs[j * parts + 1 : (j + 1) * parts]:
-                total = total + ref[0, :, both].astype(F32)
-            dv.append((dv_loc[here, head(h)] + total[:, DH:]).astype(BF16))
-            dk_top, dk_low = split(dk_loc[here, head(h)] + total[:, :DH])
-            dk.append(nt(dk_top, cum_ref[j, h]).astype(BF16))
-            key = key_ref[here, head(h)]
-            key = jnp.concatenate([key, key], axis=0)
-            dcum = tn(key, jnp.concatenate([dk_top, dk_low], axis=0))
-            dcum_out[j, h] = dcum_in[j, h] + dcum
-        dk_rows.append(jnp.concatenate(dk, axis=1))
-        dv_rows.append(jnp.concatenate(dv, axis=1))
-    grads = (dq_ref[...], jnp.concatenate(dk_rows, axis=0), jnp.concatenate(dv_rows, axis=0))
-
-    for t in range(count):
+    if parts:
+        dk_rows, dv_rows = [], []
+        for j in range(size):
+            here = slice(j * BLK, (j + 1) * BLK)
+            dk, dv = [], []
+            for h in range(heads):
+                both = slice(2 * h * DH, (2 * h + 2) * DH)
+                total = part_refs[j * parts][0, :, both].astype(F32)
+                for ref in part_refs[j * parts + 1 : (j + 1) * parts]:
+                    total = total + ref[0, :, both].astype(F32)
+                dv.append((dv_loc[here, head(h)] + total[:, DH:]).astype(BF16))
+                dk_top, dk_low = split(dk_loc[here, head(h)] + total[:, :DH])
+                dk.append(nt(dk_top, cum_ref[j, h]).astype(BF16))
+                key = key_ref[here, head(h)]
+                key = jnp.concatenate([key, key], axis=0)
+                dcum = tn(key, jnp.concatenate([dk_top, dk_low], axis=0))
+                dcum_out[j, h] = dcum_in[j, h] + dcum
+            dk_rows.append(jnp.concatenate(dk, axis=1))
+            dv_rows.append(jnp.concatenate(dv, axis=1))
+        dk_all, dv_all = jnp.concatenate(dk_rows, axis=0), jnp.concatenate(dv_rows, axis=0)
+        dk_out[...] = dk_all
+        dv_out[...] = dv_all
+        grads = (dq_ref[...], dk_all, dv_all)
+    else:
+        grads = (dq_ref[...], dk_ref[...], dv_ref[...])
+
+    for t in range(outs * per):
         term = None
         for w, grad in enumerate(grads):
             copies[3 * t + w].wait()
             part = nt(tiles[t, w], grad)
             term = part if term is None else term + part
-        term = term.T.astype(BF16)
-        m, spot = t // per, slice(t % per * tile, (t % per + 1) * tile)
-        ends = [sum(layout[: i + 1]) for i in range(len(layout))]
-        at = next(i for i, end in enumerate(ends) if m < end)
-        out_refs[at][m - ends[at] + layout[at], :, spot] = term
-
-
-def run_project(
-    block, layout, flip, after, parts, dk_loc, dv_loc, dq, key_rows, dcum, cum, weights
-):
-    size, groups = len(parts), sum(layout)
+        spot = slice(t % per * tile, (t % per + 1) * tile)
+        out_refs[t // per][0, :, spot] = term.T.astype(BF16)
+
+
+def run_project(block, size, groups, chunks, flip, after, parts, finished, arrays, weights):
+    dk_loc, dv_loc, dq, key_rows, dcum, cum = arrays
     width = dq.shape[1]
     heads = width // DH
     model = weights[0].shape[0]
     chunk = model // groups
     tile = min(512, chunk)
+    rows = size * BLK
+    tile_count = len(chunks) * chunk // tile
 
     def part_spec(index):
         return pl.BlockSpec((1, BLK, 2 * width), lambda t: (index, 0, 0))
@@ -460,41 +468,39 @@
     def whole(*shape):
         return pl.BlockSpec(shape, lambda t: (0,) * len(shape))
 
-    rows_spec = pl.BlockSpec((size * BLK, width), lambda t: (block // size, 0))
+    rows_spec = pl.BlockSpec((rows, width), lambda t: (block // size, 0))
     head_spec = pl.BlockSpec((size, heads, DH, DH), lambda t: (block // size, 0, 0, 0))
     flat = [part for row in parts for part in row]
-    rows = size * BLK
-    return pl.pallas_call(
-        functools.partial(project_kernel, heads, len(parts[0]), size, layout),
+    out_specs = [whole(1, rows, chunk)] * len(chunks)
+    out_shape = [jax.ShapeDtypeStruct((1, rows, chunk), BF16)] * len(chunks)
+    if parts:
+        in_specs = [part_spec(index) for _, index in flat] + [rows_spec] * 4 + [head_spec] * 2
+        inputs = [part for part, _ in flat] + [dk_loc, dv_loc, dq, key_rows, dcum, cum]
+        out_specs += [whole(size, heads, DH, DH)] + [whole(rows, width)] * 2
+        out_shape += [jax.ShapeDtypeStruct((size, heads, DH, DH), F32)]
+        out_shape += [jax.ShapeDtypeStruct((rows, width), BF16)] * 2
+    else:
+        in_specs = [rows_spec] + [whole(rows, width)] * 2
+        inputs = [dq, *finished]
+    return pl.pallas_call(
+        functools.partial(
+            project_kernel, heads, len(parts[0]) if parts else 0, size, groups, chunks
+        ),
         grid=(1,),
         in_specs=in_smem(1)
-        + [whole(16, 128)]
-        + [part_spec(index) for _, index in flat]
-        + [rows_spec] * 4
-        + [head_spec] * 2
+        + [whole(1, 16, 128)]
+        + in_specs
         + [pl.BlockSpec(memory_space=pl.ANY)] * 3,
-        out_specs=[whole(count, rows, chunk) for count in layout] + [whole(size, heads, DH, DH)],
+        out_specs=out_specs,
         scratch_shapes=[
-            pltpu.VMEM((model // tile, 3, tile, width), BF16),
-            pltpu.SemaphoreType.DMA((model // tile, 3)),
+            pltpu.VMEM((tile_count, 3, tile, width), BF16),
+            pltpu.SemaphoreType.DMA((tile_count, 3)),
         ],
-        out_shape=[jax.ShapeDtypeStruct((count, rows, chunk), BF16) for count in layout]
-        + [jax.ShapeDtypeStruct((size, heads, DH, DH), F32)],
-        compiler_params=grant(60),
-        cost_estimate=cost(12),
+        out_shape=out_shape,
+        compiler_params=grant(60),
+        cost_estimate=cost(3 * len(chunks)),
         name="project",
-    )(
-        flip,
-        after,
-        *[part for part, _ in flat],
-        dk_loc,
-        dv_loc,
-        dq,
-        key_rows,
-        dcum,
-        cum,
-        *weights,
-    )
+    )(flip, after, *inputs, *weights)
 
 
 def adjoint_kernel(heads, blocks, ints_ref, after_ref, *refs):
@@ -581,49 +587,62 @@
     return lax.ppermute(value, "head", pairs)
 
 
-def fold_kernel(rest_ref, inward_ref, after_ref, out_ref):
-    out_ref[...] = (rest_ref[...].astype(F32) + inward_ref[...].astype(F32)).astype(BF16)
-
-
-def run_fold(rest, inward, after):
-    count, rows, width = rest.shape
-    later = pl.BlockSpec((1, rows, width), lambda t: (t + 1, 0, 0))
-    return pl.pallas_call(
-        fold_kernel,
-        grid=(count - 1,),
-        out_shape=jax.ShapeDtypeStruct((count - 1, rows, width), BF16),
-        in_specs=[later, later, pl.BlockSpec((16, 128), lambda t: (0, 0))],
-        out_specs=pl.BlockSpec((1, rows, width), lambda t: (t, 0, 0)),
-        compiler_params=grant(60),
-        cost_estimate=cost(2),
-        name="fold",
-    )(rest, inward, after)
-
-
 INWARD = [(0, 1), (3, 2)]
 MIDDLE = [(1, 2), (2, 1)]
 OUTWARD = [(1, 0), (2, 3)]
 
 
-def line_scatter(first, rest, inward, after):
+def near_kernel(ends_ref, first_ref, near_ref, inward_ref, out_ref):
+    mine = jnp.where(ends_ref[0] > 0, first_ref[0], near_ref[0]).astype(F32)
+    out_ref[...] = mine + inward_ref[0].astype(F32)
+
+
+def run_near(ends, first, near, inward):
+    return pl.pallas_call(
+        near_kernel,
+        out_shape=jax.ShapeDtypeStruct(first.shape[1:], F32),
+        in_specs=in_smem(1) + in_vmem(3),
+        out_specs=pl.BlockSpec(memory_space=pltpu.VMEM),
+        compiler_params=grant(60),
+        cost_estimate=cost(16),
+        name="near_sum",
+    )(ends, first, near, inward)
+
+
+def line_scatter(share, first, near, far, last):
     place = lax.axis_index("head")
-    ends = (place == 0) | (place == 3)
-    swapped = slide(run_fold(rest, inward, after), MIDDLE)
-    outward = slide(first + swapped[1:], OUTWARD)
-    total = jnp.where(ends, first, rest[:1]).astype(F32) + inward[:1].astype(F32)
-    total = total + swapped[:1].astype(F32) + outward.astype(F32)
-    return total[0].astype(BF16), swapped
-
-
-def line_scatter_apart(first, near, far, last):
-    place = lax.axis_index("head")
-    ends = (place == 0) | (place == 3)
+    ends = ((place == 0) | (place == 3)).astype(jnp.int32).reshape(1)
     in_last, in_far, in_near = slide(last, INWARD), slide(far, INWARD), slide(near, INWARD)
     swap_last, swap_far = slide(last + in_last, MIDDLE), slide(far + in_far, MIDDLE)
     outward = slide(first + swap_last, OUTWARD)
-    total = jnp.where(ends, first, near).astype(F32) + in_near.astype(F32)
-    total = total + swap_far.astype(F32) + outward.astype(F32)
-    return total[0].astype(BF16)
+    total = run_near(ends, first, near, in_near)
+    return run_share(share, total, swap_far, outward), swap_last
+
+
+def share_kernel(*refs):
+    total_ref, far_ref, outward_ref, out_ref = refs[-4:]
+    far = far_ref[0].astype(F32) + outward_ref[0].astype(F32)
+    out_ref[...] = (total_ref[...] + far).astype(BF16)
+
+
+def run_share(share, total, far, outward):
+    rows, width = total.shape
+    place = 0 if share is None else 1
+    tile = min(512, width)
+    part = pl.BlockSpec((1, rows, tile), lambda t: (0, 0, t))
+    given = [] if share is None else [share]
+    return pl.pallas_call(
+        share_kernel,
+        grid=(width // tile,),
+        out_shape=jax.ShapeDtypeStruct((2 * rows, width), BF16),
+        in_specs=[pl.BlockSpec(memory_space=pl.ANY)] * len(given)
+        + [pl.BlockSpec((rows, tile), lambda t: (0, t)), part, part],
+        out_specs=pl.BlockSpec((rows, tile), lambda t: (place, t)),
+        input_output_aliases={0: 0} if given else {},
+        compiler_params=grant(60),
+        cost_estimate=cost(2),
+        name="share",
+    )(*given, total, far, outward)
 
 
 def shards(
@@ -668,7 +687,8 @@
         sources = [lax.all_gather(key_rows, "ctx"), lax.all_gather(value_rows, "ctx")]
         places = [((0, 0), (1, 0))]
 
-    rounds = ((0, 1), (1, blocks - 1), (blocks, 1), (blocks + 1, blocks - 1))
+    half = blocks // 2
+    rounds = tuple((first, half) for first in range(0, 2 * blocks, half))
     dq, dcum, dk_loc, dv_loc, *outs = run_attend(
         ints,
         sources,
@@ -681,50 +701,51 @@
     weights = (w_query, w_key, w_value)
     flip = jnp.where(by_hand & (lax.axis_index("head") >= 2), 1, 0).astype(jnp.int32).reshape(1)
 
-    def project(block, layout, after, parts):
+    arrays = (dk_loc, dv_loc, dq, key_rows, dcum, local)
+
+    def project(block, size, chunks, after, parts, finished=()):
         return run_project(
-            block, layout, flip, after, parts, dk_loc, dv_loc, dq, key_rows, dcum, local, weights
+            block, size, groups, chunks, flip, after, parts, finished, arrays, weights
         )
 
-    share = jnp.zeros((tok_rows, w_query.shape[0] // groups), BF16)
     if by_hand:
-        got = hop(outs[2], core, 8)
-        got = [got, hop(lax.optimization_barrier((outs[3], got))[0], core, 8)]
-
-        def give_back(j, afters):
-            source, first = min(j, 1), max(j - 1, 0)
-            sent = run_merge(outs[source], got[source], first, 1, [part[0] for part in afters])
+        got_0 = hop(outs[2], core, 8)
+        got_1 = hop(lax.optimization_barrier((outs[3], got_0))[0], core, 8)
+        sent_0 = run_merge(outs[0], got_0, 0, half, [])
+        sent_1 = run_merge(outs[1], got_1, 0, half, [sent_0[0]])
+
+        def give_back(own, got, sent):
             back = [hop(part, t, 8) for part, t in zip(sent, (across, along, across + along))]
-            near = [part.reshape(-1, BLK, 2 * width) for part in (outs[source], got[source])]
-            return [(part, 4 * first) for part in near] + [(part, 0) for part in back], sent, back
-
-        joint, apart = (1, groups - 1), (1,) * groups
-        parts_0, _, back_0 = give_back(0, [])
-        parts_1, sent_1, back_1 = give_back(1, back_0)
-        *terms_0, dcum_0 = project(0, joint, sent_1[2][0], [parts_0])
-        inward_0 = slide(terms_0[1], INWARD)
-        parts_2, sent_2, back_2 = give_back(2, back_1 + [terms_0[1]])
-        *terms_1, dcum_1 = project(1, joint, sent_2[2][0], [parts_1])
-        inward_1 = slide(terms_1[1], INWARD)
-        parts_3, _, back_3 = give_back(3, back_2 + [terms_1[1], inward_0])
-        *terms_2, dcum_2 = project(2, apart, inward_1[0], [parts_2, parts_3])
-        done_0, _ = line_scatter(*terms_0, inward_0, back_3[2][0])
-        done_1, swapped = line_scatter(*terms_1, inward_1, back_3[2][0])
-        done_2 = line_scatter_apart(*terms_2)
-        late = swapped[0]
-        dcums = [dcum_0, dcum_1, dcum_2]
-        for j, done in enumerate((done_0, done_1, done_2)):
-            share = lax.dynamic_update_slice(share, done, (j * BLK, 0))
+            near = [part.reshape(-1, BLK, 2 * width) for part in (own, got)]
+            parts = [
+                [(part, 4 * j) for part in near] + [(part, j) for part in back]
+                for j in range(half)
+            ]
+            return parts, back
+
+        parts_0, back_0 = give_back(outs[0], got_0, sent_0)
+        *sent_1, _ = lax.optimization_barrier((*sent_1, back_0))
+        parts_1, back_1 = give_back(outs[1], got_1, sent_1)
+        far_0, last_0, dcum_0, *finished = project(0, half, (2, 3), sent_1[0], parts_0)
+        first_0, near_0 = project(0, half, (0, 1), far_0, (), finished)
+        share, late = line_scatter(None, first_0, near_0, far_0, last_0)
+        *terms_1, dcum_1, _, _ = project(half, half, (0, 1, 2, 3), key_rows[None], parts_1)
+        share, _ = line_scatter(share, *terms_1)
+        dcums = [dcum_0, dcum_1]
     else:
         spots = (owners * blocks + offsets).reshape(-1)
         empty = jnp.zeros((ctx_count * blocks, BLK, 2 * width), BF16)
         filled = empty.at[spots].add(outs[0])
         back = lax.psum_scatter(filled, "ctx", scatter_dimension=0, tiled=True)
         late, dcums = key_rows, []
+        share = jnp.zeros((tok_rows, w_query.shape[0] // groups), BF16)
         for j in range(blocks):
-            *terms, dcum_out = project(j, (groups,), key_rows, [[(back, j)]])
+            *terms, dcum_out, _, _ = project(
+                j, 1, tuple(range(groups)), key_rows[None], [[(back, j)]]
+            )
             dcums.append(dcum_out)
-            done = lax.psum_scatter(terms[0], "head", scatter_dimension=0, tiled=False)
+            term = jnp.concatenate(terms, axis=0)
+            done = lax.psum_scatter(term, "head", scatter_dimension=0, tiled=False)
             share = lax.dynamic_update_slice(share, done, (j * BLK, 0))
 
     sums = run_adjoint(ints, late, dcums, unit, rows, inverse, heads, blocks)

time: 249 us -> 229 us (0.920)
  starting transfers between devices: 60.3 us -> 48.9 us
  local copies, waits for them, and re-layouts: 16.6 us -> 10.2 us
  waiting for transfers between devices: 65.2 us -> 69.3 us
  Pallas kernels: 95.6 us -> 91.7 us
  other arithmetic: 9.61 us -> 6.47 us
    ppermute x32 -> x26, starting transfers between devices: 28.2 us -> 21 us  [hop(): return lax.ppermute(value, 'ctx', [(i, i ^ distance) for i in range(count)])]
    ppermute x12, waiting for transfers between devices: 13.5 us -> 19.5 us  [slide(): return lax.ppermute(value, 'head', pairs)]
    squeeze x4 -> x0, local copies, waits for them, and re-layouts: 4.9 us -> none  [the longest x3 4.11 us: give_back(): part[0]]
    ppermute x12, starting transfers between devices: 28.7 us -> 24.5 us  [slide(): return lax.ppermute(value, 'head', pairs)]
    dynamic_update_slice x2 -> x0, other arithmetic: 2.99 us -> none  [shards(): share = lax.dynamic_update_slice(share, done, (j * BLK, 0))]
    pallas_call x5 -> x7, Pallas kernels: 43.7 us -> 41 us  [the longest x3 31.5 us: run_project(): pl.pallas_call(functools.partial(project_kernel, heads, len(parts[0]) if...]
    add x4 -> x6, other arithmetic: 3.08 us -> 5.12 us  [the longest x2 2.27 us: line_scatter(): last + in_last]
    ppermute x32 -> x26, waiting for transfers between devices: 51.6 us -> 49.8 us  [hop(): return lax.ppermute(value, 'ctx', [(i, i ^ distance) for i in range(count)])]
  transfers between devices with their start and end apart: 45 -> 39, of which waited for: 20 -> 16; matrix products, arithmetic and copies ran while one was open for 7% -> 4% of each run, Pallas kernels for 25% -> 32%
where the time goes in v1:
time: 229 us; the launch traced here: 227 us
  Pallas kernels  91.7 us (40%)
  waiting for transfers between devices  69.3 us (30%)
  starting transfers between devices  48.9 us (21%)
  local copies, waits for them, and re-layouts  10.2 us (4%)
  other arithmetic  6.47 us (3%)
    ppermute x26, waiting for transfers between devices, hop(): return lax.ppermute(value, 'ctx', [(i, i ^ distance) for i in range(count)])  49.8 us
    pallas_call x3, Pallas kernels, run_project(): pl.pallas_call(functools.partial(project_kernel, heads, len(parts[0]) if...  31.5 us
    ppermute x12, starting transfers between devices, slide(): return lax.ppermute(value, 'head', pairs)  24.5 us
    ppermute x26, starting transfers between devices, hop(): return lax.ppermute(value, 'ctx', [(i, i ^ distance) for i in range(count)])  21 us
    ppermute x12, waiting for transfers between devices, slide(): return lax.ppermute(value, 'head', pairs)  19.5 us
    pallas_call x1, Pallas kernels, run_attend(): pl.pallas_call(functools.partial(attend_kernel, heads, blocks, places, pi...  16.4 us
    pallas_call x1, Pallas kernels, run_rotate(): pl.pallas_call(functools.partial(rotate_kernel, heads, blocks), out_shape...  10.9 us
    unnamed x70, local copies, waits for them, and re-layouts  8.25 us
  transfers between devices with their start and end apart: 39, of which 16 were waited for; matrix products, arithmetic and copies ran while one was open for 4% of the time, Pallas kernels for 32%

profile of v1, /device:TPU:0, one launch (start us, length us, event | category | flops | bytes accessed | tf_op | source)
XLA Modules:
  0.0 227.5 jit_solution(7425651990302526868)
XLA Ops:
  1.1 2.6 %collective-permute-start.9 = (bf16[512,512]{1,0:T(8,128)(2,1)}, bf16[512,512]{1,0:T(8,128)(2,1)S(1)}, u32[]{:S(2)}, u32[]{:S(2)}) collective-permute-start(bf16[512,512]{1,0:T(8,128)(2,1)} %refs_13_.3), channel_id=1, source_target_pairs={{0,16},{4,20},{8,24},{12,28},{16,0},{20,4},{24,8},{28,12},{1,17},{... | collective-permute-start | bytes 1572872 | tf_op jit(solution)/shard_map/ppermute | solution.py:583
  8.3 2.9 %collective-permute-start.3 = (f32[8,512]{1,0:T(8,128)S(1)}, f32[8,512]{1,0:T(8,128)S(1)}, u32[]{:S(2)}, u32[]{:S(2)}) collective-permute-start(f32[8,512]{1,0:T(8,128)S(1)} %pad_maximum_fusion.refs_0_), channel_id=1, source_target_pairs={{0,24},{4,28},{8,16},{12,20},{16,8},{20,12},{24,0},{28,4},{1,25},{... | collective-permute-start | bytes 49160 | tf_op jit(solution)/shard_map/ppermute | solution.py:583
  11.9 6.6 %collective-permute-done.1.refs_1_ = f32[8,512]{1,0:T(8,128)S(1)} collective-permute-done((f32[8,512]{1,0:T(8,128)S(1)}, f32[8,512]{1,0:T(8,128)S(1)}, u32[]{:S(2)}, u32[]{:S(2)}) %collective-permute-start.1) | collective-permute-done | bytes 16416 | tf_op jit(solution)/shard_map/ppermute | solution.py:583
  21.6 5.4 %house_chain.1 = (f32[32,512]{1,0:T(8,128)}, f32[32,512]{1,0:T(8,128)}, f32[4,32,32]{2,1,0:T(8,128)}, f32[4,128,32]{2,1,0:T(8,128)}) custom-call(s32[17]{0:T(128)} %pad_add_fusion.ints_ref.refs_0_.base_ref, f32[8,512]{1,0:T(8,128)} %copy-done.13, f32[8,512]{1,0:T(8,128)} %copy-done.31, f32[8,512]{1,0:T(8,128)} %copy-done.32, f32[8,512]{1,0:T(8,128)} %copy-done.33), custom_call_target="tpu_custom_call" | custom-call | flops 6899999744 | bytes 1048576 | tf_op jit(solution)/shard_map/house_chain/pallas_call | solution.py:115
  27.8 3.9 %collective-permute-done.6.refs_5_ = bf16[512,512]{1,0:T(8,128)(2,1)S(1)} collective-permute-done((bf16[512,512]{1,0:T(8,128)(2,1)}, bf16[512,512]{1,0:T(8,128)(2,1)S(1)}, u32[]{:S(2)}, u32[]{:S(2)}) %collective-permute-start.6) | collective-permute-done | bytes 524320 | tf_op jit(solution)/shard_map/ppermute | solution.py:583
  31.8 3.3 %collective-permute-done.8.refs_10_ = bf16[512,512]{1,0:T(8,128)(2,1)S(1)} collective-permute-done((bf16[512,512]{1,0:T(8,128)(2,1)}, bf16[512,512]{1,0:T(8,128)(2,1)S(1)}, u32[]{:S(2)}, u32[]{:S(2)}) %collective-permute-start.8) | collective-permute-done | bytes 524320 | tf_op jit(solution)/shard_map/ppermute | solution.py:583
  35.5 10.9 %rotate.1 = (bf16[512,512]{1,0:T(8,128)(2,1)}, bf16[512,512]{1,0:T(8,128)(2,1)}, bf16[4,4,128,128]{3,2,1,0:T(8,128)(2,1)}, bf16[8,4,256,128]{3,2,1,0:T(8,128)(2,1)}) custom-call(s32[17]{0:T(128)} %pad_add_fusion.ints_ref.refs_0_.base_ref, f32[32,512]{1,0:T(8,128)} %get-tuple-element.48.rows_ref.refs_3_, f32[4,128,32]{2,1,0:T(8,128)} %get-tuple-element.49.unit_t_ref, ...), custom_call_target="tpu_custom_call" | custom-call | flops 10350000128 | bytes 1048576 | tf_op jit(solution)/shard_map/rotate/pallas_call | solution.py:181
  54.8 16.4 %attend.1 = (bf16[512,512]{1,0:T(8,128)(2,1)}, f32[4,4,128,128]{3,2,1,0:T(8,128)}, f32[512,512]{1,0:T(8,128)}, f32[512,512]{1,0:T(8,128)}, bf16[2,4,128,1024]{3,...) custom-call(s32[17]{0:T(128)} %pad_add_fusion.ints_ref.refs_0_.base_, ...), custom_call_target="tpu_custom_call" | custom-call | flops 17250000896 | bytes 1048576 | tf_op jit(solution)/shard_map/attend/pallas_call | solution.py:354
  71.4 4.2 %collective-permute-done.18.got_ref = bf16[2,4,128,1024]{3,2,1,0:T(8,128)(2,1)S(1)} collective-permute-done((bf16[2,4,128,1024]{3,2,1,0:T(8,128)(2,1)}, bf16[2,4,128,1024]{3,2,1,0:T(8,128)(2,1)S(1)}, u32[]{:S(2)}, u32[]{:S(2)}) %collective-permute-start.18) | collective-permute-done | bytes 2097184 | tf_op jit(solution)/shard_map/ppermute | solution.py:583
  77.0 4.1 %merge.2 = (bf16[2,128,1024]{2,1,0:T(8,128)(2,1)}, bf16[2,128,1024]{2,1,0:T(8,128)(2,1)}, bf16[2,128,1024]{2,1,0:T(8,128)(2,1)}) custom-call(bf16[2,4,128,1024]{3,2,1,0:T(8,128)(2,1)} %get-tuple-element.62.own_ref, bf16[2,4,128,1024]{3,2,1,0:T(8,128)(2,1)} %copy-done), custom_call_target="tpu_custom_call" | custom-call | flops 2300000000 | bytes 1048576 | tf_op jit(solution)/shard_map/merge/pallas_call | solution.py:383
  84.5 4.1 %merge.3 = (bf16[2,128,1024]{2,1,0:T(8,128)(2,1)}, bf16[2,128,1024]{2,1,0:T(8,128)(2,1)}, bf16[2,128,1024]{2,1,0:T(8,128)(2,1)}) custom-call(bf16[2,4,128,1024]{3,2,1,0:T(8,128)(2,1)} %get-tuple-element.58.own_ref, bf16[2,4,128,1024]{3,2,1,0:T(8,128)(2,1)} %collective-permute-done.19.got_ref, bf16[2,128,1024]{2,1,0:T(8,128)(2,1)} %get-tuple-element.63.refs_0_), custom_call_target="tpu_custom_call" | custom-call | flops 2300000000 | bytes 1048576 | tf_op jit(solution)/shard_map/merge/pallas_call | solution.py:383
  88.6 7.4 %collective-permute-done.20.refs_2_.refs_7_ = bf16[2,128,1024]{2,1,0:T(8,128)(2,1)S(1)} collective-permute-done((bf16[2,128,1024]{2,1,0:T(8,128)(2,1)}, bf16[2,128,1024]{2,1,0:T(8,128)(2,1)S(1)}, u32[]{:S(2)}, u32[]{:S(2)}) %collective-permute-start.20) | collective-permute-done | bytes 524320 | tf_op jit(solution)/shard_map/ppermute | solution.py:583
  96.0 9.9 %collective-permute-done.21.refs_3_.refs_8_ = bf16[2,128,1024]{2,1,0:T(8,128)(2,1)S(1)} collective-permute-done((bf16[2,128,1024]{2,1,0:T(8,128)(2,1)}, bf16[2,128,1024]{2,1,0:T(8,128)(2,1)S(1)}, u32[]{:S(2)}, u32[]{:S(2)}) %collective-permute-start.21) | collective-permute-done | bytes 524320 | tf_op jit(solution)/shard_map/ppermute | solution.py:583
  110.9 9.3 %project.3 = (bf16[1,256,1024]{2,1,0:T(8,128)(2,1)}, bf16[1,256,1024]{2,1,0:T(8,128)(2,1)}, f32[2,4,128,128]{3,2,1,0:T(8,128)}, bf16[256,512]{1,0:T(8,128)(2,1)}, bf16[256,512]{1,0:T(8,128)(2,1)}) custom-call(s32[1]{0:T(128)} %bitcast.1.flip_ref, bf16[2,128,1024]{2,1,0:T(8,128)(2,1)} %get-tuple-element.69.after_ref, bf16[8,128,1024]{2,1,0:T(8,128)(2,1)} %bitcast.8, ...), custom_call_target="tpu_custom_call" | custom-call | flops 6899999744 | bytes 1048576 | tf_op jit(solution)/shard_map/project/pallas_call | solution.py:485
  120.2 3.5 %collective-permute-start.26 = (bf16[1,256,1024]{2,1,0:T(8,128)(2,1)}, bf16[1,256,1024]{2,1,0:T(8,128)(2,1)S(1)}, u32[]{:S(2)}, u32[]{:S(2)}) collective-permute-start(bf16[1,256,1024]{2,1,0:T(8,128)(2,1)} %get-tuple-element.79), channel_id=1, source_target_pairs={{0,1},{3,2},{4,5},{7,6},{8,9},{11,10},{12,13},{15,14},{16,17},{19,... | collective-permute-start | bytes 1572872 | tf_op jit(solution)/shard_map/ppermute | solution.py:587
  125.1 7.2 %collective-permute-done.30.refs_3_.refs_8_ = bf16[2,128,1024]{2,1,0:T(8,128)(2,1)S(1)} collective-permute-done((bf16[2,128,1024]{2,1,0:T(8,128)(2,1)}, bf16[2,128,1024]{2,1,0:T(8,128)(2,1)S(1)}, u32[]{:S(2)}, u32[]{:S(2)}) %collective-permute-start.30) | collective-permute-done | bytes 524320 | tf_op jit(solution)/shard_map/ppermute | solution.py:583
  133.3 14.2 %project.5 = (bf16[1,256,1024]{2,1,0:T(8,128)(2,1)}, bf16[1,256,1024]{2,1,0:T(8,128)(2,1)}, bf16[1,256,1024]{2,1,0:T(8,128)(2,1)}, bf16[1,256,1024]{2,1,0:T(8,12...) custom-call(s32[1]{0:T(128)} %bitcast.1.flip_ref, ...), custom_call_target="tpu_custom_call" | custom-call | flops 13799999488 | bytes 1048576 | tf_op jit(solution)/shard_map/project/pallas_call | solution.py:485
  147.5 4.3 %collective-permute-start.35 = (bf16[1,256,1024]{2,1,0:T(8,128)(2,1)}, bf16[1,256,1024]{2,1,0:T(8,128)(2,1)}, u32[]{:S(2)}, u32[]{:S(2)}) collective-permute-start(bf16[1,256,1024]{2,1,0:T(8,128)(2,1)} %get-tuple-element.85), channel_id=1, source_target_pairs={{0,1},{3,2},{4,5},{7,6},{8,9},{11,10},{12,13},{15,14},{16,17},{19,... | collective-permute-start | bytes 1572872 | tf_op jit(solution)/shard_map/ppermute | solution.py:587
  151.8 8.0 %project.4 = (bf16[1,256,1024]{2,1,0:T(8,128)(2,1)}, bf16[1,256,1024]{2,1,0:T(8,128)(2,1)}) custom-call(s32[1]{0:T(128)} %bitcast.1.flip_ref, bf16[1,256,1024]{2,1,0:T(8,128)(2,1)} %get-tuple-element.74.after_ref, bf16[512,512]{1,0:T(8,128)(2,1)} %get-tuple-element.72.refs_12_.refs_0_, bf16[256,512]{1,0:T(8,128)(2,1)} %get-tuple-element.75.refs_1_, ...), custom_call_target="tpu_custom_call" | custom-call | flops 6899999744 | bytes 1048576 | tf_op jit(solution)/shard_map/project/pallas_call | solution.py:485
  163.0 3.3 %collective-permute-start.33 = (bf16[1,256,1024]{2,1,0:T(8,128)(2,1)S(1)}, bf16[1,256,1024]{2,1,0:T(8,128)(2,1)}, u32[]{:S(2)}, u32[]{:S(2)}) collective-permute-start(bf16[1,256,1024]{2,1,0:T(8,128)(2,1)S(1)} %copy-done.5), channel_id=1, source_target_pairs={{0,1},{3,2},{4,5},{7,6},{8,9},{11,10},{12,13},{15,14},{16,17},{19,... | collective-permute-start | bytes 1572872 | tf_op jit(solution)/shard_map/ppermute | solution.py:587
  178.7 7.2 %adjoint.1 = f32[32,1024]{1,0:T(8,128)} custom-call(s32[17]{0:T(128)} %pad_add_fusion.ints_ref.refs_0_.base_ref, bf16[1,256,1024]{2,1,0:T(8,128)(2,1)} %copy-done.10, f32[2,4,128,128]{3,2,1,0:T(8,128)} %get-tuple-element.86.refs_0_, f32[2,4,128,128]{3,2,1,0:T(8,128)} %get-tuple-element.87.refs_1_, f32[32,512]{1,0:T(8,128)} %get-tuple-element.88.refs_2_.unit_ref, ...), custom_call_target="tpu_custom_call" | custom-call | flops 2300000000 | bytes 1048576 | tf_op jit(solution)/shard_map/adjoint/pallas_call | solution.py:541
  187.7 3.4 %all-to-all-start = ((f32[8,4,1024]{2,1,0:T(4,128)}), f32[8,4,1024]{2,1,0:T(4,128)S(1)}, u32[]{:S(2)}, u32[]{:S(2)}) async-start(f32[8,4,1024]{2,1,0:T(4,128)} %reshape.47), calls=%async_computation | async-start | bytes 262144 | tf_op jit(solution)/shard_map/all_to_all | solution.py:753
  203.5 10.0 %collective-permute-done.28.refs_2_ = bf16[1,256,1024]{2,1,0:T(8,128)(2,1)S(1)} collective-permute-done((bf16[1,256,1024]{2,1,0:T(8,128)(2,1)S(1)}, bf16[1,256,1024]{2,1,0:T(8,128)(2,1)S(1)}, u32[]{:S(2)}, u32[]{:S(2)}) %collective-permute-start.28) | collective-permute-done | bytes 524320 | tf_op jit(solution)/shard_map/ppermute | solution.py:587
  216.7 7.7 %collective-permute-done.37.refs_3_ = bf16[1,256,1024]{2,1,0:T(8,128)(2,1)S(1)} collective-permute-done((bf16[1,256,1024]{2,1,0:T(8,128)(2,1)S(1)}, bf16[1,256,1024]{2,1,0:T(8,128)(2,1)S(1)}, u32[]{:S(2)}, u32[]{:S(2)}) %collective-permute-start.37) | collective-permute-done | bytes 524320 | tf_op jit(solution)/shard_map/ppermute | solution.py:587
  (150 shorter events, 66.8 us)
Async XLA Ops:
  1.1 25.9 %collective-permute-start.9 = (bf16[512,512]{1,0:T(8,128)(2,1)}, bf16[512,512]{1,0:T(8,128)(2,1)S(1)}, u32[]{:S(2)}, u32[]{:S(2)}) collective-permute-start(bf16[512,512]{1,0:T(8,128)(2,1)} %refs_13_.3), channel_id=1, source_target_pairs={{0,16},{4,20},{8,24},{12,28},{16,0},{20,4},{24,8},{28,12},{1,17},{... | collective-permute-start | bytes 1572872 | tf_op jit(solution)/shard_map/ppermute | solution.py:583
  3.7 23.6 %collective-permute-start.7 = (bf16[512,512]{1,0:T(8,128)(2,1)}, bf16[512,512]{1,0:T(8,128)(2,1)S(1)}, u32[]{:S(2)}, u32[]{:S(2)}) collective-permute-start(bf16[512,512]{1,0:T(8,128)(2,1)} %refs_20_.1), channel_id=1, source_target_pairs={{0,8},{4,12},{8,0},{12,4},{16,24},{20,28},{24,16},{28,20},{1,9},{5... | collective-permute-start | bytes 1572872 | tf_op jit(solution)/shard_map/ppermute | solution.py:583
  20.1 28.7 %collective-permute-start.4 = (bf16[512,512]{1,0:T(8,128)(2,1)}, bf16[512,512]{1,0:T(8,128)(2,1)S(1)}, u32[]{:S(2)}, u32[]{:S(2)}) collective-permute-start(bf16[512,512]{1,0:T(8,128)(2,1)} %refs_13_.3), channel_id=1, source_target_pairs={{0,4},{4,0},{8,12},{12,8},{16,20},{20,16},{24,28},{28,24},{1,5},{5... | collective-permute-start | bytes 1572872 | tf_op jit(solution)/shard_map/ppermute | solution.py:583
  20.1 14.9 %collective-permute-start.8 = (bf16[512,512]{1,0:T(8,128)(2,1)}, bf16[512,512]{1,0:T(8,128)(2,1)S(1)}, u32[]{:S(2)}, u32[]{:S(2)}) collective-permute-start(bf16[512,512]{1,0:T(8,128)(2,1)} %refs_20_.1), channel_id=1, source_target_pairs={{0,16},{4,20},{8,24},{12,28},{16,0},{20,4},{24,8},{28,12},{1,17},{... | collective-permute-start | bytes 1572872 | tf_op jit(solution)/shard_map/ppermute | solution.py:583
  27.0 21.9 %collective-permute-start.5 = (bf16[512,512]{1,0:T(8,128)(2,1)S(1)}, bf16[512,512]{1,0:T(8,128)(2,1)S(1)}, u32[]{:S(2)}, u32[]{:S(2)}) collective-permute-start(bf16[512,512]{1,0:T(8,128)(2,1)S(1)} %copy-done.14), channel_id=1, source_target_pairs={{0,4},{4,0},{8,12},{12,8},{16,20},{20,16},{24,28},{28,24},{1,5},{5... | collective-permute-start | bytes 1572872 | tf_op jit(solution)/shard_map/ppermute | solution.py:583
  27.3 21.0 %collective-permute-start.11 = (bf16[512,512]{1,0:T(8,128)(2,1)S(1)}, bf16[512,512]{1,0:T(8,128)(2,1)}, u32[]{:S(2)}, u32[]{:S(2)}) collective-permute-start(bf16[512,512]{1,0:T(8,128)(2,1)S(1)} %collective-permute-done.7.refs_6_), channel_id=1, source_target_pairs={{0,16},{4,20},{8,24},{12,28},{16,0},{20,4},{24,8},{28,12},{1,17},{... | collective-permute-start | bytes 1572872 | tf_op jit(solution)/shard_map/ppermute | solution.py:583
  31.8 17.6 %collective-permute-start.13 = (bf16[512,512]{1,0:T(8,128)(2,1)S(1)}, bf16[512,512]{1,0:T(8,128)(2,1)}, u32[]{:S(2)}, u32[]{:S(2)}) collective-permute-start(bf16[512,512]{1,0:T(8,128)(2,1)S(1)} %collective-permute-done.7.refs_6_), channel_id=1, source_target_pairs={{0,4},{4,0},{8,12},{12,8},{16,20},{20,16},{24,28},{28,24},{1,5},{5... | collective-permute-start | bytes 1572872 | tf_op jit(solution)/shard_map/ppermute | solution.py:583
  81.0 15.0 %collective-permute-start.20 = (bf16[2,128,1024]{2,1,0:T(8,128)(2,1)}, bf16[2,128,1024]{2,1,0:T(8,128)(2,1)S(1)}, u32[]{:S(2)}, u32[]{:S(2)}) collective-permute-start(bf16[2,128,1024]{2,1,0:T(8,128)(2,1)} %get-tuple-element.63.refs_0_), channel_id=1, source_target_pairs={{0,8},{4,12},{8,0},{12,4},{16,24},{20,28},{24,16},{28,20},{1,9},{5... | collective-permute-start | bytes 1572872 | tf_op jit(solution)/shard_map/ppermute | solution.py:583
  81.5 24.3 %collective-permute-start.21 = (bf16[2,128,1024]{2,1,0:T(8,128)(2,1)}, bf16[2,128,1024]{2,1,0:T(8,128)(2,1)S(1)}, u32[]{:S(2)}, u32[]{:S(2)}) collective-permute-start(bf16[2,128,1024]{2,1,0:T(8,128)(2,1)} %get-tuple-element.67), channel_id=1, source_target_pairs={{0,16},{4,20},{8,24},{12,28},{16,0},{20,4},{24,8},{28,12},{1,17},{... | collective-permute-start | bytes 1572872 | tf_op jit(solution)/shard_map/ppermute | solution.py:583
  83.1 24.3 %collective-permute-start.22 = (bf16[2,128,1024]{2,1,0:T(8,128)(2,1)}, bf16[2,128,1024]{2,1,0:T(8,128)(2,1)S(1)}, u32[]{:S(2)}, u32[]{:S(2)}) collective-permute-start(bf16[2,128,1024]{2,1,0:T(8,128)(2,1)} %get-tuple-element.68), channel_id=1, source_target_pairs={{0,24},{4,28},{8,16},{12,20},{16,8},{20,12},{24,0},{28,4},{1,25},{... | collective-permute-start | bytes 1572872 | tf_op jit(solution)/shard_map/ppermute | solution.py:583
  107.4 17.7 %collective-permute-start.29 = (bf16[2,128,1024]{2,1,0:T(8,128)(2,1)}, bf16[2,128,1024]{2,1,0:T(8,128)(2,1)S(1)}, u32[]{:S(2)}, u32[]{:S(2)}) collective-permute-start(bf16[2,128,1024]{2,1,0:T(8,128)(2,1)} %get-tuple-element.69.after_ref), channel_id=1, source_target_pairs={{0,8},{4,12},{8,0},{12,4},{16,24},{20,28},{24,16},{28,20},{1,9},{5... | collective-permute-start | bytes 1572872 | tf_op jit(solution)/shard_map/ppermute | solution.py:583
  108.3 24.0 %collective-permute-start.30 = (bf16[2,128,1024]{2,1,0:T(8,128)(2,1)}, bf16[2,128,1024]{2,1,0:T(8,128)(2,1)S(1)}, u32[]{:S(2)}, u32[]{:S(2)}) collective-permute-start(bf16[2,128,1024]{2,1,0:T(8,128)(2,1)} %get-tuple-element.80), channel_id=1, source_target_pairs={{0,16},{4,20},{8,24},{12,28},{16,0},{20,4},{24,8},{28,12},{1,17},{... | collective-permute-start | bytes 1572872 | tf_op jit(solution)/shard_map/ppermute | solution.py:583
  109.8 22.5 %collective-permute-start.31 = (bf16[2,128,1024]{2,1,0:T(8,128)(2,1)}, bf16[2,128,1024]{2,1,0:T(8,128)(2,1)S(1)}, u32[]{:S(2)}, u32[]{:S(2)}) collective-permute-start(bf16[2,128,1024]{2,1,0:T(8,128)(2,1)} %get-tuple-element.81), channel_id=1, source_target_pairs={{0,24},{4,28},{8,16},{12,20},{16,8},{20,12},{24,0},{28,4},{1,25},{... | collective-permute-start | bytes 1572872 | tf_op jit(solution)/shard_map/ppermute | solution.py:583
  120.2 41.8 %collective-permute-start.26 = (bf16[1,256,1024]{2,1,0:T(8,128)(2,1)}, bf16[1,256,1024]{2,1,0:T(8,128)(2,1)S(1)}, u32[]{:S(2)}, u32[]{:S(2)}) collective-permute-start(bf16[1,256,1024]{2,1,0:T(8,128)(2,1)} %get-tuple-element.79), channel_id=1, source_target_pairs={{0,1},{3,2},{4,5},{7,6},{8,9},{11,10},{12,13},{15,14},{16,17},{19,... | collective-permute-start | bytes 1572872 | tf_op jit(solution)/shard_map/ppermute | solution.py:587
  123.8 42.5 %collective-permute-start.24 = (bf16[1,256,1024]{2,1,0:T(8,128)(2,1)}, bf16[1,256,1024]{2,1,0:T(8,128)(2,1)S(1)}, u32[]{:S(2)}, u32[]{:S(2)}) collective-permute-start(bf16[1,256,1024]{2,1,0:T(8,128)(2,1)} %get-tuple-element.74.after_ref), channel_id=1, source_target_pairs={{0,1},{3,2},{4,5},{7,6},{8,9},{11,10},{12,13},{15,14},{16,17},{19,... | collective-permute-start | bytes 1572872 | tf_op jit(solution)/shard_map/ppermute | solution.py:587
  147.5 21.1 %collective-permute-start.35 = (bf16[1,256,1024]{2,1,0:T(8,128)(2,1)}, bf16[1,256,1024]{2,1,0:T(8,128)(2,1)}, u32[]{:S(2)}, u32[]{:S(2)}) collective-permute-start(bf16[1,256,1024]{2,1,0:T(8,128)(2,1)} %get-tuple-element.85), channel_id=1, source_target_pairs={{0,1},{3,2},{4,5},{7,6},{8,9},{11,10},{12,13},{15,14},{16,17},{19,... | collective-permute-start | bytes 1572872 | tf_op jit(solution)/shard_map/ppermute | solution.py:587
  162.3 15.6 %collective-permute-start.27 = (bf16[1,256,1024]{2,1,0:T(8,128)(2,1)S(1)}, bf16[1,256,1024]{2,1,0:T(8,128)(2,1)S(1)}, u32[]{:S(2)}, u32[]{:S(2)}) collective-permute-start(bf16[1,256,1024]{2,1,0:T(8,128)(2,1)S(1)} %add.19), channel_id=1, source_target_pairs={{1,2},{2,1},{5,6},{6,5},{9,10},{10,9},{13,14},{14,13},{17,18},{18,... | collective-permute-start | bytes 1572872 | tf_op jit(solution)/shard_map/ppermute | solution.py:587
  163.0 28.1 %collective-permute-start.33 = (bf16[1,256,1024]{2,1,0:T(8,128)(2,1)S(1)}, bf16[1,256,1024]{2,1,0:T(8,128)(2,1)}, u32[]{:S(2)}, u32[]{:S(2)}) collective-permute-start(bf16[1,256,1024]{2,1,0:T(8,128)(2,1)S(1)} %copy-done.5), channel_id=1, source_target_pairs={{0,1},{3,2},{4,5},{7,6},{8,9},{11,10},{12,13},{15,14},{16,17},{19,... | collective-permute-start | bytes 1572872 | tf_op jit(solution)/shard_map/ppermute | solution.py:587
  166.3 31.6 %collective-permute-start.32 = (bf16[1,256,1024]{2,1,0:T(8,128)(2,1)}, bf16[1,256,1024]{2,1,0:T(8,128)(2,1)}, u32[]{:S(2)}, u32[]{:S(2)}) collective-permute-start(bf16[1,256,1024]{2,1,0:T(8,128)(2,1)} %get-tuple-element.83.near_ref), channel_id=1, source_target_pairs={{0,1},{3,2},{4,5},{7,6},{8,9},{11,10},{12,13},{15,14},{16,17},{19,... | collective-permute-start | bytes 1572872 | tf_op jit(solution)/shard_map/ppermute | solution.py:587
  168.6 34.9 %collective-permute-start.25 = (bf16[1,256,1024]{2,1,0:T(8,128)(2,1)S(1)}, bf16[1,256,1024]{2,1,0:T(8,128)(2,1)}, u32[]{:S(2)}, u32[]{:S(2)}) collective-permute-start(bf16[1,256,1024]{2,1,0:T(8,128)(2,1)S(1)} %add.18), channel_id=1, source_target_pairs={{1,2},{2,1},{5,6},{6,5},{9,10},{10,9},{13,14},{14,13},{17,18},{18,... | collective-permute-start | bytes 1572872 | tf_op jit(solution)/shard_map/ppermute | solution.py:587
  173.9 21.4 %collective-permute-start.36 = (bf16[1,256,1024]{2,1,0:T(8,128)(2,1)}, bf16[1,256,1024]{2,1,0:T(8,128)(2,1)}, u32[]{:S(2)}, u32[]{:S(2)}) collective-permute-start(bf16[1,256,1024]{2,1,0:T(8,128)(2,1)} %add.22), channel_id=1, source_target_pairs={{1,2},{2,1},{5,6},{6,5},{9,10},{10,9},{13,14},{14,13},{17,18},{18,... | collective-permute-start | bytes 1572872 | tf_op jit(solution)/shard_map/ppermute | solution.py:587
  192.3 24.4 %collective-permute-start.34 = (bf16[1,256,1024]{2,1,0:T(8,128)(2,1)S(1)}, bf16[1,256,1024]{2,1,0:T(8,128)(2,1)}, u32[]{:S(2)}, u32[]{:S(2)}) collective-permute-start(bf16[1,256,1024]{2,1,0:T(8,128)(2,1)S(1)} %add.21), channel_id=1, source_target_pairs={{1,2},{2,1},{5,6},{6,5},{9,10},{10,9},{13,14},{14,13},{17,18},{18,... | collective-permute-start | bytes 1572872 | tf_op jit(solution)/shard_map/ppermute | solution.py:587
  194.0 19.6 %collective-permute-start.28 = (bf16[1,256,1024]{2,1,0:T(8,128)(2,1)S(1)}, bf16[1,256,1024]{2,1,0:T(8,128)(2,1)S(1)}, u32[]{:S(2)}, u32[]{:S(2)}) collective-permute-start(bf16[1,256,1024]{2,1,0:T(8,128)(2,1)S(1)} %add.20), channel_id=1, source_target_pairs={{1,0},{2,3},{5,4},{6,7},{9,8},{10,11},{13,12},{14,15},{17,16},{18,... | collective-permute-start | bytes 1572872 | tf_op jit(solution)/shard_map/ppermute | solution.py:587
  196.6 27.8 %collective-permute-start.37 = (bf16[1,256,1024]{2,1,0:T(8,128)(2,1)S(1)}, bf16[1,256,1024]{2,1,0:T(8,128)(2,1)S(1)}, u32[]{:S(2)}, u32[]{:S(2)}) collective-permute-start(bf16[1,256,1024]{2,1,0:T(8,128)(2,1)S(1)} %add.23), channel_id=1, source_target_pairs={{1,0},{2,3},{5,4},{6,7},{9,8},{10,11},{13,12},{14,15},{17,16},{18,... | collective-permute-start | bytes 1572872 | tf_op jit(solution)/shard_map/ppermute | solution.py:587
  (49 other events, 358.7 us)

commit v2 on v1

--- a/solution.py
+++ b/solution.py
@@ -123,7 +123,7 @@
         in_specs=in_smem(1) + in_vmem(parts),
         out_specs=in_vmem(4),
         scratch_shapes=[pltpu.VMEM((heads, count, DH), F32), pltpu.VMEM((count, width), F32)],
-        compiler_params=grant(60),
+        compiler_params=grant(12),
         cost_estimate=cost(6),
         name="house_chain",
     )(ints, *house_parts)
@@ -188,7 +188,7 @@
         ],
         in_specs=in_smem(1) + in_vmem(4),
         out_specs=in_vmem(4),
-        compiler_params=grant(60),
+        compiler_params=grant(16),
         cost_estimate=cost(9),
         name="rotate",
     )(ints, house_rows, unit_t, query_rows, key_rows)
@@ -363,7 +363,7 @@
         in_specs=in_smem(1) + [any_spec] * len(sources) + in_vmem(7),
         out_specs=in_vmem(4) + part_specs,
         scratch_shapes=scratch,
-        compiler_params=grant(60),
+        compiler_params=grant(30),
         cost_estimate=cost(15),
         name="attend",
     )(ints, *sources, *arrays)
@@ -387,16 +387,17 @@
         in_specs=[whole] * 2
         + [pl.BlockSpec((1, 16, 128), lambda j, c: (0, 0, 0))] * len(afters),
         out_specs=[pl.BlockSpec((1, rows, lanes), lambda j, c: (j, 0, c))] * (chips - 1),
-        compiler_params=grant(60),
+        compiler_params=grant(12),
         cost_estimate=cost(2),
         name="merge",
     )(own, got, *afters)
 
 
-def project_kernel(heads, parts, size, groups, chunks, flip_ref, after_ref, *refs):
-    outs = len(chunks)
+def project_kernel(heads, parts, size, groups, layout, flip_ref, after_ref, *refs):
+    outs = len(layout)
+    chunks = [(m, i, at) for i, row in enumerate(layout) for at, m in enumerate(row)]
     tiles, sems = refs[-2:]
-    per = tiles.shape[0] // outs
+    per = tiles.shape[0] // len(chunks)
     tile = tiles.shape[2]
     if parts:
         part_refs, refs = refs[: size * parts], refs[size * parts :]
@@ -407,8 +408,8 @@
         dq_ref, dk_ref, dv_ref = refs[:3]
         weight_refs, out_refs = refs[3:6], refs[6 : 6 + outs]
     copies = []
-    for t in range(outs * per):
-        m = chunks[t // per]
+    for t in range(len(chunks) * per):
+        m = chunks[t // per][0]
         row = ((m + flip_ref[0] * (groups - 1 - 2 * m)) * per + t % per) * tile
         rows = pl.ds(pl.multiple_of(row, tile), tile)
         for w, ref in enumerate(weight_refs):
@@ -442,17 +443,18 @@
     else:
         grads = (dq_ref[...], dk_ref[...], dv_ref[...])
 
-    for t in range(outs * per):
+    for t in range(len(chunks) * per):
         term = None
         for w, grad in enumerate(grads):
             copies[3 * t + w].wait()
             part = nt(tiles[t, w], grad)
             term = part if term is None else term + part
         spot = slice(t % per * tile, (t % per + 1) * tile)
-        out_refs[t // per][0, :, spot] = term.T.astype(BF16)
-
-
-def run_project(block, size, groups, chunks, flip, after, parts, finished, arrays, weights):
+        _, out, at = chunks[t // per]
+        out_refs[out][at, :, spot] = term.T.astype(BF16)
+
+
+def run_project(block, size, groups, layout, flip, after, parts, finished, arrays, weights):
     dk_loc, dv_loc, dq, key_rows, dcum, cum = arrays
     width = dq.shape[1]
     heads = width // DH
@@ -460,7 +462,7 @@
     chunk = model // groups
     tile = min(512, chunk)
     rows = size * BLK
-    tile_count = len(chunks) * chunk // tile
+    tile_count = sum(map(len, layout)) * chunk // tile
 
     def part_spec(index):
         return pl.BlockSpec((1, BLK, 2 * width), lambda t: (index, 0, 0))
@@ -471,8 +473,8 @@
     rows_spec = pl.BlockSpec((rows, width), lambda t: (block // size, 0))
     head_spec = pl.BlockSpec((size, heads, DH, DH), lambda t: (block // size, 0, 0, 0))
     flat = [part for row in parts for part in row]
-    out_specs = [whole(1, rows, chunk)] * len(chunks)
-    out_shape = [jax.ShapeDtypeStruct((1, rows, chunk), BF16)] * len(chunks)
+    out_specs = [whole(len(row), rows, chunk) for row in layout]
+    out_shape = [jax.ShapeDtypeStruct((len(row), rows, chunk), BF16) for row in layout]
     if parts:
         in_specs = [part_spec(index) for _, index in flat] + [rows_spec] * 4 + [head_spec] * 2
         inputs = [part for part, _ in flat] + [dk_loc, dv_loc, dq, key_rows, dcum, cum]
@@ -484,7 +486,7 @@
         inputs = [dq, *finished]
     return pl.pallas_call(
         functools.partial(
-            project_kernel, heads, len(parts[0]) if parts else 0, size, groups, chunks
+            project_kernel, heads, len(parts[0]) if parts else 0, size, groups, layout
         ),
         grid=(1,),
         in_specs=in_smem(1)
@@ -498,7 +500,7 @@
         ],
         out_shape=out_shape,
         compiler_params=grant(60),
-        cost_estimate=cost(3 * len(chunks)),
+        cost_estimate=cost(3 * sum(map(len, layout))),
         name="project",
     )(flip, after, *inputs, *weights)
 
@@ -549,7 +551,7 @@
     )(ints, after, *dcums, unit, rows, inverse)
 
 
-def house_kernel(heads, blocks, base_ref, got_ref, unit_ref, rows_ref, house_ref, out_ref):
+def house_kernel(heads, blocks, base_ref, after_ref, got_ref, unit_ref, rows_ref, house_ref, out_ref):
     count, width = unit_ref.shape
     total = jnp.sum(got_ref[...], axis=0)
     for h in range(heads):
@@ -567,16 +569,16 @@
         out_ref[:, head(h)] = (dunit - unit * inner) / lengths
 
 
-def run_house(ints, got, unit, rows, house_dirs, heads, blocks):
+def run_house(ints, after, got, unit, rows, house_dirs, heads, blocks):
     return pl.pallas_call(
         functools.partial(house_kernel, heads, blocks),
         out_shape=jax.ShapeDtypeStruct(house_dirs.shape, F32),
-        in_specs=[pl.BlockSpec(memory_space=pltpu.SMEM)] + in_vmem(4),
+        in_specs=in_smem(1) + [pl.BlockSpec(memory_space=pl.ANY)] + in_vmem(4),
         out_specs=pl.BlockSpec(memory_space=pltpu.VMEM),
         compiler_params=grant(60),
         cost_estimate=cost(2),
         name="house_grad",
-    )(ints, got, unit, rows, house_dirs)
+    )(ints, after, got, unit, rows, house_dirs)
 
 
 def hop(value, distance, count):
@@ -598,51 +600,63 @@
 
 
 def run_near(ends, first, near, inward):
+    _, rows, width = first.shape
     return pl.pallas_call(
         near_kernel,
-        out_shape=jax.ShapeDtypeStruct(first.shape[1:], F32),
-        in_specs=in_smem(1) + in_vmem(3),
-        out_specs=pl.BlockSpec(memory_space=pltpu.VMEM),
+        grid=(1,),
+        out_shape=jax.ShapeDtypeStruct((rows, width), F32),
+        in_specs=in_smem(1) + [pl.BlockSpec((1, rows, width), lambda t: (0, 0, 0))] * 3,
+        out_specs=pl.BlockSpec((rows, width), lambda t: (0, 0)),
         compiler_params=grant(60),
         cost_estimate=cost(16),
         name="near_sum",
     )(ends, first, near, inward)
 
 
-def line_scatter(share, first, near, far, last):
-    place = lax.axis_index("head")
-    ends = ((place == 0) | (place == 3)).astype(jnp.int32).reshape(1)
-    in_last, in_far, in_near = slide(last, INWARD), slide(far, INWARD), slide(near, INWARD)
-    swap_last, swap_far = slide(last + in_last, MIDDLE), slide(far + in_far, MIDDLE)
-    outward = slide(first + swap_last, OUTWARD)
-    total = run_near(ends, first, near, in_near)
-    return run_share(share, total, swap_far, outward), swap_last
-
-
 def share_kernel(*refs):
     total_ref, far_ref, outward_ref, out_ref = refs[-4:]
     far = far_ref[0].astype(F32) + outward_ref[0].astype(F32)
     out_ref[...] = (total_ref[...] + far).astype(BF16)
 
 
-def run_share(share, total, far, outward):
+def run_share(share, band, bands, total, far, outward):
     rows, width = total.shape
-    place = 0 if share is None else 1
     tile = min(512, width)
     part = pl.BlockSpec((1, rows, tile), lambda t: (0, 0, t))
     given = [] if share is None else [share]
     return pl.pallas_call(
         share_kernel,
         grid=(width // tile,),
-        out_shape=jax.ShapeDtypeStruct((2 * rows, width), BF16),
+        out_shape=jax.ShapeDtypeStruct((bands * rows, width), BF16),
         in_specs=[pl.BlockSpec(memory_space=pl.ANY)] * len(given)
         + [pl.BlockSpec((rows, tile), lambda t: (0, t)), part, part],
-        out_specs=pl.BlockSpec((rows, tile), lambda t: (place, t)),
+        out_specs=pl.BlockSpec((rows, tile), lambda t: (band, t)),
         input_output_aliases={0: 0} if given else {},
         compiler_params=grant(60),
         cost_estimate=cost(2),
         name="share",
     )(*given, total, far, outward)
+
+
+def line_ends():
+    place = lax.axis_index("head")
+    return ((place == 0) | (place == 3)).astype(jnp.int32).reshape(1)
+
+
+def line_scatter(share, band, bands, first, rest):
+    inward = slide(rest, INWARD)
+    swapped = slide(rest[1:] + inward[1:], MIDDLE)
+    outward = slide(first + swapped[1:], OUTWARD)
+    total = run_near(line_ends(), first, rest, inward)
+    return run_share(share, band, bands, total, swapped, outward), outward
+
+
+def line_scatter_apart(share, band, bands, first, near, far, last):
+    in_last, in_far, in_near = slide(last, INWARD), slide(far, INWARD), slide(near, INWARD)
+    swap_last, swap_far = slide(last + in_last, MIDDLE), slide(far + in_far, MIDDLE)
+    outward = slide(first + swap_last, OUTWARD)
+    total = run_near(line_ends(), first, near, in_near)
+    return run_share(share, band, bands, total, swap_far, outward)
 
 
 def shards(
@@ -687,8 +701,7 @@
         sources = [lax.all_gather(key_rows, "ctx"), lax.all_gather(value_rows, "ctx")]
         places = [((0, 0), (1, 0))]
 
-    half = blocks // 2
-    rounds = tuple((first, half) for first in range(0, 2 * blocks, half))
+    rounds = ((0, 1), (1, blocks - 1), (blocks, 1), (blocks + 1, blocks - 1))
     dq, dcum, dk_loc, dv_loc, *outs = run_attend(
         ints,
         sources,
@@ -703,55 +716,58 @@
 
     arrays = (dk_loc, dv_loc, dq, key_rows, dcum, local)
 
-    def project(block, size, chunks, after, parts, finished=()):
-        return run_project(
-            block, size, groups, chunks, flip, after, parts, finished, arrays, weights
-        )
+    def project(block, layout, after, parts):
+        size = len(parts)
+        return run_project(block, size, groups, layout, flip, after, parts, (), arrays, weights)
 
     if by_hand:
         got_0 = hop(outs[2], core, 8)
         got_1 = hop(lax.optimization_barrier((outs[3], got_0))[0], core, 8)
-        sent_0 = run_merge(outs[0], got_0, 0, half, [])
-        sent_1 = run_merge(outs[1], got_1, 0, half, [sent_0[0]])
-
-        def give_back(own, got, sent):
+        sent_0 = run_merge(outs[0], got_0, 0, 1, [])
+        sent_1 = run_merge(outs[1], got_1, 0, 1, [sent_0[0]])
+        sent_2 = run_merge(outs[1], got_1, 1, 2, [sent_1[0]])
+
+        def give_back(own, got, first, sent):
             back = [hop(part, t, 8) for part, t in zip(sent, (across, along, across + along))]
             near = [part.reshape(-1, BLK, 2 * width) for part in (own, got)]
-            parts = [
-                [(part, 4 * j) for part in near] + [(part, j) for part in back]
-                for j in range(half)
-            ]
+            parts = []
+            for j in range(sent[0].shape[0]):
+                mine = [(part, 4 * (first + j)) for part in near]
+                parts.append(mine + [(part, j) for part in back])
             return parts, back
 
-        parts_0, back_0 = give_back(outs[0], got_0, sent_0)
+        parts_0, back_0 = give_back(outs[0], got_0, 0, sent_0)
         *sent_1, _ = lax.optimization_barrier((*sent_1, back_0))
-        parts_1, back_1 = give_back(outs[1], got_1, sent_1)
-        far_0, last_0, dcum_0, *finished = project(0, half, (2, 3), sent_1[0], parts_0)
-        first_0, near_0 = project(0, half, (0, 1), far_0, (), finished)
-        share, late = line_scatter(None, first_0, near_0, far_0, last_0)
-        *terms_1, dcum_1, _, _ = project(half, half, (0, 1, 2, 3), key_rows[None], parts_1)
-        share, _ = line_scatter(share, *terms_1)
-        dcums = [dcum_0, dcum_1]
+        parts_1, back_1 = give_back(outs[1], got_1, 0, sent_1)
+        *sent_2, _ = lax.optimization_barrier((*sent_2, back_1))
+        parts_2, _ = give_back(outs[1], got_1, 1, sent_2)
+        joint, apart = ((0,), (1, 2, 3)), ((0,), (1,), (2,), (3,))
+        *terms_0, dcum_0, _, _ = project(0, joint, sent_1[0], parts_0)
+        *terms_1, dcum_1, _, _ = project(1, joint, sent_2[0], parts_1)
+        *terms_2, dcum_2, _, _ = project(2, apart, terms_1[0], parts_2)
+        share, late = line_scatter(None, 0, 4, *terms_0)
+        share, later = line_scatter(share, 1, 4, *terms_1)
+        share = line_scatter_apart(share, 1, 2, *terms_2)
+        dcums = [dcum_0, dcum_1, dcum_2]
     else:
         spots = (owners * blocks + offsets).reshape(-1)
         empty = jnp.zeros((ctx_count * blocks, BLK, 2 * width), BF16)
         filled = empty.at[spots].add(outs[0])
         back = lax.psum_scatter(filled, "ctx", scatter_dimension=0, tiled=True)
-        late, dcums = key_rows, []
+        late, later, dcums = key_rows, key_rows, []
         share = jnp.zeros((tok_rows, w_query.shape[0] // groups), BF16)
         for j in range(blocks):
-            *terms, dcum_out, _, _ = project(
-                j, 1, tuple(range(groups)), key_rows[None], [[(back, j)]]
+            term, dcum_out, _, _ = project(
+                j, (tuple(range(groups)),), key_rows[None], [[(back, j)]]
             )
             dcums.append(dcum_out)
-            term = jnp.concatenate(terms, axis=0)
             done = lax.psum_scatter(term, "head", scatter_dimension=0, tiled=False)
             share = lax.dynamic_update_slice(share, done, (j * BLK, 0))
 
     sums = run_adjoint(ints, late, dcums, unit, rows, inverse, heads, blocks)
     sums = sums.reshape(ctx_count, blocks, 2 * width)
     got = lax.all_to_all(sums, "ctx", split_axis=0, concat_axis=0, tiled=True)
-    house_grad = run_house(ints, got, unit, rows, house_dirs, heads, blocks)
+    house_grad = run_house(ints, later, got, unit, rows, house_dirs, heads, blocks)
     return (share, house_grad)
 
 

time: 229 us -> 224 us (0.978)
  waiting for transfers between devices: 69.3 us -> 60.1 us
  local copies, waits for them, and re-layouts: 10.2 us -> 13.4 us
  Pallas kernels: 91.7 us -> 94.8 us
    ppermute x26 -> x29, waiting for transfers between devices: 49.8 us -> 34.7 us  [hop(): return lax.ppermute(value, 'ctx', [(i, i ^ distance) for i in range(count)])]
    pallas_call x3, Pallas kernels: 31.5 us -> 39.7 us  [run_project(): pl.pallas_call(functools.partial(project_kernel, heads, len(parts[0]) if...]
    ppermute x12, starting transfers between devices: 24.5 us -> 20 us  [slide(): return lax.ppermute(value, 'head', pairs)]
    ppermute x12, waiting for transfers between devices: 19.5 us -> 23.4 us  [slide(): return lax.ppermute(value, 'head', pairs)]
    ppermute x26 -> x29, starting transfers between devices: 21 us -> 24.6 us  [hop(): return lax.ppermute(value, 'ctx', [(i, i ^ distance) for i in range(count)])]
    unnamed x70 -> x68, local copies, waits for them, and re-layouts: 8.25 us -> 11.6 us
    pallas_call x2 -> x3, Pallas kernels: 8.18 us -> 5.29 us  [run_merge(): pl.pallas_call(merge_kernel, grid=(size, cut), out_shape=[jax.ShapeDtypeS...]
    pallas_call x2 -> x3, Pallas kernels: 4.57 us -> 6.17 us  [run_share(): pl.pallas_call(share_kernel, grid=(width // tile,), out_shape=jax.ShapeDt...]
  transfers between devices with their start and end apart: 39 -> 42, of which waited for: 16 -> 20; matrix products, arithmetic and copies ran while one was open for 4% -> 4% of each run, Pallas kernels for 32% -> 35%
where the time goes in v2:
time: 224 us; the launch traced here: 223 us
  Pallas kernels  94.8 us (42%)
  waiting for transfers between devices  60.1 us (27%)
  starting transfers between devices  47.9 us (21%)
  local copies, waits for them, and re-layouts  13.4 us (6%)
  other arithmetic  5.51 us (2%)
    pallas_call x3, Pallas kernels, run_project(): pl.pallas_call(functools.partial(project_kernel, heads, len(parts[0]) if...  39.7 us
    ppermute x29, waiting for transfers between devices, hop(): return lax.ppermute(value, 'ctx', [(i, i ^ distance) for i in range(count)])  34.7 us
    ppermute x29, starting transfers between devices, hop(): return lax.ppermute(value, 'ctx', [(i, i ^ distance) for i in range(count)])  24.6 us
    ppermute x12, waiting for transfers between devices, slide(): return lax.ppermute(value, 'head', pairs)  23.4 us
    ppermute x12, starting transfers between devices, slide(): return lax.ppermute(value, 'head', pairs)  20 us
    pallas_call x1, Pallas kernels, run_attend(): pl.pallas_call(functools.partial(attend_kernel, heads, blocks, places, pi...  14.2 us
    unnamed x68, local copies, waits for them, and re-layouts  11.6 us
    pallas_call x1, Pallas kernels, run_rotate(): pl.pallas_call(functools.partial(rotate_kernel, heads, blocks), out_shape...  8.62 us
  transfers between devices with their start and end apart: 42, of which 20 were waited for; matrix products, arithmetic and copies ran while one was open for 4% of the time, Pallas kernels for 35%

profile of v2, /device:TPU:0, one launch (start us, length us, event | category | flops | bytes accessed | tf_op | source)
XLA Modules:
  0.0 222.7 jit_solution(7426601472222703612)
XLA Ops:
  1.1 2.6 %collective-permute-start.9 = (bf16[512,512]{1,0:T(8,128)(2,1)}, bf16[512,512]{1,0:T(8,128)(2,1)S(1)}, u32[]{:S(2)}, u32[]{:S(2)}) collective-permute-start(bf16[512,512]{1,0:T(8,128)(2,1)} %refs_13_.5), channel_id=1, source_target_pairs={{0,16},{4,20},{8,24},{12,28},{16,0},{20,4},{24,8},{28,12},{1,17},{... | collective-permute-start | bytes 1572872 | tf_op jit(solution)/shard_map/ppermute | solution.py:585
  8.3 2.9 %collective-permute-start.3 = (f32[8,512]{1,0:T(8,128)S(1)}, f32[8,512]{1,0:T(8,128)S(1)}, u32[]{:S(2)}, u32[]{:S(2)}) collective-permute-start(f32[8,512]{1,0:T(8,128)S(1)} %pad_maximum_fusion.refs_0_), channel_id=1, source_target_pairs={{0,24},{4,28},{8,16},{12,20},{16,8},{20,12},{24,0},{28,4},{1,25},{... | collective-permute-start | bytes 49160 | tf_op jit(solution)/shard_map/ppermute | solution.py:585
  11.3 7.2 %collective-permute-done.1.refs_1_ = f32[8,512]{1,0:T(8,128)S(1)} collective-permute-done((f32[8,512]{1,0:T(8,128)S(1)}, f32[8,512]{1,0:T(8,128)S(1)}, u32[]{:S(2)}, u32[]{:S(2)}) %collective-permute-start.1) | collective-permute-done | bytes 16416 | tf_op jit(solution)/shard_map/ppermute | solution.py:585
  21.6 4.4 %house_chain.1 = (f32[32,512]{1,0:T(8,128)S(1)}, f32[32,512]{1,0:T(8,128)S(1)}, f32[4,32,32]{2,1,0:T(8,128)S(1)}, f32[4,128,32]{2,1,0:T(8,128)S(1)}) custom-call(s32[17]{0:T(128)S(1)} %pad_add_fusion.ints_ref.refs_0_.base_ref, f32[8,512]{1,0:T(8,128)S(1)} %pad_maximum_fusion.refs_0_, f32[8,512]{1,0:T(8,128)S(1)} %collective-permute-done.1.refs_1_, ...), custom_call_target="tpu_custom_call" | custom-call | flops 6899999744 | bytes 1048576 | tf_op jit(solution)/shard_map/house_chain/pallas_call | solution.py:115
  28.1 3.6 %collective-permute-done.6.refs_5_ = bf16[512,512]{1,0:T(8,128)(2,1)S(1)} collective-permute-done((bf16[512,512]{1,0:T(8,128)(2,1)}, bf16[512,512]{1,0:T(8,128)(2,1)S(1)}, u32[]{:S(2)}, u32[]{:S(2)}) %collective-permute-start.6) | collective-permute-done | bytes 524320 | tf_op jit(solution)/shard_map/ppermute | solution.py:585
  31.7 3.3 %collective-permute-done.8.refs_10_ = bf16[512,512]{1,0:T(8,128)(2,1)S(1)} collective-permute-done((bf16[512,512]{1,0:T(8,128)(2,1)}, bf16[512,512]{1,0:T(8,128)(2,1)S(1)}, u32[]{:S(2)}, u32[]{:S(2)}) %collective-permute-start.8) | collective-permute-done | bytes 524320 | tf_op jit(solution)/shard_map/ppermute | solution.py:585
  35.4 8.6 %rotate.1 = (bf16[512,512]{1,0:T(8,128)(2,1)S(1)}, bf16[512,512]{1,0:T(8,128)(2,1)S(1)}, bf16[4,4,128,128]{3,2,1,0:T(8,128)(2,1)S(1)}, bf16[8,4,256,128]{3,2,1,0:T(8,128)(2,1)S(1)}) custom-call(s32[17]{0:T(128)S(1)} %pad_add_fusion.ints_ref.refs_0_.base_ref, f32[32,512]{1,0:T(8,128)S(1)} %get-tuple-element.53.rows_ref.refs_4_, ...), custom_call_target="tpu_custom_call" | custom-call | flops 10350000128 | bytes 1048576 | tf_op jit(solution)/shard_map/rotate/pallas_call | solution.py:181
  44.1 4.1 %collective-permute-done.10.refs_13_ = bf16[512,512]{1,0:T(8,128)(2,1)S(1)} collective-permute-done((bf16[512,512]{1,0:T(8,128)(2,1)S(1)}, bf16[512,512]{1,0:T(8,128)(2,1)S(1)}, u32[]{:S(2)}, u32[]{:S(2)}) %collective-permute-start.10) | collective-permute-done | bytes 524320 | tf_op jit(solution)/shard_map/ppermute | solution.py:585
  53.1 14.2 %attend.1 = (bf16[512,512]{1,0:T(8,128)(2,1)S(1)}, f32[4,4,128,128]{3,2,1,0:T(8,128)S(1)}, f32[512,512]{1,0:T(8,128)S(1)}, f32[512,512]{1,0:T(8,128)S(1)}, bf16[...) custom-call(s32[17]{0:T(128)S(1)} %pad_add_fusion.ints_ref.refs_0_.b, ...), custom_call_target="tpu_custom_call" | custom-call | flops 17250000896 | bytes 1048576 | tf_op jit(solution)/shard_map/attend/pallas_call | solution.py:354
  68.3 2.5 %collective-permute-done.18.got_ref = bf16[1,4,128,1024]{3,2,1,0:T(8,128)(2,1)S(1)} collective-permute-done((bf16[1,4,128,1024]{3,2,1,0:T(8,128)(2,1)S(1)}, bf16[1,4,128,1024]{3,2,1,0:T(8,128)(2,1)S(1)}, u32[]{:S(2)}, u32[]{:S(2)}) %collective-permute-start.18) | collective-permute-done | bytes 1048608 | tf_op jit(solution)/shard_map/ppermute | solution.py:585
  76.7 3.0 %copy-done.8 = bf16[3,4,128,1024]{3,2,1,0:T(8,128)(2,1)S(1)} copy-done((bf16[3,4,128,1024]{3,2,1,0:T(8,128)(2,1)S(1)}, bf16[3,4,128,1024]{3,2,1,0:T(8,128)(2,1)}, u32[]{:S(2)}) %copy-start.8) | copy-done | bytes 3145752
  81.7 4.4 %collective-permute-done.21.refs_3_ = bf16[1,128,1024]{2,1,0:T(8,128)(2,1)} collective-permute-done((bf16[1,128,1024]{2,1,0:T(8,128)(2,1)}, bf16[1,128,1024]{2,1,0:T(8,128)(2,1)}, u32[]{:S(2)}, u32[]{:S(2)}) %collective-permute-start.21) | collective-permute-done | bytes 262176 | tf_op jit(solution)/shard_map/ppermute | solution.py:585
  91.2 12.7 %project.3 = (bf16[1,128,1024]{2,1,0:T(8,128)(2,1)}, bf16[3,128,1024]{2,1,0:T(8,128)(2,1)}, f32[1,4,128,128]{3,2,1,0:T(8,128)}, bf16[128,512]{1,0:T(8,128)(2,1)}, bf16[128,512]{1,0:T(8,128)(2,1)}) custom-call(s32[1]{0:T(128)} %bitcast.1.flip_ref, bf16[1,128,1024]{2,1,0:T(8,128)(2,1)} %get-tuple-element.74.after_ref.refs_0_, bf16[4,128,1024]{2,1,0:T(8,128)(2,1)} %bitcast.14, ...), custom_call_target="tpu_custom_call" | custom-call | flops 13799999488 | bytes 1048576 | tf_op jit(solution)/shard_map/project/pallas_call | solution.py:487
  103.9 4.4 %collective-permute-start.23 = (bf16[3,128,1024]{2,1,0:T(8,128)(2,1)}, bf16[3,128,1024]{2,1,0:T(8,128)(2,1)}, u32[]{:S(2)}, u32[]{:S(2)}) collective-permute-start(bf16[3,128,1024]{2,1,0:T(8,128)(2,1)} %get-tuple-element.80.near_ref), channel_id=1, source_target_pairs={{0,1},{3,2},{4,5},{7,6},{8,9},{11,10},{12,13},{15,14},{16,17},{19,... | collective-permute-start | bytes 2359304 | tf_op jit(solution)/shard_map/ppermute | solution.py:589
  110.2 2.5 %merge.5 = (bf16[2,128,1024]{2,1,0:T(8,128)(2,1)}, bf16[2,128,1024]{2,1,0:T(8,128)(2,1)}, bf16[2,128,1024]{2,1,0:T(8,128)(2,1)S(1)}) custom-call(bf16[3,4,128,1024]{3,2,1,0:T(8,128)(2,1)S(1)} %copy-done.9, bf16[3,4,128,1024]{3,2,1,0:T(8,128)(2,1)S(1)} %collective-permute-done.19.got_ref, bf16[1,128,1024]{2,1,0:T(8,128)(2,1)} %get-tuple-element.74.after_ref.refs_0_), custom_call_target="tpu_custom_call" | custom-call | flops 2300000000 | bytes 1048576 | tf_op jit(solution)/shard_map/merge/pallas_call | solution.py:383
  116.3 12.8 %project.4 = (bf16[1,128,1024]{2,1,0:T(8,128)(2,1)}, bf16[3,128,1024]{2,1,0:T(8,128)(2,1)}, f32[1,4,128,128]{3,2,1,0:T(8,128)}, bf16[128,512]{1,0:T(8,128)(2,1)}, bf16[128,512]{1,0:T(8,128)(2,1)}) custom-call(s32[1]{0:T(128)} %bitcast.1.flip_ref, bf16[2,128,1024]{2,1,0:T(8,128)(2,1)} %get-tuple-element.86.after_ref, bf16[12,128,1024]{2,1,0:T(8,128)(2,1)} %bitcast.11, ...), custom_call_target="tpu_custom_call" | custom-call | flops 13799999488 | bytes 1048576 | tf_op jit(solution)/shard_map/project/pallas_call | solution.py:487
  133.9 2.9 %collective-permute-done.33.refs_3_.refs_8_ = bf16[2,128,1024]{2,1,0:T(8,128)(2,1)S(1)} collective-permute-done((bf16[2,128,1024]{2,1,0:T(8,128)(2,1)}, bf16[2,128,1024]{2,1,0:T(8,128)(2,1)S(1)}, u32[]{:S(2)}, u32[]{:S(2)}) %collective-permute-start.33) | collective-permute-done | bytes 524320 | tf_op jit(solution)/shard_map/ppermute | solution.py:585
  137.8 14.2 %project.5 = (bf16[1,256,1024]{2,1,0:T(8,128)(2,1)}, bf16[1,256,1024]{2,1,0:T(8,128)(2,1)}, bf16[1,256,1024]{2,1,0:T(8,128)(2,1)}, bf16[1,256,1024]{2,1,0:T(8,12...) custom-call(s32[1]{0:T(128)} %bitcast.1.flip_ref, ...), custom_call_target="tpu_custom_call" | custom-call | flops 13799999488 | bytes 1048576 | tf_op jit(solution)/shard_map/project/pallas_call | solution.py:487
  166.9 10.3 %collective-permute-done.36 = bf16[1,256,1024]{2,1,0:T(8,128)(2,1)S(1)} collective-permute-done((bf16[1,256,1024]{2,1,0:T(8,128)(2,1)}, bf16[1,256,1024]{2,1,0:T(8,128)(2,1)S(1)}, u32[]{:S(2)}, u32[]{:S(2)}) %collective-permute-start.36) | collective-permute-done | bytes 524320 | tf_op jit(solution)/shard_map/ppermute | solution.py:589
  178.1 6.4 %collective-permute-done.35.inward_ref = bf16[1,256,1024]{2,1,0:T(8,128)(2,1)} collective-permute-done((bf16[1,256,1024]{2,1,0:T(8,128)(2,1)}, bf16[1,256,1024]{2,1,0:T(8,128)(2,1)}, u32[]{:S(2)}, u32[]{:S(2)}) %collective-permute-start.35) | collective-permute-done | bytes 524320 | tf_op jit(solution)/shard_map/ppermute | solution.py:589
  190.2 7.3 %adjoint.1 = f32[32,1024]{1,0:T(8,128)} custom-call(s32[17]{0:T(128)} %copy-done, bf16[1,128,1024]{2,1,0:T(8,128)(2,1)} %copy-done.32, f32[1,4,128,128]{3,2,1,0:T(8,128)} %get-tuple-element.95.refs_0_, f32[1,4,128,128]{3,2,1,0:T(8,128)} %get-tuple-element.96.refs_1_, f32[2,4,128,128]{3,2,1,0:T(8,128)} %get-tuple-element.97.refs_2_, f32[32,512]{1,0:T(8,128)} %copy-done.16, ...), custom_call_target="tpu_custom_call" | custom-call | flops 2300000000 | bytes 1048576 | tf_op jit(solution)/shard_map/adjoint/pallas_call | solution.py:543
  199.2 3.4 %all-to-all-start = ((f32[8,4,1024]{2,1,0:T(4,128)}), f32[8,4,1024]{2,1,0:T(4,128)S(1)}, u32[]{:S(2)}, u32[]{:S(2)}) async-start(f32[8,4,1024]{2,1,0:T(4,128)} %reshape.50), calls=%async_computation | async-start | bytes 262144 | tf_op jit(solution)/shard_map/all_to_all | solution.py:769
  208.7 2.6 %house_grad.1 = f32[4,512]{1,0:T(4,128)} custom-call(s32[17]{0:T(128)} %copy-done, bf16[1,128,1024]{2,1,0:T(8,128)(2,1)} %collective-permute-done.31.refs_3_.after_ref, f32[8,4,1024]{2,1,0:T(4,128)} %copy-done.26, f32[32,512]{1,0:T(8,128)} %copy-done.16, f32[32,512]{1,0:T(8,128)} %copy-done.17, f32[4,512]{1,0:T(4,128)} %house_ref.1), custom_call_target="tpu_custom_call" | custom-call | flops 2300000000 | bytes 1048576 | tf_op jit(solution)/shard_map/house_grad/pallas_call | solution.py:573
  213.1 6.4 %collective-permute-done.40.refs_3_ = bf16[1,256,1024]{2,1,0:T(8,128)(2,1)S(1)} collective-permute-done((bf16[1,256,1024]{2,1,0:T(8,128)(2,1)S(1)}, bf16[1,256,1024]{2,1,0:T(8,128)(2,1)S(1)}, u32[]{:S(2)}, u32[]{:S(2)}) %collective-permute-start.40) | collective-permute-done | bytes 524320 | tf_op jit(solution)/shard_map/ppermute | solution.py:589
  (158 shorter events, 74.9 us)
Async XLA Ops:
  1.1 26.1 %collective-permute-start.9 = (bf16[512,512]{1,0:T(8,128)(2,1)}, bf16[512,512]{1,0:T(8,128)(2,1)S(1)}, u32[]{:S(2)}, u32[]{:S(2)}) collective-permute-start(bf16[512,512]{1,0:T(8,128)(2,1)} %refs_13_.5), channel_id=1, source_target_pairs={{0,16},{4,20},{8,24},{12,28},{16,0},{20,4},{24,8},{28,12},{1,17},{... | collective-permute-start | bytes 1572872 | tf_op jit(solution)/shard_map/ppermute | solution.py:585
  3.7 23.8 %collective-permute-start.7 = (bf16[512,512]{1,0:T(8,128)(2,1)}, bf16[512,512]{1,0:T(8,128)(2,1)S(1)}, u32[]{:S(2)}, u32[]{:S(2)}) collective-permute-start(bf16[512,512]{1,0:T(8,128)(2,1)} %refs_20_.1), channel_id=1, source_target_pairs={{0,8},{4,12},{8,0},{12,4},{16,24},{20,28},{24,16},{28,20},{1,9},{5... | collective-permute-start | bytes 1572872 | tf_op jit(solution)/shard_map/ppermute | solution.py:585
  20.1 28.6 %collective-permute-start.4 = (bf16[512,512]{1,0:T(8,128)(2,1)}, bf16[512,512]{1,0:T(8,128)(2,1)S(1)}, u32[]{:S(2)}, u32[]{:S(2)}) collective-permute-start(bf16[512,512]{1,0:T(8,128)(2,1)} %refs_13_.5), channel_id=1, source_target_pairs={{0,4},{4,0},{8,12},{12,8},{16,20},{20,16},{24,28},{28,24},{1,5},{5... | collective-permute-start | bytes 1572872 | tf_op jit(solution)/shard_map/ppermute | solution.py:585
  20.1 14.9 %collective-permute-start.8 = (bf16[512,512]{1,0:T(8,128)(2,1)}, bf16[512,512]{1,0:T(8,128)(2,1)S(1)}, u32[]{:S(2)}, u32[]{:S(2)}) collective-permute-start(bf16[512,512]{1,0:T(8,128)(2,1)} %refs_20_.1), channel_id=1, source_target_pairs={{0,16},{4,20},{8,24},{12,28},{16,0},{20,4},{24,8},{28,12},{1,17},{... | collective-permute-start | bytes 1572872 | tf_op jit(solution)/shard_map/ppermute | solution.py:585
  27.3 21.5 %collective-permute-start.5 = (bf16[512,512]{1,0:T(8,128)(2,1)S(1)}, bf16[512,512]{1,0:T(8,128)(2,1)S(1)}, u32[]{:S(2)}, u32[]{:S(2)}) collective-permute-start(bf16[512,512]{1,0:T(8,128)(2,1)S(1)} %copy-done.3), channel_id=1, source_target_pairs={{0,4},{4,0},{8,12},{12,8},{16,20},{20,16},{24,28},{28,24},{1,5},{5... | collective-permute-start | bytes 1572872 | tf_op jit(solution)/shard_map/ppermute | solution.py:585
  27.6 20.6 %collective-permute-start.11 = (bf16[512,512]{1,0:T(8,128)(2,1)S(1)}, bf16[512,512]{1,0:T(8,128)(2,1)S(1)}, u32[]{:S(2)}, u32[]{:S(2)}) collective-permute-start(bf16[512,512]{1,0:T(8,128)(2,1)S(1)} %collective-permute-done.7.refs_6_), channel_id=1, source_target_pairs={{0,16},{4,20},{8,24},{12,28},{16,0},{20,4},{24,8},{28,12},{1,17},{... | collective-permute-start | bytes 1572872 | tf_op jit(solution)/shard_map/ppermute | solution.py:585
  31.7 17.5 %collective-permute-start.13 = (bf16[512,512]{1,0:T(8,128)(2,1)S(1)}, bf16[512,512]{1,0:T(8,128)(2,1)S(1)}, u32[]{:S(2)}, u32[]{:S(2)}) collective-permute-start(bf16[512,512]{1,0:T(8,128)(2,1)S(1)} %collective-permute-done.7.refs_6_), channel_id=1, source_target_pairs={{0,4},{4,0},{8,12},{12,8},{16,20},{20,16},{24,28},{28,24},{1,5},{5... | collective-permute-start | bytes 1572872 | tf_op jit(solution)/shard_map/ppermute | solution.py:585
  87.7 25.0 %collective-permute-start.26 = (bf16[1,128,1024]{2,1,0:T(8,128)(2,1)}, bf16[1,128,1024]{2,1,0:T(8,128)(2,1)}, u32[]{:S(2)}, u32[]{:S(2)}) collective-permute-start(bf16[1,128,1024]{2,1,0:T(8,128)(2,1)} %get-tuple-element.74.after_ref.refs_0_), channel_id=1, source_target_pairs={{0,8},{4,12},{8,0},{12,4},{16,24},{20,28},{24,16},{28,20},{1,9},{5... | collective-permute-start | bytes 786440 | tf_op jit(solution)/shard_map/ppermute | solution.py:585
  88.5 24.2 %collective-permute-start.27 = (bf16[1,128,1024]{2,1,0:T(8,128)(2,1)}, bf16[1,128,1024]{2,1,0:T(8,128)(2,1)}, u32[]{:S(2)}, u32[]{:S(2)}) collective-permute-start(bf16[1,128,1024]{2,1,0:T(8,128)(2,1)} %get-tuple-element.84), channel_id=1, source_target_pairs={{0,16},{4,20},{8,24},{12,28},{16,0},{20,4},{24,8},{28,12},{1,17},{... | collective-permute-start | bytes 786440 | tf_op jit(solution)/shard_map/ppermute | solution.py:585
  90.0 22.7 %collective-permute-start.28 = (bf16[1,128,1024]{2,1,0:T(8,128)(2,1)S(1)}, bf16[1,128,1024]{2,1,0:T(8,128)(2,1)}, u32[]{:S(2)}, u32[]{:S(2)}) collective-permute-start(bf16[1,128,1024]{2,1,0:T(8,128)(2,1)S(1)} %get-tuple-element.85), channel_id=1, source_target_pairs={{0,24},{4,28},{8,16},{12,20},{16,8},{20,12},{24,0},{28,4},{1,25},{... | collective-permute-start | bytes 786440 | tf_op jit(solution)/shard_map/ppermute | solution.py:585
  103.9 27.4 %collective-permute-start.23 = (bf16[3,128,1024]{2,1,0:T(8,128)(2,1)}, bf16[3,128,1024]{2,1,0:T(8,128)(2,1)}, u32[]{:S(2)}, u32[]{:S(2)}) collective-permute-start(bf16[3,128,1024]{2,1,0:T(8,128)(2,1)} %get-tuple-element.80.near_ref), channel_id=1, source_target_pairs={{0,1},{3,2},{4,5},{7,6},{8,9},{11,10},{12,13},{15,14},{16,17},{19,... | collective-permute-start | bytes 2359304 | tf_op jit(solution)/shard_map/ppermute | solution.py:589
  112.7 21.2 %collective-permute-start.32 = (bf16[2,128,1024]{2,1,0:T(8,128)(2,1)}, bf16[2,128,1024]{2,1,0:T(8,128)(2,1)S(1)}, u32[]{:S(2)}, u32[]{:S(2)}) collective-permute-start(bf16[2,128,1024]{2,1,0:T(8,128)(2,1)} %get-tuple-element.86.after_ref), channel_id=1, source_target_pairs={{0,8},{4,12},{8,0},{12,4},{16,24},{20,28},{24,16},{28,20},{1,9},{5... | collective-permute-start | bytes 1572872 | tf_op jit(solution)/shard_map/ppermute | solution.py:585
  113.6 23.2 %collective-permute-start.33 = (bf16[2,128,1024]{2,1,0:T(8,128)(2,1)}, bf16[2,128,1024]{2,1,0:T(8,128)(2,1)S(1)}, u32[]{:S(2)}, u32[]{:S(2)}) collective-permute-start(bf16[2,128,1024]{2,1,0:T(8,128)(2,1)} %get-tuple-element.89), channel_id=1, source_target_pairs={{0,16},{4,20},{8,24},{12,28},{16,0},{20,4},{24,8},{28,12},{1,17},{... | collective-permute-start | bytes 1572872 | tf_op jit(solution)/shard_map/ppermute | solution.py:585
  115.1 21.7 %collective-permute-start.34 = (bf16[2,128,1024]{2,1,0:T(8,128)(2,1)S(1)}, bf16[2,128,1024]{2,1,0:T(8,128)(2,1)S(1)}, u32[]{:S(2)}, u32[]{:S(2)}) collective-permute-start(bf16[2,128,1024]{2,1,0:T(8,128)(2,1)S(1)} %get-tuple-element.90), channel_id=1, source_target_pairs={{0,24},{4,28},{8,16},{12,20},{16,8},{20,12},{24,0},{28,4},{1,25},{... | collective-permute-start | bytes 1572872 | tf_op jit(solution)/shard_map/ppermute | solution.py:585
  129.1 29.7 %collective-permute-start.29 = (bf16[3,128,1024]{2,1,0:T(8,128)(2,1)}, bf16[3,128,1024]{2,1,0:T(8,128)(2,1)}, u32[]{:S(2)}, u32[]{:S(2)}) collective-permute-start(bf16[3,128,1024]{2,1,0:T(8,128)(2,1)} %get-tuple-element.88.near_ref), channel_id=1, source_target_pairs={{0,1},{3,2},{4,5},{7,6},{8,9},{11,10},{12,13},{15,14},{16,17},{19,... | collective-permute-start | bytes 2359304 | tf_op jit(solution)/shard_map/ppermute | solution.py:589
  132.4 31.0 %collective-permute-start.24 = (bf16[2,128,1024]{2,1,0:T(8,128)(2,1)S(1)}, bf16[2,128,1024]{2,1,0:T(8,128)(2,1)}, u32[]{:S(2)}, u32[]{:S(2)}) collective-permute-start(bf16[2,128,1024]{2,1,0:T(8,128)(2,1)S(1)} %slice_add_fusion.1), channel_id=1, source_target_pairs={{1,2},{2,1},{5,6},{6,5},{9,10},{10,9},{13,14},{14,13},{17,18},{18,... | collective-permute-start | bytes 1572872 | tf_op jit(solution)/shard_map/ppermute | solution.py:589
  153.3 23.9 %collective-permute-start.36 = (bf16[1,256,1024]{2,1,0:T(8,128)(2,1)}, bf16[1,256,1024]{2,1,0:T(8,128)(2,1)S(1)}, u32[]{:S(2)}, u32[]{:S(2)}) collective-permute-start(bf16[1,256,1024]{2,1,0:T(8,128)(2,1)} %get-tuple-element.93), channel_id=1, source_target_pairs={{0,1},{3,2},{4,5},{7,6},{8,9},{11,10},{12,13},{15,14},{16,17},{19,... | collective-permute-start | bytes 1572872 | tf_op jit(solution)/shard_map/ppermute | solution.py:589
  154.6 29.9 %collective-permute-start.35 = (bf16[1,256,1024]{2,1,0:T(8,128)(2,1)}, bf16[1,256,1024]{2,1,0:T(8,128)(2,1)}, u32[]{:S(2)}, u32[]{:S(2)}) collective-permute-start(bf16[1,256,1024]{2,1,0:T(8,128)(2,1)} %get-tuple-element.92.near_ref), channel_id=1, source_target_pairs={{0,1},{3,2},{4,5},{7,6},{8,9},{11,10},{12,13},{15,14},{16,17},{19,... | collective-permute-start | bytes 1572872 | tf_op jit(solution)/shard_map/ppermute | solution.py:589
  159.9 27.1 %collective-permute-start.30 = (bf16[2,128,1024]{2,1,0:T(8,128)(2,1)S(1)}, bf16[2,128,1024]{2,1,0:T(8,128)(2,1)}, u32[]{:S(2)}, u32[]{:S(2)}) collective-permute-start(bf16[2,128,1024]{2,1,0:T(8,128)(2,1)S(1)} %slice_add_fusion), channel_id=1, source_target_pairs={{1,2},{2,1},{5,6},{6,5},{9,10},{10,9},{13,14},{14,13},{17,18},{18,... | collective-permute-start | bytes 1572872 | tf_op jit(solution)/shard_map/ppermute | solution.py:589
  164.5 25.1 %collective-permute-start.25 = (bf16[1,128,1024]{2,1,0:T(8,128)(2,1)S(1)}, bf16[1,128,1024]{2,1,0:T(8,128)(2,1)S(1)}, u32[]{:S(2)}, u32[]{:S(2)}) collective-permute-start(bf16[1,128,1024]{2,1,0:T(8,128)(2,1)S(1)} %slice_add_fusion.3), channel_id=1, source_target_pairs={{1,0},{2,3},{5,4},{6,7},{9,8},{10,11},{13,12},{14,15},{17,16},{18,... | collective-permute-start | bytes 786440 | tf_op jit(solution)/shard_map/ppermute | solution.py:589
  166.2 36.4 %collective-permute-start.39 = (bf16[1,256,1024]{2,1,0:T(8,128)(2,1)S(1)}, bf16[1,256,1024]{2,1,0:T(8,128)(2,1)S(1)}, u32[]{:S(2)}, u32[]{:S(2)}) collective-permute-start(bf16[1,256,1024]{2,1,0:T(8,128)(2,1)S(1)} %add.26), channel_id=1, source_target_pairs={{1,2},{2,1},{5,6},{6,5},{9,10},{10,9},{13,14},{14,13},{17,18},{18,... | collective-permute-start | bytes 1572872 | tf_op jit(solution)/shard_map/ppermute | solution.py:589
  177.4 35.8 %collective-permute-start.37 = (bf16[1,256,1024]{2,1,0:T(8,128)(2,1)S(1)}, bf16[1,256,1024]{2,1,0:T(8,128)(2,1)S(1)}, u32[]{:S(2)}, u32[]{:S(2)}) collective-permute-start(bf16[1,256,1024]{2,1,0:T(8,128)(2,1)S(1)} %add.25), channel_id=1, source_target_pairs={{1,2},{2,1},{5,6},{6,5},{9,10},{10,9},{13,14},{14,13},{17,18},{18,... | collective-permute-start | bytes 1572872 | tf_op jit(solution)/shard_map/ppermute | solution.py:589
  188.0 20.0 %collective-permute-start.31 = (bf16[1,128,1024]{2,1,0:T(8,128)(2,1)S(1)}, bf16[1,128,1024]{2,1,0:T(8,128)(2,1)}, u32[]{:S(2)}, u32[]{:S(2)}) collective-permute-start(bf16[1,128,1024]{2,1,0:T(8,128)(2,1)S(1)} %slice_add_fusion.2), channel_id=1, source_target_pairs={{1,0},{2,3},{5,4},{6,7},{9,8},{10,11},{13,12},{14,15},{17,16},{18,... | collective-permute-start | bytes 786440 | tf_op jit(solution)/shard_map/ppermute | solution.py:589
  202.8 16.8 %collective-permute-start.40 = (bf16[1,256,1024]{2,1,0:T(8,128)(2,1)S(1)}, bf16[1,256,1024]{2,1,0:T(8,128)(2,1)S(1)}, u32[]{:S(2)}, u32[]{:S(2)}) collective-permute-start(bf16[1,256,1024]{2,1,0:T(8,128)(2,1)S(1)} %add.27), channel_id=1, source_target_pairs={{1,0},{2,3},{5,4},{6,7},{9,8},{10,11},{13,12},{14,15},{17,16},{18,... | collective-permute-start | bytes 1572872 | tf_op jit(solution)/shard_map/ppermute | solution.py:589
  (51 other events, 442.3 us)

commit v3 on v2

--- a/solution.py
+++ b/solution.py
@@ -77,7 +77,7 @@
 
 def chain_kernel(heads, parts, ints_ref, *refs):
     house_refs = refs[:parts]
-    unit_ref, rows_ref, inv_ref, unit_t_ref, unit_h, house_all = refs[parts:]
+    unit_ref, rows_ref, inv_ref, wide_ref, tall_ref, unit_h, house_all = refs[parts:]
     count = unit_ref.shape[0]
     span = count // parts
     for t, ref in enumerate(house_refs):
@@ -104,8 +104,12 @@
     eye_wide = (iota((DH, DH), 0) == iota((DH, DH), 1)).astype(F32)
     for h in range(heads):
         units = unit_ref[:, head(h)]
-        rows_ref[:, head(h)] = nn_high(inv_ref[h], units)
-        unit_t_ref[h] = nt_high(eye_wide, units)
+        rows = nn_high(inv_ref[h], units)
+        rows_ref[:, head(h)] = rows
+        unit_hi, unit_lo = split(nt_high(eye_wide, units))
+        rows_hi, rows_lo = split(rows)
+        wide_ref[h] = jnp.concatenate([unit_hi, unit_hi, unit_lo], axis=1)
+        tall_ref[h] = jnp.concatenate([rows_hi, rows_lo, rows_hi], axis=0)
 
 
 def run_chain(ints, house_parts, heads):
@@ -118,10 +122,11 @@
             jax.ShapeDtypeStruct((count, width), F32),
             jax.ShapeDtypeStruct((count, width), F32),
             jax.ShapeDtypeStruct((heads, count, count), F32),
-            jax.ShapeDtypeStruct((heads, DH, count), F32),
+            jax.ShapeDtypeStruct((heads, DH, 3 * count), BF16),
+            jax.ShapeDtypeStruct((heads, 3 * count, DH), BF16),
         ],
         in_specs=in_smem(1) + in_vmem(parts),
-        out_specs=in_vmem(4),
+        out_specs=in_vmem(5),
         scratch_shapes=[pltpu.VMEM((heads, count, DH), F32), pltpu.VMEM((count, width), F32)],
         compiler_params=grant(12),
         cost_estimate=cost(6),
@@ -133,8 +138,8 @@
     heads,
     blocks,
     ints_ref,
-    rows_ref,
-    unit_t_ref,
+    wide_ref,
+    tall_ref,
     query_ref,
     key_ref,
     qrot_ref,
@@ -142,13 +147,14 @@
     local_ref,
     listed_ref,
 ):
-    count = rows_ref.shape[0]
+    count = wide_ref.shape[2] // 3
     entries = blocks * MAXL
+    column = iota((DH, 3 * count), 1) % count
     eye = (iota((DH, DH), 0) == iota((DH, DH), 1)).astype(F32)
 
     def cumulative(h, block):
-        kept = jnp.where(iota((DH, count), 1) <= block, unit_t_ref[h], 0.0)
-        return split(eye - 2.0 * nn_high(kept, rows_ref[:, head(h)]))
+        kept = jnp.where(column <= block, wide_ref[h].astype(F32), 0.0).astype(BF16)
+        return split(eye - 2.0 * nn(kept, tall_ref[h]))
 
     base = ints_ref[0] * blocks
 
@@ -175,7 +181,7 @@
     lax.fori_loop(0, entries, listed_block, 0)
 
 
-def run_rotate(ints, house_rows, unit_t, query_rows, key_rows, heads, blocks):
+def run_rotate(ints, wide, tall, query_rows, key_rows, heads, blocks):
     rows, width = query_rows.shape
     entries = blocks * MAXL
     return pl.pallas_call(
@@ -191,7 +197,7 @@
         compiler_params=grant(16),
         cost_estimate=cost(9),
         name="rotate",
-    )(ints, house_rows, unit_t, query_rows, key_rows)
+    )(ints, wide, tall, query_rows, key_rows)
 
 
 def attend_kernel(heads, blocks, places, pieces, *refs):
@@ -393,20 +399,18 @@
     )(own, got, *afters)
 
 
-def project_kernel(heads, parts, size, groups, layout, flip_ref, after_ref, *refs):
+def project_kernel(heads, parts, size, groups, before, layout, afters, flip_ref, *refs):
+    refs = refs[afters:]
     outs = len(layout)
     chunks = [(m, i, at) for i, row in enumerate(layout) for at, m in enumerate(row)]
     tiles, sems = refs[-2:]
     per = tiles.shape[0] // len(chunks)
     tile = tiles.shape[2]
-    if parts:
-        part_refs, refs = refs[: size * parts], refs[size * parts :]
-        dk_loc, dv_loc, dq_ref, key_ref, dcum_in, cum_ref = refs[:6]
-        weight_refs, out_refs = refs[6:9], refs[9 : 9 + outs]
-        dcum_out, dk_out, dv_out = refs[9 + outs : 12 + outs]
-    else:
-        dq_ref, dk_ref, dv_ref = refs[:3]
-        weight_refs, out_refs = refs[3:6], refs[6 : 6 + outs]
+    part_refs, refs = refs[: size * parts], refs[size * parts :]
+    before_refs, refs = refs[:before], refs[before:]
+    dk_loc, dv_loc, dq_ref, key_ref, dcum_in, cum_ref = refs[:6]
+    weight_refs, out_refs = refs[6:9], refs[9 : 9 + outs]
+    dcum_out, dk_out, dv_out = refs[9 + outs : 12 + outs]
     copies = []
     for t in range(len(chunks) * per):
         m = chunks[t // per][0]
@@ -417,46 +421,48 @@
             copy.start()
             copies.append(copy)
 
-    if parts:
-        dk_rows, dv_rows = [], []
-        for j in range(size):
-            here = slice(j * BLK, (j + 1) * BLK)
-            dk, dv = [], []
-            for h in range(heads):
-                both = slice(2 * h * DH, (2 * h + 2) * DH)
-                total = part_refs[j * parts][0, :, both].astype(F32)
-                for ref in part_refs[j * parts + 1 : (j + 1) * parts]:
-                    total = total + ref[0, :, both].astype(F32)
-                dv.append((dv_loc[here, head(h)] + total[:, DH:]).astype(BF16))
-                dk_top, dk_low = split(dk_loc[here, head(h)] + total[:, :DH])
-                dk.append(nt(dk_top, cum_ref[j, h]).astype(BF16))
-                key = key_ref[here, head(h)]
-                key = jnp.concatenate([key, key], axis=0)
-                dcum = tn(key, jnp.concatenate([dk_top, dk_low], axis=0))
-                dcum_out[j, h] = dcum_in[j, h] + dcum
-            dk_rows.append(jnp.concatenate(dk, axis=1))
-            dv_rows.append(jnp.concatenate(dv, axis=1))
-        dk_all, dv_all = jnp.concatenate(dk_rows, axis=0), jnp.concatenate(dv_rows, axis=0)
-        dk_out[...] = dk_all
-        dv_out[...] = dv_all
-        grads = (dq_ref[...], dk_all, dv_all)
-    else:
-        grads = (dq_ref[...], dk_ref[...], dv_ref[...])
+    earlier = ()
+    dk_rows, dv_rows = [], []
+    for j in range(size):
+        here = slice(j * BLK, (j + 1) * BLK)
+        dk, dv = [], []
+        for h in range(heads):
+            both = slice(2 * h * DH, (2 * h + 2) * DH)
+            total = part_refs[j * parts][0, :, both].astype(F32)
+            for ref in part_refs[j * parts + 1 : (j + 1) * parts]:
+                total = total + ref[0, :, both].astype(F32)
+            dv.append((dv_loc[here, head(h)] + total[:, DH:]).astype(BF16))
+            dk_top, dk_low = split(dk_loc[here, head(h)] + total[:, :DH])
+            dk.append(nt(dk_top, cum_ref[j, h]).astype(BF16))
+            key = key_ref[here, head(h)]
+            key = jnp.concatenate([key, key], axis=0)
+            dcum = tn(key, jnp.concatenate([dk_top, dk_low], axis=0))
+            dcum_out[j, h] = dcum_in[j, h] + dcum
+        dk_rows.append(jnp.concatenate(dk, axis=1))
+        dv_rows.append(jnp.concatenate(dv, axis=1))
+    dk_all, dv_all = jnp.concatenate(dk_rows, axis=0), jnp.concatenate(dv_rows, axis=0)
+    dk_out[...] = dk_all
+    dv_out[...] = dv_all
+    grads = (dq_ref[...], dk_all, dv_all)
+    if before:
+        earlier = [
+            jnp.concatenate([old[...], new], axis=0) for old, new in zip(before_refs, grads)
+        ]
 
     for t in range(len(chunks) * per):
         term = None
-        for w, grad in enumerate(grads):
+        m, out, at = chunks[t // per]
+        for w, grad in enumerate(earlier if before and m == 0 else grads):
             copies[3 * t + w].wait()
             part = nt(tiles[t, w], grad)
             term = part if term is None else term + part
         spot = slice(t % per * tile, (t % per + 1) * tile)
-        _, out, at = chunks[t // per]
         out_refs[out][at, :, spot] = term.T.astype(BF16)
 
 
-def run_project(block, size, groups, layout, flip, after, parts, finished, arrays, weights):
+def run_project(block, groups, layout, flip, afters, parts, before, arrays, weights):
     dk_loc, dv_loc, dq, key_rows, dcum, cum = arrays
-    width = dq.shape[1]
+    size, width = len(parts), dq.shape[1]
     heads = width // DH
     model = weights[0].shape[0]
     chunk = model // groups
@@ -473,39 +479,57 @@
     rows_spec = pl.BlockSpec((rows, width), lambda t: (block // size, 0))
     head_spec = pl.BlockSpec((size, heads, DH, DH), lambda t: (block // size, 0, 0, 0))
     flat = [part for row in parts for part in row]
-    out_specs = [whole(len(row), rows, chunk) for row in layout]
-    out_shape = [jax.ShapeDtypeStruct((len(row), rows, chunk), BF16) for row in layout]
-    if parts:
-        in_specs = [part_spec(index) for _, index in flat] + [rows_spec] * 4 + [head_spec] * 2
-        inputs = [part for part, _ in flat] + [dk_loc, dv_loc, dq, key_rows, dcum, cum]
-        out_specs += [whole(size, heads, DH, DH)] + [whole(rows, width)] * 2
-        out_shape += [jax.ShapeDtypeStruct((size, heads, DH, DH), F32)]
-        out_shape += [jax.ShapeDtypeStruct((rows, width), BF16)] * 2
-    else:
-        in_specs = [rows_spec] + [whole(rows, width)] * 2
-        inputs = [dq, *finished]
+    heights = [2 * rows if before and row == (0,) else rows for row in layout]
+    shapes = [(len(row), height, chunk) for row, height in zip(layout, heights)]
     return pl.pallas_call(
         functools.partial(
-            project_kernel, heads, len(parts[0]) if parts else 0, size, groups, layout
+            project_kernel,
+            heads,
+            len(parts[0]),
+            size,
+            groups,
+            len(before),
+            layout,
+            len(afters),
         ),
         grid=(1,),
         in_specs=in_smem(1)
-        + [whole(1, 16, 128)]
-        + in_specs
+        + [whole(1, 16, 128)] * len(afters)
+        + [part_spec(index) for _, index in flat]
+        + [whole(rows, width)] * len(before)
+        + [rows_spec] * 4
+        + [head_spec] * 2
         + [pl.BlockSpec(memory_space=pl.ANY)] * 3,
-        out_specs=out_specs,
+        out_specs=[whole(*shape) for shape in shapes]
+        + [whole(size, heads, DH, DH)]
+        + [whole(rows, width)] * 2,
         scratch_shapes=[
             pltpu.VMEM((tile_count, 3, tile, width), BF16),
             pltpu.SemaphoreType.DMA((tile_count, 3)),
         ],
-        out_shape=out_shape,
+        out_shape=[jax.ShapeDtypeStruct(shape, BF16) for shape in shapes]
+        + [jax.ShapeDtypeStruct((size, heads, DH, DH), F32)]
+        + [jax.ShapeDtypeStruct((rows, width), BF16)] * 2,
         compiler_params=grant(60),
         cost_estimate=cost(3 * sum(map(len, layout))),
         name="project",
-    )(flip, after, *inputs, *weights)
-
-
-def adjoint_kernel(heads, blocks, ints_ref, after_ref, *refs):
+    )(
+        flip,
+        *afters,
+        *[part for part, _ in flat],
+        *before,
+        dk_loc,
+        dv_loc,
+        dq,
+        key_rows,
+        dcum,
+        cum,
+        *weights,
+    )
+
+
+def adjoint_kernel(heads, blocks, afters, ints_ref, *refs):
+    refs = refs[afters:]
     dcums = [ref.at[j] for ref in refs[:-4] for j in range(ref.shape[0])]
     unit_ref, rows_ref, inv_ref, out_ref = refs[-4:]
     count, width = unit_ref.shape
@@ -538,17 +562,19 @@
         out_ref[:, slice(width + h * DH, width + (h + 1) * DH)] = y_total
 
 
-def run_adjoint(ints, after, dcums, unit, rows, inverse, heads, blocks):
+def run_adjoint(ints, afters, dcums, unit, rows, inverse, heads, blocks):
     count, width = unit.shape
     return pl.pallas_call(
-        functools.partial(adjoint_kernel, heads, blocks),
+        functools.partial(adjoint_kernel, heads, blocks, len(afters)),
         out_shape=jax.ShapeDtypeStruct((count, 2 * width), F32),
-        in_specs=in_smem(1) + [pl.BlockSpec(memory_space=pl.ANY)] + in_vmem(len(dcums) + 3),
+        in_specs=in_smem(1)
+        + [pl.BlockSpec(memory_space=pl.ANY)] * len(afters)
+        + in_vmem(len(dcums) + 3),
         out_specs=pl.BlockSpec(memory_space=pltpu.VMEM),
         compiler_params=grant(60),
         cost_estimate=cost(2),
         name="adjoint",
-    )(ints, after, *dcums, unit, rows, inverse)
+    )(ints, *afters, *dcums, unit, rows, inverse)
 
 
 def house_kernel(heads, blocks, base_ref, after_ref, got_ref, unit_ref, rows_ref, house_ref, out_ref):
@@ -608,7 +634,7 @@
         in_specs=in_smem(1) + [pl.BlockSpec((1, rows, width), lambda t: (0, 0, 0))] * 3,
         out_specs=pl.BlockSpec((rows, width), lambda t: (0, 0)),
         compiler_params=grant(60),
-        cost_estimate=cost(16),
+        cost_estimate=cost(5),
         name="near_sum",
     )(ends, first, near, inward)
 
@@ -643,20 +669,23 @@
     return ((place == 0) | (place == 3)).astype(jnp.int32).reshape(1)
 
 
-def line_scatter(share, band, bands, first, rest):
-    inward = slide(rest, INWARD)
-    swapped = slide(rest[1:] + inward[1:], MIDDLE)
+def line_scatter(share, band, bands, first, rest, inward, inner):
+    swapped = slide(inner, MIDDLE)
     outward = slide(first + swapped[1:], OUTWARD)
     total = run_near(line_ends(), first, rest, inward)
     return run_share(share, band, bands, total, swapped, outward), outward
 
 
-def line_scatter_apart(share, band, bands, first, near, far, last):
+def line_scatter_apart(share, band, bands, first, near, far, last, meanwhile):
     in_last, in_far, in_near = slide(last, INWARD), slide(far, INWARD), slide(near, INWARD)
-    swap_last, swap_far = slide(last + in_last, MIDDLE), slide(far + in_far, MIDDLE)
+    sum_last = last + in_last
+    swap_last = slide(sum_last, MIDDLE)
+    other = meanwhile(sum_last)
+    sum_far, _ = lax.optimization_barrier((far + in_far, other))
+    swap_far = slide(sum_far, MIDDLE)
     outward = slide(first + swap_last, OUTWARD)
     total = run_near(line_ends(), first, near, in_near)
-    return run_share(share, band, bands, total, swap_far, outward)
+    return run_share(share, band, bands, total, swap_far, outward), other
 
 
 def shards(
@@ -675,23 +704,23 @@
         upper = (my_index & core) != 0
         low, high = jnp.where(upper, other, house_dirs), jnp.where(upper, house_dirs, other)
         house_pair = jnp.concatenate([low, high], axis=0)
-        house_parts = [house_pair] + [hop(house_pair, t, 8) for t in (2, 4, 6)]
         value_x, key_y = hop(value_rows, across, 8), hop(key_rows, along, 8)
-        key_late, value_late, *_ = lax.optimization_barrier((key_rows, value_rows, *house_parts))
-        key_x, value_y = hop(key_late, across, 8), hop(value_late, along, 8)
+        key_x, value_y = hop(key_rows, across, 8), hop(value_rows, along, 8)
+        house_late, *_ = lax.optimization_barrier((house_pair, value_x, key_y))
+        house_parts = [house_pair] + [hop(house_late, t, 8) for t in (2, 4, 6)]
         key_d, value_d = hop(key_y, across, 8), hop(value_x, along, 8)
     else:
         house_parts = [lax.all_gather(house_dirs, "ctx", axis=0, tiled=True)]
 
-    unit, rows, inverse, unit_t = run_chain(ints, house_parts, heads)
+    unit, rows, inverse, wide, tall = run_chain(ints, house_parts, heads)
     qrot, krot, local, listed_cum = run_rotate(
-        ints, rows, unit_t, query_rows, key_rows, heads, blocks
+        ints, wide, tall, query_rows, key_rows, heads, blocks
     )
     if by_hand:
-        late = lax.optimization_barrier((key_x, value_y, key_d, value_d, qrot))
-        siblings = (key_late, value_late, late[0], value_x, key_y, late[1], late[2], late[3])
-        siblings = [hop(part, core, 8) for part in siblings]
         own = (key_rows, value_rows, key_x, value_x, key_y, value_y, key_d, value_d)
+        early = lax.optimization_barrier((*own[:6], *house_parts))[:6]
+        late = lax.optimization_barrier((*own[6:], qrot))[:2]
+        siblings = [hop(part, core, 8) for part in (*early, *late)]
         sources, places = [], []
         for t in range(4):
             for pair in (own[2 * t : 2 * t + 2], siblings[2 * t : 2 * t + 2]):
@@ -716,9 +745,8 @@
 
     arrays = (dk_loc, dv_loc, dq, key_rows, dcum, local)
 
-    def project(block, layout, after, parts):
-        size = len(parts)
-        return run_project(block, size, groups, layout, flip, after, parts, (), arrays, weights)
+    def project(block, layout, afters, parts, before=()):
+        return run_project(block, groups, layout, flip, afters, parts, before, arrays, weights)
 
     if by_hand:
         got_0 = hop(outs[2], core, 8)
@@ -737,34 +765,45 @@
             return parts, back
 
         parts_0, back_0 = give_back(outs[0], got_0, 0, sent_0)
-        *sent_1, _ = lax.optimization_barrier((*sent_1, back_0))
-        parts_1, back_1 = give_back(outs[1], got_1, 0, sent_1)
-        *sent_2, _ = lax.optimization_barrier((*sent_2, back_1))
-        parts_2, _ = give_back(outs[1], got_1, 1, sent_2)
-        joint, apart = ((0,), (1, 2, 3)), ((0,), (1,), (2,), (3,))
-        *terms_0, dcum_0, _, _ = project(0, joint, sent_1[0], parts_0)
-        *terms_1, dcum_1, _, _ = project(1, joint, sent_2[0], parts_1)
-        *terms_2, dcum_2, _, _ = project(2, apart, terms_1[0], parts_2)
-        share, late = line_scatter(None, 0, 4, *terms_0)
-        share, later = line_scatter(share, 1, 4, *terms_1)
-        share = line_scatter_apart(share, 1, 2, *terms_2)
-        dcums = [dcum_0, dcum_1, dcum_2]
+        *later_1, _, _ = lax.optimization_barrier((*sent_1, back_0, sent_2))
+        parts_1, back_1 = give_back(outs[1], got_1, 0, later_1)
+        *later_2, _ = lax.optimization_barrier((*sent_2, back_1))
+        parts_2, _ = give_back(outs[1], got_1, 1, later_2)
+        rest_0, dcum_0, *grads_0 = project(0, ((1, 2, 3),), [sent_2[0]], parts_0)
+        before = (dq, *grads_0)
+        split_off = ((0,), (1, 2, 3))
+        firsts, rest_1, dcum_1, *_ = project(1, split_off, [rest_0], parts_1, before)
+        inward_0, inward_1 = slide(rest_0, INWARD), slide(rest_1, INWARD)
+        sum_0, sum_1 = rest_0[1:] + inward_0[1:], rest_1[1:] + inward_1[1:]
+        apart = ((0,), (1,), (2,), (3,))
+        *terms, dcum_2, _, _ = project(2, apart, [rest_1, sum_0], parts_2)
+        share, earlier = line_scatter(None, 0, 4, firsts[:, :BLK], rest_0, inward_0, sum_0)
+        share, later = line_scatter(share, 1, 4, firsts[:, BLK:], rest_1, inward_1, sum_1)
+
+        def adjoint_sums(after):
+            dcums = [dcum_0, dcum_1, dcum_2]
+            afters = (after, earlier)
+            return run_adjoint(ints, afters, dcums, unit, rows, inverse, heads, blocks)
+
+        share, sums = line_scatter_apart(share, 1, 2, *terms, adjoint_sums)
     else:
         spots = (owners * blocks + offsets).reshape(-1)
         empty = jnp.zeros((ctx_count * blocks, BLK, 2 * width), BF16)
         filled = empty.at[spots].add(outs[0])
         back = lax.psum_scatter(filled, "ctx", scatter_dimension=0, tiled=True)
-        late, later, dcums = key_rows, key_rows, []
+        dcums = []
         share = jnp.zeros((tok_rows, w_query.shape[0] // groups), BF16)
         for j in range(blocks):
             term, dcum_out, _, _ = project(
-                j, (tuple(range(groups)),), key_rows[None], [[(back, j)]]
+                j, (tuple(range(groups)),), [], [[(back, j)]]
             )
             dcums.append(dcum_out)
             done = lax.psum_scatter(term, "head", scatter_dimension=0, tiled=False)
             share = lax.dynamic_update_slice(share, done, (j * BLK, 0))
 
-    sums = run_adjoint(ints, late, dcums, unit, rows, inverse, heads, blocks)
+        sums = run_adjoint(ints, (), dcums, unit, rows, inverse, heads, blocks)
+        later = key_rows
+
     sums = sums.reshape(ctx_count, blocks, 2 * width)
     got = lax.all_to_all(sums, "ctx", split_axis=0, concat_axis=0, tiled=True)
     house_grad = run_house(ints, later, got, unit, rows, house_dirs, heads, blocks)

time: 224 us -> 228 us (1.018)
  local copies, waits for them, and re-layouts: 13.4 us -> 20.9 us
  Pallas kernels: 94.8 us -> 88 us
    unnamed x68 -> x86, local copies, waits for them, and re-layouts: 11.6 us -> 19.1 us
    ppermute x12, waiting for transfers between devices: 23.4 us -> 30.5 us  [slide(): return lax.ppermute(value, 'head', pairs)]
    ppermute x29, waiting for transfers between devices: 34.7 us -> 31.6 us  [hop(): return lax.ppermute(value, 'ctx', [(i, i ^ distance) for i in range(count)])]
    pallas_call x1, Pallas kernels: 8.62 us -> 5.55 us  [run_rotate(): pl.pallas_call(functools.partial(rotate_kernel, heads, blocks), out_shape...]
  transfers between devices with their start and end apart: 42 -> 42, of which waited for: 20 -> 17; matrix products, arithmetic and copies ran while one was open for 4% -> 4% of each run, Pallas kernels for 35% -> 32%
where the time goes in v3:
time: 228 us; the launch traced here: 227 us
  Pallas kernels  88 us (39%)
  waiting for transfers between devices  62.1 us (27%)
  starting transfers between devices  48.3 us (21%)
  local copies, waits for them, and re-layouts  20.9 us (9%)
  other arithmetic  6.5 us (3%)
    pallas_call x3, Pallas kernels, run_project(): pl.pallas_call(functools.partial(project_kernel, heads, len(parts[0]), si...  37.9 us
    ppermute x29, waiting for transfers between devices, hop(): return lax.ppermute(value, 'ctx', [(i, i ^ distance) for i in range(count)])  31.6 us
    ppermute x12, waiting for transfers between devices, slide(): return lax.ppermute(value, 'head', pairs)  30.5 us
    ppermute x29, starting transfers between devices, hop(): return lax.ppermute(value, 'ctx', [(i, i ^ distance) for i in range(count)])  25.4 us
    ppermute x12, starting transfers between devices, slide(): return lax.ppermute(value, 'head', pairs)  19.5 us
    unnamed x86, local copies, waits for them, and re-layouts  19.1 us
    pallas_call x1, Pallas kernels, run_attend(): pl.pallas_call(functools.partial(attend_kernel, heads, blocks, places, pi...  14.2 us
    pallas_call x1, Pallas kernels, run_adjoint(): pl.pallas_call(functools.partial(adjoint_kernel, heads, blocks, len(after...  7.32 us
  transfers between devices with their start and end apart: 42, of which 17 were waited for; matrix products, arithmetic and copies ran while one was open for 4% of the time, Pallas kernels for 32%

profile of v3, /device:TPU:0, one launch (start us, length us, event | category | flops | bytes accessed | tf_op | source)
XLA Modules:
  0.0 226.8 jit_solution(10481215098690979330)
XLA Ops:
  0.6 3.0 %collective-permute-start.1 = (bf16[512,512]{1,0:T(8,128)(2,1)}, bf16[512,512]{1,0:T(8,128)(2,1)S(1)}, u32[]{:S(2)}, u32[]{:S(2)}) collective-permute-start(bf16[512,512]{1,0:T(8,128)(2,1)} %refs_20_.2), channel_id=1, source_target_pairs={{0,8},{4,12},{8,0},{12,4},{16,24},{20,28},{24,16},{28,20},{1,9},{5... | collective-permute-start | bytes 1572872 | tf_op jit(solution)/shard_map/ppermute | solution.py:611
  8.2 8.4 %collective-permute-done.1.refs_6_ = bf16[512,512]{1,0:T(8,128)(2,1)S(1)} collective-permute-done((bf16[512,512]{1,0:T(8,128)(2,1)}, bf16[512,512]{1,0:T(8,128)(2,1)S(1)}, u32[]{:S(2)}, u32[]{:S(2)}) %collective-permute-start.1) | collective-permute-done | bytes 524320 | tf_op jit(solution)/shard_map/ppermute | solution.py:611
  22.3 5.1 %collective-permute-done.refs_5_ = bf16[512,512]{1,0:T(8,128)(2,1)S(1)} collective-permute-done((bf16[512,512]{1,0:T(8,128)(2,1)}, bf16[512,512]{1,0:T(8,128)(2,1)S(1)}, u32[]{:S(2)}, u32[]{:S(2)}) %collective-permute-start) | collective-permute-done | bytes 524320 | tf_op jit(solution)/shard_map/ppermute | solution.py:611
  31.3 4.5 %house_chain.1 = (f32[32,512]{1,0:T(8,128)S(1)}, f32[32,512]{1,0:T(8,128)S(1)}, f32[4,32,32]{2,1,0:T(8,128)S(1)}, bf16[4,128,96]{2,1,0:T(8,128)(2,1)S(1)}, bf16[4,96,128]{2,1,0:T(8,128)(2,1)S(1)}) custom-call(s32[17]{0:T(128)S(1)} %pad_add_fusion.ints_ref.refs_0_.base_ref, f32[8,512]{1,0:T(8,128)S(1)} %pad_maximum_fusion.refs_0_, ...), custom_call_target="tpu_custom_call" | custom-call | flops 6899999744 | bytes 1048576 | tf_op jit(solution)/shard_map/house_chain/pallas_call | solution.py:119
  37.7 5.6 %rotate.1 = (bf16[512,512]{1,0:T(8,128)(2,1)S(1)}, bf16[512,512]{1,0:T(8,128)(2,1)S(1)}, bf16[4,4,128,128]{3,2,1,0:T(8,128)(2,1)S(1)}, bf16[8,4,256,128]{3,2,1,0:T(8,128)(2,1)S(1)}) custom-call(s32[17]{0:T(128)S(1)} %pad_add_fusion.ints_ref.refs_0_.base_ref, bf16[4,128,96]{2,1,0:T(8,128)(2,1)S(1)} %get-tuple-element.64.wide_ref, ...), custom_call_target="tpu_custom_call" | custom-call | flops 10350000128 | bytes 1048576 | tf_op jit(solution)/shard_map/rotate/pallas_call | solution.py:187
  48.3 14.2 %attend.1 = (bf16[512,512]{1,0:T(8,128)(2,1)S(1)}, f32[4,4,128,128]{3,2,1,0:T(8,128)S(1)}, f32[512,512]{1,0:T(8,128)S(1)}, f32[512,512]{1,0:T(8,128)S(1)}, bf16[...) custom-call(s32[17]{0:T(128)S(1)} %pad_add_fusion.ints_ref.refs_0_.b, ...), custom_call_target="tpu_custom_call" | custom-call | flops 17250000896 | bytes 1048576 | tf_op jit(solution)/shard_map/attend/pallas_call | solution.py:360
  69.4 2.3 %collective-permute-done.18.got_ref = bf16[1,4,128,1024]{3,2,1,0:T(8,128)(2,1)S(1)} collective-permute-done((bf16[1,4,128,1024]{3,2,1,0:T(8,128)(2,1)S(1)}, bf16[1,4,128,1024]{3,2,1,0:T(8,128)(2,1)S(1)}, u32[]{:S(2)}, u32[]{:S(2)}) %collective-permute-start.18) | collective-permute-done | bytes 1048608 | tf_op jit(solution)/shard_map/ppermute | solution.py:611
  76.8 2.7 %collective-permute-start.22 = (bf16[1,128,1024]{2,1,0:T(8,128)(2,1)S(1)}, bf16[1,128,1024]{2,1,0:T(8,128)(2,1)S(1)}, u32[]{:S(2)}, u32[]{:S(2)}) collective-permute-start(bf16[1,128,1024]{2,1,0:T(8,128)(2,1)S(1)} %get-tuple-element.81), channel_id=1, source_target_pairs={{0,24},{4,28},{8,16},{12,20},{16,8},{20,12},{24,0},{28,4},{1,25},{... | collective-permute-start | bytes 786440 | tf_op jit(solution)/shard_map/ppermute | solution.py:611
  85.1 5.0 %collective-permute-done.21.refs_4_ = bf16[1,128,1024]{2,1,0:T(8,128)(2,1)S(1)} collective-permute-done((bf16[1,128,1024]{2,1,0:T(8,128)(2,1)S(1)}, bf16[1,128,1024]{2,1,0:T(8,128)(2,1)S(1)}, u32[]{:S(2)}, u32[]{:S(2)}) %collective-permute-start.21) | collective-permute-done | bytes 262176 | tf_op jit(solution)/shard_map/ppermute | solution.py:611
  93.8 10.5 %project.3 = (bf16[3,128,1024]{2,1,0:T(8,128)(2,1)}, f32[1,4,128,128]{3,2,1,0:T(8,128)}, bf16[128,512]{1,0:T(8,128)(2,1)}, bf16[128,512]{1,0:T(8,128)(2,1)}) custom-call(s32[1]{0:T(128)} %bitcast.1.flip_ref, bf16[2,128,1024]{2,1,0:T(8,128)(2,1)} %copy-done.10, bf16[4,128,1024]{2,1,0:T(8,128)(2,1)} %bitcast.14, bf16[4,128,1024]{2,1,0:T(8,128)(2,1)} %bitcast.10, ...), custom_call_target="tpu_custom_call" | custom-call | flops 10350000128 | bytes 1048576 | tf_op jit(solution)/shard_map/project/pallas_call | solution.py:484
  104.3 3.8 %collective-permute-start.26 = (bf16[3,128,1024]{2,1,0:T(8,128)(2,1)}, bf16[3,128,1024]{2,1,0:T(8,128)(2,1)S(1)}, u32[]{:S(2)}, u32[]{:S(2)}) collective-permute-start(bf16[3,128,1024]{2,1,0:T(8,128)(2,1)} %get-tuple-element.86.refs_0_.near_ref), channel_id=1, source_target_pairs={{0,1},{3,2},{4,5},{7,6},{8,9},{11,10},{12,13},{15,14},{16,17},{19,... | collective-permute-start | bytes 2359304 | tf_op jit(solution)/shard_map/ppermute | solution.py:615
  111.7 13.1 %project.4 = (bf16[1,256,1024]{2,1,0:T(8,128)(2,1)}, bf16[3,128,1024]{2,1,0:T(8,128)(2,1)}, f32[1,4,128,128]{3,2,1,0:T(8,128)}, bf16[128,512]{1,0:T(8,128)(2,1)}, bf16[128,512]{1,0:T(8,128)(2,1)}) custom-call(s32[1]{0:T(128)} %bitcast.1.flip_ref, bf16[3,128,1024]{2,1,0:T(8,128)(2,1)} %get-tuple-element.86.refs_0_.near_ref, bf16[12,128,1024]{2,1,0:T(8,128)(2,1)} %bitcast.11, ...), custom_call_target="tpu_custom_call" | custom-call | flops 13799999488 | bytes 1048576 | tf_op jit(solution)/shard_map/project/pallas_call | solution.py:484
  128.0 4.4 %collective-permute-done.33.refs_5_.refs_10_ = bf16[2,128,1024]{2,1,0:T(8,128)(2,1)} collective-permute-done((bf16[2,128,1024]{2,1,0:T(8,128)(2,1)S(1)}, bf16[2,128,1024]{2,1,0:T(8,128)(2,1)}, u32[]{:S(2)}, u32[]{:S(2)}) %collective-permute-start.33) | collective-permute-done | bytes 524320 | tf_op jit(solution)/shard_map/ppermute | solution.py:611
  132.4 14.3 %project.5 = (bf16[1,256,1024]{2,1,0:T(8,128)(2,1)}, bf16[1,256,1024]{2,1,0:T(8,128)(2,1)}, bf16[1,256,1024]{2,1,0:T(8,128)(2,1)}, bf16[1,256,1024]{2,1,0:T(8,12...) custom-call(s32[1]{0:T(128)} %bitcast.1.flip_ref, ...), custom_call_target="tpu_custom_call" | custom-call | flops 13799999488 | bytes 1048576 | tf_op jit(solution)/shard_map/project/pallas_call | solution.py:484
  156.0 5.1 %collective-permute-done.37 = bf16[1,256,1024]{2,1,0:T(8,128)(2,1)S(1)} collective-permute-done((bf16[1,256,1024]{2,1,0:T(8,128)(2,1)}, bf16[1,256,1024]{2,1,0:T(8,128)(2,1)S(1)}, u32[]{:S(2)}, u32[]{:S(2)}) %collective-permute-start.37) | collective-permute-done | bytes 524320 | tf_op jit(solution)/shard_map/ppermute | solution.py:615
  163.1 9.3 %collective-permute-done.36 = bf16[1,256,1024]{2,1,0:T(8,128)(2,1)S(1)} collective-permute-done((bf16[1,256,1024]{2,1,0:T(8,128)(2,1)}, bf16[1,256,1024]{2,1,0:T(8,128)(2,1)S(1)}, u32[]{:S(2)}, u32[]{:S(2)}) %collective-permute-start.36) | collective-permute-done | bytes 524320 | tf_op jit(solution)/shard_map/ppermute | solution.py:615
  172.5 7.3 %collective-permute-done.35.inward_ref = bf16[1,256,1024]{2,1,0:T(8,128)(2,1)} collective-permute-done((bf16[1,256,1024]{2,1,0:T(8,128)(2,1)}, bf16[1,256,1024]{2,1,0:T(8,128)(2,1)}, u32[]{:S(2)}, u32[]{:S(2)}) %collective-permute-start.35) | collective-permute-done | bytes 524320 | tf_op jit(solution)/shard_map/ppermute | solution.py:615
  179.8 2.5 %near_sum.5.refs_1_ = f32[256,1024]{1,0:T(8,128)} custom-call(s32[1]{0:T(128)} %bitcast.ends_ref, bf16[1,256,1024]{2,1,0:T(8,128)(2,1)} %get-tuple-element.101.first_ref, bf16[1,256,1024]{2,1,0:T(8,128)(2,1)} %get-tuple-element.102.near_ref, bf16[1,256,1024]{2,1,0:T(8,128)(2,1)} %collective-permute-done.35.inward_ref), custom_call_target="tpu_custom_call" | custom-call | flops 5750000128 | bytes 1048576 | tf_op jit(solution)/shard_map/near_sum/pallas_call | solution.py:630
  191.1 2.5 %collective-permute-done.28.refs_2_.refs_1_ = bf16[1,128,1024]{2,1,0:T(8,128)(2,1)S(1)} collective-permute-done((bf16[1,128,1024]{2,1,0:T(8,128)(2,1)S(1)}, bf16[1,128,1024]{2,1,0:T(8,128)(2,1)S(1)}, u32[]{:S(2)}, u32[]{:S(2)}) %collective-permute-start.28) | collective-permute-done | bytes 262176 | tf_op jit(solution)/shard_map/ppermute | solution.py:615
  194.3 7.3 %adjoint.1 = f32[32,1024]{1,0:T(8,128)} custom-call(s32[17]{0:T(128)} %copy-done, bf16[1,256,1024]{2,1,0:T(8,128)(2,1)} %copy-done.26, bf16[1,128,1024]{2,1,0:T(8,128)(2,1)} %copy-done.38, f32[1,4,128,128]{3,2,1,0:T(8,128)} %get-tuple-element.105.refs_2_, f32[1,4,128,128]{3,2,1,0:T(8,128)} %get-tuple-element.106.refs_3_, ...), custom_call_target="tpu_custom_call" | custom-call | flops 2300000000 | bytes 1048576 | tf_op jit(solution)/shard_map/adjoint/pallas_call | solution.py:567
  203.2 3.4 %all-to-all-start = ((f32[8,4,1024]{2,1,0:T(4,128)}), f32[8,4,1024]{2,1,0:T(4,128)S(1)}, u32[]{:S(2)}, u32[]{:S(2)}) async-start(f32[8,4,1024]{2,1,0:T(4,128)} %reshape.50), calls=%async_computation | async-start | bytes 262144 | tf_op jit(solution)/shard_map/all_to_all | solution.py:808
  214.0 2.6 %house_grad.1 = f32[4,512]{1,0:T(4,128)} custom-call(s32[17]{0:T(128)} %copy-done, bf16[1,128,1024]{2,1,0:T(8,128)(2,1)} %copy-done.34, f32[8,4,1024]{2,1,0:T(4,128)} %copy-done.31, f32[32,512]{1,0:T(8,128)} %copy-done.21, f32[32,512]{1,0:T(8,128)} %copy-done.22, f32[4,512]{1,0:T(4,128)} %house_ref.1), custom_call_target="tpu_custom_call" | custom-call | flops 2300000000 | bytes 1048576 | tf_op jit(solution)/shard_map/house_grad/pallas_call | solution.py:599
  216.6 6.3 %collective-permute-done.40.refs_3_ = bf16[1,256,1024]{2,1,0:T(8,128)(2,1)S(1)} collective-permute-done((bf16[1,256,1024]{2,1,0:T(8,128)(2,1)S(1)}, bf16[1,256,1024]{2,1,0:T(8,128)(2,1)S(1)}, u32[]{:S(2)}, u32[]{:S(2)}) %collective-permute-start.40) | collective-permute-done | bytes 524320 | tf_op jit(solution)/shard_map/ppermute | solution.py:615
  224.5 2.3 %share.5 = bf16[512,1024]{1,0:T(8,128)(2,1)} custom-call(bf16[512,1024]{1,0:T(8,128)(2,1)} %share.4.refs_0_, f32[256,1024]{1,0:T(8,128)} %near_sum.5.refs_1_, bf16[1,256,1024]{2,1,0:T(8,128)(2,1)} %copy-done.33, bf16[1,256,1024]{2,1,0:T(8,128)(2,1)} %copy-done.32), custom_call_target="tpu_custom_call", output_to_operand_aliasing={{}: (0, {})} | custom-call | flops 2300000000 | bytes 1048576 | tf_op jit(solution)/shard_map/share/pallas_call | solution.py:653
  (175 shorter events, 80.3 us)
Async XLA Ops:
  0.6 16.0 %collective-permute-start.1 = (bf16[512,512]{1,0:T(8,128)(2,1)}, bf16[512,512]{1,0:T(8,128)(2,1)S(1)}, u32[]{:S(2)}, u32[]{:S(2)}) collective-permute-start(bf16[512,512]{1,0:T(8,128)(2,1)} %refs_20_.2), channel_id=1, source_target_pairs={{0,8},{4,12},{8,0},{12,4},{16,24},{20,28},{24,16},{28,20},{1,9},{5... | collective-permute-start | bytes 1572872 | tf_op jit(solution)/shard_map/ppermute | solution.py:611
  3.6 15.1 %collective-permute-start.2 = (bf16[512,512]{1,0:T(8,128)(2,1)}, bf16[512,512]{1,0:T(8,128)(2,1)S(1)}, u32[]{:S(2)}, u32[]{:S(2)}) collective-permute-start(bf16[512,512]{1,0:T(8,128)(2,1)} %refs_15_.3), channel_id=1, source_target_pairs={{0,16},{4,20},{8,24},{12,28},{16,0},{20,4},{24,8},{28,12},{1,17},{... | collective-permute-start | bytes 1572872 | tf_op jit(solution)/shard_map/ppermute | solution.py:611
  5.2 22.2 %collective-permute-start = (bf16[512,512]{1,0:T(8,128)(2,1)}, bf16[512,512]{1,0:T(8,128)(2,1)S(1)}, u32[]{:S(2)}, u32[]{:S(2)}) collective-permute-start(bf16[512,512]{1,0:T(8,128)(2,1)} %refs_15_.3), channel_id=1, source_target_pairs={{0,8},{4,12},{8,0},{12,4},{16,24},{20,28},{24,16},{28,20},{1,9},{5... | collective-permute-start | bytes 1572872 | tf_op jit(solution)/shard_map/ppermute | solution.py:611
  5.7 23.4 %collective-permute-start.3 = (bf16[512,512]{1,0:T(8,128)(2,1)}, bf16[512,512]{1,0:T(8,128)(2,1)S(1)}, u32[]{:S(2)}, u32[]{:S(2)}) collective-permute-start(bf16[512,512]{1,0:T(8,128)(2,1)} %refs_20_.2), channel_id=1, source_target_pairs={{0,16},{4,20},{8,24},{12,28},{16,0},{20,4},{24,8},{28,12},{1,17},{... | collective-permute-start | bytes 1572872 | tf_op jit(solution)/shard_map/ppermute | solution.py:611
  27.4 15.9 %collective-permute-start.14 = (bf16[512,512]{1,0:T(8,128)(2,1)S(1)}, bf16[512,512]{1,0:T(8,128)(2,1)S(1)}, u32[]{:S(2)}, u32[]{:S(2)}) collective-permute-start(bf16[512,512]{1,0:T(8,128)(2,1)S(1)} %collective-permute-done.2.refs_9_), channel_id=1, source_target_pairs={{0,8},{4,12},{8,0},{12,4},{16,24},{20,28},{24,16},{28,20},{1,9},{5... | collective-permute-start | bytes 1572872 | tf_op jit(solution)/shard_map/ppermute | solution.py:611
  29.1 14.7 %collective-permute-start.15 = (bf16[512,512]{1,0:T(8,128)(2,1)S(1)}, bf16[512,512]{1,0:T(8,128)(2,1)S(1)}, u32[]{:S(2)}, u32[]{:S(2)}) collective-permute-start(bf16[512,512]{1,0:T(8,128)(2,1)S(1)} %collective-permute-done.1.refs_6_), channel_id=1, source_target_pairs={{0,16},{4,20},{8,24},{12,28},{16,0},{20,4},{24,8},{28,12},{1,17},{... | collective-permute-start | bytes 1572872 | tf_op jit(solution)/shard_map/ppermute | solution.py:611
  76.5 13.7 %collective-permute-start.21 = (bf16[1,128,1024]{2,1,0:T(8,128)(2,1)S(1)}, bf16[1,128,1024]{2,1,0:T(8,128)(2,1)S(1)}, u32[]{:S(2)}, u32[]{:S(2)}) collective-permute-start(bf16[1,128,1024]{2,1,0:T(8,128)(2,1)S(1)} %get-tuple-element.80), channel_id=1, source_target_pairs={{0,16},{4,20},{8,24},{12,28},{16,0},{20,4},{24,8},{28,12},{1,17},{... | collective-permute-start | bytes 786440 | tf_op jit(solution)/shard_map/ppermute | solution.py:611
  90.2 17.9 %collective-permute-start.23 = (bf16[1,128,1024]{2,1,0:T(8,128)(2,1)}, bf16[1,128,1024]{2,1,0:T(8,128)(2,1)S(1)}, u32[]{:S(2)}, u32[]{:S(2)}) collective-permute-start(bf16[1,128,1024]{2,1,0:T(8,128)(2,1)} %get-tuple-element.91.refs_0_), channel_id=1, source_target_pairs={{0,8},{4,12},{8,0},{12,4},{16,24},{20,28},{24,16},{28,20},{1,9},{5... | collective-permute-start | bytes 786440 | tf_op jit(solution)/shard_map/ppermute | solution.py:611
  91.8 16.3 %collective-permute-start.24 = (bf16[1,128,1024]{2,1,0:T(8,128)(2,1)}, bf16[1,128,1024]{2,1,0:T(8,128)(2,1)S(1)}, u32[]{:S(2)}, u32[]{:S(2)}) collective-permute-start(bf16[1,128,1024]{2,1,0:T(8,128)(2,1)} %get-tuple-element.92), channel_id=1, source_target_pairs={{0,16},{4,20},{8,24},{12,28},{16,0},{20,4},{24,8},{28,12},{1,17},{... | collective-permute-start | bytes 786440 | tf_op jit(solution)/shard_map/ppermute | solution.py:611
  92.3 15.8 %collective-permute-start.25 = (bf16[1,128,1024]{2,1,0:T(8,128)(2,1)S(1)}, bf16[1,128,1024]{2,1,0:T(8,128)(2,1)S(1)}, u32[]{:S(2)}, u32[]{:S(2)}) collective-permute-start(bf16[1,128,1024]{2,1,0:T(8,128)(2,1)S(1)} %get-tuple-element.93), channel_id=1, source_target_pairs={{0,24},{4,28},{8,16},{12,20},{16,8},{20,12},{24,0},{28,4},{1,25},{... | collective-permute-start | bytes 786440 | tf_op jit(solution)/shard_map/ppermute | solution.py:611
  104.3 22.8 %collective-permute-start.26 = (bf16[3,128,1024]{2,1,0:T(8,128)(2,1)}, bf16[3,128,1024]{2,1,0:T(8,128)(2,1)S(1)}, u32[]{:S(2)}, u32[]{:S(2)}) collective-permute-start(bf16[3,128,1024]{2,1,0:T(8,128)(2,1)} %get-tuple-element.86.refs_0_.near_ref), channel_id=1, source_target_pairs={{0,1},{3,2},{4,5},{7,6},{8,9},{11,10},{12,13},{15,14},{16,17},{19,... | collective-permute-start | bytes 2359304 | tf_op jit(solution)/shard_map/ppermute | solution.py:615
  108.1 19.9 %collective-permute-start.32 = (bf16[2,128,1024]{2,1,0:T(8,128)(2,1)S(1)}, bf16[2,128,1024]{2,1,0:T(8,128)(2,1)}, u32[]{:S(2)}, u32[]{:S(2)}) collective-permute-start(bf16[2,128,1024]{2,1,0:T(8,128)(2,1)S(1)} %copy-done.11), channel_id=1, source_target_pairs={{0,8},{4,12},{8,0},{12,4},{16,24},{20,28},{24,16},{28,20},{1,9},{5... | collective-permute-start | bytes 1572872 | tf_op jit(solution)/shard_map/ppermute | solution.py:611
  109.7 22.8 %collective-permute-start.33 = (bf16[2,128,1024]{2,1,0:T(8,128)(2,1)S(1)}, bf16[2,128,1024]{2,1,0:T(8,128)(2,1)}, u32[]{:S(2)}, u32[]{:S(2)}) collective-permute-start(bf16[2,128,1024]{2,1,0:T(8,128)(2,1)S(1)} %copy-done.9), channel_id=1, source_target_pairs={{0,16},{4,20},{8,24},{12,28},{16,0},{20,4},{24,8},{28,12},{1,17},{... | collective-permute-start | bytes 1572872 | tf_op jit(solution)/shard_map/ppermute | solution.py:611
  110.2 22.3 %collective-permute-start.34 = (bf16[2,128,1024]{2,1,0:T(8,128)(2,1)S(1)}, bf16[2,128,1024]{2,1,0:T(8,128)(2,1)}, u32[]{:S(2)}, u32[]{:S(2)}) collective-permute-start(bf16[2,128,1024]{2,1,0:T(8,128)(2,1)S(1)} %get-tuple-element.100), channel_id=1, source_target_pairs={{0,24},{4,28},{8,16},{12,20},{16,8},{20,12},{24,0},{28,4},{1,25},{... | collective-permute-start | bytes 1572872 | tf_op jit(solution)/shard_map/ppermute | solution.py:611
  124.8 28.5 %collective-permute-start.29 = (bf16[3,128,1024]{2,1,0:T(8,128)(2,1)}, bf16[3,128,1024]{2,1,0:T(8,128)(2,1)}, u32[]{:S(2)}, u32[]{:S(2)}) collective-permute-start(bf16[3,128,1024]{2,1,0:T(8,128)(2,1)} %get-tuple-element.97.near_ref.refs_0_), channel_id=1, source_target_pairs={{0,1},{3,2},{4,5},{7,6},{8,9},{11,10},{12,13},{15,14},{16,17},{19,... | collective-permute-start | bytes 2359304 | tf_op jit(solution)/shard_map/ppermute | solution.py:615
  146.8 14.3 %collective-permute-start.37 = (bf16[1,256,1024]{2,1,0:T(8,128)(2,1)}, bf16[1,256,1024]{2,1,0:T(8,128)(2,1)S(1)}, u32[]{:S(2)}, u32[]{:S(2)}) collective-permute-start(bf16[1,256,1024]{2,1,0:T(8,128)(2,1)} %get-tuple-element.104), channel_id=1, source_target_pairs={{0,1},{3,2},{4,5},{7,6},{8,9},{11,10},{12,13},{15,14},{16,17},{19,... | collective-permute-start | bytes 1572872 | tf_op jit(solution)/shard_map/ppermute | solution.py:615
  148.5 23.9 %collective-permute-start.36 = (bf16[1,256,1024]{2,1,0:T(8,128)(2,1)}, bf16[1,256,1024]{2,1,0:T(8,128)(2,1)S(1)}, u32[]{:S(2)}, u32[]{:S(2)}) collective-permute-start(bf16[1,256,1024]{2,1,0:T(8,128)(2,1)} %get-tuple-element.103), channel_id=1, source_target_pairs={{0,1},{3,2},{4,5},{7,6},{8,9},{11,10},{12,13},{15,14},{16,17},{19,... | collective-permute-start | bytes 1572872 | tf_op jit(solution)/shard_map/ppermute | solution.py:615
  149.8 30.0 %collective-permute-start.35 = (bf16[1,256,1024]{2,1,0:T(8,128)(2,1)}, bf16[1,256,1024]{2,1,0:T(8,128)(2,1)}, u32[]{:S(2)}, u32[]{:S(2)}) collective-permute-start(bf16[1,256,1024]{2,1,0:T(8,128)(2,1)} %get-tuple-element.102.near_ref), channel_id=1, source_target_pairs={{0,1},{3,2},{4,5},{7,6},{8,9},{11,10},{12,13},{15,14},{16,17},{19,... | collective-permute-start | bytes 1572872 | tf_op jit(solution)/shard_map/ppermute | solution.py:615
  151.9 30.4 %collective-permute-start.27 = (bf16[2,128,1024]{2,1,0:T(8,128)(2,1)S(1)}, bf16[2,128,1024]{2,1,0:T(8,128)(2,1)}, u32[]{:S(2)}, u32[]{:S(2)}) collective-permute-start(bf16[2,128,1024]{2,1,0:T(8,128)(2,1)S(1)} %copy-done.25), channel_id=1, source_target_pairs={{1,2},{2,1},{5,6},{6,5},{9,10},{10,9},{13,14},{14,13},{17,18},{18,... | collective-permute-start | bytes 1572872 | tf_op jit(solution)/shard_map/ppermute | solution.py:615
  154.6 27.7 %collective-permute-start.30 = (bf16[2,128,1024]{2,1,0:T(8,128)(2,1)S(1)}, bf16[2,128,1024]{2,1,0:T(8,128)(2,1)}, u32[]{:S(2)}, u32[]{:S(2)}) collective-permute-start(bf16[2,128,1024]{2,1,0:T(8,128)(2,1)S(1)} %slice_add_fusion), channel_id=1, source_target_pairs={{1,2},{2,1},{5,6},{6,5},{9,10},{10,9},{13,14},{14,13},{17,18},{18,... | collective-permute-start | bytes 1572872 | tf_op jit(solution)/shard_map/ppermute | solution.py:615
  162.4 44.2 %collective-permute-start.39 = (bf16[1,256,1024]{2,1,0:T(8,128)(2,1)S(1)}, bf16[1,256,1024]{2,1,0:T(8,128)(2,1)S(1)}, u32[]{:S(2)}, u32[]{:S(2)}) collective-permute-start(bf16[1,256,1024]{2,1,0:T(8,128)(2,1)S(1)} %add.26.refs_0_), channel_id=1, source_target_pairs={{1,2},{2,1},{5,6},{6,5},{9,10},{10,9},{13,14},{14,13},{17,18},{18,... | collective-permute-start | bytes 1572872 | tf_op jit(solution)/shard_map/ppermute | solution.py:615
  185.5 25.2 %collective-permute-start.31 = (bf16[1,128,1024]{2,1,0:T(8,128)(2,1)S(1)}, bf16[1,128,1024]{2,1,0:T(8,128)(2,1)S(1)}, u32[]{:S(2)}, u32[]{:S(2)}) collective-permute-start(bf16[1,128,1024]{2,1,0:T(8,128)(2,1)S(1)} %get-tuple-element.112), channel_id=1, source_target_pairs={{1,0},{2,3},{5,4},{6,7},{9,8},{10,11},{13,12},{14,15},{17,16},{18,... | collective-permute-start | bytes 786440 | tf_op jit(solution)/shard_map/ppermute | solution.py:615
  206.8 16.1 %collective-permute-start.40 = (bf16[1,256,1024]{2,1,0:T(8,128)(2,1)S(1)}, bf16[1,256,1024]{2,1,0:T(8,128)(2,1)S(1)}, u32[]{:S(2)}, u32[]{:S(2)}) collective-permute-start(bf16[1,256,1024]{2,1,0:T(8,128)(2,1)S(1)} %add.27), channel_id=1, source_target_pairs={{1,0},{2,3},{5,4},{6,7},{9,8},{10,11},{13,12},{14,15},{17,16},{18,... | collective-permute-start | bytes 1572872 | tf_op jit(solution)/shard_map/ppermute | solution.py:615
  208.1 14.8 %collective-permute-start.38 = (bf16[1,256,1024]{2,1,0:T(8,128)(2,1)S(1)}, bf16[1,256,1024]{2,1,0:T(8,128)(2,1)S(1)}, u32[]{:S(2)}, u32[]{:S(2)}) collective-permute-start(bf16[1,256,1024]{2,1,0:T(8,128)(2,1)S(1)} %add.25), channel_id=1, source_target_pairs={{1,2},{2,1},{5,6},{6,5},{9,10},{10,9},{13,14},{14,13},{17,18},{18,... | collective-permute-start | bytes 1572872 | tf_op jit(solution)/shard_map/ppermute | solution.py:615
  (60 other events, 433.5 us)

commit v4 on v3

--- a/solution.py
+++ b/solution.py
@@ -209,7 +209,7 @@
     dq_ref, dcum_ref, dk_ref, dv_ref = refs[7:11]
     outs = refs[11 : 11 + max(len(pieces), 1)]
     refs = refs[11 + max(len(pieces), 1) :]
-    far_keys, far_values, sems = refs[:3]
+    dq_all, dcum_all, dk_all, dv_all, grad_sems, far_keys, far_values, sems = refs[:8]
     entries = blocks * MAXL
     scaling = DH ** (-0.5)
     log_scale = scaling * math.log2(math.e)
@@ -236,7 +236,7 @@
 
     out_copies = []
     if pieces:
-        payloads, out_sems = refs[3 : 3 + heads], refs[3 + heads]
+        payloads, out_sems = refs[8 : 8 + heads], refs[8 + heads]
         for payload in payloads:
             payload[...] = jnp.zeros_like(payload)
     for kind, slots in ((0, far_keys), (1, far_values)):
@@ -303,8 +303,8 @@
             total = pairs[b][b]
             for a in range(b + 1, blocks):
                 total = total + pairs[a][b]
-            dk_ref[spans[b], lanes] = total[:, :DH] * scaling
-            dv_ref[spans[b], lanes] = total[:, DH:]
+            dk_all[h, spans[b]] = total[:, :DH] * scaling
+            dv_all[h, spans[b]] = total[:, DH:]
         for e in range(entries):
             pair = pairs[e // MAXL][e // MAXL + 1 + e % MAXL]
             dkey, dvalue = (pair[:, :DH] * scaling).astype(BF16), pair[:, DH:].astype(BF16)
@@ -323,10 +323,21 @@
             halves.append(split(tn(wide, tall) * scaling))
         for a in steps:
             dq_top, dq_low = halves[a]
-            dq_ref[spans[a], lanes] = nt(dq_top, local_ref[a, h]).astype(BF16)
+            dq_all[h, spans[a]] = nt(dq_top, local_ref[a, h]).astype(BF16)
             query = query_ref[spans[a], lanes]
             query = jnp.concatenate([query, query], axis=0)
-            dcum_ref[a, h] = tn(query, jnp.concatenate([dq_top, dq_low], axis=0))
+            dcum_all[h, a] = tn(query, jnp.concatenate([dq_top, dq_low], axis=0))
+        for i, (source, where) in enumerate(
+            (
+                (dk_all.at[h], dk_ref.at[:, lanes]),
+                (dv_all.at[h], dv_ref.at[:, lanes]),
+                (dq_all.at[h], dq_ref.at[:, lanes]),
+                (dcum_all.at[h], dcum_ref.at[:, h]),
+            )
+        ):
+            copy = pltpu.make_async_copy(source, where, grad_sems.at[i, h])
+            copy.start()
+            out_copies.append(copy)
         for i, (first, size) in enumerate(pieces):
             where = outs[i].at[:, :, :, 2 * h * DH : (2 * h + 2) * DH]
             source = payloads[h].at[pl.ds(first, size)]
@@ -342,6 +353,11 @@
     entries = blocks * MAXL
     any_spec = pl.BlockSpec(memory_space=pl.ANY)
     scratch = [
+        pltpu.VMEM((heads, rows, DH), BF16),
+        pltpu.VMEM((heads, blocks, DH, DH), F32),
+        pltpu.VMEM((heads, rows, DH), F32),
+        pltpu.VMEM((heads, rows, DH), F32),
+        pltpu.SemaphoreType.DMA((4, heads)),
         pltpu.VMEM((entries, BLK, width), BF16),
         pltpu.VMEM((entries, BLK, width), BF16),
         pltpu.SemaphoreType.DMA((2, entries)),
@@ -367,9 +383,9 @@
         ]
         + out_parts,
         in_specs=in_smem(1) + [any_spec] * len(sources) + in_vmem(7),
-        out_specs=in_vmem(4) + part_specs,
+        out_specs=[pl.BlockSpec(memory_space=pltpu.HBM)] * 4 + part_specs,
         scratch_shapes=scratch,
-        compiler_params=grant(30),
+        compiler_params=grant(58),
         cost_estimate=cost(15),
         name="attend",
     )(ints, *sources, *arrays)
@@ -577,7 +593,7 @@
     )(ints, *afters, *dcums, unit, rows, inverse)
 
 
-def house_kernel(heads, blocks, base_ref, after_ref, got_ref, unit_ref, rows_ref, house_ref, out_ref):
+def house_kernel(heads, blocks, base_ref, got_ref, unit_ref, rows_ref, house_ref, out_ref):
     count, width = unit_ref.shape
     total = jnp.sum(got_ref[...], axis=0)
     for h in range(heads):
@@ -595,16 +611,16 @@
         out_ref[:, head(h)] = (dunit - unit * inner) / lengths
 
 
-def run_house(ints, after, got, unit, rows, house_dirs, heads, blocks):
+def run_house(ints, got, unit, rows, house_dirs, heads, blocks):
     return pl.pallas_call(
         functools.partial(house_kernel, heads, blocks),
         out_shape=jax.ShapeDtypeStruct(house_dirs.shape, F32),
-        in_specs=in_smem(1) + [pl.BlockSpec(memory_space=pl.ANY)] + in_vmem(4),
+        in_specs=in_smem(1) + in_vmem(4),
         out_specs=pl.BlockSpec(memory_space=pltpu.VMEM),
         compiler_params=grant(60),
         cost_estimate=cost(2),
         name="house_grad",
-    )(ints, after, got, unit, rows, house_dirs)
+    )(ints, got, unit, rows, house_dirs)
 
 
 def hop(value, distance, count):
@@ -671,21 +687,24 @@
 
 def line_scatter(share, band, bands, first, rest, inward, inner):
     swapped = slide(inner, MIDDLE)
-    outward = slide(first + swapped[1:], OUTWARD)
+    outer = first + swapped[1:]
+    outward = slide(outer, OUTWARD)
     total = run_near(line_ends(), first, rest, inward)
-    return run_share(share, band, bands, total, swapped, outward), outward
-
-
-def line_scatter_apart(share, band, bands, first, near, far, last, meanwhile):
+    return run_share(share, band, bands, total, swapped, outward), swapped, outer
+
+
+def line_scatter_apart(share, band, bands, first, near, far, last, ready, exchange, earlier):
     in_last, in_far, in_near = slide(last, INWARD), slide(far, INWARD), slide(near, INWARD)
+    in_last, ready = lax.optimization_barrier((in_last, ready))
     sum_last = last + in_last
+    ready, *_ = lax.optimization_barrier((ready, sum_last, earlier))
+    got = exchange(ready)
     swap_last = slide(sum_last, MIDDLE)
-    other = meanwhile(sum_last)
-    sum_far, _ = lax.optimization_barrier((far + in_far, other))
-    swap_far = slide(sum_far, MIDDLE)
+    in_far, got = lax.optimization_barrier((in_far, got))
+    swap_far = slide(far + in_far, MIDDLE)
     outward = slide(first + swap_last, OUTWARD)
     total = run_near(line_ends(), first, near, in_near)
-    return run_share(share, band, bands, total, swap_far, outward), other
+    return run_share(share, band, bands, total, swap_far, outward), got
 
 
 def shards(
@@ -748,6 +767,10 @@
     def project(block, layout, afters, parts, before=()):
         return run_project(block, groups, layout, flip, afters, parts, before, arrays, weights)
 
+    def share_sums(sums):
+        sums = sums.reshape(ctx_count, blocks, 2 * width)
+        return lax.all_to_all(sums, "ctx", split_axis=0, concat_axis=0, tiled=True)
+
     if by_hand:
         got_0 = hop(outs[2], core, 8)
         got_1 = hop(lax.optimization_barrier((outs[3], got_0))[0], core, 8)
@@ -774,18 +797,21 @@
         split_off = ((0,), (1, 2, 3))
         firsts, rest_1, dcum_1, *_ = project(1, split_off, [rest_0], parts_1, before)
         inward_0, inward_1 = slide(rest_0, INWARD), slide(rest_1, INWARD)
-        sum_0, sum_1 = rest_0[1:] + inward_0[1:], rest_1[1:] + inward_1[1:]
         apart = ((0,), (1,), (2,), (3,))
-        *terms, dcum_2, _, _ = project(2, apart, [rest_1, sum_0], parts_2)
-        share, earlier = line_scatter(None, 0, 4, firsts[:, :BLK], rest_0, inward_0, sum_0)
-        share, later = line_scatter(share, 1, 4, firsts[:, BLK:], rest_1, inward_1, sum_1)
-
-        def adjoint_sums(after):
-            dcums = [dcum_0, dcum_1, dcum_2]
-            afters = (after, earlier)
-            return run_adjoint(ints, afters, dcums, unit, rows, inverse, heads, blocks)
-
-        share, sums = line_scatter_apart(share, 1, 2, *terms, adjoint_sums)
+        *terms, dcum_2, _, _ = project(2, apart, [rest_1], parts_2)
+        share, swapped_0, outer_0 = line_scatter(
+            None, 0, 4, firsts[:, :BLK], rest_0, inward_0, rest_0[1:] + inward_0[1:]
+        )
+        inward_1, _ = lax.optimization_barrier((inward_1, swapped_0))
+        sum_1 = rest_1[1:] + inward_1[1:]
+        share, _, outer_1 = line_scatter(
+            share, 1, 4, firsts[:, BLK:], rest_1, inward_1, sum_1
+        )
+        dcums = [dcum_0, dcum_1, dcum_2]
+        sums = run_adjoint(ints, (sum_1, outer_0), dcums, unit, rows, inverse, heads, blocks)
+        share, got = line_scatter_apart(
+            share, 1, 2, *terms, sums, share_sums, outer_1
+        )
     else:
         spots = (owners * blocks + offsets).reshape(-1)
         empty = jnp.zeros((ctx_count * blocks, BLK, 2 * width), BF16)
@@ -801,12 +827,9 @@
             done = lax.psum_scatter(term, "head", scatter_dimension=0, tiled=False)
             share = lax.dynamic_update_slice(share, done, (j * BLK, 0))
 
-        sums = run_adjoint(ints, (), dcums, unit, rows, inverse, heads, blocks)
-        later = key_rows
-
-    sums = sums.reshape(ctx_count, blocks, 2 * width)
-    got = lax.all_to_all(sums, "ctx", split_axis=0, concat_axis=0, tiled=True)
-    house_grad = run_house(ints, later, got, unit, rows, house_dirs, heads, blocks)
+        got = share_sums(run_adjoint(ints, (), dcums, unit, rows, inverse, heads, blocks))
+
+    house_grad = run_house(ints, got, unit, rows, house_dirs, heads, blocks)
     return (share, house_grad)
 
 

time: 228 us -> 211 us (0.925)
  waiting for transfers between devices: 62.1 us -> 51.1 us
  local copies, waits for them, and re-layouts: 20.9 us -> 16.9 us
    ppermute x12, waiting for transfers between devices: 30.5 us -> 19.3 us  [slide(): return lax.ppermute(value, 'head', pairs)]
    unnamed x86 -> x110, local copies, waits for them, and re-layouts: 19.1 us -> 15.1 us
  transfers between devices with their start and end apart: 42 -> 42, of which waited for: 17 -> 15; matrix products, arithmetic and copies ran while one was open for 4% -> 4% of each run, Pallas kernels for 32% -> 34%
where the time goes in v4:
time: 211 us; the launch traced here: 210 us
  Pallas kernels  88.6 us (42%)
  waiting for transfers between devices  51.1 us (24%)
  starting transfers between devices  47.4 us (22%)
  local copies, waits for them, and re-layouts  16.9 us (8%)
  other arithmetic  4.72 us (2%)
    pallas_call x3, Pallas kernels, run_project(): pl.pallas_call(functools.partial(project_kernel, heads, len(parts[0]), si...  37.9 us
    ppermute x29, waiting for transfers between devices, hop(): return lax.ppermute(value, 'ctx', [(i, i ^ distance) for i in range(count)])  30.4 us
    ppermute x29, starting transfers between devices, hop(): return lax.ppermute(value, 'ctx', [(i, i ^ distance) for i in range(count)])  25.5 us
    ppermute x12, waiting for transfers between devices, slide(): return lax.ppermute(value, 'head', pairs)  19.3 us
    ppermute x12, starting transfers between devices, slide(): return lax.ppermute(value, 'head', pairs)  18.5 us
    unnamed x110, local copies, waits for them, and re-layouts  15.1 us
    pallas_call x1, Pallas kernels, run_attend(): pl.pallas_call(functools.partial(attend_kernel, heads, blocks, places, pi...  14.7 us
    pallas_call x1, Pallas kernels, run_adjoint(): pl.pallas_call(functools.partial(adjoint_kernel, heads, blocks, len(after...  7.32 us
  transfers between devices with their start and end apart: 42, of which 15 were waited for; matrix products, arithmetic and copies ran while one was open for 4% of the time, Pallas kernels for 34%

profile of v4, /device:TPU:0, one launch (start us, length us, event | category | flops | bytes accessed | tf_op | source)
XLA Modules:
  0.0 209.9 jit_solution(5361217119857066081)
XLA Ops:
  0.6 3.0 %collective-permute-start.1 = (bf16[512,512]{1,0:T(8,128)(2,1)}, bf16[512,512]{1,0:T(8,128)(2,1)S(1)}, u32[]{:S(2)}, u32[]{:S(2)}) collective-permute-start(bf16[512,512]{1,0:T(8,128)(2,1)} %refs_20_.1), channel_id=1, source_target_pairs={{0,8},{4,12},{8,0},{12,4},{16,24},{20,28},{24,16},{28,20},{1,9},{5... | collective-permute-start | bytes 1572872 | tf_op jit(solution)/shard_map/ppermute | solution.py:627
  8.2 8.4 %collective-permute-done.1.refs_6_ = bf16[512,512]{1,0:T(8,128)(2,1)S(1)} collective-permute-done((bf16[512,512]{1,0:T(8,128)(2,1)}, bf16[512,512]{1,0:T(8,128)(2,1)S(1)}, u32[]{:S(2)}, u32[]{:S(2)}) %collective-permute-start.1) | collective-permute-done | bytes 524320 | tf_op jit(solution)/shard_map/ppermute | solution.py:627
  16.6 2.1 collective-permute-done.2.refs_9_
  22.3 5.1 %collective-permute-done.refs_5_ = bf16[512,512]{1,0:T(8,128)(2,1)S(1)} collective-permute-done((bf16[512,512]{1,0:T(8,128)(2,1)}, bf16[512,512]{1,0:T(8,128)(2,1)S(1)}, u32[]{:S(2)}, u32[]{:S(2)}) %collective-permute-start) | collective-permute-done | bytes 524320 | tf_op jit(solution)/shard_map/ppermute | solution.py:627
  31.3 4.5 %house_chain.1 = (f32[32,512]{1,0:T(8,128)S(1)}, f32[32,512]{1,0:T(8,128)S(1)}, f32[4,32,32]{2,1,0:T(8,128)S(1)}, bf16[4,128,96]{2,1,0:T(8,128)(2,1)S(1)}, bf16[4,96,128]{2,1,0:T(8,128)(2,1)S(1)}) custom-call(s32[17]{0:T(128)S(1)} %pad_add_fusion.ints_ref.refs_0_.base_ref, f32[8,512]{1,0:T(8,128)S(1)} %pad_maximum_fusion.refs_0_, ...), custom_call_target="tpu_custom_call" | custom-call | flops 6899999744 | bytes 1048576 | tf_op jit(solution)/shard_map/house_chain/pallas_call | solution.py:119
  37.7 5.6 %rotate.1 = (bf16[512,512]{1,0:T(8,128)(2,1)S(1)}, bf16[512,512]{1,0:T(8,128)(2,1)S(1)}, bf16[4,4,128,128]{3,2,1,0:T(8,128)(2,1)S(1)}, bf16[8,4,256,128]{3,2,1,0:T(8,128)(2,1)S(1)}) custom-call(s32[17]{0:T(128)S(1)} %pad_add_fusion.ints_ref.refs_0_.base_ref, bf16[4,128,96]{2,1,0:T(8,128)(2,1)S(1)} %get-tuple-element.69.wide_ref, ...), custom_call_target="tpu_custom_call" | custom-call | flops 10350000128 | bytes 1048576 | tf_op jit(solution)/shard_map/rotate/pallas_call | solution.py:187
  52.9 14.7 %attend.1 = (bf16[512,512]{1,0:T(8,128)(2,1)}, f32[4,4,128,128]{3,2,1,0:T(8,128)}, f32[512,512]{1,0:T(8,128)}, f32[512,512]{1,0:T(8,128)}, bf16[1,4,128,1024]{3,...) custom-call(s32[17]{0:T(128)} %copy-done, ...), custom_call_target="tpu_custom_call" | custom-call | flops 17250000896 | bytes 1048576 | tf_op jit(solution)/shard_map/attend/pallas_call | solution.py:376
  68.0 2.5 %collective-permute-done.18.got_ref = bf16[1,4,128,1024]{3,2,1,0:T(8,128)(2,1)S(1)} collective-permute-done((bf16[1,4,128,1024]{3,2,1,0:T(8,128)(2,1)}, bf16[1,4,128,1024]{3,2,1,0:T(8,128)(2,1)S(1)}, u32[]{:S(2)}, u32[]{:S(2)}) %collective-permute-start.18) | collective-permute-done | bytes 1048608 | tf_op jit(solution)/shard_map/ppermute | solution.py:627
  75.7 2.7 %collective-permute-start.22 = (bf16[1,128,1024]{2,1,0:T(8,128)(2,1)S(1)}, bf16[1,128,1024]{2,1,0:T(8,128)(2,1)S(1)}, u32[]{:S(2)}, u32[]{:S(2)}) collective-permute-start(bf16[1,128,1024]{2,1,0:T(8,128)(2,1)S(1)} %get-tuple-element.86), channel_id=1, source_target_pairs={{0,24},{4,28},{8,16},{12,20},{16,8},{20,12},{24,0},{28,4},{1,25},{... | collective-permute-start | bytes 786440 | tf_op jit(solution)/shard_map/ppermute | solution.py:627
  84.1 5.1 %collective-permute-done.21.refs_4_ = bf16[1,128,1024]{2,1,0:T(8,128)(2,1)S(1)} collective-permute-done((bf16[1,128,1024]{2,1,0:T(8,128)(2,1)S(1)}, bf16[1,128,1024]{2,1,0:T(8,128)(2,1)S(1)}, u32[]{:S(2)}, u32[]{:S(2)}) %collective-permute-start.21) | collective-permute-done | bytes 262176 | tf_op jit(solution)/shard_map/ppermute | solution.py:627
  92.7 10.5 %project.3 = (bf16[3,128,1024]{2,1,0:T(8,128)(2,1)}, f32[1,4,128,128]{3,2,1,0:T(8,128)}, bf16[128,512]{1,0:T(8,128)(2,1)}, bf16[128,512]{1,0:T(8,128)(2,1)}) custom-call(s32[1]{0:T(128)} %bitcast.1.flip_ref, bf16[2,128,1024]{2,1,0:T(8,128)(2,1)} %copy-done.8, bf16[4,128,1024]{2,1,0:T(8,128)(2,1)} %bitcast.14, bf16[4,128,1024]{2,1,0:T(8,128)(2,1)} %bitcast.10, ...), custom_call_target="tpu_custom_call" | custom-call | flops 10350000128 | bytes 1048576 | tf_op jit(solution)/shard_map/project/pallas_call | solution.py:500
  103.3 4.5 %collective-permute-start.26 = (bf16[3,128,1024]{2,1,0:T(8,128)(2,1)}, bf16[3,128,1024]{2,1,0:T(8,128)(2,1)}, u32[]{:S(2)}, u32[]{:S(2)}) collective-permute-start(bf16[3,128,1024]{2,1,0:T(8,128)(2,1)} %get-tuple-element.91.refs_0_.near_ref), channel_id=1, source_target_pairs={{0,1},{3,2},{4,5},{7,6},{8,9},{11,10},{12,13},{15,14},{16,17},{19,... | collective-permute-start | bytes 2359304 | tf_op jit(solution)/shard_map/ppermute | solution.py:631
  111.4 13.1 %project.4 = (bf16[1,256,1024]{2,1,0:T(8,128)(2,1)}, bf16[3,128,1024]{2,1,0:T(8,128)(2,1)}, f32[1,4,128,128]{3,2,1,0:T(8,128)}, bf16[128,512]{1,0:T(8,128)(2,1)}, bf16[128,512]{1,0:T(8,128)(2,1)}) custom-call(s32[1]{0:T(128)} %bitcast.1.flip_ref, bf16[3,128,1024]{2,1,0:T(8,128)(2,1)} %get-tuple-element.91.refs_0_.near_ref, bf16[12,128,1024]{2,1,0:T(8,128)(2,1)} %bitcast.11, ...), custom_call_target="tpu_custom_call" | custom-call | flops 13799999488 | bytes 1048576 | tf_op jit(solution)/shard_map/project/pallas_call | solution.py:500
  124.5 2.3 %collective-permute-start.29 = (bf16[3,128,1024]{2,1,0:T(8,128)(2,1)}, bf16[3,128,1024]{2,1,0:T(8,128)(2,1)}, u32[]{:S(2)}, u32[]{:S(2)}) collective-permute-start(bf16[3,128,1024]{2,1,0:T(8,128)(2,1)} %get-tuple-element.102.near_ref.refs_0_), channel_id=1, source_target_pairs={{0,1},{3,2},{4,5},{7,6},{8,9},{11,10},{12,13},{15,14},{16,17},{19,... | collective-permute-start | bytes 2359304 | tf_op jit(solution)/shard_map/ppermute | solution.py:631
  129.0 3.2 %collective-permute-done.33.refs_4_.refs_9_ = bf16[2,128,1024]{2,1,0:T(8,128)(2,1)} collective-permute-done((bf16[2,128,1024]{2,1,0:T(8,128)(2,1)S(1)}, bf16[2,128,1024]{2,1,0:T(8,128)(2,1)}, u32[]{:S(2)}, u32[]{:S(2)}) %collective-permute-start.33) | collective-permute-done | bytes 524320 | tf_op jit(solution)/shard_map/ppermute | solution.py:627
  132.1 14.2 %project.5 = (bf16[1,256,1024]{2,1,0:T(8,128)(2,1)}, bf16[1,256,1024]{2,1,0:T(8,128)(2,1)}, bf16[1,256,1024]{2,1,0:T(8,128)(2,1)}, bf16[1,256,1024]{2,1,0:T(8,12...) custom-call(s32[1]{0:T(128)} %bitcast.1.flip_ref, ...), custom_call_target="tpu_custom_call" | custom-call | flops 13799999488 | bytes 1048576 | tf_op jit(solution)/shard_map/project/pallas_call | solution.py:500
  146.3 2.1 collective-permute-start.35
  153.1 7.2 %collective-permute-done.35.inward_ref = bf16[1,256,1024]{2,1,0:T(8,128)(2,1)} collective-permute-done((bf16[1,256,1024]{2,1,0:T(8,128)(2,1)}, bf16[1,256,1024]{2,1,0:T(8,128)(2,1)}, u32[]{:S(2)}, u32[]{:S(2)}) %collective-permute-start.35) | collective-permute-done | bytes 524320 | tf_op jit(solution)/shard_map/ppermute | solution.py:631
  160.3 2.5 %near_sum.5.refs_1_ = f32[256,1024]{1,0:T(8,128)} custom-call(s32[1]{0:T(128)} %bitcast.ends_ref, bf16[1,256,1024]{2,1,0:T(8,128)(2,1)} %get-tuple-element.107.first_ref, bf16[1,256,1024]{2,1,0:T(8,128)(2,1)} %get-tuple-element.108.near_ref, bf16[1,256,1024]{2,1,0:T(8,128)(2,1)} %collective-permute-done.35.inward_ref), custom_call_target="tpu_custom_call" | custom-call | flops 5750000128 | bytes 1048576 | tf_op jit(solution)/shard_map/near_sum/pallas_call | solution.py:646
  165.1 7.3 %adjoint.1 = f32[32,1024]{1,0:T(8,128)} custom-call(s32[17]{0:T(128)} %copy-done, bf16[2,128,1024]{2,1,0:T(8,128)(2,1)} %copy-done.22, bf16[1,128,1024]{2,1,0:T(8,128)(2,1)} %copy-done.26, f32[1,4,128,128]{3,2,1,0:T(8,128)} %get-tuple-element.111.refs_2_, f32[1,4,128,128]{3,2,1,0:T(8,128)} %get-tuple-element.112.refs_3_, ...), custom_call_target="tpu_custom_call" | custom-call | flops 2300000000 | bytes 1048576 | tf_op jit(solution)/shard_map/adjoint/pallas_call | solution.py:583
  176.2 3.4 %all-to-all-start = ((f32[8,4,1024]{2,1,0:T(4,128)}), f32[8,4,1024]{2,1,0:T(4,128)S(1)}, u32[]{:S(2)}, u32[]{:S(2)}) async-start(f32[8,4,1024]{2,1,0:T(4,128)} %reshape.50), calls=%async_computation | async-start | bytes 262144 | tf_op jit(solution)/shard_map/all_to_all | solution.py:772
  187.5 2.6 %house_grad.1 = f32[4,512]{1,0:T(4,128)} custom-call(s32[17]{0:T(128)} %copy-done, f32[8,4,1024]{2,1,0:T(4,128)} %copy-done.27, f32[32,512]{1,0:T(8,128)} %copy-done.13, f32[32,512]{1,0:T(8,128)} %copy-done.14, f32[4,512]{1,0:T(4,128)} %house_ref.1), custom_call_target="tpu_custom_call" | custom-call | flops 2300000000 | bytes 1048576 | tf_op jit(solution)/shard_map/house_grad/pallas_call | solution.py:615
  194.7 12.1 %collective-permute-done.40.refs_3_ = bf16[1,256,1024]{2,1,0:T(8,128)(2,1)S(1)} collective-permute-done((bf16[1,256,1024]{2,1,0:T(8,128)(2,1)S(1)}, bf16[1,256,1024]{2,1,0:T(8,128)(2,1)S(1)}, u32[]{:S(2)}, u32[]{:S(2)}) %collective-permute-start.40) | collective-permute-done | bytes 524320 | tf_op jit(solution)/shard_map/ppermute | solution.py:631
  207.6 2.3 %share.5 = bf16[512,1024]{1,0:T(8,128)(2,1)} custom-call(bf16[512,1024]{1,0:T(8,128)(2,1)} %share.4.refs_0_, f32[256,1024]{1,0:T(8,128)} %near_sum.5.refs_1_, bf16[1,256,1024]{2,1,0:T(8,128)(2,1)} %copy-done.44, bf16[1,256,1024]{2,1,0:T(8,128)(2,1)} %copy-done.46), custom_call_target="tpu_custom_call", output_to_operand_aliasing={{}: (0, {})} | custom-call | flops 2300000000 | bytes 1048576 | tf_op jit(solution)/shard_map/share/pallas_call | solution.py:669
  (199 shorter events, 67.9 us)
Async XLA Ops:
  0.6 16.0 %collective-permute-start.1 = (bf16[512,512]{1,0:T(8,128)(2,1)}, bf16[512,512]{1,0:T(8,128)(2,1)S(1)}, u32[]{:S(2)}, u32[]{:S(2)}) collective-permute-start(bf16[512,512]{1,0:T(8,128)(2,1)} %refs_20_.1), channel_id=1, source_target_pairs={{0,8},{4,12},{8,0},{12,4},{16,24},{20,28},{24,16},{28,20},{1,9},{5... | collective-permute-start | bytes 1572872 | tf_op jit(solution)/shard_map/ppermute | solution.py:627
  3.6 15.1 %collective-permute-start.2 = (bf16[512,512]{1,0:T(8,128)(2,1)}, bf16[512,512]{1,0:T(8,128)(2,1)S(1)}, u32[]{:S(2)}, u32[]{:S(2)}) collective-permute-start(bf16[512,512]{1,0:T(8,128)(2,1)} %refs_14_.3), channel_id=1, source_target_pairs={{0,16},{4,20},{8,24},{12,28},{16,0},{20,4},{24,8},{28,12},{1,17},{... | collective-permute-start | bytes 1572872 | tf_op jit(solution)/shard_map/ppermute | solution.py:627
  5.2 22.2 %collective-permute-start = (bf16[512,512]{1,0:T(8,128)(2,1)}, bf16[512,512]{1,0:T(8,128)(2,1)S(1)}, u32[]{:S(2)}, u32[]{:S(2)}) collective-permute-start(bf16[512,512]{1,0:T(8,128)(2,1)} %refs_14_.3), channel_id=1, source_target_pairs={{0,8},{4,12},{8,0},{12,4},{16,24},{20,28},{24,16},{28,20},{1,9},{5... | collective-permute-start | bytes 1572872 | tf_op jit(solution)/shard_map/ppermute | solution.py:627
  5.7 23.4 %collective-permute-start.3 = (bf16[512,512]{1,0:T(8,128)(2,1)}, bf16[512,512]{1,0:T(8,128)(2,1)S(1)}, u32[]{:S(2)}, u32[]{:S(2)}) collective-permute-start(bf16[512,512]{1,0:T(8,128)(2,1)} %refs_20_.1), channel_id=1, source_target_pairs={{0,16},{4,20},{8,24},{12,28},{16,0},{20,4},{24,8},{28,12},{1,17},{... | collective-permute-start | bytes 1572872 | tf_op jit(solution)/shard_map/ppermute | solution.py:627
  27.4 19.7 %collective-permute-start.14 = (bf16[512,512]{1,0:T(8,128)(2,1)S(1)}, bf16[512,512]{1,0:T(8,128)(2,1)S(1)}, u32[]{:S(2)}, u32[]{:S(2)}) collective-permute-start(bf16[512,512]{1,0:T(8,128)(2,1)S(1)} %collective-permute-done.2.refs_9_), channel_id=1, source_target_pairs={{0,8},{4,12},{8,0},{12,4},{16,24},{20,28},{24,16},{28,20},{1,9},{5... | collective-permute-start | bytes 1572872 | tf_op jit(solution)/shard_map/ppermute | solution.py:627
  29.1 18.4 %collective-permute-start.15 = (bf16[512,512]{1,0:T(8,128)(2,1)S(1)}, bf16[512,512]{1,0:T(8,128)(2,1)S(1)}, u32[]{:S(2)}, u32[]{:S(2)}) collective-permute-start(bf16[512,512]{1,0:T(8,128)(2,1)S(1)} %collective-permute-done.1.refs_6_), channel_id=1, source_target_pairs={{0,16},{4,20},{8,24},{12,28},{16,0},{20,4},{24,8},{28,12},{1,17},{... | collective-permute-start | bytes 1572872 | tf_op jit(solution)/shard_map/ppermute | solution.py:627
  30.6 17.0 %collective-permute-start.10 = (bf16[512,512]{1,0:T(8,128)(2,1)S(1)}, bf16[512,512]{1,0:T(8,128)(2,1)S(1)}, u32[]{:S(2)}, u32[]{:S(2)}) collective-permute-start(bf16[512,512]{1,0:T(8,128)(2,1)S(1)} %collective-permute-done.refs_5_), channel_id=1, source_target_pairs={{0,4},{4,0},{8,12},{12,8},{16,20},{20,16},{24,28},{28,24},{1,5},{5... | collective-permute-start | bytes 1572872 | tf_op jit(solution)/shard_map/ppermute | solution.py:627
  30.7 17.4 %collective-permute-start.11 = (bf16[512,512]{1,0:T(8,128)(2,1)S(1)}, bf16[512,512]{1,0:T(8,128)(2,1)S(1)}, u32[]{:S(2)}, u32[]{:S(2)}) collective-permute-start(bf16[512,512]{1,0:T(8,128)(2,1)S(1)} %collective-permute-done.1.refs_6_), channel_id=1, source_target_pairs={{0,4},{4,0},{8,12},{12,8},{16,20},{20,16},{24,28},{28,24},{1,5},{5... | collective-permute-start | bytes 1572872 | tf_op jit(solution)/shard_map/ppermute | solution.py:627
  31.2 17.0 %collective-permute-start.12 = (bf16[512,512]{1,0:T(8,128)(2,1)S(1)}, bf16[512,512]{1,0:T(8,128)(2,1)S(1)}, u32[]{:S(2)}, u32[]{:S(2)}) collective-permute-start(bf16[512,512]{1,0:T(8,128)(2,1)S(1)} %collective-permute-done.2.refs_9_), channel_id=1, source_target_pairs={{0,4},{4,0},{8,12},{12,8},{16,20},{20,16},{24,28},{28,24},{1,5},{5... | collective-permute-start | bytes 1572872 | tf_op jit(solution)/shard_map/ppermute | solution.py:627
  89.2 18.6 %collective-permute-start.23 = (bf16[1,128,1024]{2,1,0:T(8,128)(2,1)}, bf16[1,128,1024]{2,1,0:T(8,128)(2,1)S(1)}, u32[]{:S(2)}, u32[]{:S(2)}) collective-permute-start(bf16[1,128,1024]{2,1,0:T(8,128)(2,1)} %get-tuple-element.96.refs_0_), channel_id=1, source_target_pairs={{0,8},{4,12},{8,0},{12,4},{16,24},{20,28},{24,16},{28,20},{1,9},{5... | collective-permute-start | bytes 786440 | tf_op jit(solution)/shard_map/ppermute | solution.py:627
  90.7 17.1 %collective-permute-start.24 = (bf16[1,128,1024]{2,1,0:T(8,128)(2,1)}, bf16[1,128,1024]{2,1,0:T(8,128)(2,1)S(1)}, u32[]{:S(2)}, u32[]{:S(2)}) collective-permute-start(bf16[1,128,1024]{2,1,0:T(8,128)(2,1)} %get-tuple-element.97), channel_id=1, source_target_pairs={{0,16},{4,20},{8,24},{12,28},{16,0},{20,4},{24,8},{28,12},{1,17},{... | collective-permute-start | bytes 786440 | tf_op jit(solution)/shard_map/ppermute | solution.py:627
  91.2 16.6 %collective-permute-start.25 = (bf16[1,128,1024]{2,1,0:T(8,128)(2,1)S(1)}, bf16[1,128,1024]{2,1,0:T(8,128)(2,1)S(1)}, u32[]{:S(2)}, u32[]{:S(2)}) collective-permute-start(bf16[1,128,1024]{2,1,0:T(8,128)(2,1)S(1)} %get-tuple-element.98), channel_id=1, source_target_pairs={{0,24},{4,28},{8,16},{12,20},{16,8},{20,12},{24,0},{28,4},{1,25},{... | collective-permute-start | bytes 786440 | tf_op jit(solution)/shard_map/ppermute | solution.py:627
  103.3 23.5 %collective-permute-start.26 = (bf16[3,128,1024]{2,1,0:T(8,128)(2,1)}, bf16[3,128,1024]{2,1,0:T(8,128)(2,1)}, u32[]{:S(2)}, u32[]{:S(2)}) collective-permute-start(bf16[3,128,1024]{2,1,0:T(8,128)(2,1)} %get-tuple-element.91.refs_0_.near_ref), channel_id=1, source_target_pairs={{0,1},{3,2},{4,5},{7,6},{8,9},{11,10},{12,13},{15,14},{16,17},{19,... | collective-permute-start | bytes 2359304 | tf_op jit(solution)/shard_map/ppermute | solution.py:631
  107.8 21.1 %collective-permute-start.32 = (bf16[2,128,1024]{2,1,0:T(8,128)(2,1)S(1)}, bf16[2,128,1024]{2,1,0:T(8,128)(2,1)}, u32[]{:S(2)}, u32[]{:S(2)}) collective-permute-start(bf16[2,128,1024]{2,1,0:T(8,128)(2,1)S(1)} %copy-done.9), channel_id=1, source_target_pairs={{0,8},{4,12},{8,0},{12,4},{16,24},{20,28},{24,16},{28,20},{1,9},{5... | collective-permute-start | bytes 1572872 | tf_op jit(solution)/shard_map/ppermute | solution.py:627
  109.4 22.8 %collective-permute-start.33 = (bf16[2,128,1024]{2,1,0:T(8,128)(2,1)S(1)}, bf16[2,128,1024]{2,1,0:T(8,128)(2,1)}, u32[]{:S(2)}, u32[]{:S(2)}) collective-permute-start(bf16[2,128,1024]{2,1,0:T(8,128)(2,1)S(1)} %copy-done.7), channel_id=1, source_target_pairs={{0,16},{4,20},{8,24},{12,28},{16,0},{20,4},{24,8},{28,12},{1,17},{... | collective-permute-start | bytes 1572872 | tf_op jit(solution)/shard_map/ppermute | solution.py:627
  109.9 22.3 %collective-permute-start.34 = (bf16[2,128,1024]{2,1,0:T(8,128)(2,1)S(1)}, bf16[2,128,1024]{2,1,0:T(8,128)(2,1)}, u32[]{:S(2)}, u32[]{:S(2)}) collective-permute-start(bf16[2,128,1024]{2,1,0:T(8,128)(2,1)S(1)} %get-tuple-element.106), channel_id=1, source_target_pairs={{0,24},{4,28},{8,16},{12,20},{16,8},{20,12},{24,0},{28,4},{1,25},{... | collective-permute-start | bytes 1572872 | tf_op jit(solution)/shard_map/ppermute | solution.py:627
  124.5 26.5 %collective-permute-start.29 = (bf16[3,128,1024]{2,1,0:T(8,128)(2,1)}, bf16[3,128,1024]{2,1,0:T(8,128)(2,1)}, u32[]{:S(2)}, u32[]{:S(2)}) collective-permute-start(bf16[3,128,1024]{2,1,0:T(8,128)(2,1)} %get-tuple-element.102.near_ref.refs_0_), channel_id=1, source_target_pairs={{0,1},{3,2},{4,5},{7,6},{8,9},{11,10},{12,13},{15,14},{16,17},{19,... | collective-permute-start | bytes 2359304 | tf_op jit(solution)/shard_map/ppermute | solution.py:631
  127.9 23.2 %collective-permute-start.27 = (bf16[2,128,1024]{2,1,0:T(8,128)(2,1)S(1)}, bf16[2,128,1024]{2,1,0:T(8,128)(2,1)S(1)}, u32[]{:S(2)}, u32[]{:S(2)}) collective-permute-start(bf16[2,128,1024]{2,1,0:T(8,128)(2,1)S(1)} %slice_add_fusion), channel_id=1, source_target_pairs={{1,2},{2,1},{5,6},{6,5},{9,10},{10,9},{13,14},{14,13},{17,18},{18,... | collective-permute-start | bytes 1572872 | tf_op jit(solution)/shard_map/ppermute | solution.py:631
  146.3 14.0 %collective-permute-start.35 = (bf16[1,256,1024]{2,1,0:T(8,128)(2,1)}, bf16[1,256,1024]{2,1,0:T(8,128)(2,1)}, u32[]{:S(2)}, u32[]{:S(2)}) collective-permute-start(bf16[1,256,1024]{2,1,0:T(8,128)(2,1)} %get-tuple-element.108.near_ref), channel_id=1, source_target_pairs={{0,1},{3,2},{4,5},{7,6},{8,9},{11,10},{12,13},{15,14},{16,17},{19,... | collective-permute-start | bytes 1572872 | tf_op jit(solution)/shard_map/ppermute | solution.py:631
  148.4 24.0 %collective-permute-start.37 = (bf16[1,256,1024]{2,1,0:T(8,128)(2,1)}, bf16[1,256,1024]{2,1,0:T(8,128)(2,1)S(1)}, u32[]{:S(2)}, u32[]{:S(2)}) collective-permute-start(bf16[1,256,1024]{2,1,0:T(8,128)(2,1)} %get-tuple-element.110), channel_id=1, source_target_pairs={{0,1},{3,2},{4,5},{7,6},{8,9},{11,10},{12,13},{15,14},{16,17},{19,... | collective-permute-start | bytes 1572872 | tf_op jit(solution)/shard_map/ppermute | solution.py:631
  149.7 34.0 %collective-permute-start.36 = (bf16[1,256,1024]{2,1,0:T(8,128)(2,1)}, bf16[1,256,1024]{2,1,0:T(8,128)(2,1)S(1)}, u32[]{:S(2)}, u32[]{:S(2)}) collective-permute-start(bf16[1,256,1024]{2,1,0:T(8,128)(2,1)} %get-tuple-element.109), channel_id=1, source_target_pairs={{0,1},{3,2},{4,5},{7,6},{8,9},{11,10},{12,13},{15,14},{16,17},{19,... | collective-permute-start | bytes 1572872 | tf_op jit(solution)/shard_map/ppermute | solution.py:631
  163.8 26.3 %collective-permute-start.28 = (bf16[1,128,1024]{2,1,0:T(8,128)(2,1)S(1)}, bf16[1,128,1024]{2,1,0:T(8,128)(2,1)S(1)}, u32[]{:S(2)}, u32[]{:S(2)}) collective-permute-start(bf16[1,128,1024]{2,1,0:T(8,128)(2,1)S(1)} %get-tuple-element.123.refs_1_), channel_id=1, source_target_pairs={{1,0},{2,3},{5,4},{6,7},{9,8},{10,11},{13,12},{14,15},{17,16},{18,... | collective-permute-start | bytes 786440 | tf_op jit(solution)/shard_map/ppermute | solution.py:631
  173.3 19.4 %collective-permute-start.31 = (bf16[1,128,1024]{2,1,0:T(8,128)(2,1)S(1)}, bf16[1,128,1024]{2,1,0:T(8,128)(2,1)}, u32[]{:S(2)}, u32[]{:S(2)}) collective-permute-start(bf16[1,128,1024]{2,1,0:T(8,128)(2,1)S(1)} %get-tuple-element.122), channel_id=1, source_target_pairs={{1,0},{2,3},{5,4},{6,7},{9,8},{10,11},{13,12},{14,15},{17,16},{18,... | collective-permute-start | bytes 786440 | tf_op jit(solution)/shard_map/ppermute | solution.py:631
  186.2 20.6 %collective-permute-start.40 = (bf16[1,256,1024]{2,1,0:T(8,128)(2,1)S(1)}, bf16[1,256,1024]{2,1,0:T(8,128)(2,1)S(1)}, u32[]{:S(2)}, u32[]{:S(2)}) collective-permute-start(bf16[1,256,1024]{2,1,0:T(8,128)(2,1)S(1)} %add.27), channel_id=1, source_target_pairs={{1,0},{2,3},{5,4},{6,7},{9,8},{10,11},{13,12},{14,15},{17,16},{18,... | collective-permute-start | bytes 1572872 | tf_op jit(solution)/shard_map/ppermute | solution.py:631
  (72 other events, 467.3 us)

commit v5 on v4

--- a/solution.py
+++ b/solution.py
@@ -365,7 +365,7 @@
     if pieces:
         chips = len(places) // 2
         out_parts = [
-            jax.ShapeDtypeStruct((size, chips, BLK, 2 * width), BF16) for _, size in pieces
+            pltpu.HBM((size, chips, BLK, 2 * width), BF16) for _, size in pieces
         ]
         part_specs = [any_spec] * len(pieces)
         scratch += [pltpu.VMEM((2 * blocks, chips, BLK, 2 * DH), BF16)] * heads
@@ -376,16 +376,16 @@
     return pl.pallas_call(
         functools.partial(attend_kernel, heads, blocks, places, pieces),
         out_shape=[
-            jax.ShapeDtypeStruct((rows, width), BF16),
-            jax.ShapeDtypeStruct((blocks, heads, DH, DH), F32),
-            jax.ShapeDtypeStruct((rows, width), F32),
-            jax.ShapeDtypeStruct((rows, width), F32),
+            pltpu.HBM((rows, width), BF16),
+            pltpu.HBM((blocks, heads, DH, DH), F32),
+            pltpu.HBM((rows, width), F32),
+            pltpu.HBM((rows, width), F32),
         ]
         + out_parts,
         in_specs=in_smem(1) + [any_spec] * len(sources) + in_vmem(7),
         out_specs=[pl.BlockSpec(memory_space=pltpu.HBM)] * 4 + part_specs,
         scratch_shapes=scratch,
-        compiler_params=grant(58),
+        compiler_params=grant(36),
         cost_estimate=cost(15),
         name="attend",
     )(ints, *sources, *arrays)
@@ -409,7 +409,7 @@
         in_specs=[whole] * 2
         + [pl.BlockSpec((1, 16, 128), lambda j, c: (0, 0, 0))] * len(afters),
         out_specs=[pl.BlockSpec((1, rows, lanes), lambda j, c: (j, 0, c))] * (chips - 1),
-        compiler_params=grant(12),
+        compiler_params=grant(60),
         cost_estimate=cost(2),
         name="merge",
     )(own, got, *afters)
@@ -701,8 +701,10 @@
     got = exchange(ready)
     swap_last = slide(sum_last, MIDDLE)
     in_far, got = lax.optimization_barrier((in_far, got))
-    swap_far = slide(far + in_far, MIDDLE)
+    sum_far = far + in_far
+    swap_far = slide(sum_far, MIDDLE)
     outward = slide(first + swap_last, OUTWARD)
+    in_near, _ = lax.optimization_barrier((in_near, sum_far))
     total = run_near(line_ends(), first, near, in_near)
     return run_share(share, band, bands, total, swap_far, outward), got
 
@@ -732,14 +734,16 @@
         house_parts = [lax.all_gather(house_dirs, "ctx", axis=0, tiled=True)]
 
     unit, rows, inverse, wide, tall = run_chain(ints, house_parts, heads)
-    qrot, krot, local, listed_cum = run_rotate(
-        ints, wide, tall, query_rows, key_rows, heads, blocks
-    )
+    ready = query_rows
     if by_hand:
         own = (key_rows, value_rows, key_x, value_x, key_y, value_y, key_d, value_d)
         early = lax.optimization_barrier((*own[:6], *house_parts))[:6]
+        siblings = [hop(part, core, 8) for part in early]
+        ready, *_ = lax.optimization_barrier((query_rows, *siblings[:3]))
+    qrot, krot, local, listed_cum = run_rotate(ints, wide, tall, ready, key_rows, heads, blocks)
+    if by_hand:
         late = lax.optimization_barrier((*own[6:], qrot))[:2]
-        siblings = [hop(part, core, 8) for part in (*early, *late)]
+        siblings += [hop(part, core, 8) for part in late]
         sources, places = [], []
         for t in range(4):
             for pair in (own[2 * t : 2 * t + 2], siblings[2 * t : 2 * t + 2]):
@@ -802,7 +806,7 @@
         share, swapped_0, outer_0 = line_scatter(
             None, 0, 4, firsts[:, :BLK], rest_0, inward_0, rest_0[1:] + inward_0[1:]
         )
-        inward_1, _ = lax.optimization_barrier((inward_1, swapped_0))
+        inward_1, *_ = lax.optimization_barrier((inward_1, swapped_0, dcum_2))
         sum_1 = rest_1[1:] + inward_1[1:]
         share, _, outer_1 = line_scatter(
             share, 1, 4, firsts[:, BLK:], rest_1, inward_1, sum_1

time: 211 us -> 204 us (0.967)
  waiting for transfers between devices: 51.1 us -> 42.3 us
  local copies, waits for them, and re-layouts: 16.9 us -> 11 us
  Pallas kernels: 88.6 us -> 94.4 us
    ppermute x12, waiting for transfers between devices: 19.3 us -> 12.5 us  [slide(): return lax.ppermute(value, 'head', pairs)]
    unnamed x110 -> x72, local copies, waits for them, and re-layouts: 15.1 us -> 9.23 us
    pallas_call x3, Pallas kernels: 3.43 us -> 8.9 us  [run_merge(): pl.pallas_call(merge_kernel, grid=(size, cut), out_shape=[jax.ShapeDtypeS...]
    ppermute x12, starting transfers between devices: 18.5 us -> 20.8 us  [slide(): return lax.ppermute(value, 'head', pairs)]
  transfers between devices with their start and end apart: 42 -> 42, of which waited for: 15 -> 11; matrix products, arithmetic and copies ran while one was open for 4% -> 3% of each run, Pallas kernels for 34% -> 38%
where the time goes in v5:
time: 204 us; the launch traced here: 203 us
  Pallas kernels  94.4 us (46%)
  starting transfers between devices  49.1 us (24%)
  waiting for transfers between devices  42.3 us (21%)
  local copies, waits for them, and re-layouts  11 us (5%)
  other arithmetic  4.52 us (2%)
    pallas_call x3, Pallas kernels, run_project(): pl.pallas_call(functools.partial(project_kernel, heads, len(parts[0]), si...  37.8 us
    ppermute x29, waiting for transfers between devices, hop(): return lax.ppermute(value, 'ctx', [(i, i ^ distance) for i in range(count)])  28.4 us
    ppermute x29, starting transfers between devices, hop(): return lax.ppermute(value, 'ctx', [(i, i ^ distance) for i in range(count)])  24.9 us
    ppermute x12, starting transfers between devices, slide(): return lax.ppermute(value, 'head', pairs)  20.8 us
    pallas_call x1, Pallas kernels, run_attend(): pl.pallas_call(functools.partial(attend_kernel, heads, blocks, places, pi...  15.2 us
    ppermute x12, waiting for transfers between devices, slide(): return lax.ppermute(value, 'head', pairs)  12.5 us
    unnamed x72, local copies, waits for them, and re-layouts  9.23 us
    pallas_call x3, Pallas kernels, run_merge(): pl.pallas_call(merge_kernel, grid=(size, cut), out_shape=[jax.ShapeDtypeS...  8.9 us
  transfers between devices with their start and end apart: 42, of which 11 were waited for; matrix products, arithmetic and copies ran while one was open for 3% of the time, Pallas kernels for 38%

profile of v5, /device:TPU:0, one launch (start us, length us, event | category | flops | bytes accessed | tf_op | source)
XLA Modules:
  0.0 202.5 jit_solution(1069335738124066895)
XLA Ops:
  0.6 3.0 %collective-permute-start.1 = (bf16[512,512]{1,0:T(8,128)(2,1)}, bf16[512,512]{1,0:T(8,128)(2,1)S(1)}, u32[]{:S(2)}, u32[]{:S(2)}) collective-permute-start(bf16[512,512]{1,0:T(8,128)(2,1)} %refs_20_.1), channel_id=1, source_target_pairs={{0,8},{4,12},{8,0},{12,4},{16,24},{20,28},{24,16},{28,20},{1,9},{5... | collective-permute-start | bytes 1572872 | tf_op jit(solution)/shard_map/ppermute | solution.py:627
  8.2 8.4 %collective-permute-done.1.refs_6_ = bf16[512,512]{1,0:T(8,128)(2,1)S(1)} collective-permute-done((bf16[512,512]{1,0:T(8,128)(2,1)}, bf16[512,512]{1,0:T(8,128)(2,1)S(1)}, u32[]{:S(2)}, u32[]{:S(2)}) %collective-permute-start.1) | collective-permute-done | bytes 524320 | tf_op jit(solution)/shard_map/ppermute | solution.py:627
  22.3 5.1 %collective-permute-done.refs_5_ = bf16[512,512]{1,0:T(8,128)(2,1)S(1)} collective-permute-done((bf16[512,512]{1,0:T(8,128)(2,1)}, bf16[512,512]{1,0:T(8,128)(2,1)S(1)}, u32[]{:S(2)}, u32[]{:S(2)}) %collective-permute-start) | collective-permute-done | bytes 524320 | tf_op jit(solution)/shard_map/ppermute | solution.py:627
  31.3 4.5 %house_chain.1 = (f32[32,512]{1,0:T(8,128)S(1)}, f32[32,512]{1,0:T(8,128)S(1)}, f32[4,32,32]{2,1,0:T(8,128)S(1)}, bf16[4,128,96]{2,1,0:T(8,128)(2,1)S(1)}, bf16[4,96,128]{2,1,0:T(8,128)(2,1)S(1)}) custom-call(s32[17]{0:T(128)S(1)} %pad_add_fusion.ints_ref.refs_0_.base_ref, f32[8,512]{1,0:T(8,128)S(1)} %pad_maximum_fusion.refs_0_, ...), custom_call_target="tpu_custom_call" | custom-call | flops 6899999744 | bytes 1048576 | tf_op jit(solution)/shard_map/house_chain/pallas_call | solution.py:119
  38.7 5.5 %rotate.1 = (bf16[512,512]{1,0:T(8,128)(2,1)S(1)}, bf16[512,512]{1,0:T(8,128)(2,1)S(1)}, bf16[4,4,128,128]{3,2,1,0:T(8,128)(2,1)S(1)}, bf16[8,4,256,128]{3,2,1,0:T(8,128)(2,1)S(1)}) custom-call(s32[17]{0:T(128)S(1)} %pad_add_fusion.ints_ref.refs_0_.base_ref, bf16[4,128,96]{2,1,0:T(8,128)(2,1)S(1)} %get-tuple-element.71.wide_ref, ...), custom_call_target="tpu_custom_call" | custom-call | flops 10350000128 | bytes 1048576 | tf_op jit(solution)/shard_map/rotate/pallas_call | solution.py:187
  47.0 15.2 %attend.1 = (bf16[512,512]{1,0:T(8,128)(2,1)}, f32[4,4,128,128]{3,2,1,0:T(8,128)}, f32[512,512]{1,0:T(8,128)}, f32[512,512]{1,0:T(8,128)}, bf16[1,4,128,1024]{3,...) custom-call(s32[17]{0:T(128)S(1)} %pad_add_fusion.ints_ref.refs_0_.b, ...), custom_call_target="tpu_custom_call" | custom-call | flops 17250000896 | bytes 1048576 | tf_op jit(solution)/shard_map/attend/pallas_call | solution.py:376
  62.4 2.8 %collective-permute-done.18.got_ref = bf16[1,4,128,1024]{3,2,1,0:T(8,128)(2,1)S(1)} collective-permute-done((bf16[1,4,128,1024]{3,2,1,0:T(8,128)(2,1)}, bf16[1,4,128,1024]{3,2,1,0:T(8,128)(2,1)S(1)}, u32[]{:S(2)}, u32[]{:S(2)}) %collective-permute-start.18) | collective-permute-done | bytes 1048608 | tf_op jit(solution)/shard_map/ppermute | solution.py:627
  66.2 2.3 %merge.3 = (bf16[1,128,1024]{2,1,0:T(8,128)(2,1)}, bf16[1,128,1024]{2,1,0:T(8,128)(2,1)}, bf16[1,128,1024]{2,1,0:T(8,128)(2,1)}) custom-call(bf16[1,4,128,1024]{3,2,1,0:T(8,128)(2,1)} %get-tuple-element.84.own_ref, bf16[1,4,128,1024]{3,2,1,0:T(8,128)(2,1)} %copy-done.22), custom_call_target="tpu_custom_call" | custom-call | flops 2300000000 | bytes 1048576 | tf_op jit(solution)/shard_map/merge/pallas_call | solution.py:405
  69.4 2.7 %collective-permute-start.22 = (bf16[1,128,1024]{2,1,0:T(8,128)(2,1)}, bf16[1,128,1024]{2,1,0:T(8,128)(2,1)}, u32[]{:S(2)}, u32[]{:S(2)}) collective-permute-start(bf16[1,128,1024]{2,1,0:T(8,128)(2,1)} %get-tuple-element.89), channel_id=1, source_target_pairs={{0,24},{4,28},{8,16},{12,20},{16,8},{20,12},{24,0},{28,4},{1,25},{... | collective-permute-start | bytes 786440 | tf_op jit(solution)/shard_map/ppermute | solution.py:627
  73.8 2.3 %merge.4 = (bf16[1,128,1024]{2,1,0:T(8,128)(2,1)}, bf16[1,128,1024]{2,1,0:T(8,128)(2,1)}, bf16[1,128,1024]{2,1,0:T(8,128)(2,1)}) custom-call(bf16[3,4,128,1024]{3,2,1,0:T(8,128)(2,1)} %get-tuple-element.80.own_ref, bf16[3,4,128,1024]{3,2,1,0:T(8,128)(2,1)} %copy-done.21, bf16[1,128,1024]{2,1,0:T(8,128)(2,1)} %get-tuple-element.85.refs_0_), custom_call_target="tpu_custom_call" | custom-call | flops 2300000000 | bytes 1048576 | tf_op jit(solution)/shard_map/merge/pallas_call | solution.py:405
  76.1 4.2 %merge.5 = (bf16[2,128,1024]{2,1,0:T(8,128)(2,1)}, bf16[2,128,1024]{2,1,0:T(8,128)(2,1)}, bf16[2,128,1024]{2,1,0:T(8,128)(2,1)}) custom-call(bf16[3,4,128,1024]{3,2,1,0:T(8,128)(2,1)} %get-tuple-element.80.own_ref, bf16[3,4,128,1024]{3,2,1,0:T(8,128)(2,1)} %copy-done.21, bf16[1,128,1024]{2,1,0:T(8,128)(2,1)} %get-tuple-element.99.refs_0_), custom_call_target="tpu_custom_call" | custom-call | flops 2300000000 | bytes 1048576 | tf_op jit(solution)/shard_map/merge/pallas_call | solution.py:405
  80.4 2.9 %collective-permute-done.21.refs_4_ = bf16[1,128,1024]{2,1,0:T(8,128)(2,1)S(1)} collective-permute-done((bf16[1,128,1024]{2,1,0:T(8,128)(2,1)}, bf16[1,128,1024]{2,1,0:T(8,128)(2,1)S(1)}, u32[]{:S(2)}, u32[]{:S(2)}) %collective-permute-start.21) | collective-permute-done | bytes 262176 | tf_op jit(solution)/shard_map/ppermute | solution.py:627
  86.8 10.4 %project.3 = (bf16[3,128,1024]{2,1,0:T(8,128)(2,1)}, f32[1,4,128,128]{3,2,1,0:T(8,128)}, bf16[128,512]{1,0:T(8,128)(2,1)}, bf16[128,512]{1,0:T(8,128)(2,1)}) custom-call(s32[1]{0:T(128)} %bitcast.1.flip_ref, bf16[2,128,1024]{2,1,0:T(8,128)(2,1)} %get-tuple-element.106.refs_0_, bf16[4,128,1024]{2,1,0:T(8,128)(2,1)} %bitcast.14, ...), custom_call_target="tpu_custom_call" | custom-call | flops 10350000128 | bytes 1048576 | tf_op jit(solution)/shard_map/project/pallas_call | solution.py:500
  97.3 3.8 %collective-permute-start.26 = (bf16[3,128,1024]{2,1,0:T(8,128)(2,1)}, bf16[3,128,1024]{2,1,0:T(8,128)(2,1)S(1)}, u32[]{:S(2)}, u32[]{:S(2)}) collective-permute-start(bf16[3,128,1024]{2,1,0:T(8,128)(2,1)} %get-tuple-element.94.refs_0_.near_ref), channel_id=1, source_target_pairs={{0,1},{3,2},{4,5},{7,6},{8,9},{11,10},{12,13},{15,14},{16,17},{19,... | collective-permute-start | bytes 2359304 | tf_op jit(solution)/shard_map/ppermute | solution.py:631
  104.7 13.1 %project.4 = (bf16[1,256,1024]{2,1,0:T(8,128)(2,1)}, bf16[3,128,1024]{2,1,0:T(8,128)(2,1)}, f32[1,4,128,128]{3,2,1,0:T(8,128)}, bf16[128,512]{1,0:T(8,128)(2,1)}, bf16[128,512]{1,0:T(8,128)(2,1)}) custom-call(s32[1]{0:T(128)} %bitcast.1.flip_ref, bf16[3,128,1024]{2,1,0:T(8,128)(2,1)} %get-tuple-element.94.refs_0_.near_ref, bf16[12,128,1024]{2,1,0:T(8,128)(2,1)} %bitcast.11, ...), custom_call_target="tpu_custom_call" | custom-call | flops 13799999488 | bytes 1048576 | tf_op jit(solution)/shard_map/project/pallas_call | solution.py:500
  121.0 4.9 %collective-permute-done.31.refs_4_.refs_9_ = bf16[2,128,1024]{2,1,0:T(8,128)(2,1)} collective-permute-done((bf16[2,128,1024]{2,1,0:T(8,128)(2,1)}, bf16[2,128,1024]{2,1,0:T(8,128)(2,1)}, u32[]{:S(2)}, u32[]{:S(2)}) %collective-permute-start.31) | collective-permute-done | bytes 524320 | tf_op jit(solution)/shard_map/ppermute | solution.py:627
  125.9 14.2 %project.5 = (bf16[1,256,1024]{2,1,0:T(8,128)(2,1)}, bf16[1,256,1024]{2,1,0:T(8,128)(2,1)}, bf16[1,256,1024]{2,1,0:T(8,128)(2,1)}, bf16[1,256,1024]{2,1,0:T(8,12...) custom-call(s32[1]{0:T(128)} %bitcast.1.flip_ref, ...), custom_call_target="tpu_custom_call" | custom-call | flops 13799999488 | bytes 1048576 | tf_op jit(solution)/shard_map/project/pallas_call | solution.py:500
  142.1 4.3 %collective-permute-start.37 = (bf16[1,256,1024]{2,1,0:T(8,128)(2,1)}, bf16[1,256,1024]{2,1,0:T(8,128)(2,1)S(1)}, u32[]{:S(2)}, u32[]{:S(2)}) collective-permute-start(bf16[1,256,1024]{2,1,0:T(8,128)(2,1)} %get-tuple-element.114), channel_id=1, source_target_pairs={{0,1},{3,2},{4,5},{7,6},{8,9},{11,10},{12,13},{15,14},{16,17},{19,... | collective-permute-start | bytes 1572872 | tf_op jit(solution)/shard_map/ppermute | solution.py:631
  154.1 7.3 %adjoint.1 = f32[32,1024]{1,0:T(8,128)} custom-call(s32[17]{0:T(128)} %copy-done, bf16[2,128,1024]{2,1,0:T(8,128)(2,1)} %copy-done.12, bf16[1,128,1024]{2,1,0:T(8,128)(2,1)} %copy-done.17, f32[1,4,128,128]{3,2,1,0:T(8,128)} %get-tuple-element.115.refs_2_, f32[1,4,128,128]{3,2,1,0:T(8,128)} %get-tuple-element.116.refs_3_, ...), custom_call_target="tpu_custom_call" | custom-call | flops 2300000000 | bytes 1048576 | tf_op jit(solution)/shard_map/adjoint/pallas_call | solution.py:583
  165.3 3.4 %all-to-all-start = ((f32[8,4,1024]{2,1,0:T(4,128)}), f32[8,4,1024]{2,1,0:T(4,128)S(1)}, u32[]{:S(2)}, u32[]{:S(2)}) async-start(f32[8,4,1024]{2,1,0:T(4,128)} %reshape.50), calls=%async_computation | async-start | bytes 262144 | tf_op jit(solution)/shard_map/all_to_all | solution.py:776
  175.0 2.9 %collective-permute-done.35.inward_ref = bf16[1,256,1024]{2,1,0:T(8,128)(2,1)} collective-permute-done((bf16[1,256,1024]{2,1,0:T(8,128)(2,1)}, bf16[1,256,1024]{2,1,0:T(8,128)(2,1)}, u32[]{:S(2)}, u32[]{:S(2)}) %collective-permute-start.35) | collective-permute-done | bytes 524320 | tf_op jit(solution)/shard_map/ppermute | solution.py:631
  177.9 2.5 %near_sum.5.refs_1_ = f32[256,1024]{1,0:T(8,128)} custom-call(s32[1]{0:T(128)} %bitcast.ends_ref, bf16[1,256,1024]{2,1,0:T(8,128)(2,1)} %get-tuple-element.111.first_ref, bf16[1,256,1024]{2,1,0:T(8,128)(2,1)} %get-tuple-element.112.near_ref, bf16[1,256,1024]{2,1,0:T(8,128)(2,1)} %collective-permute-done.35.inward_ref), custom_call_target="tpu_custom_call" | custom-call | flops 5750000128 | bytes 1048576 | tf_op jit(solution)/shard_map/near_sum/pallas_call | solution.py:646
  181.9 2.6 %house_grad.1 = f32[4,512]{1,0:T(4,128)} custom-call(s32[17]{0:T(128)} %copy-done, f32[8,4,1024]{2,1,0:T(4,128)} %copy-done.18, f32[32,512]{1,0:T(8,128)} %copy-done.6, f32[32,512]{1,0:T(8,128)} %copy-done.7, f32[4,512]{1,0:T(4,128)} %house_ref.1), custom_call_target="tpu_custom_call" | custom-call | flops 2300000000 | bytes 1048576 | tf_op jit(solution)/shard_map/house_grad/pallas_call | solution.py:615
  189.8 9.6 %collective-permute-done.40.refs_3_ = bf16[1,256,1024]{2,1,0:T(8,128)(2,1)S(1)} collective-permute-done((bf16[1,256,1024]{2,1,0:T(8,128)(2,1)S(1)}, bf16[1,256,1024]{2,1,0:T(8,128)(2,1)S(1)}, u32[]{:S(2)}, u32[]{:S(2)}) %collective-permute-start.40) | collective-permute-done | bytes 524320 | tf_op jit(solution)/shard_map/ppermute | solution.py:631
  (161 shorter events, 63.4 us)
Async XLA Ops:
  0.6 16.0 %collective-permute-start.1 = (bf16[512,512]{1,0:T(8,128)(2,1)}, bf16[512,512]{1,0:T(8,128)(2,1)S(1)}, u32[]{:S(2)}, u32[]{:S(2)}) collective-permute-start(bf16[512,512]{1,0:T(8,128)(2,1)} %refs_20_.1), channel_id=1, source_target_pairs={{0,8},{4,12},{8,0},{12,4},{16,24},{20,28},{24,16},{28,20},{1,9},{5... | collective-permute-start | bytes 1572872 | tf_op jit(solution)/shard_map/ppermute | solution.py:627
  3.6 15.1 %collective-permute-start.2 = (bf16[512,512]{1,0:T(8,128)(2,1)}, bf16[512,512]{1,0:T(8,128)(2,1)S(1)}, u32[]{:S(2)}, u32[]{:S(2)}) collective-permute-start(bf16[512,512]{1,0:T(8,128)(2,1)} %refs_14_.3), channel_id=1, source_target_pairs={{0,16},{4,20},{8,24},{12,28},{16,0},{20,4},{24,8},{28,12},{1,17},{... | collective-permute-start | bytes 1572872 | tf_op jit(solution)/shard_map/ppermute | solution.py:627
  5.2 22.2 %collective-permute-start = (bf16[512,512]{1,0:T(8,128)(2,1)}, bf16[512,512]{1,0:T(8,128)(2,1)S(1)}, u32[]{:S(2)}, u32[]{:S(2)}) collective-permute-start(bf16[512,512]{1,0:T(8,128)(2,1)} %refs_14_.3), channel_id=1, source_target_pairs={{0,8},{4,12},{8,0},{12,4},{16,24},{20,28},{24,16},{28,20},{1,9},{5... | collective-permute-start | bytes 1572872 | tf_op jit(solution)/shard_map/ppermute | solution.py:627
  5.7 23.4 %collective-permute-start.3 = (bf16[512,512]{1,0:T(8,128)(2,1)}, bf16[512,512]{1,0:T(8,128)(2,1)S(1)}, u32[]{:S(2)}, u32[]{:S(2)}) collective-permute-start(bf16[512,512]{1,0:T(8,128)(2,1)} %refs_20_.1), channel_id=1, source_target_pairs={{0,16},{4,20},{8,24},{12,28},{16,0},{20,4},{24,8},{28,12},{1,17},{... | collective-permute-start | bytes 1572872 | tf_op jit(solution)/shard_map/ppermute | solution.py:627
  27.4 16.9 %collective-permute-start.14 = (bf16[512,512]{1,0:T(8,128)(2,1)S(1)}, bf16[512,512]{1,0:T(8,128)(2,1)S(1)}, u32[]{:S(2)}, u32[]{:S(2)}) collective-permute-start(bf16[512,512]{1,0:T(8,128)(2,1)S(1)} %collective-permute-done.2.refs_9_), channel_id=1, source_target_pairs={{0,8},{4,12},{8,0},{12,4},{16,24},{20,28},{24,16},{28,20},{1,9},{5... | collective-permute-start | bytes 1572872 | tf_op jit(solution)/shard_map/ppermute | solution.py:627
  29.1 15.1 %collective-permute-start.15 = (bf16[512,512]{1,0:T(8,128)(2,1)S(1)}, bf16[512,512]{1,0:T(8,128)(2,1)S(1)}, u32[]{:S(2)}, u32[]{:S(2)}) collective-permute-start(bf16[512,512]{1,0:T(8,128)(2,1)S(1)} %collective-permute-done.1.refs_6_), channel_id=1, source_target_pairs={{0,16},{4,20},{8,24},{12,28},{16,0},{20,4},{24,8},{28,12},{1,17},{... | collective-permute-start | bytes 1572872 | tf_op jit(solution)/shard_map/ppermute | solution.py:627
  69.2 14.1 %collective-permute-start.21 = (bf16[1,128,1024]{2,1,0:T(8,128)(2,1)}, bf16[1,128,1024]{2,1,0:T(8,128)(2,1)S(1)}, u32[]{:S(2)}, u32[]{:S(2)}) collective-permute-start(bf16[1,128,1024]{2,1,0:T(8,128)(2,1)} %get-tuple-element.88), channel_id=1, source_target_pairs={{0,16},{4,20},{8,24},{12,28},{16,0},{20,4},{24,8},{28,12},{1,17},{... | collective-permute-start | bytes 786440 | tf_op jit(solution)/shard_map/ppermute | solution.py:627
  83.3 17.8 %collective-permute-start.23 = (bf16[1,128,1024]{2,1,0:T(8,128)(2,1)S(1)}, bf16[1,128,1024]{2,1,0:T(8,128)(2,1)S(1)}, u32[]{:S(2)}, u32[]{:S(2)}) collective-permute-start(bf16[1,128,1024]{2,1,0:T(8,128)(2,1)S(1)} %copy-done.33), channel_id=1, source_target_pairs={{0,8},{4,12},{8,0},{12,4},{16,24},{20,28},{24,16},{28,20},{1,9},{5... | collective-permute-start | bytes 786440 | tf_op jit(solution)/shard_map/ppermute | solution.py:627
  84.8 16.2 %collective-permute-start.24 = (bf16[1,128,1024]{2,1,0:T(8,128)(2,1)S(1)}, bf16[1,128,1024]{2,1,0:T(8,128)(2,1)S(1)}, u32[]{:S(2)}, u32[]{:S(2)}) collective-permute-start(bf16[1,128,1024]{2,1,0:T(8,128)(2,1)S(1)} %copy-done.31), channel_id=1, source_target_pairs={{0,16},{4,20},{8,24},{12,28},{16,0},{20,4},{24,8},{28,12},{1,17},{... | collective-permute-start | bytes 786440 | tf_op jit(solution)/shard_map/ppermute | solution.py:627
  85.3 15.7 %collective-permute-start.25 = (bf16[1,128,1024]{2,1,0:T(8,128)(2,1)S(1)}, bf16[1,128,1024]{2,1,0:T(8,128)(2,1)S(1)}, u32[]{:S(2)}, u32[]{:S(2)}) collective-permute-start(bf16[1,128,1024]{2,1,0:T(8,128)(2,1)S(1)} %copy-done.28), channel_id=1, source_target_pairs={{0,24},{4,28},{8,16},{12,20},{16,8},{20,12},{24,0},{28,4},{1,25},{... | collective-permute-start | bytes 786440 | tf_op jit(solution)/shard_map/ppermute | solution.py:627
  97.3 22.8 %collective-permute-start.26 = (bf16[3,128,1024]{2,1,0:T(8,128)(2,1)}, bf16[3,128,1024]{2,1,0:T(8,128)(2,1)S(1)}, u32[]{:S(2)}, u32[]{:S(2)}) collective-permute-start(bf16[3,128,1024]{2,1,0:T(8,128)(2,1)} %get-tuple-element.94.refs_0_.near_ref), channel_id=1, source_target_pairs={{0,1},{3,2},{4,5},{7,6},{8,9},{11,10},{12,13},{15,14},{16,17},{19,... | collective-permute-start | bytes 2359304 | tf_op jit(solution)/shard_map/ppermute | solution.py:631
  101.1 19.9 %collective-permute-start.30 = (bf16[2,128,1024]{2,1,0:T(8,128)(2,1)}, bf16[2,128,1024]{2,1,0:T(8,128)(2,1)}, u32[]{:S(2)}, u32[]{:S(2)}) collective-permute-start(bf16[2,128,1024]{2,1,0:T(8,128)(2,1)} %get-tuple-element.106.refs_0_), channel_id=1, source_target_pairs={{0,8},{4,12},{8,0},{12,4},{16,24},{20,28},{24,16},{28,20},{1,9},{5... | collective-permute-start | bytes 1572872 | tf_op jit(solution)/shard_map/ppermute | solution.py:627
  102.6 23.2 %collective-permute-start.31 = (bf16[2,128,1024]{2,1,0:T(8,128)(2,1)}, bf16[2,128,1024]{2,1,0:T(8,128)(2,1)}, u32[]{:S(2)}, u32[]{:S(2)}) collective-permute-start(bf16[2,128,1024]{2,1,0:T(8,128)(2,1)} %get-tuple-element.107), channel_id=1, source_target_pairs={{0,16},{4,20},{8,24},{12,28},{16,0},{20,4},{24,8},{28,12},{1,17},{... | collective-permute-start | bytes 1572872 | tf_op jit(solution)/shard_map/ppermute | solution.py:627
  103.1 22.7 %collective-permute-start.32 = (bf16[2,128,1024]{2,1,0:T(8,128)(2,1)}, bf16[2,128,1024]{2,1,0:T(8,128)(2,1)}, u32[]{:S(2)}, u32[]{:S(2)}) collective-permute-start(bf16[2,128,1024]{2,1,0:T(8,128)(2,1)} %get-tuple-element.108), channel_id=1, source_target_pairs={{0,24},{4,28},{8,16},{12,20},{16,8},{20,12},{24,0},{28,4},{1,25},{... | collective-permute-start | bytes 1572872 | tf_op jit(solution)/shard_map/ppermute | solution.py:627
  117.8 22.3 %collective-permute-start.29 = (bf16[3,128,1024]{2,1,0:T(8,128)(2,1)}, bf16[3,128,1024]{2,1,0:T(8,128)(2,1)}, u32[]{:S(2)}, u32[]{:S(2)}) collective-permute-start(bf16[3,128,1024]{2,1,0:T(8,128)(2,1)} %get-tuple-element.105.refs_0_.near_ref), channel_id=1, source_target_pairs={{0,1},{3,2},{4,5},{7,6},{8,9},{11,10},{12,13},{15,14},{16,17},{19,... | collective-permute-start | bytes 2359304 | tf_op jit(solution)/shard_map/ppermute | solution.py:631
  120.1 20.0 %collective-permute-start.27 = (bf16[2,128,1024]{2,1,0:T(8,128)(2,1)S(1)}, bf16[2,128,1024]{2,1,0:T(8,128)(2,1)S(1)}, u32[]{:S(2)}, u32[]{:S(2)}) collective-permute-start(bf16[2,128,1024]{2,1,0:T(8,128)(2,1)S(1)} %slice_add_fusion), channel_id=1, source_target_pairs={{1,2},{2,1},{5,6},{6,5},{9,10},{10,9},{13,14},{14,13},{17,18},{18,... | collective-permute-start | bytes 1572872 | tf_op jit(solution)/shard_map/ppermute | solution.py:631
  142.1 19.3 %collective-permute-start.37 = (bf16[1,256,1024]{2,1,0:T(8,128)(2,1)}, bf16[1,256,1024]{2,1,0:T(8,128)(2,1)S(1)}, u32[]{:S(2)}, u32[]{:S(2)}) collective-permute-start(bf16[1,256,1024]{2,1,0:T(8,128)(2,1)} %get-tuple-element.114), channel_id=1, source_target_pairs={{0,1},{3,2},{4,5},{7,6},{8,9},{11,10},{12,13},{15,14},{16,17},{19,... | collective-permute-start | bytes 1572872 | tf_op jit(solution)/shard_map/ppermute | solution.py:631
  146.5 26.2 %collective-permute-start.36 = (bf16[1,256,1024]{2,1,0:T(8,128)(2,1)}, bf16[1,256,1024]{2,1,0:T(8,128)(2,1)S(1)}, u32[]{:S(2)}, u32[]{:S(2)}) collective-permute-start(bf16[1,256,1024]{2,1,0:T(8,128)(2,1)} %get-tuple-element.113), channel_id=1, source_target_pairs={{0,1},{3,2},{4,5},{7,6},{8,9},{11,10},{12,13},{15,14},{16,17},{19,... | collective-permute-start | bytes 1572872 | tf_op jit(solution)/shard_map/ppermute | solution.py:631
  147.8 30.1 %collective-permute-start.35 = (bf16[1,256,1024]{2,1,0:T(8,128)(2,1)}, bf16[1,256,1024]{2,1,0:T(8,128)(2,1)}, u32[]{:S(2)}, u32[]{:S(2)}) collective-permute-start(bf16[1,256,1024]{2,1,0:T(8,128)(2,1)} %get-tuple-element.112.near_ref), channel_id=1, source_target_pairs={{0,1},{3,2},{4,5},{7,6},{8,9},{11,10},{12,13},{15,14},{16,17},{19,... | collective-permute-start | bytes 1572872 | tf_op jit(solution)/shard_map/ppermute | solution.py:631
  152.6 31.9 %collective-permute-start.28 = (bf16[1,128,1024]{2,1,0:T(8,128)(2,1)S(1)}, bf16[1,128,1024]{2,1,0:T(8,128)(2,1)S(1)}, u32[]{:S(2)}, u32[]{:S(2)}) collective-permute-start(bf16[1,128,1024]{2,1,0:T(8,128)(2,1)S(1)} %get-tuple-element.127.refs_1_), channel_id=1, source_target_pairs={{1,0},{2,3},{5,4},{6,7},{9,8},{10,11},{13,12},{14,15},{17,16},{18,... | collective-permute-start | bytes 786440 | tf_op jit(solution)/shard_map/ppermute | solution.py:631
  161.7 18.7 %collective-permute-start.39 = (bf16[1,256,1024]{2,1,0:T(8,128)(2,1)S(1)}, bf16[1,256,1024]{2,1,0:T(8,128)(2,1)S(1)}, u32[]{:S(2)}, u32[]{:S(2)}) collective-permute-start(bf16[1,256,1024]{2,1,0:T(8,128)(2,1)S(1)} %add.25), channel_id=1, source_target_pairs={{1,2},{2,1},{5,6},{6,5},{9,10},{10,9},{13,14},{14,13},{17,18},{18,... | collective-permute-start | bytes 1572872 | tf_op jit(solution)/shard_map/ppermute | solution.py:631
  162.4 24.7 %collective-permute-start.34 = (bf16[1,128,1024]{2,1,0:T(8,128)(2,1)S(1)}, bf16[1,128,1024]{2,1,0:T(8,128)(2,1)S(1)}, u32[]{:S(2)}, u32[]{:S(2)}) collective-permute-start(bf16[1,128,1024]{2,1,0:T(8,128)(2,1)S(1)} %get-tuple-element.126), channel_id=1, source_target_pairs={{1,0},{2,3},{5,4},{6,7},{9,8},{10,11},{13,12},{14,15},{17,16},{18,... | collective-permute-start | bytes 786440 | tf_op jit(solution)/shard_map/ppermute | solution.py:631
  174.3 15.5 %collective-permute-start.38 = (bf16[1,256,1024]{2,1,0:T(8,128)(2,1)S(1)}, bf16[1,256,1024]{2,1,0:T(8,128)(2,1)S(1)}, u32[]{:S(2)}, u32[]{:S(2)}) collective-permute-start(bf16[1,256,1024]{2,1,0:T(8,128)(2,1)S(1)} %add.26), channel_id=1, source_target_pairs={{1,2},{2,1},{5,6},{6,5},{9,10},{10,9},{13,14},{14,13},{17,18},{18,... | collective-permute-start | bytes 1572872 | tf_op jit(solution)/shard_map/ppermute | solution.py:631
  180.6 18.8 %collective-permute-start.40 = (bf16[1,256,1024]{2,1,0:T(8,128)(2,1)S(1)}, bf16[1,256,1024]{2,1,0:T(8,128)(2,1)S(1)}, u32[]{:S(2)}, u32[]{:S(2)}) collective-permute-start(bf16[1,256,1024]{2,1,0:T(8,128)(2,1)S(1)} %add.27), channel_id=1, source_target_pairs={{1,0},{2,3},{5,4},{6,7},{9,8},{10,11},{13,12},{14,15},{17,16},{18,... | collective-permute-start | bytes 1572872 | tf_op jit(solution)/shard_map/ppermute | solution.py:631
  (53 other events, 430.3 us)

commit v6 on v5

--- a/solution.py
+++ b/solution.py
@@ -239,111 +239,121 @@
         payloads, out_sems = refs[8 : 8 + heads], refs[8 + heads]
         for payload in payloads:
             payload[...] = jnp.zeros_like(payload)
-    for kind, slots in ((0, far_keys), (1, far_values)):
-        for e in range(entries):
-            pltpu.make_async_copy(slots.at[e], slots.at[e], sems.at[kind, e]).wait()
-
     later = iota((BLK, BLK), 0) > iota((BLK, BLK), 1)
     empty = jnp.zeros((BLK, DH), BF16)
-    steps = range(blocks)
-    for h in range(heads):
-        lanes = head(h)
-        spans = [slice(a * BLK, (a + 1) * BLK) for a in steps]
-        both, keys, values = [], [], []
-        for a in steps:
+    def wait_far():
+        for kind, slots in ((0, far_keys), (1, far_values)):
+            for e in range(entries):
+                pltpu.make_async_copy(slots.at[e], slots.at[e], sems.at[kind, e]).wait()
+
+    spans = [slice(a * BLK, (a + 1) * BLK) for a in range(blocks)]
+    group = 2 if heads % 2 == 0 else 1
+    for start_head in range(0, heads, group):
+        steps = [(h, a) for h in range(start_head, start_head + group) for a in range(blocks)]
+        both, keys, values, scores, dprobs, tops = {}, {}, {}, {}, {}, {}
+
+        def score(step, b, key, value):
+            pair = nt(jnp.concatenate([key, value], axis=1), both[step])
+            part = pair[:, :BLK] * log_scale
+            if b == step[1]:
+                part = jnp.where(later, -jnp.inf, part)
+            keys[step].append(key)
+            scores[step].append(part)
+            dprobs[step].append(pair[:, BLK:])
+            tops[step] = part if b == 0 else jnp.maximum(tops[step], part)
+
+        for step in steps:
+            h, a = step
+            lanes = head(h)
             qrot, grad = qrot_ref[spans[a], lanes], grad_ref[spans[a], lanes]
             upper = jnp.concatenate([qrot, empty], axis=1)
             lower = jnp.concatenate([empty, grad], axis=1)
-            both.append(jnp.concatenate([upper, lower], axis=0))
-            keys.append([krot_ref[spans[b], lanes] for b in range(a + 1)])
-            values.append([value_ref[spans[b], lanes] for b in range(a + 1)])
+            both[step] = jnp.concatenate([upper, lower], axis=0)
+            keys[step], scores[step], dprobs[step] = [], [], []
+            for b in range(a + 1):
+                score(step, b, krot_ref[spans[b], lanes], value_ref[spans[b], lanes])
+        if start_head == 0:
+            wait_far()
+        for step in steps:
+            h, a = step
             for l in range(MAXL):
                 e = a * MAXL + l
-                raw = far_keys[e, :, lanes]
+                raw = far_keys[e, :, head(h)]
                 raw = jnp.concatenate([raw, raw], axis=1)
-                keys[a].append(nn(raw, listed_ref[e, h]).astype(BF16))
-                values[a].append(far_values[e, :, lanes])
-        scores, dprobs, tops = [], [], []
-        for a in steps:
-            scores.append([])
-            dprobs.append([])
-            top = None
-            for b in range(a + 1 + MAXL):
-                pair = nt(jnp.concatenate([keys[a][b], values[a][b]], axis=1), both[a])
-                part = pair[:, :BLK] * log_scale
-                if b == a:
-                    part = jnp.where(later, -jnp.inf, part)
-                scores[a].append(part)
-                dprobs[a].append(pair[:, BLK:])
-                top = part if top is None else jnp.maximum(top, part)
-            tops.append(jnp.max(top, axis=0, keepdims=True))
-        weights, inverses, deltas = [], [], []
-        for a in steps:
-            weights.append([])
+                key = nn(raw, listed_ref[e, h]).astype(BF16)
+                score(step, a + 1 + l, key, far_values[e, :, head(h)])
+        weights, inverses, deltas = {}, {}, {}
+        for step in steps:
+            top = jnp.max(tops[step], axis=0, keepdims=True)
+            weights[step] = []
             total, inner = None, None
-            for part, dprob in zip(scores[a], dprobs[a]):
-                weight = jnp.exp2(part - tops[a])
-                weights[a].append(weight)
+            for part, dprob in zip(scores[step], dprobs[step]):
+                weight = jnp.exp2(part - top)
+                weights[step].append(weight)
                 product = weight * dprob
                 total = weight if total is None else total + weight
                 inner = product if inner is None else inner + product
-            inverses.append(1.0 / jnp.sum(total, axis=0, keepdims=True))
-            deltas.append(jnp.sum(inner, axis=0, keepdims=True) * inverses[a])
-        dscores, pairs = [], []
-        for a in steps:
-            dscores.append([])
-            pairs.append([])
-            for b in range(a + 1 + MAXL):
-                probs = weights[a][b] * inverses[a]
-                dscore = (probs * (dprobs[a][b] - deltas[a])).astype(BF16)
-                dscores[a].append(dscore)
+            inverses[step] = 1.0 / jnp.sum(total, axis=0, keepdims=True)
+            deltas[step] = jnp.sum(inner, axis=0, keepdims=True) * inverses[step]
+        dscores, pairs = {}, {}
+        for step in steps:
+            dscores[step], pairs[step] = [], []
+            for weight, dprob in zip(weights[step], dprobs[step]):
+                probs = weight * inverses[step]
+                dscore = (probs * (dprob - deltas[step])).astype(BF16)
+                dscores[step].append(dscore)
                 wide = jnp.concatenate([dscore, probs.astype(BF16)], axis=1)
-                pairs[a].append(nn(wide, both[a]))
-        for b in steps:
-            total = pairs[b][b]
+                pairs[step].append(nn(wide, both[step]))
+        for h, b in steps:
+            total = pairs[h, b][b]
             for a in range(b + 1, blocks):
-                total = total + pairs[a][b]
+                total = total + pairs[h, a][b]
             dk_all[h, spans[b]] = total[:, :DH] * scaling
             dv_all[h, spans[b]] = total[:, DH:]
-        for e in range(entries):
-            pair = pairs[e // MAXL][e // MAXL + 1 + e % MAXL]
-            dkey, dvalue = (pair[:, :DH] * scaling).astype(BF16), pair[:, DH:].astype(BF16)
-            if pieces:
-                owner, offset = listed(ints_ref, e, entries)
-                distance = owner ^ ints_ref[0]
-                at = (distance & 1) * blocks + offset
-                payloads[h][at, distance >> 1, :, :DH] += dkey
-                payloads[h][at, distance >> 1, :, DH:] += dvalue
-            else:
-                outs[0][e, :, 2 * h * DH : (2 * h + 1) * DH] = dkey
-                outs[0][e, :, (2 * h + 1) * DH : (2 * h + 2) * DH] = dvalue
-        halves = []
-        for a in steps:
-            wide, tall = jnp.concatenate(dscores[a], axis=0), jnp.concatenate(keys[a], axis=0)
-            halves.append(split(tn(wide, tall) * scaling))
-        for a in steps:
-            dq_top, dq_low = halves[a]
+        for h, a in steps:
+            for l in range(MAXL):
+                e = a * MAXL + l
+                pair = pairs[h, a][a + 1 + l]
+                dkey, dvalue = (pair[:, :DH] * scaling).astype(BF16), pair[:, DH:].astype(BF16)
+                if pieces:
+                    owner, offset = listed(ints_ref, e, entries)
+                    distance = owner ^ ints_ref[0]
+                    at = (distance & 1) * blocks + offset
+                    payloads[h][at, distance >> 1, :, :DH] += dkey
+                    payloads[h][at, distance >> 1, :, DH:] += dvalue
+                else:
+                    outs[0][e, :, 2 * h * DH : (2 * h + 1) * DH] = dkey
+                    outs[0][e, :, (2 * h + 1) * DH : (2 * h + 2) * DH] = dvalue
+        halves = {}
+        for step in steps:
+            wide = jnp.concatenate(dscores[step], axis=0)
+            tall = jnp.concatenate(keys[step], axis=0)
+            halves[step] = split(tn(wide, tall) * scaling)
+        for h, a in steps:
+            dq_top, dq_low = halves[h, a]
             dq_all[h, spans[a]] = nt(dq_top, local_ref[a, h]).astype(BF16)
-            query = query_ref[spans[a], lanes]
+            query = query_ref[spans[a], head(h)]
             query = jnp.concatenate([query, query], axis=0)
             dcum_all[h, a] = tn(query, jnp.concatenate([dq_top, dq_low], axis=0))
-        for i, (source, where) in enumerate(
-            (
-                (dk_all.at[h], dk_ref.at[:, lanes]),
-                (dv_all.at[h], dv_ref.at[:, lanes]),
-                (dq_all.at[h], dq_ref.at[:, lanes]),
-                (dcum_all.at[h], dcum_ref.at[:, h]),
-            )
-        ):
-            copy = pltpu.make_async_copy(source, where, grad_sems.at[i, h])
-            copy.start()
-            out_copies.append(copy)
-        for i, (first, size) in enumerate(pieces):
-            where = outs[i].at[:, :, :, 2 * h * DH : (2 * h + 2) * DH]
-            source = payloads[h].at[pl.ds(first, size)]
-            copy = pltpu.make_async_copy(source, where, out_sems.at[i, h])
-            copy.start()
-            out_copies.append(copy)
+        for h in range(start_head, start_head + group):
+            moves = [
+                (payloads[h].at[pl.ds(first, size)], outs[i], out_sems.at[i, h])
+                for i, (first, size) in enumerate(pieces)
+            ]
+            moves = [
+                (source, where.at[:, :, :, 2 * h * DH : (2 * h + 2) * DH], sem)
+                for source, where, sem in moves
+            ]
+            moves += [
+                (dk_all.at[h], dk_ref.at[:, head(h)], grad_sems.at[0, h]),
+                (dv_all.at[h], dv_ref.at[:, head(h)], grad_sems.at[1, h]),
+                (dq_all.at[h], dq_ref.at[:, head(h)], grad_sems.at[2, h]),
+                (dcum_all.at[h], dcum_ref.at[:, h], grad_sems.at[3, h]),
+            ]
+            for source, where, sem in moves:
+                copy = pltpu.make_async_copy(source, where, sem)
+                copy.start()
+                out_copies.append(copy)
     for copy in out_copies:
         copy.wait()
 
@@ -588,7 +598,7 @@
         + in_vmem(len(dcums) + 3),
         out_specs=pl.BlockSpec(memory_space=pltpu.VMEM),
         compiler_params=grant(60),
-        cost_estimate=cost(2),
+        cost_estimate=cost(0.2),
         name="adjoint",
     )(ints, *afters, *dcums, unit, rows, inverse)
 
@@ -641,13 +651,15 @@
     out_ref[...] = mine + inward_ref[0].astype(F32)
 
 
-def run_near(ends, first, near, inward):
-    _, rows, width = first.shape
+def run_near(ends, first, band, near, inward):
+    _, rows, width = near.shape
     return pl.pallas_call(
         near_kernel,
         grid=(1,),
         out_shape=jax.ShapeDtypeStruct((rows, width), F32),
-        in_specs=in_smem(1) + [pl.BlockSpec((1, rows, width), lambda t: (0, 0, 0))] * 3,
+        in_specs=in_smem(1)
+        + [pl.BlockSpec((1, rows, width), lambda t: (0, band, 0))]
+        + [pl.BlockSpec((1, rows, width), lambda t: (0, 0, 0))] * 2,
         out_specs=pl.BlockSpec((rows, width), lambda t: (0, 0)),
         compiler_params=grant(60),
         cost_estimate=cost(5),
@@ -685,11 +697,13 @@
     return ((place == 0) | (place == 3)).astype(jnp.int32).reshape(1)
 
 
-def line_scatter(share, band, bands, first, rest, inward, inner):
+def line_scatter(share, band, bands, firsts, rest, inward, inner):
     swapped = slide(inner, MIDDLE)
-    outer = first + swapped[1:]
+    firsts, swapped = lax.optimization_barrier((firsts, swapped))
+    rows = rest.shape[1]
+    outer = firsts[:, band * rows : (band + 1) * rows] + swapped[1:]
     outward = slide(outer, OUTWARD)
-    total = run_near(line_ends(), first, rest, inward)
+    total = run_near(line_ends(), firsts, band, rest, inward)
     return run_share(share, band, bands, total, swapped, outward), swapped, outer
 
 
@@ -700,12 +714,11 @@
     ready, *_ = lax.optimization_barrier((ready, sum_last, earlier))
     got = exchange(ready)
     swap_last = slide(sum_last, MIDDLE)
-    in_far, got = lax.optimization_barrier((in_far, got))
     sum_far = far + in_far
     swap_far = slide(sum_far, MIDDLE)
     outward = slide(first + swap_last, OUTWARD)
     in_near, _ = lax.optimization_barrier((in_near, sum_far))
-    total = run_near(line_ends(), first, near, in_near)
+    total = run_near(line_ends(), first, 0, near, in_near)
     return run_share(share, band, bands, total, swap_far, outward), got
 
 
@@ -804,12 +817,12 @@
         apart = ((0,), (1,), (2,), (3,))
         *terms, dcum_2, _, _ = project(2, apart, [rest_1], parts_2)
         share, swapped_0, outer_0 = line_scatter(
-            None, 0, 4, firsts[:, :BLK], rest_0, inward_0, rest_0[1:] + inward_0[1:]
+            None, 0, 4, firsts, rest_0, inward_0, rest_0[1:] + inward_0[1:]
         )
         inward_1, *_ = lax.optimization_barrier((inward_1, swapped_0, dcum_2))
         sum_1 = rest_1[1:] + inward_1[1:]
         share, _, outer_1 = line_scatter(
-            share, 1, 4, firsts[:, BLK:], rest_1, inward_1, sum_1
+            share, 1, 4, firsts, rest_1, inward_1, sum_1
         )
         dcums = [dcum_0, dcum_1, dcum_2]
         sums = run_adjoint(ints, (sum_1, outer_0), dcums, unit, rows, inverse, heads, blocks)

time: 204 us -> 208 us (1.020)
  waiting for transfers between devices: 42.3 us -> 50.4 us
  local copies, waits for them, and re-layouts: 11 us -> 8.43 us
    ppermute x12, waiting for transfers between devices: 12.5 us -> 20.7 us  [slide(): return lax.ppermute(value, 'head', pairs)]
    unnamed x72 -> x68, local copies, waits for them, and re-layouts: 9.23 us -> 7.58 us
  transfers between devices with their start and end apart: 42 -> 42, of which waited for: 11 -> 12; matrix products, arithmetic and copies ran while one was open for 3% -> 3% of each run, Pallas kernels for 38% -> 37%
where the time goes in v6:
time: 208 us; the launch traced here: 207 us
  Pallas kernels  95.2 us (46%)
  waiting for transfers between devices  50.4 us (24%)
  starting transfers between devices  47.9 us (23%)
  local copies, waits for them, and re-layouts  8.43 us (4%)
  other arithmetic  3.53 us (2%)
    pallas_call x3, Pallas kernels, run_project(): pl.pallas_call(functools.partial(project_kernel, heads, len(parts[0]), si...  37.8 us
    ppermute x29, waiting for transfers between devices, hop(): return lax.ppermute(value, 'ctx', [(i, i ^ distance) for i in range(count)])  27.7 us
    ppermute x29, starting transfers between devices, hop(): return lax.ppermute(value, 'ctx', [(i, i ^ distance) for i in range(count)])  24.9 us
    ppermute x12, waiting for transfers between devices, slide(): return lax.ppermute(value, 'head', pairs)  20.7 us
    ppermute x12, starting transfers between devices, slide(): return lax.ppermute(value, 'head', pairs)  19.6 us
    pallas_call x1, Pallas kernels, run_attend(): pl.pallas_call(functools.partial(attend_kernel, heads, blocks, places, pi...  16 us
    pallas_call x3, Pallas kernels, run_merge(): pl.pallas_call(merge_kernel, grid=(size, cut), out_shape=[jax.ShapeDtypeS...  8.86 us
    unnamed x68, local copies, waits for them, and re-layouts  7.58 us
  transfers between devices with their start and end apart: 42, of which 12 were waited for; matrix products, arithmetic and copies ran while one was open for 3% of the time, Pallas kernels for 37%

profile of v6, /device:TPU:0, one launch (start us, length us, event | category | flops | bytes accessed | tf_op | source)
XLA Modules:
  0.0 206.6 jit_solution(7933678990249706230)
XLA Ops:
  0.6 3.0 %collective-permute-start.1 = (bf16[512,512]{1,0:T(8,128)(2,1)}, bf16[512,512]{1,0:T(8,128)(2,1)S(1)}, u32[]{:S(2)}, u32[]{:S(2)}) collective-permute-start(bf16[512,512]{1,0:T(8,128)(2,1)} %refs_20_.1), channel_id=1, source_target_pairs={{0,8},{4,12},{8,0},{12,4},{16,24},{20,28},{24,16},{28,20},{1,9},{5... | collective-permute-start | bytes 1572872 | tf_op jit(solution)/shard_map/ppermute | solution.py:637
  8.2 8.4 %collective-permute-done.1.refs_6_ = bf16[512,512]{1,0:T(8,128)(2,1)S(1)} collective-permute-done((bf16[512,512]{1,0:T(8,128)(2,1)}, bf16[512,512]{1,0:T(8,128)(2,1)S(1)}, u32[]{:S(2)}, u32[]{:S(2)}) %collective-permute-start.1) | collective-permute-done | bytes 524320 | tf_op jit(solution)/shard_map/ppermute | solution.py:637
  22.3 5.1 %collective-permute-done.refs_5_ = bf16[512,512]{1,0:T(8,128)(2,1)S(1)} collective-permute-done((bf16[512,512]{1,0:T(8,128)(2,1)}, bf16[512,512]{1,0:T(8,128)(2,1)S(1)}, u32[]{:S(2)}, u32[]{:S(2)}) %collective-permute-start) | collective-permute-done | bytes 524320 | tf_op jit(solution)/shard_map/ppermute | solution.py:637
  31.3 4.5 %house_chain.1 = (f32[32,512]{1,0:T(8,128)S(1)}, f32[32,512]{1,0:T(8,128)S(1)}, f32[4,32,32]{2,1,0:T(8,128)S(1)}, bf16[4,128,96]{2,1,0:T(8,128)(2,1)S(1)}, bf16[4,96,128]{2,1,0:T(8,128)(2,1)S(1)}) custom-call(s32[17]{0:T(128)S(1)} %pad_add_fusion.ints_ref.refs_0_.base_ref, f32[8,512]{1,0:T(8,128)S(1)} %pad_maximum_fusion.refs_0_, ...), custom_call_target="tpu_custom_call" | custom-call | flops 6899999744 | bytes 1048576 | tf_op jit(solution)/shard_map/house_chain/pallas_call | solution.py:119
  38.6 5.5 %rotate.1 = (bf16[512,512]{1,0:T(8,128)(2,1)S(1)}, bf16[512,512]{1,0:T(8,128)(2,1)S(1)}, bf16[4,4,128,128]{3,2,1,0:T(8,128)(2,1)S(1)}, bf16[8,4,256,128]{3,2,1,0:T(8,128)(2,1)S(1)}) custom-call(s32[17]{0:T(128)S(1)} %pad_add_fusion.ints_ref.refs_0_.base_ref, bf16[4,128,96]{2,1,0:T(8,128)(2,1)S(1)} %get-tuple-element.73.wide_ref, ...), custom_call_target="tpu_custom_call" | custom-call | flops 10350000128 | bytes 1048576 | tf_op jit(solution)/shard_map/rotate/pallas_call | solution.py:187
  46.9 16.0 %attend.1 = (bf16[512,512]{1,0:T(8,128)(2,1)}, f32[4,4,128,128]{3,2,1,0:T(8,128)}, f32[512,512]{1,0:T(8,128)}, f32[512,512]{1,0:T(8,128)}, bf16[1,4,128,1024]{3,...) custom-call(s32[17]{0:T(128)S(1)} %pad_add_fusion.ints_ref.refs_0_.b, ...), custom_call_target="tpu_custom_call" | custom-call | flops 17250000896 | bytes 1048576 | tf_op jit(solution)/shard_map/attend/pallas_call | solution.py:386
  63.1 2.8 %collective-permute-done.18.got_ref = bf16[1,4,128,1024]{3,2,1,0:T(8,128)(2,1)S(1)} collective-permute-done((bf16[1,4,128,1024]{3,2,1,0:T(8,128)(2,1)}, bf16[1,4,128,1024]{3,2,1,0:T(8,128)(2,1)S(1)}, u32[]{:S(2)}, u32[]{:S(2)}) %collective-permute-start.18) | collective-permute-done | bytes 1048608 | tf_op jit(solution)/shard_map/ppermute | solution.py:637
  67.0 2.3 %merge.3 = (bf16[1,128,1024]{2,1,0:T(8,128)(2,1)}, bf16[1,128,1024]{2,1,0:T(8,128)(2,1)}, bf16[1,128,1024]{2,1,0:T(8,128)(2,1)}) custom-call(bf16[1,4,128,1024]{3,2,1,0:T(8,128)(2,1)} %get-tuple-element.86.own_ref, bf16[1,4,128,1024]{3,2,1,0:T(8,128)(2,1)} %copy-done.23), custom_call_target="tpu_custom_call" | custom-call | flops 2300000000 | bytes 1048576 | tf_op jit(solution)/shard_map/merge/pallas_call | solution.py:415
  70.1 2.7 %collective-permute-start.22 = (bf16[1,128,1024]{2,1,0:T(8,128)(2,1)}, bf16[1,128,1024]{2,1,0:T(8,128)(2,1)}, u32[]{:S(2)}, u32[]{:S(2)}) collective-permute-start(bf16[1,128,1024]{2,1,0:T(8,128)(2,1)} %get-tuple-element.91), channel_id=1, source_target_pairs={{0,24},{4,28},{8,16},{12,20},{16,8},{20,12},{24,0},{28,4},{1,25},{... | collective-permute-start | bytes 786440 | tf_op jit(solution)/shard_map/ppermute | solution.py:637
  74.5 2.3 %merge.4 = (bf16[1,128,1024]{2,1,0:T(8,128)(2,1)}, bf16[1,128,1024]{2,1,0:T(8,128)(2,1)}, bf16[1,128,1024]{2,1,0:T(8,128)(2,1)}) custom-call(bf16[3,4,128,1024]{3,2,1,0:T(8,128)(2,1)} %get-tuple-element.82.own_ref, bf16[3,4,128,1024]{3,2,1,0:T(8,128)(2,1)} %copy-done.22, bf16[1,128,1024]{2,1,0:T(8,128)(2,1)} %get-tuple-element.87.refs_0_), custom_call_target="tpu_custom_call" | custom-call | flops 2300000000 | bytes 1048576 | tf_op jit(solution)/shard_map/merge/pallas_call | solution.py:415
  76.9 4.2 %merge.5 = (bf16[2,128,1024]{2,1,0:T(8,128)(2,1)}, bf16[2,128,1024]{2,1,0:T(8,128)(2,1)}, bf16[2,128,1024]{2,1,0:T(8,128)(2,1)}) custom-call(bf16[3,4,128,1024]{3,2,1,0:T(8,128)(2,1)} %get-tuple-element.82.own_ref, bf16[3,4,128,1024]{3,2,1,0:T(8,128)(2,1)} %copy-done.22, bf16[1,128,1024]{2,1,0:T(8,128)(2,1)} %get-tuple-element.101.refs_0_), custom_call_target="tpu_custom_call" | custom-call | flops 2300000000 | bytes 1048576 | tf_op jit(solution)/shard_map/merge/pallas_call | solution.py:415
  81.1 2.9 %collective-permute-done.21.refs_4_ = bf16[1,128,1024]{2,1,0:T(8,128)(2,1)S(1)} collective-permute-done((bf16[1,128,1024]{2,1,0:T(8,128)(2,1)}, bf16[1,128,1024]{2,1,0:T(8,128)(2,1)S(1)}, u32[]{:S(2)}, u32[]{:S(2)}) %collective-permute-start.21) | collective-permute-done | bytes 262176 | tf_op jit(solution)/shard_map/ppermute | solution.py:637
  87.6 10.4 %project.3 = (bf16[3,128,1024]{2,1,0:T(8,128)(2,1)}, f32[1,4,128,128]{3,2,1,0:T(8,128)}, bf16[128,512]{1,0:T(8,128)(2,1)}, bf16[128,512]{1,0:T(8,128)(2,1)}) custom-call(s32[1]{0:T(128)} %bitcast.1.flip_ref, bf16[2,128,1024]{2,1,0:T(8,128)(2,1)} %get-tuple-element.110.refs_0_, bf16[4,128,1024]{2,1,0:T(8,128)(2,1)} %bitcast.14, ...), custom_call_target="tpu_custom_call" | custom-call | flops 10350000128 | bytes 1048576 | tf_op jit(solution)/shard_map/project/pallas_call | solution.py:510
  98.0 3.8 %collective-permute-start.26 = (bf16[3,128,1024]{2,1,0:T(8,128)(2,1)}, bf16[3,128,1024]{2,1,0:T(8,128)(2,1)S(1)}, u32[]{:S(2)}, u32[]{:S(2)}) collective-permute-start(bf16[3,128,1024]{2,1,0:T(8,128)(2,1)} %get-tuple-element.96.refs_0_.near_ref), channel_id=1, source_target_pairs={{0,1},{3,2},{4,5},{7,6},{8,9},{11,10},{12,13},{15,14},{16,17},{19,... | collective-permute-start | bytes 2359304 | tf_op jit(solution)/shard_map/ppermute | solution.py:641
  105.4 13.1 %project.4 = (bf16[1,256,1024]{2,1,0:T(8,128)(2,1)}, bf16[3,128,1024]{2,1,0:T(8,128)(2,1)}, f32[1,4,128,128]{3,2,1,0:T(8,128)}, bf16[128,512]{1,0:T(8,128)(2,1)}, bf16[128,512]{1,0:T(8,128)(2,1)}) custom-call(s32[1]{0:T(128)} %bitcast.1.flip_ref, bf16[3,128,1024]{2,1,0:T(8,128)(2,1)} %get-tuple-element.96.refs_0_.near_ref, bf16[12,128,1024]{2,1,0:T(8,128)(2,1)} %bitcast.11, ...), custom_call_target="tpu_custom_call" | custom-call | flops 13799999488 | bytes 1048576 | tf_op jit(solution)/shard_map/project/pallas_call | solution.py:510
  122.4 4.2 %collective-permute-done.31.refs_4_.refs_9_ = bf16[2,128,1024]{2,1,0:T(8,128)(2,1)} collective-permute-done((bf16[2,128,1024]{2,1,0:T(8,128)(2,1)}, bf16[2,128,1024]{2,1,0:T(8,128)(2,1)}, u32[]{:S(2)}, u32[]{:S(2)}) %collective-permute-start.31) | collective-permute-done | bytes 524320 | tf_op jit(solution)/shard_map/ppermute | solution.py:637
  126.6 14.3 %project.5 = (bf16[1,256,1024]{2,1,0:T(8,128)(2,1)}, bf16[1,256,1024]{2,1,0:T(8,128)(2,1)}, bf16[1,256,1024]{2,1,0:T(8,128)(2,1)}, bf16[1,256,1024]{2,1,0:T(8,12...) custom-call(s32[1]{0:T(128)} %bitcast.1.flip_ref, ...), custom_call_target="tpu_custom_call" | custom-call | flops 13799999488 | bytes 1048576 | tf_op jit(solution)/shard_map/project/pallas_call | solution.py:510
  150.4 7.3 %adjoint.1 = f32[32,1024]{1,0:T(8,128)} custom-call(s32[17]{0:T(128)} %copy-done.3, bf16[2,128,1024]{2,1,0:T(8,128)(2,1)} %copy-done.9, bf16[1,128,1024]{2,1,0:T(8,128)(2,1)} %copy-done.10, f32[1,4,128,128]{3,2,1,0:T(8,128)} %get-tuple-element.122.refs_2_, f32[1,4,128,128]{3,2,1,0:T(8,128)} %get-tuple-element.123.refs_3_, ...), custom_call_target="tpu_custom_call" | custom-call | flops 230000000 | bytes 1048576 | tf_op jit(solution)/shard_map/adjoint/pallas_call | solution.py:593
  158.6 7.9 %collective-permute-done.36 = bf16[1,256,1024]{2,1,0:T(8,128)(2,1)S(1)} collective-permute-done((bf16[1,256,1024]{2,1,0:T(8,128)(2,1)}, bf16[1,256,1024]{2,1,0:T(8,128)(2,1)S(1)}, u32[]{:S(2)}, u32[]{:S(2)}) %collective-permute-start.36) | collective-permute-done | bytes 524320 | tf_op jit(solution)/shard_map/ppermute | solution.py:641
  168.1 6.1 %collective-permute-done.35.inward_ref = bf16[1,256,1024]{2,1,0:T(8,128)(2,1)} collective-permute-done((bf16[1,256,1024]{2,1,0:T(8,128)(2,1)}, bf16[1,256,1024]{2,1,0:T(8,128)(2,1)}, u32[]{:S(2)}, u32[]{:S(2)}) %collective-permute-start.35) | collective-permute-done | bytes 524320 | tf_op jit(solution)/shard_map/ppermute | solution.py:641
  174.3 2.5 %near_sum.5.refs_1_ = f32[256,1024]{1,0:T(8,128)} custom-call(s32[1]{0:T(128)} %bitcast.ends_ref, bf16[1,256,1024]{2,1,0:T(8,128)(2,1)} %get-tuple-element.117.first_ref, bf16[1,256,1024]{2,1,0:T(8,128)(2,1)} %get-tuple-element.118.near_ref, bf16[1,256,1024]{2,1,0:T(8,128)(2,1)} %collective-permute-done.35.inward_ref), custom_call_target="tpu_custom_call" | custom-call | flops 5750000128 | bytes 1048576 | tf_op jit(solution)/shard_map/near_sum/pallas_call | solution.py:656
  182.8 3.4 %all-to-all-start = ((f32[8,4,1024]{2,1,0:T(4,128)}), f32[8,4,1024]{2,1,0:T(4,128)S(1)}, u32[]{:S(2)}, u32[]{:S(2)}) async-start(f32[8,4,1024]{2,1,0:T(4,128)} %reshape.50), calls=%async_computation | async-start | bytes 262144 | tf_op jit(solution)/shard_map/all_to_all | solution.py:789
  192.3 2.6 %house_grad.1 = f32[4,512]{1,0:T(4,128)} custom-call(s32[17]{0:T(128)} %copy-done.3, f32[8,4,1024]{2,1,0:T(4,128)} %copy-done.21, f32[32,512]{1,0:T(8,128)} %copy-done, f32[32,512]{1,0:T(8,128)} %copy-done.1, f32[4,512]{1,0:T(4,128)} %house_ref.1), custom_call_target="tpu_custom_call" | custom-call | flops 2300000000 | bytes 1048576 | tf_op jit(solution)/shard_map/house_grad/pallas_call | solution.py:625
  196.8 6.7 %collective-permute-done.40.refs_3_ = bf16[1,256,1024]{2,1,0:T(8,128)(2,1)S(1)} collective-permute-done((bf16[1,256,1024]{2,1,0:T(8,128)(2,1)S(1)}, bf16[1,256,1024]{2,1,0:T(8,128)(2,1)S(1)}, u32[]{:S(2)}, u32[]{:S(2)}) %collective-permute-start.40) | collective-permute-done | bytes 524320 | tf_op jit(solution)/shard_map/ppermute | solution.py:641
  (158 shorter events, 63.6 us)
Async XLA Ops:
  0.6 16.0 %collective-permute-start.1 = (bf16[512,512]{1,0:T(8,128)(2,1)}, bf16[512,512]{1,0:T(8,128)(2,1)S(1)}, u32[]{:S(2)}, u32[]{:S(2)}) collective-permute-start(bf16[512,512]{1,0:T(8,128)(2,1)} %refs_20_.1), channel_id=1, source_target_pairs={{0,8},{4,12},{8,0},{12,4},{16,24},{20,28},{24,16},{28,20},{1,9},{5... | collective-permute-start | bytes 1572872 | tf_op jit(solution)/shard_map/ppermute | solution.py:637
  3.6 15.1 %collective-permute-start.2 = (bf16[512,512]{1,0:T(8,128)(2,1)}, bf16[512,512]{1,0:T(8,128)(2,1)S(1)}, u32[]{:S(2)}, u32[]{:S(2)}) collective-permute-start(bf16[512,512]{1,0:T(8,128)(2,1)} %refs_14_.3), channel_id=1, source_target_pairs={{0,16},{4,20},{8,24},{12,28},{16,0},{20,4},{24,8},{28,12},{1,17},{... | collective-permute-start | bytes 1572872 | tf_op jit(solution)/shard_map/ppermute | solution.py:637
  5.2 22.2 %collective-permute-start = (bf16[512,512]{1,0:T(8,128)(2,1)}, bf16[512,512]{1,0:T(8,128)(2,1)S(1)}, u32[]{:S(2)}, u32[]{:S(2)}) collective-permute-start(bf16[512,512]{1,0:T(8,128)(2,1)} %refs_14_.3), channel_id=1, source_target_pairs={{0,8},{4,12},{8,0},{12,4},{16,24},{20,28},{24,16},{28,20},{1,9},{5... | collective-permute-start | bytes 1572872 | tf_op jit(solution)/shard_map/ppermute | solution.py:637
  5.7 23.4 %collective-permute-start.3 = (bf16[512,512]{1,0:T(8,128)(2,1)}, bf16[512,512]{1,0:T(8,128)(2,1)S(1)}, u32[]{:S(2)}, u32[]{:S(2)}) collective-permute-start(bf16[512,512]{1,0:T(8,128)(2,1)} %refs_20_.1), channel_id=1, source_target_pairs={{0,16},{4,20},{8,24},{12,28},{16,0},{20,4},{24,8},{28,12},{1,17},{... | collective-permute-start | bytes 1572872 | tf_op jit(solution)/shard_map/ppermute | solution.py:637
  27.4 16.8 %collective-permute-start.14 = (bf16[512,512]{1,0:T(8,128)(2,1)S(1)}, bf16[512,512]{1,0:T(8,128)(2,1)S(1)}, u32[]{:S(2)}, u32[]{:S(2)}) collective-permute-start(bf16[512,512]{1,0:T(8,128)(2,1)S(1)} %collective-permute-done.2.refs_9_), channel_id=1, source_target_pairs={{0,8},{4,12},{8,0},{12,4},{16,24},{20,28},{24,16},{28,20},{1,9},{5... | collective-permute-start | bytes 1572872 | tf_op jit(solution)/shard_map/ppermute | solution.py:637
  29.1 15.1 %collective-permute-start.15 = (bf16[512,512]{1,0:T(8,128)(2,1)S(1)}, bf16[512,512]{1,0:T(8,128)(2,1)S(1)}, u32[]{:S(2)}, u32[]{:S(2)}) collective-permute-start(bf16[512,512]{1,0:T(8,128)(2,1)S(1)} %collective-permute-done.1.refs_6_), channel_id=1, source_target_pairs={{0,16},{4,20},{8,24},{12,28},{16,0},{20,4},{24,8},{28,12},{1,17},{... | collective-permute-start | bytes 1572872 | tf_op jit(solution)/shard_map/ppermute | solution.py:637
  69.9 14.1 %collective-permute-start.21 = (bf16[1,128,1024]{2,1,0:T(8,128)(2,1)}, bf16[1,128,1024]{2,1,0:T(8,128)(2,1)S(1)}, u32[]{:S(2)}, u32[]{:S(2)}) collective-permute-start(bf16[1,128,1024]{2,1,0:T(8,128)(2,1)} %get-tuple-element.90), channel_id=1, source_target_pairs={{0,16},{4,20},{8,24},{12,28},{16,0},{20,4},{24,8},{28,12},{1,17},{... | collective-permute-start | bytes 786440 | tf_op jit(solution)/shard_map/ppermute | solution.py:637
  84.0 17.8 %collective-permute-start.23 = (bf16[1,128,1024]{2,1,0:T(8,128)(2,1)S(1)}, bf16[1,128,1024]{2,1,0:T(8,128)(2,1)S(1)}, u32[]{:S(2)}, u32[]{:S(2)}) collective-permute-start(bf16[1,128,1024]{2,1,0:T(8,128)(2,1)S(1)} %copy-done.31), channel_id=1, source_target_pairs={{0,8},{4,12},{8,0},{12,4},{16,24},{20,28},{24,16},{28,20},{1,9},{5... | collective-permute-start | bytes 786440 | tf_op jit(solution)/shard_map/ppermute | solution.py:637
  85.6 16.2 %collective-permute-start.24 = (bf16[1,128,1024]{2,1,0:T(8,128)(2,1)S(1)}, bf16[1,128,1024]{2,1,0:T(8,128)(2,1)S(1)}, u32[]{:S(2)}, u32[]{:S(2)}) collective-permute-start(bf16[1,128,1024]{2,1,0:T(8,128)(2,1)S(1)} %copy-done.29), channel_id=1, source_target_pairs={{0,16},{4,20},{8,24},{12,28},{16,0},{20,4},{24,8},{28,12},{1,17},{... | collective-permute-start | bytes 786440 | tf_op jit(solution)/shard_map/ppermute | solution.py:637
  86.1 15.7 %collective-permute-start.25 = (bf16[1,128,1024]{2,1,0:T(8,128)(2,1)S(1)}, bf16[1,128,1024]{2,1,0:T(8,128)(2,1)S(1)}, u32[]{:S(2)}, u32[]{:S(2)}) collective-permute-start(bf16[1,128,1024]{2,1,0:T(8,128)(2,1)S(1)} %copy-done.26), channel_id=1, source_target_pairs={{0,24},{4,28},{8,16},{12,20},{16,8},{20,12},{24,0},{28,4},{1,25},{... | collective-permute-start | bytes 786440 | tf_op jit(solution)/shard_map/ppermute | solution.py:637
  98.0 22.7 %collective-permute-start.26 = (bf16[3,128,1024]{2,1,0:T(8,128)(2,1)}, bf16[3,128,1024]{2,1,0:T(8,128)(2,1)S(1)}, u32[]{:S(2)}, u32[]{:S(2)}) collective-permute-start(bf16[3,128,1024]{2,1,0:T(8,128)(2,1)} %get-tuple-element.96.refs_0_.near_ref), channel_id=1, source_target_pairs={{0,1},{3,2},{4,5},{7,6},{8,9},{11,10},{12,13},{15,14},{16,17},{19,... | collective-permute-start | bytes 2359304 | tf_op jit(solution)/shard_map/ppermute | solution.py:641
  101.8 20.6 %collective-permute-start.30 = (bf16[2,128,1024]{2,1,0:T(8,128)(2,1)}, bf16[2,128,1024]{2,1,0:T(8,128)(2,1)}, u32[]{:S(2)}, u32[]{:S(2)}) collective-permute-start(bf16[2,128,1024]{2,1,0:T(8,128)(2,1)} %get-tuple-element.110.refs_0_), channel_id=1, source_target_pairs={{0,8},{4,12},{8,0},{12,4},{16,24},{20,28},{24,16},{28,20},{1,9},{5... | collective-permute-start | bytes 1572872 | tf_op jit(solution)/shard_map/ppermute | solution.py:637
  103.4 23.2 %collective-permute-start.31 = (bf16[2,128,1024]{2,1,0:T(8,128)(2,1)}, bf16[2,128,1024]{2,1,0:T(8,128)(2,1)}, u32[]{:S(2)}, u32[]{:S(2)}) collective-permute-start(bf16[2,128,1024]{2,1,0:T(8,128)(2,1)} %get-tuple-element.111), channel_id=1, source_target_pairs={{0,16},{4,20},{8,24},{12,28},{16,0},{20,4},{24,8},{28,12},{1,17},{... | collective-permute-start | bytes 1572872 | tf_op jit(solution)/shard_map/ppermute | solution.py:637
  103.9 22.7 %collective-permute-start.32 = (bf16[2,128,1024]{2,1,0:T(8,128)(2,1)}, bf16[2,128,1024]{2,1,0:T(8,128)(2,1)}, u32[]{:S(2)}, u32[]{:S(2)}) collective-permute-start(bf16[2,128,1024]{2,1,0:T(8,128)(2,1)} %get-tuple-element.112), channel_id=1, source_target_pairs={{0,24},{4,28},{8,16},{12,20},{16,8},{20,12},{24,0},{28,4},{1,25},{... | collective-permute-start | bytes 1572872 | tf_op jit(solution)/shard_map/ppermute | solution.py:637
  118.5 27.5 %collective-permute-start.29 = (bf16[3,128,1024]{2,1,0:T(8,128)(2,1)}, bf16[3,128,1024]{2,1,0:T(8,128)(2,1)}, u32[]{:S(2)}, u32[]{:S(2)}) collective-permute-start(bf16[3,128,1024]{2,1,0:T(8,128)(2,1)} %get-tuple-element.109.refs_0_.near_ref), channel_id=1, source_target_pairs={{0,1},{3,2},{4,5},{7,6},{8,9},{11,10},{12,13},{15,14},{16,17},{19,... | collective-permute-start | bytes 2359304 | tf_op jit(solution)/shard_map/ppermute | solution.py:641
  120.8 25.2 %collective-permute-start.27 = (bf16[2,128,1024]{2,1,0:T(8,128)(2,1)S(1)}, bf16[2,128,1024]{2,1,0:T(8,128)(2,1)}, u32[]{:S(2)}, u32[]{:S(2)}) collective-permute-start(bf16[2,128,1024]{2,1,0:T(8,128)(2,1)S(1)} %slice_add_fusion), channel_id=1, source_target_pairs={{1,2},{2,1},{5,6},{6,5},{9,10},{10,9},{13,14},{14,13},{17,18},{18,... | collective-permute-start | bytes 1572872 | tf_op jit(solution)/shard_map/ppermute | solution.py:641
  140.9 16.8 %collective-permute-start.38 = (bf16[1,256,1024]{2,1,0:T(8,128)(2,1)}, bf16[1,256,1024]{2,1,0:T(8,128)(2,1)S(1)}, u32[]{:S(2)}, u32[]{:S(2)}) collective-permute-start(bf16[1,256,1024]{2,1,0:T(8,128)(2,1)} %get-tuple-element.121), channel_id=1, source_target_pairs={{0,1},{3,2},{4,5},{7,6},{8,9},{11,10},{12,13},{15,14},{16,17},{19,... | collective-permute-start | bytes 1572872 | tf_op jit(solution)/shard_map/ppermute | solution.py:641
  142.6 23.9 %collective-permute-start.36 = (bf16[1,256,1024]{2,1,0:T(8,128)(2,1)}, bf16[1,256,1024]{2,1,0:T(8,128)(2,1)S(1)}, u32[]{:S(2)}, u32[]{:S(2)}) collective-permute-start(bf16[1,256,1024]{2,1,0:T(8,128)(2,1)} %get-tuple-element.119), channel_id=1, source_target_pairs={{0,1},{3,2},{4,5},{7,6},{8,9},{11,10},{12,13},{15,14},{16,17},{19,... | collective-permute-start | bytes 1572872 | tf_op jit(solution)/shard_map/ppermute | solution.py:641
  143.9 30.4 %collective-permute-start.35 = (bf16[1,256,1024]{2,1,0:T(8,128)(2,1)}, bf16[1,256,1024]{2,1,0:T(8,128)(2,1)}, u32[]{:S(2)}, u32[]{:S(2)}) collective-permute-start(bf16[1,256,1024]{2,1,0:T(8,128)(2,1)} %get-tuple-element.118.near_ref), channel_id=1, source_target_pairs={{0,1},{3,2},{4,5},{7,6},{8,9},{11,10},{12,13},{15,14},{16,17},{19,... | collective-permute-start | bytes 1572872 | tf_op jit(solution)/shard_map/ppermute | solution.py:641
  147.2 33.6 %collective-permute-start.33 = (bf16[2,128,1024]{2,1,0:T(8,128)(2,1)S(1)}, bf16[2,128,1024]{2,1,0:T(8,128)(2,1)S(1)}, u32[]{:S(2)}, u32[]{:S(2)}) collective-permute-start(bf16[2,128,1024]{2,1,0:T(8,128)(2,1)S(1)} %slice_add_fusion.1.refs_0_), channel_id=1, source_target_pairs={{1,2},{2,1},{5,6},{6,5},{9,10},{10,9},{13,14},{14,13},{17,18},{18,... | collective-permute-start | bytes 1572872 | tf_op jit(solution)/shard_map/ppermute | solution.py:641
  148.9 29.9 %collective-permute-start.28 = (bf16[1,128,1024]{2,1,0:T(8,128)(2,1)S(1)}, bf16[1,128,1024]{2,1,0:T(8,128)(2,1)}, u32[]{:S(2)}, u32[]{:S(2)}) collective-permute-start(bf16[1,128,1024]{2,1,0:T(8,128)(2,1)S(1)} %slice_add_fusion.3.refs_1_), channel_id=1, source_target_pairs={{1,0},{2,3},{5,4},{6,7},{9,8},{10,11},{13,12},{14,15},{17,16},{18,... | collective-permute-start | bytes 786440 | tf_op jit(solution)/shard_map/ppermute | solution.py:641
  157.9 28.3 %collective-permute-start.39 = (bf16[1,256,1024]{2,1,0:T(8,128)(2,1)S(1)}, bf16[1,256,1024]{2,1,0:T(8,128)(2,1)S(1)}, u32[]{:S(2)}, u32[]{:S(2)}) collective-permute-start(bf16[1,256,1024]{2,1,0:T(8,128)(2,1)S(1)} %add.26), channel_id=1, source_target_pairs={{1,2},{2,1},{5,6},{6,5},{9,10},{10,9},{13,14},{14,13},{17,18},{18,... | collective-permute-start | bytes 1572872 | tf_op jit(solution)/shard_map/ppermute | solution.py:641
  166.7 30.1 %collective-permute-start.37 = (bf16[1,256,1024]{2,1,0:T(8,128)(2,1)S(1)}, bf16[1,256,1024]{2,1,0:T(8,128)(2,1)}, u32[]{:S(2)}, u32[]{:S(2)}) collective-permute-start(bf16[1,256,1024]{2,1,0:T(8,128)(2,1)S(1)} %add.25), channel_id=1, source_target_pairs={{1,2},{2,1},{5,6},{6,5},{9,10},{10,9},{13,14},{14,13},{17,18},{18,... | collective-permute-start | bytes 1572872 | tf_op jit(solution)/shard_map/ppermute | solution.py:641
  186.4 17.1 %collective-permute-start.40 = (bf16[1,256,1024]{2,1,0:T(8,128)(2,1)S(1)}, bf16[1,256,1024]{2,1,0:T(8,128)(2,1)S(1)}, u32[]{:S(2)}, u32[]{:S(2)}) collective-permute-start(bf16[1,256,1024]{2,1,0:T(8,128)(2,1)S(1)} %add.27), channel_id=1, source_target_pairs={{1,0},{2,3},{5,4},{6,7},{9,8},{10,11},{13,12},{14,15},{17,16},{18,... | collective-permute-start | bytes 1572872 | tf_op jit(solution)/shard_map/ppermute | solution.py:641
  (51 other events, 440.7 us)

commit v7 on v6

--- a/solution.py
+++ b/solution.py
@@ -247,7 +247,7 @@
                 pltpu.make_async_copy(slots.at[e], slots.at[e], sems.at[kind, e]).wait()
 
     spans = [slice(a * BLK, (a + 1) * BLK) for a in range(blocks)]
-    group = 2 if heads % 2 == 0 else 1
+    group = 1
     for start_head in range(0, heads, group):
         steps = [(h, a) for h in range(start_head, start_head + group) for a in range(blocks)]
         both, keys, values, scores, dprobs, tops = {}, {}, {}, {}, {}, {}
@@ -425,20 +425,11 @@
     )(own, got, *afters)
 
 
-def project_kernel(heads, parts, size, groups, before, layout, afters, flip_ref, *refs):
-    refs = refs[afters:]
-    outs = len(layout)
-    chunks = [(m, i, at) for i, row in enumerate(layout) for at, m in enumerate(row)]
-    tiles, sems = refs[-2:]
-    per = tiles.shape[0] // len(chunks)
-    tile = tiles.shape[2]
-    part_refs, refs = refs[: size * parts], refs[size * parts :]
-    before_refs, refs = refs[:before], refs[before:]
-    dk_loc, dv_loc, dq_ref, key_ref, dcum_in, cum_ref = refs[:6]
-    weight_refs, out_refs = refs[6:9], refs[9 : 9 + outs]
-    dcum_out, dk_out, dv_out = refs[9 + outs : 12 + outs]
+def start_tiles(chunks, groups, flip_ref, weight_refs, tiles, sems):
+    count, _, tile, _ = tiles.shape
+    per = count // len(chunks)
     copies = []
-    for t in range(len(chunks) * per):
+    for t in range(count):
         m = chunks[t // per][0]
         row = ((m + flip_ref[0] * (groups - 1 - 2 * m)) * per + t % per) * tile
         rows = pl.ds(pl.multiple_of(row, tile), tile)
@@ -446,7 +437,34 @@
             copy = pltpu.make_async_copy(ref.at[rows], tiles.at[t, w], sems.at[t, w])
             copy.start()
             copies.append(copy)
-
+    return copies
+
+
+def multiply_tiles(chunks, copies, tiles, out_refs, grads_of):
+    count, _, tile, _ = tiles.shape
+    per = count // len(chunks)
+    for t in range(count):
+        term = None
+        m, out, at = chunks[t // per]
+        for w, grad in enumerate(grads_of(m)):
+            copies[3 * t + w].wait()
+            part = nt(tiles[t, w], grad)
+            term = part if term is None else term + part
+        spot = slice(t % per * tile, (t % per + 1) * tile)
+        out_refs[out][at, :, spot] = term.T.astype(BF16)
+
+
+def project_kernel(heads, parts, size, groups, before, layout, afters, flip_ref, *refs):
+    refs = refs[afters:]
+    outs = len(layout)
+    chunks = [(m, i, at) for i, row in enumerate(layout) for at, m in enumerate(row)]
+    tiles, sems = refs[-2:]
+    part_refs, refs = refs[: size * parts], refs[size * parts :]
+    before_refs, refs = refs[:before], refs[before:]
+    dk_loc, dv_loc, dq_ref, key_ref, dcum_in, cum_ref = refs[:6]
+    weight_refs, out_refs = refs[6:9], refs[9 : 9 + outs]
+    dcum_out, dk_out, dv_out = refs[9 + outs : 12 + outs]
+    copies = start_tiles(chunks, groups, flip_ref, weight_refs, tiles, sems)
     earlier = ()
     dk_rows, dv_rows = [], []
     for j in range(size):
@@ -475,15 +493,49 @@
             jnp.concatenate([old[...], new], axis=0) for old, new in zip(before_refs, grads)
         ]
 
-    for t in range(len(chunks) * per):
-        term = None
-        m, out, at = chunks[t // per]
-        for w, grad in enumerate(earlier if before and m == 0 else grads):
-            copies[3 * t + w].wait()
-            part = nt(tiles[t, w], grad)
-            term = part if term is None else term + part
-        spot = slice(t % per * tile, (t % per + 1) * tile)
-        out_refs[out][at, :, spot] = term.T.astype(BF16)
+    multiply_tiles(
+        chunks, copies, tiles, out_refs, lambda m: earlier if before and m == 0 else grads
+    )
+
+
+def project_more_kernel(groups, layout, afters, flip_ref, *refs):
+    refs = refs[afters:]
+    chunks = [(m, i, at) for i, row in enumerate(layout) for at, m in enumerate(row)]
+    tiles, sems = refs[-2:]
+    copies = start_tiles(chunks, groups, flip_ref, refs[3:6], tiles, sems)
+    grads = [ref[...] for ref in refs[:3]]
+    multiply_tiles(chunks, copies, tiles, refs[6:-2], lambda m: grads)
+
+
+def run_project_more(block, groups, layout, flip, afters, dq, dk, dv, weights):
+    rows, width = dk.shape
+    model = weights[0].shape[0]
+    chunk = model // groups
+    tile = min(512, chunk)
+    tile_count = sum(map(len, layout)) * chunk // tile
+
+    def whole(*shape):
+        return pl.BlockSpec(shape, lambda t: (0,) * len(shape))
+
+    shapes = [(len(row), rows, chunk) for row in layout]
+    return pl.pallas_call(
+        functools.partial(project_more_kernel, groups, layout, len(afters)),
+        grid=(1,),
+        in_specs=in_smem(1)
+        + [whole(1, 16, 128)] * len(afters)
+        + [pl.BlockSpec((rows, width), lambda t: (block * BLK // rows, 0))]
+        + [whole(rows, width)] * 2
+        + [pl.BlockSpec(memory_space=pl.ANY)] * 3,
+        out_specs=[whole(*shape) for shape in shapes],
+        scratch_shapes=[
+            pltpu.VMEM((tile_count, 3, tile, width), BF16),
+            pltpu.SemaphoreType.DMA((tile_count, 3)),
+        ],
+        out_shape=[jax.ShapeDtypeStruct(shape, BF16) for shape in shapes],
+        compiler_params=grant(60),
+        cost_estimate=cost(3 * sum(map(len, layout))),
+        name="project_more",
+    )(flip, *afters, dq, dk, dv, *weights)
 
 
 def run_project(block, groups, layout, flip, afters, parts, before, arrays, weights):
@@ -707,19 +759,19 @@
     return run_share(share, band, bands, total, swapped, outward), swapped, outer
 
 
-def line_scatter_apart(share, band, bands, first, near, far, last, ready, exchange, earlier):
+def line_scatter_apart(share, band, bands, first, near, far, last, meanwhile, earlier):
     in_last, in_far, in_near = slide(last, INWARD), slide(far, INWARD), slide(near, INWARD)
-    in_last, ready = lax.optimization_barrier((in_last, ready))
+    in_last, first = lax.optimization_barrier((in_last, first))
     sum_last = last + in_last
-    ready, *_ = lax.optimization_barrier((ready, sum_last, earlier))
-    got = exchange(ready)
     swap_last = slide(sum_last, MIDDLE)
-    sum_far = far + in_far
-    swap_far = slide(sum_far, MIDDLE)
-    outward = slide(first + swap_last, OUTWARD)
-    in_near, _ = lax.optimization_barrier((in_near, sum_far))
+    other = meanwhile(sum_last)
+    in_far, *_ = lax.optimization_barrier((in_far, other, earlier))
+    swap_far = slide(far + in_far, MIDDLE)
+    outer = first + swap_last
+    outward = slide(outer, OUTWARD)
+    in_near, _ = lax.optimization_barrier((in_near, outer))
     total = run_near(line_ends(), first, 0, near, in_near)
-    return run_share(share, band, bands, total, swap_far, outward), got
+    return run_share(share, band, bands, total, swap_far, outward), other
 
 
 def shards(
@@ -814,8 +866,7 @@
         split_off = ((0,), (1, 2, 3))
         firsts, rest_1, dcum_1, *_ = project(1, split_off, [rest_0], parts_1, before)
         inward_0, inward_1 = slide(rest_0, INWARD), slide(rest_1, INWARD)
-        apart = ((0,), (1,), (2,), (3,))
-        *terms, dcum_2, _, _ = project(2, apart, [rest_1], parts_2)
+        far, last, dcum_2, *grads_2 = project(2, ((2,), (3,)), [rest_1], parts_2)
         share, swapped_0, outer_0 = line_scatter(
             None, 0, 4, firsts, rest_0, inward_0, rest_0[1:] + inward_0[1:]
         )
@@ -824,11 +875,18 @@
         share, _, outer_1 = line_scatter(
             share, 1, 4, firsts, rest_1, inward_1, sum_1
         )
-        dcums = [dcum_0, dcum_1, dcum_2]
-        sums = run_adjoint(ints, (sum_1, outer_0), dcums, unit, rows, inverse, heads, blocks)
-        share, got = line_scatter_apart(
-            share, 1, 2, *terms, sums, share_sums, outer_1
+        first, near = run_project_more(
+            2, groups, ((0,), (1,)), flip, [sum_1], dq, *grads_2, weights
         )
+
+        def meanwhile(after):
+            dcums = [dcum_0, dcum_1, dcum_2]
+            return run_adjoint(ints, (after, outer_0), dcums, unit, rows, inverse, heads, blocks)
+
+        share, sums = line_scatter_apart(
+            share, 1, 2, first, near, far, last, meanwhile, outer_1
+        )
+        got = share_sums(sums)
     else:
         spots = (owners * blocks + offsets).reshape(-1)
         empty = jnp.zeros((ctx_count * blocks, BLK, 2 * width), BF16)

time: 208 us -> 210 us (level)
  waiting for transfers between devices: 50.4 us -> 39.8 us
  starting transfers between devices: 47.9 us -> 53.7 us
  local copies, waits for them, and re-layouts: 8.43 us -> 11.7 us
  Pallas kernels: 95.2 us -> 98 us
    ppermute x12, waiting for transfers between devices: 20.7 us -> 12.3 us  [slide(): return lax.ppermute(value, 'head', pairs)]
    pallas_call x0 -> x1, Pallas kernels: none -> 7.94 us  [run_project_more(): pl.pallas_call(functools.partial(project_more_kernel, groups, layout, len...]
    ppermute x12, starting transfers between devices: 19.6 us -> 25.3 us  [slide(): return lax.ppermute(value, 'head', pairs)]
    pallas_call x3, Pallas kernels: 37.8 us -> 32.8 us  [run_project(): pl.pallas_call(functools.partial(project_kernel, heads, len(parts[0]), si...]
    unnamed x68 -> x76, local copies, waits for them, and re-layouts: 7.58 us -> 9.94 us
  transfers between devices with their start and end apart: 42 -> 42, of which waited for: 12 -> 11; matrix products, arithmetic and copies ran while one was open for 3% -> 4% of each run, Pallas kernels for 37% -> 38%
where the time goes in v7:
time: 210 us; the launch traced here: 209 us
  Pallas kernels  98 us (47%)
  starting transfers between devices  53.7 us (26%)
  waiting for transfers between devices  39.8 us (19%)
  local copies, waits for them, and re-layouts  11.7 us (6%)
  other arithmetic  4.67 us (2%)
    pallas_call x3, Pallas kernels, run_project(): pl.pallas_call(functools.partial(project_kernel, heads, len(parts[0]), si...  32.8 us
    ppermute x29, waiting for transfers between devices, hop(): return lax.ppermute(value, 'ctx', [(i, i ^ distance) for i in range(count)])  27.4 us
    ppermute x12, starting transfers between devices, slide(): return lax.ppermute(value, 'head', pairs)  25.3 us
    ppermute x29, starting transfers between devices, hop(): return lax.ppermute(value, 'ctx', [(i, i ^ distance) for i in range(count)])  25 us
    pallas_call x1, Pallas kernels, run_attend(): pl.pallas_call(functools.partial(attend_kernel, heads, blocks, places, pi...  15.8 us
    ppermute x12, waiting for transfers between devices, slide(): return lax.ppermute(value, 'head', pairs)  12.3 us
    unnamed x76, local copies, waits for them, and re-layouts  9.94 us
    pallas_call x3, Pallas kernels, run_merge(): pl.pallas_call(merge_kernel, grid=(size, cut), out_shape=[jax.ShapeDtypeS...  8.8 us
  transfers between devices with their start and end apart: 42, of which 11 were waited for; matrix products, arithmetic and copies ran while one was open for 4% of the time, Pallas kernels for 38%

profile of v7, /device:TPU:0, one launch (start us, length us, event | category | flops | bytes accessed | tf_op | source)
XLA Modules:
  0.0 208.9 jit_solution(7665102644979577907)
XLA Ops:
  0.6 3.0 %collective-permute-start.1 = (bf16[512,512]{1,0:T(8,128)(2,1)}, bf16[512,512]{1,0:T(8,128)(2,1)S(1)}, u32[]{:S(2)}, u32[]{:S(2)}) collective-permute-start(bf16[512,512]{1,0:T(8,128)(2,1)} %refs_20_.1), channel_id=1, source_target_pairs={{0,8},{4,12},{8,0},{12,4},{16,24},{20,28},{24,16},{28,20},{1,9},{5... | collective-permute-start | bytes 1572872 | tf_op jit(solution)/shard_map/ppermute | solution.py:689
  8.2 8.4 %collective-permute-done.1.refs_6_ = bf16[512,512]{1,0:T(8,128)(2,1)S(1)} collective-permute-done((bf16[512,512]{1,0:T(8,128)(2,1)}, bf16[512,512]{1,0:T(8,128)(2,1)S(1)}, u32[]{:S(2)}, u32[]{:S(2)}) %collective-permute-start.1) | collective-permute-done | bytes 524320 | tf_op jit(solution)/shard_map/ppermute | solution.py:689
  22.3 5.1 %collective-permute-done.refs_5_ = bf16[512,512]{1,0:T(8,128)(2,1)S(1)} collective-permute-done((bf16[512,512]{1,0:T(8,128)(2,1)}, bf16[512,512]{1,0:T(8,128)(2,1)S(1)}, u32[]{:S(2)}, u32[]{:S(2)}) %collective-permute-start) | collective-permute-done | bytes 524320 | tf_op jit(solution)/shard_map/ppermute | solution.py:689
  31.3 4.5 %house_chain.1 = (f32[32,512]{1,0:T(8,128)S(1)}, f32[32,512]{1,0:T(8,128)S(1)}, f32[4,32,32]{2,1,0:T(8,128)S(1)}, bf16[4,128,96]{2,1,0:T(8,128)(2,1)S(1)}, bf16[4,96,128]{2,1,0:T(8,128)(2,1)S(1)}) custom-call(s32[17]{0:T(128)S(1)} %pad_add_fusion.ints_ref.refs_0_.base_ref, f32[8,512]{1,0:T(8,128)S(1)} %pad_maximum_fusion.refs_0_, ...), custom_call_target="tpu_custom_call" | custom-call | flops 6899999744 | bytes 1048576 | tf_op jit(solution)/shard_map/house_chain/pallas_call | solution.py:119
  38.6 5.5 %rotate.1 = (bf16[512,512]{1,0:T(8,128)(2,1)S(1)}, bf16[512,512]{1,0:T(8,128)(2,1)S(1)}, bf16[4,4,128,128]{3,2,1,0:T(8,128)(2,1)S(1)}, bf16[8,4,256,128]{3,2,1,0:T(8,128)(2,1)S(1)}) custom-call(s32[17]{0:T(128)S(1)} %pad_add_fusion.ints_ref.refs_0_.base_ref, bf16[4,128,96]{2,1,0:T(8,128)(2,1)S(1)} %get-tuple-element.75.wide_ref, ...), custom_call_target="tpu_custom_call" | custom-call | flops 10350000128 | bytes 1048576 | tf_op jit(solution)/shard_map/rotate/pallas_call | solution.py:187
  47.0 15.8 %attend.1 = (bf16[512,512]{1,0:T(8,128)(2,1)}, f32[4,4,128,128]{3,2,1,0:T(8,128)}, f32[512,512]{1,0:T(8,128)}, f32[512,512]{1,0:T(8,128)}, bf16[1,4,128,1024]{3,...) custom-call(s32[17]{0:T(128)S(1)} %pad_add_fusion.ints_ref.refs_0_.b, ...), custom_call_target="tpu_custom_call" | custom-call | flops 17250000896 | bytes 1048576 | tf_op jit(solution)/shard_map/attend/pallas_call | solution.py:386
  63.0 2.7 %collective-permute-done.18.got_ref = bf16[1,4,128,1024]{3,2,1,0:T(8,128)(2,1)S(1)} collective-permute-done((bf16[1,4,128,1024]{3,2,1,0:T(8,128)(2,1)}, bf16[1,4,128,1024]{3,2,1,0:T(8,128)(2,1)S(1)}, u32[]{:S(2)}, u32[]{:S(2)}) %collective-permute-start.18) | collective-permute-done | bytes 1048608 | tf_op jit(solution)/shard_map/ppermute | solution.py:689
  66.9 2.3 %merge.3 = (bf16[1,128,1024]{2,1,0:T(8,128)(2,1)}, bf16[1,128,1024]{2,1,0:T(8,128)(2,1)}, bf16[1,128,1024]{2,1,0:T(8,128)(2,1)}) custom-call(bf16[1,4,128,1024]{3,2,1,0:T(8,128)(2,1)} %get-tuple-element.88.own_ref, bf16[1,4,128,1024]{3,2,1,0:T(8,128)(2,1)} %copy-done.25), custom_call_target="tpu_custom_call" | custom-call | flops 2300000000 | bytes 1048576 | tf_op jit(solution)/shard_map/merge/pallas_call | solution.py:415
  70.0 2.7 %collective-permute-start.22 = (bf16[1,128,1024]{2,1,0:T(8,128)(2,1)}, bf16[1,128,1024]{2,1,0:T(8,128)(2,1)}, u32[]{:S(2)}, u32[]{:S(2)}) collective-permute-start(bf16[1,128,1024]{2,1,0:T(8,128)(2,1)} %get-tuple-element.93), channel_id=1, source_target_pairs={{0,24},{4,28},{8,16},{12,20},{16,8},{20,12},{24,0},{28,4},{1,25},{... | collective-permute-start | bytes 786440 | tf_op jit(solution)/shard_map/ppermute | solution.py:689
  76.7 4.1 %merge.5 = (bf16[2,128,1024]{2,1,0:T(8,128)(2,1)}, bf16[2,128,1024]{2,1,0:T(8,128)(2,1)}, bf16[2,128,1024]{2,1,0:T(8,128)(2,1)}) custom-call(bf16[3,4,128,1024]{3,2,1,0:T(8,128)(2,1)} %get-tuple-element.84.own_ref, bf16[3,4,128,1024]{3,2,1,0:T(8,128)(2,1)} %copy-done.9, bf16[1,128,1024]{2,1,0:T(8,128)(2,1)} %get-tuple-element.103.refs_0_), custom_call_target="tpu_custom_call" | custom-call | flops 2300000000 | bytes 1048576 | tf_op jit(solution)/shard_map/merge/pallas_call | solution.py:415
  80.9 3.0 %collective-permute-done.21.refs_4_ = bf16[1,128,1024]{2,1,0:T(8,128)(2,1)S(1)} collective-permute-done((bf16[1,128,1024]{2,1,0:T(8,128)(2,1)}, bf16[1,128,1024]{2,1,0:T(8,128)(2,1)S(1)}, u32[]{:S(2)}, u32[]{:S(2)}) %collective-permute-start.21) | collective-permute-done | bytes 262176 | tf_op jit(solution)/shard_map/ppermute | solution.py:689
  87.5 10.4 %project.3 = (bf16[3,128,1024]{2,1,0:T(8,128)(2,1)}, f32[1,4,128,128]{3,2,1,0:T(8,128)}, bf16[128,512]{1,0:T(8,128)(2,1)}, bf16[128,512]{1,0:T(8,128)(2,1)}) custom-call(s32[1]{0:T(128)} %bitcast.1.flip_ref, bf16[2,128,1024]{2,1,0:T(8,128)(2,1)} %get-tuple-element.112.refs_0_, bf16[4,128,1024]{2,1,0:T(8,128)(2,1)} %bitcast.14, ...), custom_call_target="tpu_custom_call" | custom-call | flops 10350000128 | bytes 1048576 | tf_op jit(solution)/shard_map/project/pallas_call | solution.py:562
  97.9 4.4 %collective-permute-start.26 = (bf16[3,128,1024]{2,1,0:T(8,128)(2,1)}, bf16[3,128,1024]{2,1,0:T(8,128)(2,1)}, u32[]{:S(2)}, u32[]{:S(2)}) collective-permute-start(bf16[3,128,1024]{2,1,0:T(8,128)(2,1)} %get-tuple-element.98.refs_0_.near_ref), channel_id=1, source_target_pairs={{0,1},{3,2},{4,5},{7,6},{8,9},{11,10},{12,13},{15,14},{16,17},{19,... | collective-permute-start | bytes 2359304 | tf_op jit(solution)/shard_map/ppermute | solution.py:693
  105.9 13.1 %project.4 = (bf16[1,256,1024]{2,1,0:T(8,128)(2,1)}, bf16[3,128,1024]{2,1,0:T(8,128)(2,1)}, f32[1,4,128,128]{3,2,1,0:T(8,128)}, bf16[128,512]{1,0:T(8,128)(2,1)}, bf16[128,512]{1,0:T(8,128)(2,1)}) custom-call(s32[1]{0:T(128)} %bitcast.1.flip_ref, bf16[3,128,1024]{2,1,0:T(8,128)(2,1)} %get-tuple-element.98.refs_0_.near_ref, bf16[12,128,1024]{2,1,0:T(8,128)(2,1)} %bitcast.7, ...), custom_call_target="tpu_custom_call" | custom-call | flops 13799999488 | bytes 1048576 | tf_op jit(solution)/shard_map/project/pallas_call | solution.py:562
  123.1 3.9 %collective-permute-done.31.refs_4_.refs_9_ = bf16[2,128,1024]{2,1,0:T(8,128)(2,1)S(1)} collective-permute-done((bf16[2,128,1024]{2,1,0:T(8,128)(2,1)}, bf16[2,128,1024]{2,1,0:T(8,128)(2,1)S(1)}, u32[]{:S(2)}, u32[]{:S(2)}) %collective-permute-start.31) | collective-permute-done | bytes 524320 | tf_op jit(solution)/shard_map/ppermute | solution.py:689
  128.6 9.3 %project.5 = (bf16[1,256,1024]{2,1,0:T(8,128)(2,1)}, bf16[1,256,1024]{2,1,0:T(8,128)(2,1)}, f32[2,4,128,128]{3,2,1,0:T(8,128)}, bf16[256,512]{1,0:T(8,128)(2,1)}, bf16[256,512]{1,0:T(8,128)(2,1)}) custom-call(s32[1]{0:T(128)} %bitcast.1.flip_ref, bf16[3,128,1024]{2,1,0:T(8,128)(2,1)} %get-tuple-element.111.refs_0_.near_ref, bf16[12,128,1024]{2,1,0:T(8,128)(2,1)} %bitcast.8, ...), custom_call_target="tpu_custom_call" | custom-call | flops 6899999744 | bytes 1048576 | tf_op jit(solution)/shard_map/project/pallas_call | solution.py:562
  142.2 7.9 %project_more.1 = (bf16[1,256,1024]{2,1,0:T(8,128)(2,1)}, bf16[1,256,1024]{2,1,0:T(8,128)(2,1)}) custom-call(s32[1]{0:T(128)} %bitcast.1.flip_ref, bf16[2,128,1024]{2,1,0:T(8,128)(2,1)} %copy-done.20, bf16[512,512]{1,0:T(8,128)(2,1)} %get-tuple-element.96.refs_8_.refs_6_.refs_11_.refs_13_.refs_1_, bf16[256,512]{1,0:T(8,128)(2,1)} %get-tuple-element.120.refs_2_, ...), custom_call_target="tpu_custom_call" | custom-call | flops 6899999744 | bytes 1048576 | tf_op jit(solution)/shard_map/project_more/pallas_call | solution.py:521
  155.3 7.3 %adjoint.1 = f32[32,1024]{1,0:T(8,128)} custom-call(s32[17]{0:T(128)} %copy-done.5, bf16[1,256,1024]{2,1,0:T(8,128)(2,1)} %copy-done.14, bf16[1,128,1024]{2,1,0:T(8,128)(2,1)} %copy-done.15, f32[1,4,128,128]{3,2,1,0:T(8,128)} %get-tuple-element.128.refs_2_, f32[1,4,128,128]{3,2,1,0:T(8,128)} %get-tuple-element.129.refs_3_, ...), custom_call_target="tpu_custom_call" | custom-call | flops 230000000 | bytes 1048576 | tf_op jit(solution)/shard_map/adjoint/pallas_call | solution.py:645
  164.2 3.4 %all-to-all-start = ((f32[8,4,1024]{2,1,0:T(4,128)}), f32[8,4,1024]{2,1,0:T(4,128)S(1)}, u32[]{:S(2)}, u32[]{:S(2)}) async-start(f32[8,4,1024]{2,1,0:T(4,128)} %reshape.50), calls=%async_computation | async-start | bytes 262144 | tf_op jit(solution)/shard_map/all_to_all | solution.py:841
  167.6 8.6 %collective-permute-start.36 = (bf16[1,256,1024]{2,1,0:T(8,128)(2,1)}, bf16[1,256,1024]{2,1,0:T(8,128)(2,1)}, u32[]{:S(2)}, u32[]{:S(2)}) collective-permute-start(bf16[1,256,1024]{2,1,0:T(8,128)(2,1)} %get-tuple-element.124.near_ref), channel_id=1, source_target_pairs={{0,1},{3,2},{4,5},{7,6},{8,9},{11,10},{12,13},{15,14},{16,17},{19,... | collective-permute-start | bytes 1572872 | tf_op jit(solution)/shard_map/ppermute | solution.py:693
  178.8 2.6 %house_grad.1 = f32[4,512]{1,0:T(4,128)} custom-call(s32[17]{0:T(128)} %copy-done.5, f32[8,4,1024]{2,1,0:T(4,128)} %copy-done.24, f32[32,512]{1,0:T(8,128)} %copy-done.2, f32[32,512]{1,0:T(8,128)} %copy-done.3, f32[4,512]{1,0:T(4,128)} %house_ref.1), custom_call_target="tpu_custom_call" | custom-call | flops 2300000000 | bytes 1048576 | tf_op jit(solution)/shard_map/house_grad/pallas_call | solution.py:677
  190.1 2.4 %near_sum.5.refs_1_ = f32[256,1024]{1,0:T(8,128)} custom-call(s32[1]{0:T(128)} %bitcast.ends_ref, bf16[1,256,1024]{2,1,0:T(8,128)(2,1)} %get-tuple-element.123.first_ref, bf16[1,256,1024]{2,1,0:T(8,128)(2,1)} %get-tuple-element.124.near_ref, bf16[1,256,1024]{2,1,0:T(8,128)(2,1)} %collective-permute-done.36.inward_ref), custom_call_target="tpu_custom_call" | custom-call | flops 5750000128 | bytes 1048576 | tf_op jit(solution)/shard_map/near_sum/pallas_call | solution.py:708
  192.6 2.9 %collective-permute-done.34.refs_3_ = bf16[1,128,1024]{2,1,0:T(8,128)(2,1)S(1)} collective-permute-done((bf16[1,128,1024]{2,1,0:T(8,128)(2,1)S(1)}, bf16[1,128,1024]{2,1,0:T(8,128)(2,1)S(1)}, u32[]{:S(2)}, u32[]{:S(2)}) %collective-permute-start.34) | collective-permute-done | bytes 262176 | tf_op jit(solution)/shard_map/ppermute | solution.py:693
  198.1 7.7 %collective-permute-done.40.refs_3_ = bf16[1,256,1024]{2,1,0:T(8,128)(2,1)S(1)} collective-permute-done((bf16[1,256,1024]{2,1,0:T(8,128)(2,1)S(1)}, bf16[1,256,1024]{2,1,0:T(8,128)(2,1)S(1)}, u32[]{:S(2)}, u32[]{:S(2)}) %collective-permute-start.40) | collective-permute-done | bytes 524320 | tf_op jit(solution)/shard_map/ppermute | solution.py:693
  (167 shorter events, 66.6 us)
Async XLA Ops:
  0.6 16.0 %collective-permute-start.1 = (bf16[512,512]{1,0:T(8,128)(2,1)}, bf16[512,512]{1,0:T(8,128)(2,1)S(1)}, u32[]{:S(2)}, u32[]{:S(2)}) collective-permute-start(bf16[512,512]{1,0:T(8,128)(2,1)} %refs_20_.1), channel_id=1, source_target_pairs={{0,8},{4,12},{8,0},{12,4},{16,24},{20,28},{24,16},{28,20},{1,9},{5... | collective-permute-start | bytes 1572872 | tf_op jit(solution)/shard_map/ppermute | solution.py:689
  3.6 15.1 %collective-permute-start.2 = (bf16[512,512]{1,0:T(8,128)(2,1)}, bf16[512,512]{1,0:T(8,128)(2,1)S(1)}, u32[]{:S(2)}, u32[]{:S(2)}) collective-permute-start(bf16[512,512]{1,0:T(8,128)(2,1)} %refs_14_.3), channel_id=1, source_target_pairs={{0,16},{4,20},{8,24},{12,28},{16,0},{20,4},{24,8},{28,12},{1,17},{... | collective-permute-start | bytes 1572872 | tf_op jit(solution)/shard_map/ppermute | solution.py:689
  5.2 22.2 %collective-permute-start = (bf16[512,512]{1,0:T(8,128)(2,1)}, bf16[512,512]{1,0:T(8,128)(2,1)S(1)}, u32[]{:S(2)}, u32[]{:S(2)}) collective-permute-start(bf16[512,512]{1,0:T(8,128)(2,1)} %refs_14_.3), channel_id=1, source_target_pairs={{0,8},{4,12},{8,0},{12,4},{16,24},{20,28},{24,16},{28,20},{1,9},{5... | collective-permute-start | bytes 1572872 | tf_op jit(solution)/shard_map/ppermute | solution.py:689
  5.7 23.4 %collective-permute-start.3 = (bf16[512,512]{1,0:T(8,128)(2,1)}, bf16[512,512]{1,0:T(8,128)(2,1)S(1)}, u32[]{:S(2)}, u32[]{:S(2)}) collective-permute-start(bf16[512,512]{1,0:T(8,128)(2,1)} %refs_20_.1), channel_id=1, source_target_pairs={{0,16},{4,20},{8,24},{12,28},{16,0},{20,4},{24,8},{28,12},{1,17},{... | collective-permute-start | bytes 1572872 | tf_op jit(solution)/shard_map/ppermute | solution.py:689
  27.4 16.8 %collective-permute-start.14 = (bf16[512,512]{1,0:T(8,128)(2,1)S(1)}, bf16[512,512]{1,0:T(8,128)(2,1)S(1)}, u32[]{:S(2)}, u32[]{:S(2)}) collective-permute-start(bf16[512,512]{1,0:T(8,128)(2,1)S(1)} %collective-permute-done.2.refs_9_), channel_id=1, source_target_pairs={{0,8},{4,12},{8,0},{12,4},{16,24},{20,28},{24,16},{28,20},{1,9},{5... | collective-permute-start | bytes 1572872 | tf_op jit(solution)/shard_map/ppermute | solution.py:689
  29.1 15.1 %collective-permute-start.15 = (bf16[512,512]{1,0:T(8,128)(2,1)S(1)}, bf16[512,512]{1,0:T(8,128)(2,1)S(1)}, u32[]{:S(2)}, u32[]{:S(2)}) collective-permute-start(bf16[512,512]{1,0:T(8,128)(2,1)S(1)} %collective-permute-done.1.refs_6_), channel_id=1, source_target_pairs={{0,16},{4,20},{8,24},{12,28},{16,0},{20,4},{24,8},{28,12},{1,17},{... | collective-permute-start | bytes 1572872 | tf_op jit(solution)/shard_map/ppermute | solution.py:689
  69.8 14.1 %collective-permute-start.21 = (bf16[1,128,1024]{2,1,0:T(8,128)(2,1)}, bf16[1,128,1024]{2,1,0:T(8,128)(2,1)S(1)}, u32[]{:S(2)}, u32[]{:S(2)}) collective-permute-start(bf16[1,128,1024]{2,1,0:T(8,128)(2,1)} %get-tuple-element.92), channel_id=1, source_target_pairs={{0,16},{4,20},{8,24},{12,28},{16,0},{20,4},{24,8},{28,12},{1,17},{... | collective-permute-start | bytes 786440 | tf_op jit(solution)/shard_map/ppermute | solution.py:689
  83.9 18.4 %collective-permute-start.23 = (bf16[1,128,1024]{2,1,0:T(8,128)(2,1)S(1)}, bf16[1,128,1024]{2,1,0:T(8,128)(2,1)S(1)}, u32[]{:S(2)}, u32[]{:S(2)}) collective-permute-start(bf16[1,128,1024]{2,1,0:T(8,128)(2,1)S(1)} %copy-done.34), channel_id=1, source_target_pairs={{0,8},{4,12},{8,0},{12,4},{16,24},{20,28},{24,16},{28,20},{1,9},{5... | collective-permute-start | bytes 786440 | tf_op jit(solution)/shard_map/ppermute | solution.py:689
  85.4 16.8 %collective-permute-start.24 = (bf16[1,128,1024]{2,1,0:T(8,128)(2,1)S(1)}, bf16[1,128,1024]{2,1,0:T(8,128)(2,1)S(1)}, u32[]{:S(2)}, u32[]{:S(2)}) collective-permute-start(bf16[1,128,1024]{2,1,0:T(8,128)(2,1)S(1)} %copy-done.32), channel_id=1, source_target_pairs={{0,16},{4,20},{8,24},{12,28},{16,0},{20,4},{24,8},{28,12},{1,17},{... | collective-permute-start | bytes 786440 | tf_op jit(solution)/shard_map/ppermute | solution.py:689
  86.0 16.3 %collective-permute-start.25 = (bf16[1,128,1024]{2,1,0:T(8,128)(2,1)S(1)}, bf16[1,128,1024]{2,1,0:T(8,128)(2,1)S(1)}, u32[]{:S(2)}, u32[]{:S(2)}) collective-permute-start(bf16[1,128,1024]{2,1,0:T(8,128)(2,1)S(1)} %copy-done.29), channel_id=1, source_target_pairs={{0,24},{4,28},{8,16},{12,20},{16,8},{20,12},{24,0},{28,4},{1,25},{... | collective-permute-start | bytes 786440 | tf_op jit(solution)/shard_map/ppermute | solution.py:689
  97.9 22.5 %collective-permute-start.26 = (bf16[3,128,1024]{2,1,0:T(8,128)(2,1)}, bf16[3,128,1024]{2,1,0:T(8,128)(2,1)}, u32[]{:S(2)}, u32[]{:S(2)}) collective-permute-start(bf16[3,128,1024]{2,1,0:T(8,128)(2,1)} %get-tuple-element.98.refs_0_.near_ref), channel_id=1, source_target_pairs={{0,1},{3,2},{4,5},{7,6},{8,9},{11,10},{12,13},{15,14},{16,17},{19,... | collective-permute-start | bytes 2359304 | tf_op jit(solution)/shard_map/ppermute | solution.py:693
  102.3 20.8 %collective-permute-start.30 = (bf16[2,128,1024]{2,1,0:T(8,128)(2,1)}, bf16[2,128,1024]{2,1,0:T(8,128)(2,1)S(1)}, u32[]{:S(2)}, u32[]{:S(2)}) collective-permute-start(bf16[2,128,1024]{2,1,0:T(8,128)(2,1)} %get-tuple-element.112.refs_0_), channel_id=1, source_target_pairs={{0,8},{4,12},{8,0},{12,4},{16,24},{20,28},{24,16},{28,20},{1,9},{5... | collective-permute-start | bytes 1572872 | tf_op jit(solution)/shard_map/ppermute | solution.py:689
  103.9 23.1 %collective-permute-start.31 = (bf16[2,128,1024]{2,1,0:T(8,128)(2,1)}, bf16[2,128,1024]{2,1,0:T(8,128)(2,1)S(1)}, u32[]{:S(2)}, u32[]{:S(2)}) collective-permute-start(bf16[2,128,1024]{2,1,0:T(8,128)(2,1)} %get-tuple-element.113), channel_id=1, source_target_pairs={{0,16},{4,20},{8,24},{12,28},{16,0},{20,4},{24,8},{28,12},{1,17},{... | collective-permute-start | bytes 1572872 | tf_op jit(solution)/shard_map/ppermute | solution.py:689
  104.4 22.6 %collective-permute-start.32 = (bf16[2,128,1024]{2,1,0:T(8,128)(2,1)}, bf16[2,128,1024]{2,1,0:T(8,128)(2,1)S(1)}, u32[]{:S(2)}, u32[]{:S(2)}) collective-permute-start(bf16[2,128,1024]{2,1,0:T(8,128)(2,1)} %get-tuple-element.114), channel_id=1, source_target_pairs={{0,24},{4,28},{8,16},{12,20},{16,8},{20,12},{24,0},{28,4},{1,25},{... | collective-permute-start | bytes 1572872 | tf_op jit(solution)/shard_map/ppermute | solution.py:689
  119.0 21.6 %collective-permute-start.29 = (bf16[3,128,1024]{2,1,0:T(8,128)(2,1)}, bf16[3,128,1024]{2,1,0:T(8,128)(2,1)S(1)}, u32[]{:S(2)}, u32[]{:S(2)}) collective-permute-start(bf16[3,128,1024]{2,1,0:T(8,128)(2,1)} %get-tuple-element.111.refs_0_.near_ref), channel_id=1, source_target_pairs={{0,1},{3,2},{4,5},{7,6},{8,9},{11,10},{12,13},{15,14},{16,17},{19,... | collective-permute-start | bytes 2359304 | tf_op jit(solution)/shard_map/ppermute | solution.py:693
  121.5 19.1 %collective-permute-start.27 = (bf16[2,128,1024]{2,1,0:T(8,128)(2,1)S(1)}, bf16[2,128,1024]{2,1,0:T(8,128)(2,1)}, u32[]{:S(2)}, u32[]{:S(2)}) collective-permute-start(bf16[2,128,1024]{2,1,0:T(8,128)(2,1)S(1)} %slice_add_fusion), channel_id=1, source_target_pairs={{1,2},{2,1},{5,6},{6,5},{9,10},{10,9},{13,14},{14,13},{17,18},{18,... | collective-permute-start | bytes 1572872 | tf_op jit(solution)/shard_map/ppermute | solution.py:693
  137.9 14.0 %collective-permute-start.35 = (bf16[1,256,1024]{2,1,0:T(8,128)(2,1)}, bf16[1,256,1024]{2,1,0:T(8,128)(2,1)S(1)}, u32[]{:S(2)}, u32[]{:S(2)}) collective-permute-start(bf16[1,256,1024]{2,1,0:T(8,128)(2,1)} %get-tuple-element.119), channel_id=1, source_target_pairs={{0,1},{3,2},{4,5},{7,6},{8,9},{11,10},{12,13},{15,14},{16,17},{19,... | collective-permute-start | bytes 1572872 | tf_op jit(solution)/shard_map/ppermute | solution.py:693
  139.2 46.5 %collective-permute-start.38 = (bf16[1,256,1024]{2,1,0:T(8,128)(2,1)}, bf16[1,256,1024]{2,1,0:T(8,128)(2,1)S(1)}, u32[]{:S(2)}, u32[]{:S(2)}) collective-permute-start(bf16[1,256,1024]{2,1,0:T(8,128)(2,1)} %get-tuple-element.127), channel_id=1, source_target_pairs={{0,1},{3,2},{4,5},{7,6},{8,9},{11,10},{12,13},{15,14},{16,17},{19,... | collective-permute-start | bytes 1572872 | tf_op jit(solution)/shard_map/ppermute | solution.py:693
  140.7 42.7 %collective-permute-start.33 = (bf16[2,128,1024]{2,1,0:T(8,128)(2,1)S(1)}, bf16[2,128,1024]{2,1,0:T(8,128)(2,1)}, u32[]{:S(2)}, u32[]{:S(2)}) collective-permute-start(bf16[2,128,1024]{2,1,0:T(8,128)(2,1)S(1)} %slice_add_fusion.1.refs_0_), channel_id=1, source_target_pairs={{1,2},{2,1},{5,6},{6,5},{9,10},{10,9},{13,14},{14,13},{17,18},{18,... | collective-permute-start | bytes 1572872 | tf_op jit(solution)/shard_map/ppermute | solution.py:693
  153.3 33.3 %collective-permute-start.37 = (bf16[1,256,1024]{2,1,0:T(8,128)(2,1)S(1)}, bf16[1,256,1024]{2,1,0:T(8,128)(2,1)S(1)}, u32[]{:S(2)}, u32[]{:S(2)}) collective-permute-start(bf16[1,256,1024]{2,1,0:T(8,128)(2,1)S(1)} %add.25.refs_0_), channel_id=1, source_target_pairs={{1,2},{2,1},{5,6},{6,5},{9,10},{10,9},{13,14},{14,13},{17,18},{18,... | collective-permute-start | bytes 1572872 | tf_op jit(solution)/shard_map/ppermute | solution.py:693
  154.0 27.4 %collective-permute-start.28 = (bf16[1,128,1024]{2,1,0:T(8,128)(2,1)S(1)}, bf16[1,128,1024]{2,1,0:T(8,128)(2,1)}, u32[]{:S(2)}, u32[]{:S(2)}) collective-permute-start(bf16[1,128,1024]{2,1,0:T(8,128)(2,1)S(1)} %slice_add_fusion.3.refs_1_), channel_id=1, source_target_pairs={{1,0},{2,3},{5,4},{6,7},{9,8},{10,11},{13,12},{14,15},{17,16},{18,... | collective-permute-start | bytes 786440 | tf_op jit(solution)/shard_map/ppermute | solution.py:693
  164.2 13.9 %all-to-all-start = ((f32[8,4,1024]{2,1,0:T(4,128)}), f32[8,4,1024]{2,1,0:T(4,128)S(1)}, u32[]{:S(2)}, u32[]{:S(2)}) async-start(f32[8,4,1024]{2,1,0:T(4,128)} %reshape.50), calls=%async_computation | async-start | bytes 262144 | tf_op jit(solution)/shard_map/all_to_all | solution.py:841
  167.6 22.6 %collective-permute-start.36 = (bf16[1,256,1024]{2,1,0:T(8,128)(2,1)}, bf16[1,256,1024]{2,1,0:T(8,128)(2,1)}, u32[]{:S(2)}, u32[]{:S(2)}) collective-permute-start(bf16[1,256,1024]{2,1,0:T(8,128)(2,1)} %get-tuple-element.124.near_ref), channel_id=1, source_target_pairs={{0,1},{3,2},{4,5},{7,6},{8,9},{11,10},{12,13},{15,14},{16,17},{19,... | collective-permute-start | bytes 1572872 | tf_op jit(solution)/shard_map/ppermute | solution.py:693
  186.8 19.0 %collective-permute-start.40 = (bf16[1,256,1024]{2,1,0:T(8,128)(2,1)S(1)}, bf16[1,256,1024]{2,1,0:T(8,128)(2,1)S(1)}, u32[]{:S(2)}, u32[]{:S(2)}) collective-permute-start(bf16[1,256,1024]{2,1,0:T(8,128)(2,1)S(1)} %add.26), channel_id=1, source_target_pairs={{1,0},{2,3},{5,4},{6,7},{9,8},{10,11},{13,12},{14,15},{17,16},{18,... | collective-permute-start | bytes 1572872 | tf_op jit(solution)/shard_map/ppermute | solution.py:693
  (55 other events, 371.4 us)

commit v8 on v5

--- a/solution.py
+++ b/solution.py
@@ -415,20 +415,11 @@
     )(own, got, *afters)
 
 
-def project_kernel(heads, parts, size, groups, before, layout, afters, flip_ref, *refs):
-    refs = refs[afters:]
-    outs = len(layout)
-    chunks = [(m, i, at) for i, row in enumerate(layout) for at, m in enumerate(row)]
-    tiles, sems = refs[-2:]
-    per = tiles.shape[0] // len(chunks)
-    tile = tiles.shape[2]
-    part_refs, refs = refs[: size * parts], refs[size * parts :]
-    before_refs, refs = refs[:before], refs[before:]
-    dk_loc, dv_loc, dq_ref, key_ref, dcum_in, cum_ref = refs[:6]
-    weight_refs, out_refs = refs[6:9], refs[9 : 9 + outs]
-    dcum_out, dk_out, dv_out = refs[9 + outs : 12 + outs]
+def start_tiles(chunks, groups, flip_ref, weight_refs, tiles, sems):
+    count, _, tile, _ = tiles.shape
+    per = count // len(chunks)
     copies = []
-    for t in range(len(chunks) * per):
+    for t in range(count):
         m = chunks[t // per][0]
         row = ((m + flip_ref[0] * (groups - 1 - 2 * m)) * per + t % per) * tile
         rows = pl.ds(pl.multiple_of(row, tile), tile)
@@ -436,7 +427,34 @@
             copy = pltpu.make_async_copy(ref.at[rows], tiles.at[t, w], sems.at[t, w])
             copy.start()
             copies.append(copy)
-
+    return copies
+
+
+def multiply_tiles(chunks, copies, tiles, out_refs, grads_of):
+    count, _, tile, _ = tiles.shape
+    per = count // len(chunks)
+    for t in range(count):
+        term = None
+        m, out, at = chunks[t // per]
+        for w, grad in enumerate(grads_of(m)):
+            copies[3 * t + w].wait()
+            part = nt(tiles[t, w], grad)
+            term = part if term is None else term + part
+        spot = slice(t % per * tile, (t % per + 1) * tile)
+        out_refs[out][at, :, spot] = term.T.astype(BF16)
+
+
+def project_kernel(heads, parts, size, groups, before, layout, afters, flip_ref, *refs):
+    refs = refs[afters:]
+    outs = len(layout)
+    chunks = [(m, i, at) for i, row in enumerate(layout) for at, m in enumerate(row)]
+    tiles, sems = refs[-2:]
+    part_refs, refs = refs[: size * parts], refs[size * parts :]
+    before_refs, refs = refs[:before], refs[before:]
+    dk_loc, dv_loc, dq_ref, key_ref, dcum_in, cum_ref = refs[:6]
+    weight_refs, out_refs = refs[6:9], refs[9 : 9 + outs]
+    dcum_out, dk_out, dv_out = refs[9 + outs : 12 + outs]
+    copies = start_tiles(chunks, groups, flip_ref, weight_refs, tiles, sems)
     earlier = ()
     dk_rows, dv_rows = [], []
     for j in range(size):
@@ -465,15 +483,49 @@
             jnp.concatenate([old[...], new], axis=0) for old, new in zip(before_refs, grads)
         ]
 
-    for t in range(len(chunks) * per):
-        term = None
-        m, out, at = chunks[t // per]
-        for w, grad in enumerate(earlier if before and m == 0 else grads):
-            copies[3 * t + w].wait()
-            part = nt(tiles[t, w], grad)
-            term = part if term is None else term + part
-        spot = slice(t % per * tile, (t % per + 1) * tile)
-        out_refs[out][at, :, spot] = term.T.astype(BF16)
+    multiply_tiles(
+        chunks, copies, tiles, out_refs, lambda m: earlier if before and m == 0 else grads
+    )
+
+
+def project_more_kernel(groups, layout, afters, flip_ref, *refs):
+    refs = refs[afters:]
+    chunks = [(m, i, at) for i, row in enumerate(layout) for at, m in enumerate(row)]
+    tiles, sems = refs[-2:]
+    copies = start_tiles(chunks, groups, flip_ref, refs[3:6], tiles, sems)
+    grads = [ref[...] for ref in refs[:3]]
+    multiply_tiles(chunks, copies, tiles, refs[6:-2], lambda m: grads)
+
+
+def run_project_more(block, groups, layout, flip, afters, dq, dk, dv, weights):
+    rows, width = dk.shape
+    model = weights[0].shape[0]
+    chunk = model // groups
+    tile = min(512, chunk)
+    tile_count = sum(map(len, layout)) * chunk // tile
+
+    def whole(*shape):
+        return pl.BlockSpec(shape, lambda t: (0,) * len(shape))
+
+    shapes = [(len(row), rows, chunk) for row in layout]
+    return pl.pallas_call(
+        functools.partial(project_more_kernel, groups, layout, len(afters)),
+        grid=(1,),
+        in_specs=in_smem(1)
+        + [whole(1, 16, 128)] * len(afters)
+        + [pl.BlockSpec((rows, width), lambda t: (block * BLK // rows, 0))]
+        + [whole(rows, width)] * 2
+        + [pl.BlockSpec(memory_space=pl.ANY)] * 3,
+        out_specs=[whole(*shape) for shape in shapes],
+        scratch_shapes=[
+            pltpu.VMEM((tile_count, 3, tile, width), BF16),
+            pltpu.SemaphoreType.DMA((tile_count, 3)),
+        ],
+        out_shape=[jax.ShapeDtypeStruct(shape, BF16) for shape in shapes],
+        compiler_params=grant(60),
+        cost_estimate=cost(3 * sum(map(len, layout))),
+        name="project_more",
+    )(flip, *afters, dq, dk, dv, *weights)
 
 
 def run_project(block, groups, layout, flip, afters, parts, before, arrays, weights):
@@ -588,7 +640,7 @@
         + in_vmem(len(dcums) + 3),
         out_specs=pl.BlockSpec(memory_space=pltpu.VMEM),
         compiler_params=grant(60),
-        cost_estimate=cost(2),
+        cost_estimate=cost(0.2),
         name="adjoint",
     )(ints, *afters, *dcums, unit, rows, inverse)
 
@@ -641,13 +693,15 @@
     out_ref[...] = mine + inward_ref[0].astype(F32)
 
 
-def run_near(ends, first, near, inward):
-    _, rows, width = first.shape
+def run_near(ends, first, band, near, inward):
+    _, rows, width = near.shape
     return pl.pallas_call(
         near_kernel,
         grid=(1,),
         out_shape=jax.ShapeDtypeStruct((rows, width), F32),
-        in_specs=in_smem(1) + [pl.BlockSpec((1, rows, width), lambda t: (0, 0, 0))] * 3,
+        in_specs=in_smem(1)
+        + [pl.BlockSpec((1, rows, width), lambda t: (0, band, 0))]
+        + [pl.BlockSpec((1, rows, width), lambda t: (0, 0, 0))] * 2,
         out_specs=pl.BlockSpec((rows, width), lambda t: (0, 0)),
         compiler_params=grant(60),
         cost_estimate=cost(5),
@@ -685,28 +739,32 @@
     return ((place == 0) | (place == 3)).astype(jnp.int32).reshape(1)
 
 
-def line_scatter(share, band, bands, first, rest, inward, inner):
+def line_scatter(band, firsts, rest, inward, inner):
     swapped = slide(inner, MIDDLE)
-    outer = first + swapped[1:]
+    firsts, swapped = lax.optimization_barrier((firsts, swapped))
+    rows = rest.shape[1]
+    outer = firsts[:, band * rows : (band + 1) * rows] + swapped[1:]
     outward = slide(outer, OUTWARD)
-    total = run_near(line_ends(), first, rest, inward)
-    return run_share(share, band, bands, total, swapped, outward), swapped, outer
-
-
-def line_scatter_apart(share, band, bands, first, near, far, last, ready, exchange, earlier):
+    return swapped, outward, outer
+
+
+def line_scatter_apart(first, near, far, last, meanwhile, exchange, earlier):
     in_last, in_far, in_near = slide(last, INWARD), slide(far, INWARD), slide(near, INWARD)
-    in_last, ready = lax.optimization_barrier((in_last, ready))
+    in_last, first = lax.optimization_barrier((in_last, first))
     sum_last = last + in_last
-    ready, *_ = lax.optimization_barrier((ready, sum_last, earlier))
-    got = exchange(ready)
     swap_last = slide(sum_last, MIDDLE)
-    in_far, got = lax.optimization_barrier((in_far, got))
+    other = meanwhile(sum_last)
+    in_far, other = lax.optimization_barrier((in_far, other))
     sum_far = far + in_far
     swap_far = slide(sum_far, MIDDLE)
-    outward = slide(first + swap_last, OUTWARD)
-    in_near, _ = lax.optimization_barrier((in_near, sum_far))
-    total = run_near(line_ends(), first, near, in_near)
-    return run_share(share, band, bands, total, swap_far, outward), got
+    other, _ = lax.optimization_barrier((other, sum_far))
+    other = exchange(other)
+    swap_last, _ = lax.optimization_barrier((swap_last, earlier))
+    outer = first + swap_last
+    outward = slide(outer, OUTWARD)
+    other, in_near, _ = lax.optimization_barrier((other, in_near, outer))
+    total = run_near(line_ends(), first, 0, near, in_near)
+    return total, swap_far, outward, other, outer
 
 
 def shards(
@@ -801,21 +859,30 @@
         split_off = ((0,), (1, 2, 3))
         firsts, rest_1, dcum_1, *_ = project(1, split_off, [rest_0], parts_1, before)
         inward_0, inward_1 = slide(rest_0, INWARD), slide(rest_1, INWARD)
-        apart = ((0,), (1,), (2,), (3,))
-        *terms, dcum_2, _, _ = project(2, apart, [rest_1], parts_2)
-        share, swapped_0, outer_0 = line_scatter(
-            None, 0, 4, firsts[:, :BLK], rest_0, inward_0, rest_0[1:] + inward_0[1:]
+        far, last, dcum_2, *grads_2 = project(2, ((2,), (3,)), [rest_1], parts_2)
+        swapped_0, outward_0, outer_0 = line_scatter(
+            0, firsts, rest_0, inward_0, rest_0[1:] + inward_0[1:]
         )
         inward_1, *_ = lax.optimization_barrier((inward_1, swapped_0, dcum_2))
         sum_1 = rest_1[1:] + inward_1[1:]
-        share, _, outer_1 = line_scatter(
-            share, 1, 4, firsts[:, BLK:], rest_1, inward_1, sum_1
+        swapped_1, outward_1, outer_1 = line_scatter(1, firsts, rest_1, inward_1, sum_1)
+        first, near = run_project_more(
+            2, groups, ((0,), (1,)), flip, [sum_1], dq, *grads_2, weights
         )
-        dcums = [dcum_0, dcum_1, dcum_2]
-        sums = run_adjoint(ints, (sum_1, outer_0), dcums, unit, rows, inverse, heads, blocks)
-        share, got = line_scatter_apart(
-            share, 1, 2, *terms, sums, share_sums, outer_1
+
+        def meanwhile(after):
+            dcums = [dcum_0, dcum_1, dcum_2]
+            return run_adjoint(ints, (after, outer_0), dcums, unit, rows, inverse, heads, blocks)
+
+        total_2, swapped_2, outward_2, got, outer_2 = line_scatter_apart(
+            first, near, far, last, meanwhile, share_sums, outer_1
         )
+        inward_0, inward_1, _ = lax.optimization_barrier((inward_0, inward_1, outer_2))
+        total_0 = run_near(line_ends(), firsts, 0, rest_0, inward_0)
+        total_1 = run_near(line_ends(), firsts, 1, rest_1, inward_1)
+        share = run_share(None, 0, 4, total_0, swapped_0, outward_0)
+        share = run_share(share, 1, 4, total_1, swapped_1, outward_1)
+        share = run_share(share, 1, 2, total_2, swapped_2, outward_2)
     else:
         spots = (owners * blocks + offsets).reshape(-1)
         empty = jnp.zeros((ctx_count * blocks, BLK, 2 * width), BF16)

time: 204 us -> 206 us (level)
  waiting for transfers between devices: 42.3 us -> 33.5 us
  starting transfers between devices: 49.1 us -> 55.3 us
  Pallas kernels: 94.4 us -> 97.3 us
    pallas_call x0 -> x1, Pallas kernels: none -> 7.95 us  [run_project_more(): pl.pallas_call(functools.partial(project_more_kernel, groups, layout, len...]
    ppermute x12, waiting for transfers between devices: 12.5 us -> 5.28 us  [slide(): return lax.ppermute(value, 'head', pairs)]
    ppermute x12, starting transfers between devices: 20.8 us -> 27 us  [slide(): return lax.ppermute(value, 'head', pairs)]
    pallas_call x3, Pallas kernels: 37.8 us -> 32.8 us  [run_project(): pl.pallas_call(functools.partial(project_kernel, heads, len(parts[0]), si...]
  transfers between devices with their start and end apart: 42 -> 42, of which waited for: 11 -> 10; matrix products, arithmetic and copies ran while one was open for 3% -> 5% of each run, Pallas kernels for 38% -> 39%
where the time goes in v8:
time: 206 us; the launch traced here: 205 us
  Pallas kernels  97.3 us (47%)
  starting transfers between devices  55.3 us (27%)
  waiting for transfers between devices  33.5 us (16%)
  local copies, waits for them, and re-layouts  11.1 us (5%)
  other arithmetic  6.56 us (3%)
    pallas_call x3, Pallas kernels, run_project(): pl.pallas_call(functools.partial(project_kernel, heads, len(parts[0]), si...  32.8 us
    ppermute x29, waiting for transfers between devices, hop(): return lax.ppermute(value, 'ctx', [(i, i ^ distance) for i in range(count)])  27.6 us
    ppermute x12, starting transfers between devices, slide(): return lax.ppermute(value, 'head', pairs)  27 us
    ppermute x29, starting transfers between devices, hop(): return lax.ppermute(value, 'ctx', [(i, i ^ distance) for i in range(count)])  25 us
    pallas_call x1, Pallas kernels, run_attend(): pl.pallas_call(functools.partial(attend_kernel, heads, blocks, places, pi...  15.2 us
    unnamed x72, local copies, waits for them, and re-layouts  9.3 us
    pallas_call x3, Pallas kernels, run_merge(): pl.pallas_call(merge_kernel, grid=(size, cut), out_shape=[jax.ShapeDtypeS...  8.82 us
    pallas_call x1, Pallas kernels, run_project_more(): pl.pallas_call(functools.partial(project_more_kernel, groups, layout, len...  7.95 us
  transfers between devices with their start and end apart: 42, of which 10 were waited for; matrix products, arithmetic and copies ran while one was open for 5% of the time, Pallas kernels for 39%

profile of v8, /device:TPU:0, one launch (start us, length us, event | category | flops | bytes accessed | tf_op | source)
XLA Modules:
  0.0 204.8 jit_solution(9865985806984929586)
XLA Ops:
  0.6 3.0 %collective-permute-start.1 = (bf16[512,512]{1,0:T(8,128)(2,1)}, bf16[512,512]{1,0:T(8,128)(2,1)S(1)}, u32[]{:S(2)}, u32[]{:S(2)}) collective-permute-start(bf16[512,512]{1,0:T(8,128)(2,1)} %refs_20_.1), channel_id=1, source_target_pairs={{0,8},{4,12},{8,0},{12,4},{16,24},{20,28},{24,16},{28,20},{1,9},{5... | collective-permute-start | bytes 1572872 | tf_op jit(solution)/shard_map/ppermute | solution.py:679
  8.2 8.4 %collective-permute-done.1.refs_6_ = bf16[512,512]{1,0:T(8,128)(2,1)S(1)} collective-permute-done((bf16[512,512]{1,0:T(8,128)(2,1)}, bf16[512,512]{1,0:T(8,128)(2,1)S(1)}, u32[]{:S(2)}, u32[]{:S(2)}) %collective-permute-start.1) | collective-permute-done | bytes 524320 | tf_op jit(solution)/shard_map/ppermute | solution.py:679
  22.3 5.1 %collective-permute-done.refs_5_ = bf16[512,512]{1,0:T(8,128)(2,1)S(1)} collective-permute-done((bf16[512,512]{1,0:T(8,128)(2,1)}, bf16[512,512]{1,0:T(8,128)(2,1)S(1)}, u32[]{:S(2)}, u32[]{:S(2)}) %collective-permute-start) | collective-permute-done | bytes 524320 | tf_op jit(solution)/shard_map/ppermute | solution.py:679
  31.3 4.5 %house_chain.1 = (f32[32,512]{1,0:T(8,128)S(1)}, f32[32,512]{1,0:T(8,128)S(1)}, f32[4,32,32]{2,1,0:T(8,128)S(1)}, bf16[4,128,96]{2,1,0:T(8,128)(2,1)S(1)}, bf16[4,96,128]{2,1,0:T(8,128)(2,1)S(1)}) custom-call(s32[17]{0:T(128)S(1)} %pad_add_fusion.ints_ref.refs_0_.base_ref, f32[8,512]{1,0:T(8,128)S(1)} %pad_maximum_fusion.refs_0_, ...), custom_call_target="tpu_custom_call" | custom-call | flops 6899999744 | bytes 1048576 | tf_op jit(solution)/shard_map/house_chain/pallas_call | solution.py:119
  38.7 5.6 %rotate.1 = (bf16[512,512]{1,0:T(8,128)(2,1)S(1)}, bf16[512,512]{1,0:T(8,128)(2,1)S(1)}, bf16[4,4,128,128]{3,2,1,0:T(8,128)(2,1)S(1)}, bf16[8,4,256,128]{3,2,1,0:T(8,128)(2,1)S(1)}) custom-call(s32[17]{0:T(128)S(1)} %pad_add_fusion.ints_ref.refs_0_.base_ref, bf16[4,128,96]{2,1,0:T(8,128)(2,1)S(1)} %get-tuple-element.81.wide_ref, ...), custom_call_target="tpu_custom_call" | custom-call | flops 10350000128 | bytes 1048576 | tf_op jit(solution)/shard_map/rotate/pallas_call | solution.py:187
  47.0 15.2 %attend.1 = (bf16[512,512]{1,0:T(8,128)(2,1)}, f32[4,4,128,128]{3,2,1,0:T(8,128)}, f32[512,512]{1,0:T(8,128)}, f32[512,512]{1,0:T(8,128)}, bf16[1,4,128,1024]{3,...) custom-call(s32[17]{0:T(128)S(1)} %pad_add_fusion.ints_ref.refs_0_.b, ...), custom_call_target="tpu_custom_call" | custom-call | flops 17250000896 | bytes 1048576 | tf_op jit(solution)/shard_map/attend/pallas_call | solution.py:376
  62.4 2.7 %collective-permute-done.18.got_ref = bf16[1,4,128,1024]{3,2,1,0:T(8,128)(2,1)S(1)} collective-permute-done((bf16[1,4,128,1024]{3,2,1,0:T(8,128)(2,1)}, bf16[1,4,128,1024]{3,2,1,0:T(8,128)(2,1)S(1)}, u32[]{:S(2)}, u32[]{:S(2)}) %collective-permute-start.18) | collective-permute-done | bytes 1048608 | tf_op jit(solution)/shard_map/ppermute | solution.py:679
  66.3 2.3 %merge.3 = (bf16[1,128,1024]{2,1,0:T(8,128)(2,1)}, bf16[1,128,1024]{2,1,0:T(8,128)(2,1)}, bf16[1,128,1024]{2,1,0:T(8,128)(2,1)}) custom-call(bf16[1,4,128,1024]{3,2,1,0:T(8,128)(2,1)} %get-tuple-element.94.own_ref, bf16[1,4,128,1024]{3,2,1,0:T(8,128)(2,1)} %copy-done.24), custom_call_target="tpu_custom_call" | custom-call | flops 2300000000 | bytes 1048576 | tf_op jit(solution)/shard_map/merge/pallas_call | solution.py:405
  69.4 2.7 %collective-permute-start.22 = (bf16[1,128,1024]{2,1,0:T(8,128)(2,1)}, bf16[1,128,1024]{2,1,0:T(8,128)(2,1)}, u32[]{:S(2)}, u32[]{:S(2)}) collective-permute-start(bf16[1,128,1024]{2,1,0:T(8,128)(2,1)} %get-tuple-element.99), channel_id=1, source_target_pairs={{0,24},{4,28},{8,16},{12,20},{16,8},{20,12},{24,0},{28,4},{1,25},{... | collective-permute-start | bytes 786440 | tf_op jit(solution)/shard_map/ppermute | solution.py:679
  73.8 2.3 %merge.4 = (bf16[1,128,1024]{2,1,0:T(8,128)(2,1)}, bf16[1,128,1024]{2,1,0:T(8,128)(2,1)}, bf16[1,128,1024]{2,1,0:T(8,128)(2,1)}) custom-call(bf16[3,4,128,1024]{3,2,1,0:T(8,128)(2,1)} %get-tuple-element.90.own_ref, bf16[3,4,128,1024]{3,2,1,0:T(8,128)(2,1)} %copy-done.9, bf16[1,128,1024]{2,1,0:T(8,128)(2,1)} %get-tuple-element.95.refs_0_), custom_call_target="tpu_custom_call" | custom-call | flops 2300000000 | bytes 1048576 | tf_op jit(solution)/shard_map/merge/pallas_call | solution.py:405
  76.1 4.2 %merge.5 = (bf16[2,128,1024]{2,1,0:T(8,128)(2,1)}, bf16[2,128,1024]{2,1,0:T(8,128)(2,1)}, bf16[2,128,1024]{2,1,0:T(8,128)(2,1)}) custom-call(bf16[3,4,128,1024]{3,2,1,0:T(8,128)(2,1)} %get-tuple-element.90.own_ref, bf16[3,4,128,1024]{3,2,1,0:T(8,128)(2,1)} %copy-done.9, bf16[1,128,1024]{2,1,0:T(8,128)(2,1)} %get-tuple-element.109.refs_0_), custom_call_target="tpu_custom_call" | custom-call | flops 2300000000 | bytes 1048576 | tf_op jit(solution)/shard_map/merge/pallas_call | solution.py:405
  80.3 3.0 %collective-permute-done.21.refs_4_ = bf16[1,128,1024]{2,1,0:T(8,128)(2,1)S(1)} collective-permute-done((bf16[1,128,1024]{2,1,0:T(8,128)(2,1)}, bf16[1,128,1024]{2,1,0:T(8,128)(2,1)S(1)}, u32[]{:S(2)}, u32[]{:S(2)}) %collective-permute-start.21) | collective-permute-done | bytes 262176 | tf_op jit(solution)/shard_map/ppermute | solution.py:679
  86.8 10.4 %project.3 = (bf16[3,128,1024]{2,1,0:T(8,128)(2,1)}, f32[1,4,128,128]{3,2,1,0:T(8,128)}, bf16[128,512]{1,0:T(8,128)(2,1)}, bf16[128,512]{1,0:T(8,128)(2,1)}) custom-call(s32[1]{0:T(128)} %bitcast.1.flip_ref, bf16[2,128,1024]{2,1,0:T(8,128)(2,1)} %get-tuple-element.117.refs_0_, bf16[4,128,1024]{2,1,0:T(8,128)(2,1)} %bitcast.14, ...), custom_call_target="tpu_custom_call" | custom-call | flops 10350000128 | bytes 1048576 | tf_op jit(solution)/shard_map/project/pallas_call | solution.py:552
  97.3 3.8 %collective-permute-start.26 = (bf16[3,128,1024]{2,1,0:T(8,128)(2,1)}, bf16[3,128,1024]{2,1,0:T(8,128)(2,1)S(1)}, u32[]{:S(2)}, u32[]{:S(2)}) collective-permute-start(bf16[3,128,1024]{2,1,0:T(8,128)(2,1)} %get-tuple-element.104.refs_0_.near_ref), channel_id=1, source_target_pairs={{0,1},{3,2},{4,5},{7,6},{8,9},{11,10},{12,13},{15,14},{16,17},{19,... | collective-permute-start | bytes 2359304 | tf_op jit(solution)/shard_map/ppermute | solution.py:683
  104.7 13.1 %project.4 = (bf16[1,256,1024]{2,1,0:T(8,128)(2,1)}, bf16[3,128,1024]{2,1,0:T(8,128)(2,1)}, f32[1,4,128,128]{3,2,1,0:T(8,128)}, bf16[128,512]{1,0:T(8,128)(2,1)}, bf16[128,512]{1,0:T(8,128)(2,1)}) custom-call(s32[1]{0:T(128)} %bitcast.1.flip_ref, bf16[3,128,1024]{2,1,0:T(8,128)(2,1)} %get-tuple-element.104.refs_0_.near_ref, bf16[12,128,1024]{2,1,0:T(8,128)(2,1)} %bitcast.7, ...), custom_call_target="tpu_custom_call" | custom-call | flops 13799999488 | bytes 1048576 | tf_op jit(solution)/shard_map/project/pallas_call | solution.py:552
  121.7 4.1 %collective-permute-done.30.refs_4_.refs_9_ = bf16[2,128,1024]{2,1,0:T(8,128)(2,1)S(1)} collective-permute-done((bf16[2,128,1024]{2,1,0:T(8,128)(2,1)}, bf16[2,128,1024]{2,1,0:T(8,128)(2,1)S(1)}, u32[]{:S(2)}, u32[]{:S(2)}) %collective-permute-start.30) | collective-permute-done | bytes 524320 | tf_op jit(solution)/shard_map/ppermute | solution.py:679
  127.4 9.3 %project.5 = (bf16[1,256,1024]{2,1,0:T(8,128)(2,1)}, bf16[1,256,1024]{2,1,0:T(8,128)(2,1)}, f32[2,4,128,128]{3,2,1,0:T(8,128)}, bf16[256,512]{1,0:T(8,128)(2,1)}, bf16[256,512]{1,0:T(8,128)(2,1)}) custom-call(s32[1]{0:T(128)} %bitcast.1.flip_ref, bf16[3,128,1024]{2,1,0:T(8,128)(2,1)} %get-tuple-element.115.refs_0_.near_ref, bf16[12,128,1024]{2,1,0:T(8,128)(2,1)} %bitcast.8, ...), custom_call_target="tpu_custom_call" | custom-call | flops 6899999744 | bytes 1048576 | tf_op jit(solution)/shard_map/project/pallas_call | solution.py:552
  143.0 7.9 %project_more.1 = (bf16[1,256,1024]{2,1,0:T(8,128)(2,1)}, bf16[1,256,1024]{2,1,0:T(8,128)(2,1)}) custom-call(s32[1]{0:T(128)} %bitcast.1.flip_ref, bf16[2,128,1024]{2,1,0:T(8,128)(2,1)} %copy-done.19, bf16[512,512]{1,0:T(8,128)(2,1)} %get-tuple-element.102.refs_8_.refs_6_.refs_11_.refs_13_.refs_1_, bf16[256,512]{1,0:T(8,128)(2,1)} %get-tuple-element.123.refs_2_, ...), custom_call_target="tpu_custom_call" | custom-call | flops 6899999744 | bytes 1048576 | tf_op jit(solution)/shard_map/project_more/pallas_call | solution.py:511
  152.8 7.1 %collective-permute-start.38 = (bf16[1,256,1024]{2,1,0:T(8,128)(2,1)}, bf16[1,256,1024]{2,1,0:T(8,128)(2,1)}, u32[]{:S(2)}, u32[]{:S(2)}) collective-permute-start(bf16[1,256,1024]{2,1,0:T(8,128)(2,1)} %get-tuple-element.134.near_ref), channel_id=1, source_target_pairs={{0,1},{3,2},{4,5},{7,6},{8,9},{11,10},{12,13},{15,14},{16,17},{19,... | collective-permute-start | bytes 1572872 | tf_op jit(solution)/shard_map/ppermute | solution.py:683
  162.4 7.3 %adjoint.1 = f32[32,1024]{1,0:T(8,128)} custom-call(s32[17]{0:T(128)} %copy-done.5, bf16[1,256,1024]{2,1,0:T(8,128)(2,1)} %copy-done.14, bf16[1,128,1024]{2,1,0:T(8,128)(2,1)} %copy-done.15, f32[1,4,128,128]{3,2,1,0:T(8,128)} %get-tuple-element.136.refs_2_, f32[1,4,128,128]{3,2,1,0:T(8,128)} %get-tuple-element.137.refs_3_, ...), custom_call_target="tpu_custom_call" | custom-call | flops 230000000 | bytes 1048576 | tf_op jit(solution)/shard_map/adjoint/pallas_call | solution.py:635
  174.0 3.4 %all-to-all-start = ((f32[8,4,1024]{2,1,0:T(4,128)}), f32[8,4,1024]{2,1,0:T(4,128)S(1)}, u32[]{:S(2)}, u32[]{:S(2)}) async-start(f32[8,4,1024]{2,1,0:T(4,128)} %reshape.50), calls=%async_computation | async-start | bytes 262144 | tf_op jit(solution)/shard_map/all_to_all | solution.py:834
  182.8 2.5 %near_sum.5.refs_1_ = f32[256,1024]{1,0:T(8,128)} custom-call(s32[1]{0:T(128)} %bitcast.ends_ref, bf16[1,256,1024]{2,1,0:T(8,128)(2,1)} %get-tuple-element.126.first_ref, bf16[1,256,1024]{2,1,0:T(8,128)(2,1)} %get-tuple-element.134.near_ref, bf16[1,256,1024]{2,1,0:T(8,128)(2,1)} %collective-permute-done.38.inward_ref), custom_call_target="tpu_custom_call" | custom-call | flops 5750000128 | bytes 1048576 | tf_op jit(solution)/shard_map/near_sum/pallas_call | solution.py:698
  189.3 2.6 %house_grad.1 = f32[4,512]{1,0:T(4,128)} custom-call(s32[17]{0:T(128)} %copy-done.5, f32[8,4,1024]{2,1,0:T(4,128)} %copy-done.23, f32[32,512]{1,0:T(8,128)} %copy-done.2, f32[32,512]{1,0:T(8,128)} %copy-done.3, f32[4,512]{1,0:T(4,128)} %house_ref.1), custom_call_target="tpu_custom_call" | custom-call | flops 2300000000 | bytes 1048576 | tf_op jit(solution)/shard_map/house_grad/pallas_call | solution.py:667
  196.5 5.3 %collective-permute-done.40.refs_3_ = bf16[1,256,1024]{2,1,0:T(8,128)(2,1)S(1)} collective-permute-done((bf16[1,256,1024]{2,1,0:T(8,128)(2,1)S(1)}, bf16[1,256,1024]{2,1,0:T(8,128)(2,1)S(1)}, u32[]{:S(2)}, u32[]{:S(2)}) %collective-permute-start.40) | collective-permute-done | bytes 524320 | tf_op jit(solution)/shard_map/ppermute | solution.py:683
  (163 shorter events, 68.1 us)
Async XLA Ops:
  0.6 16.0 %collective-permute-start.1 = (bf16[512,512]{1,0:T(8,128)(2,1)}, bf16[512,512]{1,0:T(8,128)(2,1)S(1)}, u32[]{:S(2)}, u32[]{:S(2)}) collective-permute-start(bf16[512,512]{1,0:T(8,128)(2,1)} %refs_20_.1), channel_id=1, source_target_pairs={{0,8},{4,12},{8,0},{12,4},{16,24},{20,28},{24,16},{28,20},{1,9},{5... | collective-permute-start | bytes 1572872 | tf_op jit(solution)/shard_map/ppermute | solution.py:679
  3.6 15.1 %collective-permute-start.2 = (bf16[512,512]{1,0:T(8,128)(2,1)}, bf16[512,512]{1,0:T(8,128)(2,1)S(1)}, u32[]{:S(2)}, u32[]{:S(2)}) collective-permute-start(bf16[512,512]{1,0:T(8,128)(2,1)} %refs_14_.3), channel_id=1, source_target_pairs={{0,16},{4,20},{8,24},{12,28},{16,0},{20,4},{24,8},{28,12},{1,17},{... | collective-permute-start | bytes 1572872 | tf_op jit(solution)/shard_map/ppermute | solution.py:679
  5.2 22.2 %collective-permute-start = (bf16[512,512]{1,0:T(8,128)(2,1)}, bf16[512,512]{1,0:T(8,128)(2,1)S(1)}, u32[]{:S(2)}, u32[]{:S(2)}) collective-permute-start(bf16[512,512]{1,0:T(8,128)(2,1)} %refs_14_.3), channel_id=1, source_target_pairs={{0,8},{4,12},{8,0},{12,4},{16,24},{20,28},{24,16},{28,20},{1,9},{5... | collective-permute-start | bytes 1572872 | tf_op jit(solution)/shard_map/ppermute | solution.py:679
  5.7 23.4 %collective-permute-start.3 = (bf16[512,512]{1,0:T(8,128)(2,1)}, bf16[512,512]{1,0:T(8,128)(2,1)S(1)}, u32[]{:S(2)}, u32[]{:S(2)}) collective-permute-start(bf16[512,512]{1,0:T(8,128)(2,1)} %refs_20_.1), channel_id=1, source_target_pairs={{0,16},{4,20},{8,24},{12,28},{16,0},{20,4},{24,8},{28,12},{1,17},{... | collective-permute-start | bytes 1572872 | tf_op jit(solution)/shard_map/ppermute | solution.py:679
  27.4 16.9 %collective-permute-start.14 = (bf16[512,512]{1,0:T(8,128)(2,1)S(1)}, bf16[512,512]{1,0:T(8,128)(2,1)S(1)}, u32[]{:S(2)}, u32[]{:S(2)}) collective-permute-start(bf16[512,512]{1,0:T(8,128)(2,1)S(1)} %collective-permute-done.2.refs_9_), channel_id=1, source_target_pairs={{0,8},{4,12},{8,0},{12,4},{16,24},{20,28},{24,16},{28,20},{1,9},{5... | collective-permute-start | bytes 1572872 | tf_op jit(solution)/shard_map/ppermute | solution.py:679
  29.1 15.1 %collective-permute-start.15 = (bf16[512,512]{1,0:T(8,128)(2,1)S(1)}, bf16[512,512]{1,0:T(8,128)(2,1)S(1)}, u32[]{:S(2)}, u32[]{:S(2)}) collective-permute-start(bf16[512,512]{1,0:T(8,128)(2,1)S(1)} %collective-permute-done.1.refs_6_), channel_id=1, source_target_pairs={{0,16},{4,20},{8,24},{12,28},{16,0},{20,4},{24,8},{28,12},{1,17},{... | collective-permute-start | bytes 1572872 | tf_op jit(solution)/shard_map/ppermute | solution.py:679
  83.3 17.8 %collective-permute-start.23 = (bf16[1,128,1024]{2,1,0:T(8,128)(2,1)S(1)}, bf16[1,128,1024]{2,1,0:T(8,128)(2,1)S(1)}, u32[]{:S(2)}, u32[]{:S(2)}) collective-permute-start(bf16[1,128,1024]{2,1,0:T(8,128)(2,1)S(1)} %copy-done.33), channel_id=1, source_target_pairs={{0,8},{4,12},{8,0},{12,4},{16,24},{20,28},{24,16},{28,20},{1,9},{5... | collective-permute-start | bytes 786440 | tf_op jit(solution)/shard_map/ppermute | solution.py:679
  84.8 16.2 %collective-permute-start.24 = (bf16[1,128,1024]{2,1,0:T(8,128)(2,1)S(1)}, bf16[1,128,1024]{2,1,0:T(8,128)(2,1)S(1)}, u32[]{:S(2)}, u32[]{:S(2)}) collective-permute-start(bf16[1,128,1024]{2,1,0:T(8,128)(2,1)S(1)} %copy-done.30), channel_id=1, source_target_pairs={{0,16},{4,20},{8,24},{12,28},{16,0},{20,4},{24,8},{28,12},{1,17},{... | collective-permute-start | bytes 786440 | tf_op jit(solution)/shard_map/ppermute | solution.py:679
  85.3 15.7 %collective-permute-start.25 = (bf16[1,128,1024]{2,1,0:T(8,128)(2,1)S(1)}, bf16[1,128,1024]{2,1,0:T(8,128)(2,1)S(1)}, u32[]{:S(2)}, u32[]{:S(2)}) collective-permute-start(bf16[1,128,1024]{2,1,0:T(8,128)(2,1)S(1)} %copy-done.27), channel_id=1, source_target_pairs={{0,24},{4,28},{8,16},{12,20},{16,8},{20,12},{24,0},{28,4},{1,25},{... | collective-permute-start | bytes 786440 | tf_op jit(solution)/shard_map/ppermute | solution.py:679
  97.3 22.7 %collective-permute-start.26 = (bf16[3,128,1024]{2,1,0:T(8,128)(2,1)}, bf16[3,128,1024]{2,1,0:T(8,128)(2,1)S(1)}, u32[]{:S(2)}, u32[]{:S(2)}) collective-permute-start(bf16[3,128,1024]{2,1,0:T(8,128)(2,1)} %get-tuple-element.104.refs_0_.near_ref), channel_id=1, source_target_pairs={{0,1},{3,2},{4,5},{7,6},{8,9},{11,10},{12,13},{15,14},{16,17},{19,... | collective-permute-start | bytes 2359304 | tf_op jit(solution)/shard_map/ppermute | solution.py:683
  101.1 20.6 %collective-permute-start.29 = (bf16[2,128,1024]{2,1,0:T(8,128)(2,1)}, bf16[2,128,1024]{2,1,0:T(8,128)(2,1)S(1)}, u32[]{:S(2)}, u32[]{:S(2)}) collective-permute-start(bf16[2,128,1024]{2,1,0:T(8,128)(2,1)} %get-tuple-element.117.refs_0_), channel_id=1, source_target_pairs={{0,8},{4,12},{8,0},{12,4},{16,24},{20,28},{24,16},{28,20},{1,9},{5... | collective-permute-start | bytes 1572872 | tf_op jit(solution)/shard_map/ppermute | solution.py:679
  102.7 23.1 %collective-permute-start.30 = (bf16[2,128,1024]{2,1,0:T(8,128)(2,1)}, bf16[2,128,1024]{2,1,0:T(8,128)(2,1)S(1)}, u32[]{:S(2)}, u32[]{:S(2)}) collective-permute-start(bf16[2,128,1024]{2,1,0:T(8,128)(2,1)} %get-tuple-element.118), channel_id=1, source_target_pairs={{0,16},{4,20},{8,24},{12,28},{16,0},{20,4},{24,8},{28,12},{1,17},{... | collective-permute-start | bytes 1572872 | tf_op jit(solution)/shard_map/ppermute | solution.py:679
  103.2 22.6 %collective-permute-start.31 = (bf16[2,128,1024]{2,1,0:T(8,128)(2,1)}, bf16[2,128,1024]{2,1,0:T(8,128)(2,1)S(1)}, u32[]{:S(2)}, u32[]{:S(2)}) collective-permute-start(bf16[2,128,1024]{2,1,0:T(8,128)(2,1)} %get-tuple-element.119), channel_id=1, source_target_pairs={{0,24},{4,28},{8,16},{12,20},{16,8},{20,12},{24,0},{28,4},{1,25},{... | collective-permute-start | bytes 1572872 | tf_op jit(solution)/shard_map/ppermute | solution.py:679
  117.8 22.6 %collective-permute-start.27 = (bf16[3,128,1024]{2,1,0:T(8,128)(2,1)}, bf16[3,128,1024]{2,1,0:T(8,128)(2,1)}, u32[]{:S(2)}, u32[]{:S(2)}) collective-permute-start(bf16[3,128,1024]{2,1,0:T(8,128)(2,1)} %get-tuple-element.115.refs_0_.near_ref), channel_id=1, source_target_pairs={{0,1},{3,2},{4,5},{7,6},{8,9},{11,10},{12,13},{15,14},{16,17},{19,... | collective-permute-start | bytes 2359304 | tf_op jit(solution)/shard_map/ppermute | solution.py:683
  120.1 20.3 %collective-permute-start.28 = (bf16[2,128,1024]{2,1,0:T(8,128)(2,1)S(1)}, bf16[2,128,1024]{2,1,0:T(8,128)(2,1)}, u32[]{:S(2)}, u32[]{:S(2)}) collective-permute-start(bf16[2,128,1024]{2,1,0:T(8,128)(2,1)S(1)} %slice_add_fusion), channel_id=1, source_target_pairs={{1,2},{2,1},{5,6},{6,5},{9,10},{10,9},{13,14},{14,13},{17,18},{18,... | collective-permute-start | bytes 1572872 | tf_op jit(solution)/shard_map/ppermute | solution.py:683
  136.7 14.2 %collective-permute-start.32 = (bf16[1,256,1024]{2,1,0:T(8,128)(2,1)}, bf16[1,256,1024]{2,1,0:T(8,128)(2,1)S(1)}, u32[]{:S(2)}, u32[]{:S(2)}) collective-permute-start(bf16[1,256,1024]{2,1,0:T(8,128)(2,1)} %get-tuple-element.122), channel_id=1, source_target_pairs={{0,1},{3,2},{4,5},{7,6},{8,9},{11,10},{12,13},{15,14},{16,17},{19,... | collective-permute-start | bytes 1572872 | tf_op jit(solution)/shard_map/ppermute | solution.py:683
  138.3 31.4 %collective-permute-start.37 = (bf16[1,256,1024]{2,1,0:T(8,128)(2,1)}, bf16[1,256,1024]{2,1,0:T(8,128)(2,1)}, u32[]{:S(2)}, u32[]{:S(2)}) collective-permute-start(bf16[1,256,1024]{2,1,0:T(8,128)(2,1)} %get-tuple-element.135), channel_id=1, source_target_pairs={{0,1},{3,2},{4,5},{7,6},{8,9},{11,10},{12,13},{15,14},{16,17},{19,... | collective-permute-start | bytes 1572872 | tf_op jit(solution)/shard_map/ppermute | solution.py:683
  141.5 35.9 %collective-permute-start.34 = (bf16[2,128,1024]{2,1,0:T(8,128)(2,1)S(1)}, bf16[2,128,1024]{2,1,0:T(8,128)(2,1)}, u32[]{:S(2)}, u32[]{:S(2)}) collective-permute-start(bf16[2,128,1024]{2,1,0:T(8,128)(2,1)S(1)} %slice_add_fusion.1.refs_0_), channel_id=1, source_target_pairs={{1,2},{2,1},{5,6},{6,5},{9,10},{10,9},{13,14},{14,13},{17,18},{18,... | collective-permute-start | bytes 1572872 | tf_op jit(solution)/shard_map/ppermute | solution.py:683
  151.2 28.5 %collective-permute-start.33 = (bf16[1,256,1024]{2,1,0:T(8,128)(2,1)S(1)}, bf16[1,256,1024]{2,1,0:T(8,128)(2,1)}, u32[]{:S(2)}, u32[]{:S(2)}) collective-permute-start(bf16[1,256,1024]{2,1,0:T(8,128)(2,1)S(1)} %add.23.refs_0_), channel_id=1, source_target_pairs={{1,2},{2,1},{5,6},{6,5},{9,10},{10,9},{13,14},{14,13},{17,18},{18,... | collective-permute-start | bytes 1572872 | tf_op jit(solution)/shard_map/ppermute | solution.py:683
  152.8 30.1 %collective-permute-start.38 = (bf16[1,256,1024]{2,1,0:T(8,128)(2,1)}, bf16[1,256,1024]{2,1,0:T(8,128)(2,1)}, u32[]{:S(2)}, u32[]{:S(2)}) collective-permute-start(bf16[1,256,1024]{2,1,0:T(8,128)(2,1)} %get-tuple-element.134.near_ref), channel_id=1, source_target_pairs={{0,1},{3,2},{4,5},{7,6},{8,9},{11,10},{12,13},{15,14},{16,17},{19,... | collective-permute-start | bytes 1572872 | tf_op jit(solution)/shard_map/ppermute | solution.py:683
  160.8 31.0 %collective-permute-start.35 = (bf16[1,128,1024]{2,1,0:T(8,128)(2,1)S(1)}, bf16[1,128,1024]{2,1,0:T(8,128)(2,1)}, u32[]{:S(2)}, u32[]{:S(2)}) collective-permute-start(bf16[1,128,1024]{2,1,0:T(8,128)(2,1)S(1)} %slice_add_fusion.2.refs_1_), channel_id=1, source_target_pairs={{1,0},{2,3},{5,4},{6,7},{9,8},{10,11},{13,12},{14,15},{17,16},{18,... | collective-permute-start | bytes 786440 | tf_op jit(solution)/shard_map/ppermute | solution.py:683
  170.9 25.5 %collective-permute-start.39 = (bf16[1,256,1024]{2,1,0:T(8,128)(2,1)S(1)}, bf16[1,256,1024]{2,1,0:T(8,128)(2,1)}, u32[]{:S(2)}, u32[]{:S(2)}) collective-permute-start(bf16[1,256,1024]{2,1,0:T(8,128)(2,1)S(1)} %add.27), channel_id=1, source_target_pairs={{1,2},{2,1},{5,6},{6,5},{9,10},{10,9},{13,14},{14,13},{17,18},{18,... | collective-permute-start | bytes 1572872 | tf_op jit(solution)/shard_map/ppermute | solution.py:683
  178.4 15.4 %collective-permute-start.36 = (bf16[1,128,1024]{2,1,0:T(8,128)(2,1)S(1)}, bf16[1,128,1024]{2,1,0:T(8,128)(2,1)S(1)}, u32[]{:S(2)}, u32[]{:S(2)}) collective-permute-start(bf16[1,128,1024]{2,1,0:T(8,128)(2,1)S(1)} %slice_add_fusion.3), channel_id=1, source_target_pairs={{1,0},{2,3},{5,4},{6,7},{9,8},{10,11},{13,12},{14,15},{17,16},{18,... | collective-permute-start | bytes 786440 | tf_op jit(solution)/shard_map/ppermute | solution.py:683
  180.9 20.8 %collective-permute-start.40 = (bf16[1,256,1024]{2,1,0:T(8,128)(2,1)S(1)}, bf16[1,256,1024]{2,1,0:T(8,128)(2,1)S(1)}, u32[]{:S(2)}, u32[]{:S(2)}) collective-permute-start(bf16[1,256,1024]{2,1,0:T(8,128)(2,1)S(1)} %add.25), channel_id=1, source_target_pairs={{1,0},{2,3},{5,4},{6,7},{9,8},{10,11},{13,12},{14,15},{17,16},{18,... | collective-permute-start | bytes 1572872 | tf_op jit(solution)/shard_map/ppermute | solution.py:683
  (53 other events, 430.6 us)

commit v9 on v8

--- a/solution.py
+++ b/solution.py
@@ -562,7 +562,7 @@
         ),
         grid=(1,),
         in_specs=in_smem(1)
-        + [whole(1, 16, 128)] * len(afters)
+        + [whole(1, min(16, after.shape[1]), 128) for after in afters]
         + [part_spec(index) for _, index in flat]
         + [whole(rows, width)] * len(before)
         + [rows_spec] * 4
@@ -596,14 +596,15 @@
     )
 
 
-def adjoint_kernel(heads, blocks, afters, ints_ref, *refs):
+def adjoint_kernel(heads, blocks, first, carried, afters, ints_ref, *refs):
     refs = refs[afters:]
+    carry_refs, refs = refs[:carried], refs[carried:]
     dcums = [ref.at[j] for ref in refs[:-4] for j in range(ref.shape[0])]
     unit_ref, rows_ref, inv_ref, out_ref = refs[-4:]
     count, width = unit_ref.shape
-    stacked = (blocks * count, count)
+    stacked = (len(dcums) * count, count)
     eye = (iota((count, count), 0) == iota((count, count), 1)).astype(F32)
-    base = ints_ref[0] * blocks
+    base = ints_ref[0] * blocks + first
     level, col = iota(stacked, 0), iota(stacked, 1)
     row = level % count
     mine = base + level // count
@@ -615,10 +616,10 @@
         overlap = jnp.where(col <= mine, nt_high(moved, units), 0.0)
         gamma = nn_high(overlap, inverse)
         gamma = jnp.where((row < col) & (col <= mine), gamma, 0.0)
-        beta = jnp.concatenate([eye - inverse_t] * blocks, axis=0)
+        beta = jnp.concatenate([eye - inverse_t] * len(dcums), axis=0)
         beta = jnp.where(col <= mine, beta, 0.0)
         x_all = jnp.where(alive, moved - 2.0 * nn_high(gamma, units), 0.0)
-        turned = jnp.concatenate([units] * blocks, axis=0) - nn_high(beta, units)
+        turned = jnp.concatenate([units] * len(dcums), axis=0) - nn_high(beta, units)
         turned = jnp.where(alive, turned, 0.0)
         x_total, y_total = None, None
         for j, dcum in enumerate(dcums):
@@ -626,23 +627,30 @@
             y_part = nn_high(turned[here], dcum[h])
             x_total = x_all[here] if j == 0 else x_total + x_all[here]
             y_total = y_part if j == 0 else y_total + y_part
-        out_ref[:, head(h)] = x_total
-        out_ref[:, slice(width + h * DH, width + (h + 1) * DH)] = y_total
-
-
-def run_adjoint(ints, afters, dcums, unit, rows, inverse, heads, blocks):
+        for total, lanes in (
+            (x_total, head(h)),
+            (y_total, slice(width + h * DH, width + (h + 1) * DH)),
+        ):
+            for c in range(count // blocks):
+                part = total[c * blocks : (c + 1) * blocks]
+                for ref in carry_refs:
+                    part = part + ref[c, :, lanes]
+                out_ref[c, :, lanes] = part
+
+
+def run_adjoint(ints, first, carry, afters, dcums, unit, rows, inverse, heads, blocks):
     count, width = unit.shape
     return pl.pallas_call(
-        functools.partial(adjoint_kernel, heads, blocks, len(afters)),
-        out_shape=jax.ShapeDtypeStruct((count, 2 * width), F32),
+        functools.partial(adjoint_kernel, heads, blocks, first, len(carry), len(afters)),
+        out_shape=jax.ShapeDtypeStruct((count // blocks, blocks, 2 * width), F32),
         in_specs=in_smem(1)
         + [pl.BlockSpec(memory_space=pl.ANY)] * len(afters)
-        + in_vmem(len(dcums) + 3),
+        + in_vmem(len(carry) + len(dcums) + 3),
         out_specs=pl.BlockSpec(memory_space=pltpu.VMEM),
         compiler_params=grant(60),
         cost_estimate=cost(0.2),
         name="adjoint",
-    )(ints, *afters, *dcums, unit, rows, inverse)
+    )(ints, *afters, *carry, *dcums, unit, rows, inverse)
 
 
 def house_kernel(heads, blocks, base_ref, got_ref, unit_ref, rows_ref, house_ref, out_ref):
@@ -739,17 +747,62 @@
     return ((place == 0) | (place == 3)).astype(jnp.int32).reshape(1)
 
 
-def line_scatter(band, firsts, rest, inward, inner):
-    swapped = slide(inner, MIDDLE)
-    firsts, swapped = lax.optimization_barrier((firsts, swapped))
-    rows = rest.shape[1]
-    outer = firsts[:, band * rows : (band + 1) * rows] + swapped[1:]
-    outward = slide(outer, OUTWARD)
-    return swapped, outward, outer
+def outer_kernel(first_ref, low_ref, high_ref, out_ref):
+    rows = low_ref.shape[1]
+    for i, ref in enumerate((low_ref, high_ref)):
+        here = slice(i * rows, (i + 1) * rows)
+        out_ref[0, here] = (first_ref[0, here].astype(F32) + ref[0].astype(F32)).astype(BF16)
+
+
+def run_outer(firsts, low, high):
+    _, rows, width = low.shape
+    swapped = pl.BlockSpec((1, rows, width), lambda t: (1, 0, 0))
+    both = pl.BlockSpec((1, 2 * rows, width), lambda t: (0, 0, 0))
+    return pl.pallas_call(
+        outer_kernel,
+        grid=(1,),
+        out_shape=jax.ShapeDtypeStruct(firsts.shape, BF16),
+        in_specs=[both, swapped, swapped],
+        out_specs=both,
+        compiler_params=grant(60),
+        cost_estimate=cost(2),
+        name="outer",
+    )(firsts, low, high)
+
+
+def first_band_kernel(ends_ref, first_ref, outward_ref, *refs):
+    out_ref = refs[-1]
+    rows = refs[0].shape[1]
+    for i in range(2):
+        here = slice(i * rows, (i + 1) * rows)
+        rest_ref, inward_ref, swapped_ref = refs[3 * i : 3 * i + 3]
+        total = jnp.where(ends_ref[0] > 0, first_ref[0, here], rest_ref[0]).astype(F32)
+        total = total + inward_ref[0].astype(F32)
+        total = total + (swapped_ref[0].astype(F32) + outward_ref[0, here].astype(F32))
+        out_ref[here] = total.astype(BF16)
+
+
+def run_first_band(bands, firsts, outward, *parts):
+    _, height, width = firsts.shape
+    tile = min(512, width)
+    both = pl.BlockSpec((1, height, tile), lambda t: (0, 0, t))
+    part = pl.BlockSpec((1, height // 2, tile), lambda t: (0, 0, t))
+    return pl.pallas_call(
+        first_band_kernel,
+        grid=(width // tile,),
+        out_shape=jax.ShapeDtypeStruct((bands * height, width), BF16),
+        in_specs=in_smem(1) + [both] * 2 + [part] * len(parts),
+        out_specs=pl.BlockSpec((height, tile), lambda t: (0, t)),
+        compiler_params=grant(60),
+        cost_estimate=cost(2),
+        name="first_band",
+    )(line_ends(), firsts, outward, *parts)
 
 
 def line_scatter_apart(first, near, far, last, meanwhile, exchange, earlier):
-    in_last, in_far, in_near = slide(last, INWARD), slide(far, INWARD), slide(near, INWARD)
+    in_last, in_far = slide(last, INWARD), slide(far, INWARD)
+    near, in_far = lax.optimization_barrier((near, in_far))
+    in_near = slide(near, INWARD)
     in_last, first = lax.optimization_barrier((in_last, first))
     sum_last = last + in_last
     swap_last = slide(sum_last, MIDDLE)
@@ -757,12 +810,11 @@
     in_far, other = lax.optimization_barrier((in_far, other))
     sum_far = far + in_far
     swap_far = slide(sum_far, MIDDLE)
-    other, _ = lax.optimization_barrier((other, sum_far))
-    other = exchange(other)
-    swap_last, _ = lax.optimization_barrier((swap_last, earlier))
+    swap_last, *_ = lax.optimization_barrier((swap_last, earlier, sum_far))
     outer = first + swap_last
     outward = slide(outer, OUTWARD)
     other, in_near, _ = lax.optimization_barrier((other, in_near, outer))
+    other = exchange(other)
     total = run_near(line_ends(), first, 0, near, in_near)
     return total, swap_far, outward, other, outer
 
@@ -830,7 +882,6 @@
         return run_project(block, groups, layout, flip, afters, parts, before, arrays, weights)
 
     def share_sums(sums):
-        sums = sums.reshape(ctx_count, blocks, 2 * width)
         return lax.all_to_all(sums, "ctx", split_axis=0, concat_axis=0, tiled=True)
 
     if by_hand:
@@ -859,29 +910,28 @@
         split_off = ((0,), (1, 2, 3))
         firsts, rest_1, dcum_1, *_ = project(1, split_off, [rest_0], parts_1, before)
         inward_0, inward_1 = slide(rest_0, INWARD), slide(rest_1, INWARD)
-        far, last, dcum_2, *grads_2 = project(2, ((2,), (3,)), [rest_1], parts_2)
-        swapped_0, outward_0, outer_0 = line_scatter(
-            0, firsts, rest_0, inward_0, rest_0[1:] + inward_0[1:]
-        )
+        house = (unit, rows, inverse, heads, blocks)
+        sums = run_adjoint(ints, 0, (), (), [dcum_0, dcum_1], *house)
+        far, last, dcum_2, *grads_2 = project(2, ((2,), (3,)), [rest_1, sums], parts_2)
+        swapped_0 = slide(rest_0[1:] + inward_0[1:], MIDDLE)
         inward_1, *_ = lax.optimization_barrier((inward_1, swapped_0, dcum_2))
         sum_1 = rest_1[1:] + inward_1[1:]
-        swapped_1, outward_1, outer_1 = line_scatter(1, firsts, rest_1, inward_1, sum_1)
+        swapped_1 = slide(sum_1, MIDDLE)
         first, near = run_project_more(
             2, groups, ((0,), (1,)), flip, [sum_1], dq, *grads_2, weights
         )
+        outer = run_outer(firsts, swapped_0, swapped_1)
+        outward = slide(outer, OUTWARD)
 
         def meanwhile(after):
-            dcums = [dcum_0, dcum_1, dcum_2]
-            return run_adjoint(ints, (after, outer_0), dcums, unit, rows, inverse, heads, blocks)
+            return run_adjoint(ints, 2, (sums,), (after, outer), [dcum_2], *house)
 
         total_2, swapped_2, outward_2, got, outer_2 = line_scatter_apart(
-            first, near, far, last, meanwhile, share_sums, outer_1
+            first, near, far, last, meanwhile, share_sums, outer
         )
-        inward_0, inward_1, _ = lax.optimization_barrier((inward_0, inward_1, outer_2))
-        total_0 = run_near(line_ends(), firsts, 0, rest_0, inward_0)
-        total_1 = run_near(line_ends(), firsts, 1, rest_1, inward_1)
-        share = run_share(None, 0, 4, total_0, swapped_0, outward_0)
-        share = run_share(share, 1, 4, total_1, swapped_1, outward_1)
+        outward, _ = lax.optimization_barrier((outward, outer_2))
+        parts = (rest_0, inward_0, swapped_0, rest_1, inward_1, swapped_1)
+        share = run_first_band(2, firsts, outward, *parts)
         share = run_share(share, 1, 2, total_2, swapped_2, outward_2)
     else:
         spots = (owners * blocks + offsets).reshape(-1)
@@ -898,7 +948,8 @@
             done = lax.psum_scatter(term, "head", scatter_dimension=0, tiled=False)
             share = lax.dynamic_update_slice(share, done, (j * BLK, 0))
 
-        got = share_sums(run_adjoint(ints, (), dcums, unit, rows, inverse, heads, blocks))
+        sums = run_adjoint(ints, 0, (), (), dcums, unit, rows, inverse, heads, blocks)
+        got = share_sums(sums)
 
     house_grad = run_house(ints, got, unit, rows, house_dirs, heads, blocks)
     return (share, house_grad)

time: 206 us -> 201 us (0.976)
  starting transfers between devices: 55.3 us -> 51.1 us
  other arithmetic: 6.56 us -> 3.56 us
    pallas_call x1 -> x4, Pallas kernels: 7.26 us -> 15.8 us  [the longest x2 11.1 us: run_adjoint(): pl.pallas_call(functools.partial(adjoint_kernel, heads, blocks, first, le...]
    ppermute x12 -> x11, starting transfers between devices: 27 us -> 22.7 us  [slide(): return lax.ppermute(value, 'head', pairs)]
    ppermute x29, waiting for transfers between devices: 27.6 us -> 23.5 us  [hop(): return lax.ppermute(value, 'ctx', [(i, i ^ distance) for i in range(count)])]
    pallas_call x3 -> x1, Pallas kernels: 6.46 us -> 2.45 us  [run_near(): pl.pallas_call(near_kernel, grid=(1,), out_shape=jax.ShapeDtypeStruct((ro...]
    pallas_call x3 -> x1, Pallas kernels: 6.16 us -> 2.29 us  [run_share(): pl.pallas_call(share_kernel, grid=(width // tile,), out_shape=jax.ShapeDt...]
    unnamed x72 -> x70, local copies, waits for them, and re-layouts: 9.3 us -> 11.7 us
    all_to_all x1, waiting for transfers between devices: 0.61 us -> 3.01 us  [share_sums(): return lax.all_to_all(sums, 'ctx', split_axis=0, concat_axis=0, tiled=True)]
    ppermute x12 -> x11, waiting for transfers between devices: 5.28 us -> 6.53 us  [slide(): return lax.ppermute(value, 'head', pairs)]
  transfers between devices with their start and end apart: 42 -> 41, of which waited for: 10 -> 10; matrix products, arithmetic and copies ran while one was open for 5% -> 3% of each run, Pallas kernels for 39% -> 41%
where the time goes in v9:
time: 201 us; the launch traced here: 199 us
  Pallas kernels  97.9 us (49%)
  starting transfers between devices  51.1 us (25%)
  waiting for transfers between devices  33.1 us (16%)
  local copies, waits for them, and re-layouts  11.9 us (6%)
  other arithmetic  3.56 us (2%)
    pallas_call x3, Pallas kernels, run_project(): pl.pallas_call(functools.partial(project_kernel, heads, len(parts[0]), si...  32.9 us
    ppermute x29, starting transfers between devices, hop(): return lax.ppermute(value, 'ctx', [(i, i ^ distance) for i in range(count)])  25.1 us
    ppermute x29, waiting for transfers between devices, hop(): return lax.ppermute(value, 'ctx', [(i, i ^ distance) for i in range(count)])  23.5 us
    ppermute x11, starting transfers between devices, slide(): return lax.ppermute(value, 'head', pairs)  22.7 us
    pallas_call x1, Pallas kernels, run_attend(): pl.pallas_call(functools.partial(attend_kernel, heads, blocks, places, pi...  15.2 us
    unnamed x70, local copies, waits for them, and re-layouts  11.7 us
    pallas_call x2, Pallas kernels, run_adjoint(): pl.pallas_call(functools.partial(adjoint_kernel, heads, blocks, first, le...  11.1 us
    pallas_call x3, Pallas kernels, run_merge(): pl.pallas_call(merge_kernel, grid=(size, cut), out_shape=[jax.ShapeDtypeS...  8.81 us
  transfers between devices with their start and end apart: 41, of which 10 were waited for; matrix products, arithmetic and copies ran while one was open for 3% of the time, Pallas kernels for 41%

profile of v9, /device:TPU:0, one launch (start us, length us, event | category | flops | bytes accessed | tf_op | source)
XLA Modules:
  0.0 198.6 jit_solution(13747389696844420756)
XLA Ops:
  0.6 3.0 %collective-permute-start.1 = (bf16[512,512]{1,0:T(8,128)(2,1)}, bf16[512,512]{1,0:T(8,128)(2,1)S(1)}, u32[]{:S(2)}, u32[]{:S(2)}) collective-permute-start(bf16[512,512]{1,0:T(8,128)(2,1)} %refs_20_.2), channel_id=1, source_target_pairs={{0,8},{4,12},{8,0},{12,4},{16,24},{20,28},{24,16},{28,20},{1,9},{5... | collective-permute-start | bytes 1572872 | tf_op jit(solution)/shard_map/ppermute | solution.py:687
  8.2 8.4 %collective-permute-done.1.refs_6_ = bf16[512,512]{1,0:T(8,128)(2,1)S(1)} collective-permute-done((bf16[512,512]{1,0:T(8,128)(2,1)}, bf16[512,512]{1,0:T(8,128)(2,1)S(1)}, u32[]{:S(2)}, u32[]{:S(2)}) %collective-permute-start.1) | collective-permute-done | bytes 524320 | tf_op jit(solution)/shard_map/ppermute | solution.py:687
  22.3 5.1 %collective-permute-done.refs_5_ = bf16[512,512]{1,0:T(8,128)(2,1)S(1)} collective-permute-done((bf16[512,512]{1,0:T(8,128)(2,1)}, bf16[512,512]{1,0:T(8,128)(2,1)S(1)}, u32[]{:S(2)}, u32[]{:S(2)}) %collective-permute-start) | collective-permute-done | bytes 524320 | tf_op jit(solution)/shard_map/ppermute | solution.py:687
  31.3 4.5 %house_chain.1 = (f32[32,512]{1,0:T(8,128)S(1)}, f32[32,512]{1,0:T(8,128)S(1)}, f32[4,32,32]{2,1,0:T(8,128)S(1)}, bf16[4,128,96]{2,1,0:T(8,128)(2,1)S(1)}, bf16[4,96,128]{2,1,0:T(8,128)(2,1)S(1)}) custom-call(s32[17]{0:T(128)S(1)} %pad_add_fusion.ints_ref.refs_0_.base_ref, f32[8,512]{1,0:T(8,128)S(1)} %pad_maximum_fusion.refs_0_, ...), custom_call_target="tpu_custom_call" | custom-call | flops 6899999744 | bytes 1048576 | tf_op jit(solution)/shard_map/house_chain/pallas_call | solution.py:119
  38.6 5.5 %rotate.1 = (bf16[512,512]{1,0:T(8,128)(2,1)S(1)}, bf16[512,512]{1,0:T(8,128)(2,1)S(1)}, bf16[4,4,128,128]{3,2,1,0:T(8,128)(2,1)S(1)}, bf16[8,4,256,128]{3,2,1,0:T(8,128)(2,1)S(1)}) custom-call(s32[17]{0:T(128)S(1)} %pad_add_fusion.ints_ref.refs_0_.base_ref, bf16[4,128,96]{2,1,0:T(8,128)(2,1)S(1)} %get-tuple-element.77.wide_ref, ...), custom_call_target="tpu_custom_call" | custom-call | flops 10350000128 | bytes 1048576 | tf_op jit(solution)/shard_map/rotate/pallas_call | solution.py:187
  46.9 15.2 %attend.1 = (bf16[512,512]{1,0:T(8,128)(2,1)}, f32[4,4,128,128]{3,2,1,0:T(8,128)}, f32[512,512]{1,0:T(8,128)}, f32[512,512]{1,0:T(8,128)}, bf16[1,4,128,1024]{3,...) custom-call(s32[17]{0:T(128)S(1)} %pad_add_fusion.ints_ref.refs_0_.b, ...), custom_call_target="tpu_custom_call" | custom-call | flops 17250000896 | bytes 1048576 | tf_op jit(solution)/shard_map/attend/pallas_call | solution.py:376
  62.3 2.8 %collective-permute-done.18.got_ref = bf16[1,4,128,1024]{3,2,1,0:T(8,128)(2,1)S(1)} collective-permute-done((bf16[1,4,128,1024]{3,2,1,0:T(8,128)(2,1)}, bf16[1,4,128,1024]{3,2,1,0:T(8,128)(2,1)S(1)}, u32[]{:S(2)}, u32[]{:S(2)}) %collective-permute-start.18) | collective-permute-done | bytes 1048608 | tf_op jit(solution)/shard_map/ppermute | solution.py:687
  69.4 2.7 %collective-permute-start.22 = (bf16[1,128,1024]{2,1,0:T(8,128)(2,1)}, bf16[1,128,1024]{2,1,0:T(8,128)(2,1)}, u32[]{:S(2)}, u32[]{:S(2)}) collective-permute-start(bf16[1,128,1024]{2,1,0:T(8,128)(2,1)} %get-tuple-element.95), channel_id=1, source_target_pairs={{0,24},{4,28},{8,16},{12,20},{16,8},{20,12},{24,0},{28,4},{1,25},{... | collective-permute-start | bytes 786440 | tf_op jit(solution)/shard_map/ppermute | solution.py:687
  76.1 4.2 %merge.5 = (bf16[2,128,1024]{2,1,0:T(8,128)(2,1)}, bf16[2,128,1024]{2,1,0:T(8,128)(2,1)}, bf16[2,128,1024]{2,1,0:T(8,128)(2,1)}) custom-call(bf16[3,4,128,1024]{3,2,1,0:T(8,128)(2,1)} %get-tuple-element.86.own_ref, bf16[3,4,128,1024]{3,2,1,0:T(8,128)(2,1)} %copy-done.9, bf16[1,128,1024]{2,1,0:T(8,128)(2,1)} %get-tuple-element.105.refs_0_), custom_call_target="tpu_custom_call" | custom-call | flops 2300000000 | bytes 1048576 | tf_op jit(solution)/shard_map/merge/pallas_call | solution.py:405
  80.3 3.0 %collective-permute-done.21.refs_4_ = bf16[1,128,1024]{2,1,0:T(8,128)(2,1)S(1)} collective-permute-done((bf16[1,128,1024]{2,1,0:T(8,128)(2,1)}, bf16[1,128,1024]{2,1,0:T(8,128)(2,1)S(1)}, u32[]{:S(2)}, u32[]{:S(2)}) %collective-permute-start.21) | collective-permute-done | bytes 262176 | tf_op jit(solution)/shard_map/ppermute | solution.py:687
  86.8 10.5 %project.3 = (bf16[3,128,1024]{2,1,0:T(8,128)(2,1)}, f32[1,4,128,128]{3,2,1,0:T(8,128)}, bf16[128,512]{1,0:T(8,128)(2,1)}, bf16[128,512]{1,0:T(8,128)(2,1)}) custom-call(s32[1]{0:T(128)} %bitcast.1.flip_ref, bf16[2,128,1024]{2,1,0:T(8,128)(2,1)} %get-tuple-element.117.refs_0_, bf16[4,128,1024]{2,1,0:T(8,128)(2,1)} %bitcast.14, ...), custom_call_target="tpu_custom_call" | custom-call | flops 10350000128 | bytes 1048576 | tf_op jit(solution)/shard_map/project/pallas_call | solution.py:552
  97.3 3.8 %collective-permute-start.26 = (bf16[3,128,1024]{2,1,0:T(8,128)(2,1)}, bf16[3,128,1024]{2,1,0:T(8,128)(2,1)S(1)}, u32[]{:S(2)}, u32[]{:S(2)}) collective-permute-start(bf16[3,128,1024]{2,1,0:T(8,128)(2,1)} %get-tuple-element.100.refs_0_), channel_id=1, source_target_pairs={{0,1},{3,2},{4,5},{7,6},{8,9},{11,10},{12,13},{15,14},{16,17},{19,... | collective-permute-start | bytes 2359304 | tf_op jit(solution)/shard_map/ppermute | solution.py:691
  105.5 13.1 %project.4 = (bf16[1,256,1024]{2,1,0:T(8,128)(2,1)}, bf16[3,128,1024]{2,1,0:T(8,128)(2,1)}, f32[1,4,128,128]{3,2,1,0:T(8,128)}, bf16[128,512]{1,0:T(8,128)(2,1)}, bf16[128,512]{1,0:T(8,128)(2,1)}) custom-call(s32[1]{0:T(128)} %bitcast.1.flip_ref, bf16[3,128,1024]{2,1,0:T(8,128)(2,1)} %get-tuple-element.100.refs_0_, bf16[12,128,1024]{2,1,0:T(8,128)(2,1)} %bitcast.7, ...), custom_call_target="tpu_custom_call" | custom-call | flops 13799999488 | bytes 1048576 | tf_op jit(solution)/shard_map/project/pallas_call | solution.py:552
  120.8 5.6 %adjoint.2.refs_1_.refs_2_ = f32[8,4,1024]{2,1,0:T(4,128)} custom-call(s32[17]{0:T(128)} %copy-done.5, f32[1,4,128,128]{3,2,1,0:T(8,128)} %get-tuple-element.112.refs_0_, f32[1,4,128,128]{3,2,1,0:T(8,128)} %get-tuple-element.113.refs_1_, f32[32,512]{1,0:T(8,128)} %copy-done.2, f32[32,512]{1,0:T(8,128)} %copy-done.3, f32[4,32,32]{2,1,0:T(8,128)} %copy-done.4), custom_call_target="tpu_custom_call" | custom-call | flops 230000000 | bytes 1048576 | tf_op jit(solution)/shard_map/adjoint/pallas_call | solution.py:643
  129.8 9.3 %project.5 = (bf16[1,256,1024]{2,1,0:T(8,128)(2,1)}, bf16[1,256,1024]{2,1,0:T(8,128)(2,1)}, f32[2,4,128,128]{3,2,1,0:T(8,128)}, bf16[256,512]{1,0:T(8,128)(2,1)}, bf16[256,512]{1,0:T(8,128)(2,1)}) custom-call(s32[1]{0:T(128)} %bitcast.1.flip_ref, bf16[3,128,1024]{2,1,0:T(8,128)(2,1)} %get-tuple-element.111.refs_0_.refs_3_, ...), custom_call_target="tpu_custom_call" | custom-call | flops 6899999744 | bytes 1048576 | tf_op jit(solution)/shard_map/project/pallas_call | solution.py:552
  139.1 3.2 %collective-permute-start.34 = (bf16[1,256,1024]{2,1,0:T(8,128)(2,1)}, bf16[1,256,1024]{2,1,0:T(8,128)(2,1)}, u32[]{:S(2)}, u32[]{:S(2)}) collective-permute-start(bf16[1,256,1024]{2,1,0:T(8,128)(2,1)} %get-tuple-element.122), channel_id=1, source_target_pairs={{0,1},{3,2},{4,5},{7,6},{8,9},{11,10},{12,13},{15,14},{16,17},{19,... | collective-permute-start | bytes 1572872 | tf_op jit(solution)/shard_map/ppermute | solution.py:691
  145.5 7.9 %project_more.1 = (bf16[1,256,1024]{2,1,0:T(8,128)(2,1)}, bf16[1,256,1024]{2,1,0:T(8,128)(2,1)}) custom-call(s32[1]{0:T(128)} %bitcast.1.flip_ref, bf16[2,128,1024]{2,1,0:T(8,128)(2,1)} %copy-done.18, bf16[512,512]{1,0:T(8,128)(2,1)} %get-tuple-element.98.refs_8_.refs_6_.refs_11_.refs_14_.refs_1_, bf16[256,512]{1,0:T(8,128)(2,1)} %get-tuple-element.123.refs_2_, ...), custom_call_target="tpu_custom_call" | custom-call | flops 6899999744 | bytes 1048576 | tf_op jit(solution)/shard_map/project_more/pallas_call | solution.py:511
  156.1 5.8 %collective-permute-done.36 = bf16[1,256,1024]{2,1,0:T(8,128)(2,1)S(1)} collective-permute-done((bf16[1,256,1024]{2,1,0:T(8,128)(2,1)}, bf16[1,256,1024]{2,1,0:T(8,128)(2,1)S(1)}, u32[]{:S(2)}, u32[]{:S(2)}) %collective-permute-start.36) | collective-permute-done | bytes 524320 | tf_op jit(solution)/shard_map/ppermute | solution.py:691
  161.9 5.1 %collective-permute-start.37 = (bf16[1,256,1024]{2,1,0:T(8,128)(2,1)}, bf16[1,256,1024]{2,1,0:T(8,128)(2,1)}, u32[]{:S(2)}, u32[]{:S(2)}) collective-permute-start(bf16[1,256,1024]{2,1,0:T(8,128)(2,1)} %get-tuple-element.134.near_ref), channel_id=1, source_target_pairs={{0,1},{3,2},{4,5},{7,6},{8,9},{11,10},{12,13},{15,14},{16,17},{19,... | collective-permute-start | bytes 1572872 | tf_op jit(solution)/shard_map/ppermute | solution.py:691
  171.4 5.6 %adjoint.3 = f32[8,4,1024]{2,1,0:T(4,128)} custom-call(s32[17]{0:T(128)} %copy-done.5, bf16[1,256,1024]{2,1,0:T(8,128)(2,1)} %copy-done.14, bf16[1,256,1024]{2,1,0:T(8,128)(2,1)} %outer.1.refs_1_, f32[8,4,1024]{2,1,0:T(4,128)} %adjoint.2.refs_1_.refs_2_, f32[2,4,128,128]{3,2,1,0:T(8,128)} %get-tuple-element.120.refs_3_, f32[32,512]{1,0:T(8,128)} %copy-done.2, ...), custom_call_target="tpu_custom_call" | custom-call | flops 230000000 | bytes 1048576 | tf_op jit(solution)/shard_map/adjoint/pallas_call | solution.py:643
  180.1 3.4 %all-to-all-start = ((f32[8,4,1024]{2,1,0:T(4,128)}), f32[8,4,1024]{2,1,0:T(4,128)S(1)}, u32[]{:S(2)}, u32[]{:S(2)}) async-start(f32[8,4,1024]{2,1,0:T(4,128)} %adjoint.3), calls=%async_computation | async-start | bytes 262144 | tf_op jit(solution)/shard_map/all_to_all | solution.py:885
  186.0 3.0 %all-to-all-done.got_ref = f32[8,4,1024]{2,1,0:T(4,128)S(1)} async-done(((f32[8,4,1024]{2,1,0:T(4,128)}), f32[8,4,1024]{2,1,0:T(4,128)S(1)}, u32[]{:S(2)}, u32[]{:S(2)}) %all-to-all-start) | async-done | bytes 131104 | tf_op jit(solution)/shard_map/all_to_all | solution.py:885
  189.6 2.6 %house_grad.1 = f32[4,512]{1,0:T(4,128)} custom-call(s32[17]{0:T(128)} %copy-done.5, f32[8,4,1024]{2,1,0:T(4,128)} %copy-done.21, f32[32,512]{1,0:T(8,128)} %copy-done.2, f32[32,512]{1,0:T(8,128)} %copy-done.3, f32[4,512]{1,0:T(4,128)} %house_ref.1), custom_call_target="tpu_custom_call" | custom-call | flops 2300000000 | bytes 1048576 | tf_op jit(solution)/shard_map/house_grad/pallas_call | solution.py:675
  193.0 2.6 %first_band.1.refs_0_ = bf16[512,1024]{1,0:T(8,128)(2,1)} custom-call(s32[1]{0:T(128)} %bitcast.ends_ref, bf16[1,256,1024]{2,1,0:T(8,128)(2,1)} %get-tuple-element.110.first_ref, bf16[1,256,1024]{2,1,0:T(8,128)(2,1)} %copy-done.24, bf16[3,128,1024]{2,1,0:T(8,128)(2,1)} %get-tuple-element.100.refs_0_, bf16[3,128,1024]{2,1,0:T(8,128)(2,1)} %copy-done.20, ...), custom_call_target="tpu_custom_call" | custom-call | flops 2300000000 | bytes 1048576 | tf_op jit(solution)/shard_map/first_band/pallas_call | solution.py:790
  (155 shorter events, 62.1 us)
Async XLA Ops:
  0.6 16.0 %collective-permute-start.1 = (bf16[512,512]{1,0:T(8,128)(2,1)}, bf16[512,512]{1,0:T(8,128)(2,1)S(1)}, u32[]{:S(2)}, u32[]{:S(2)}) collective-permute-start(bf16[512,512]{1,0:T(8,128)(2,1)} %refs_20_.2), channel_id=1, source_target_pairs={{0,8},{4,12},{8,0},{12,4},{16,24},{20,28},{24,16},{28,20},{1,9},{5... | collective-permute-start | bytes 1572872 | tf_op jit(solution)/shard_map/ppermute | solution.py:687
  3.6 15.1 %collective-permute-start.2 = (bf16[512,512]{1,0:T(8,128)(2,1)}, bf16[512,512]{1,0:T(8,128)(2,1)S(1)}, u32[]{:S(2)}, u32[]{:S(2)}) collective-permute-start(bf16[512,512]{1,0:T(8,128)(2,1)} %refs_15_.3), channel_id=1, source_target_pairs={{0,16},{4,20},{8,24},{12,28},{16,0},{20,4},{24,8},{28,12},{1,17},{... | collective-permute-start | bytes 1572872 | tf_op jit(solution)/shard_map/ppermute | solution.py:687
  5.2 22.2 %collective-permute-start = (bf16[512,512]{1,0:T(8,128)(2,1)}, bf16[512,512]{1,0:T(8,128)(2,1)S(1)}, u32[]{:S(2)}, u32[]{:S(2)}) collective-permute-start(bf16[512,512]{1,0:T(8,128)(2,1)} %refs_15_.3), channel_id=1, source_target_pairs={{0,8},{4,12},{8,0},{12,4},{16,24},{20,28},{24,16},{28,20},{1,9},{5... | collective-permute-start | bytes 1572872 | tf_op jit(solution)/shard_map/ppermute | solution.py:687
  5.7 23.4 %collective-permute-start.3 = (bf16[512,512]{1,0:T(8,128)(2,1)}, bf16[512,512]{1,0:T(8,128)(2,1)S(1)}, u32[]{:S(2)}, u32[]{:S(2)}) collective-permute-start(bf16[512,512]{1,0:T(8,128)(2,1)} %refs_20_.2), channel_id=1, source_target_pairs={{0,16},{4,20},{8,24},{12,28},{16,0},{20,4},{24,8},{28,12},{1,17},{... | collective-permute-start | bytes 1572872 | tf_op jit(solution)/shard_map/ppermute | solution.py:687
  27.4 16.8 %collective-permute-start.14 = (bf16[512,512]{1,0:T(8,128)(2,1)S(1)}, bf16[512,512]{1,0:T(8,128)(2,1)S(1)}, u32[]{:S(2)}, u32[]{:S(2)}) collective-permute-start(bf16[512,512]{1,0:T(8,128)(2,1)S(1)} %collective-permute-done.2.refs_9_), channel_id=1, source_target_pairs={{0,8},{4,12},{8,0},{12,4},{16,24},{20,28},{24,16},{28,20},{1,9},{5... | collective-permute-start | bytes 1572872 | tf_op jit(solution)/shard_map/ppermute | solution.py:687
  29.1 15.1 %collective-permute-start.15 = (bf16[512,512]{1,0:T(8,128)(2,1)S(1)}, bf16[512,512]{1,0:T(8,128)(2,1)S(1)}, u32[]{:S(2)}, u32[]{:S(2)}) collective-permute-start(bf16[512,512]{1,0:T(8,128)(2,1)S(1)} %collective-permute-done.1.refs_6_), channel_id=1, source_target_pairs={{0,16},{4,20},{8,24},{12,28},{16,0},{20,4},{24,8},{28,12},{1,17},{... | collective-permute-start | bytes 1572872 | tf_op jit(solution)/shard_map/ppermute | solution.py:687
  69.1 14.1 %collective-permute-start.21 = (bf16[1,128,1024]{2,1,0:T(8,128)(2,1)}, bf16[1,128,1024]{2,1,0:T(8,128)(2,1)S(1)}, u32[]{:S(2)}, u32[]{:S(2)}) collective-permute-start(bf16[1,128,1024]{2,1,0:T(8,128)(2,1)} %get-tuple-element.94), channel_id=1, source_target_pairs={{0,16},{4,20},{8,24},{12,28},{16,0},{20,4},{24,8},{28,12},{1,17},{... | collective-permute-start | bytes 786440 | tf_op jit(solution)/shard_map/ppermute | solution.py:687
  83.2 17.8 %collective-permute-start.23 = (bf16[1,128,1024]{2,1,0:T(8,128)(2,1)S(1)}, bf16[1,128,1024]{2,1,0:T(8,128)(2,1)S(1)}, u32[]{:S(2)}, u32[]{:S(2)}) collective-permute-start(bf16[1,128,1024]{2,1,0:T(8,128)(2,1)S(1)} %copy-done.32), channel_id=1, source_target_pairs={{0,8},{4,12},{8,0},{12,4},{16,24},{20,28},{24,16},{28,20},{1,9},{5... | collective-permute-start | bytes 786440 | tf_op jit(solution)/shard_map/ppermute | solution.py:687
  84.8 16.2 %collective-permute-start.24 = (bf16[1,128,1024]{2,1,0:T(8,128)(2,1)S(1)}, bf16[1,128,1024]{2,1,0:T(8,128)(2,1)S(1)}, u32[]{:S(2)}, u32[]{:S(2)}) collective-permute-start(bf16[1,128,1024]{2,1,0:T(8,128)(2,1)S(1)} %copy-done.30), channel_id=1, source_target_pairs={{0,16},{4,20},{8,24},{12,28},{16,0},{20,4},{24,8},{28,12},{1,17},{... | collective-permute-start | bytes 786440 | tf_op jit(solution)/shard_map/ppermute | solution.py:687
  85.3 15.8 %collective-permute-start.25 = (bf16[1,128,1024]{2,1,0:T(8,128)(2,1)S(1)}, bf16[1,128,1024]{2,1,0:T(8,128)(2,1)S(1)}, u32[]{:S(2)}, u32[]{:S(2)}) collective-permute-start(bf16[1,128,1024]{2,1,0:T(8,128)(2,1)S(1)} %copy-done.27), channel_id=1, source_target_pairs={{0,24},{4,28},{8,16},{12,20},{16,8},{20,12},{24,0},{28,4},{1,25},{... | collective-permute-start | bytes 786440 | tf_op jit(solution)/shard_map/ppermute | solution.py:687
  97.3 29.1 %collective-permute-start.26 = (bf16[3,128,1024]{2,1,0:T(8,128)(2,1)}, bf16[3,128,1024]{2,1,0:T(8,128)(2,1)S(1)}, u32[]{:S(2)}, u32[]{:S(2)}) collective-permute-start(bf16[3,128,1024]{2,1,0:T(8,128)(2,1)} %get-tuple-element.100.refs_0_), channel_id=1, source_target_pairs={{0,1},{3,2},{4,5},{7,6},{8,9},{11,10},{12,13},{15,14},{16,17},{19,... | collective-permute-start | bytes 2359304 | tf_op jit(solution)/shard_map/ppermute | solution.py:691
  101.8 26.2 %collective-permute-start.29 = (bf16[2,128,1024]{2,1,0:T(8,128)(2,1)}, bf16[2,128,1024]{2,1,0:T(8,128)(2,1)S(1)}, u32[]{:S(2)}, u32[]{:S(2)}) collective-permute-start(bf16[2,128,1024]{2,1,0:T(8,128)(2,1)} %get-tuple-element.117.refs_0_), channel_id=1, source_target_pairs={{0,8},{4,12},{8,0},{12,4},{16,24},{20,28},{24,16},{28,20},{1,9},{5... | collective-permute-start | bytes 1572872 | tf_op jit(solution)/shard_map/ppermute | solution.py:687
  103.3 24.7 %collective-permute-start.30 = (bf16[2,128,1024]{2,1,0:T(8,128)(2,1)}, bf16[2,128,1024]{2,1,0:T(8,128)(2,1)S(1)}, u32[]{:S(2)}, u32[]{:S(2)}) collective-permute-start(bf16[2,128,1024]{2,1,0:T(8,128)(2,1)} %get-tuple-element.118), channel_id=1, source_target_pairs={{0,16},{4,20},{8,24},{12,28},{16,0},{20,4},{24,8},{28,12},{1,17},{... | collective-permute-start | bytes 1572872 | tf_op jit(solution)/shard_map/ppermute | solution.py:687
  103.8 24.2 %collective-permute-start.31 = (bf16[2,128,1024]{2,1,0:T(8,128)(2,1)}, bf16[2,128,1024]{2,1,0:T(8,128)(2,1)S(1)}, u32[]{:S(2)}, u32[]{:S(2)}) collective-permute-start(bf16[2,128,1024]{2,1,0:T(8,128)(2,1)} %get-tuple-element.119), channel_id=1, source_target_pairs={{0,24},{4,28},{8,16},{12,20},{16,8},{20,12},{24,0},{28,4},{1,25},{... | collective-permute-start | bytes 1572872 | tf_op jit(solution)/shard_map/ppermute | solution.py:687
  118.6 25.0 %collective-permute-start.28 = (bf16[3,128,1024]{2,1,0:T(8,128)(2,1)}, bf16[3,128,1024]{2,1,0:T(8,128)(2,1)}, u32[]{:S(2)}, u32[]{:S(2)}) collective-permute-start(bf16[3,128,1024]{2,1,0:T(8,128)(2,1)} %get-tuple-element.111.refs_0_.refs_3_), channel_id=1, source_target_pairs={{0,1},{3,2},{4,5},{7,6},{8,9},{11,10},{12,13},{15,14},{16,17},{19,... | collective-permute-start | bytes 2359304 | tf_op jit(solution)/shard_map/ppermute | solution.py:691
  126.4 17.2 %collective-permute-start.27 = (bf16[2,128,1024]{2,1,0:T(8,128)(2,1)S(1)}, bf16[2,128,1024]{2,1,0:T(8,128)(2,1)}, u32[]{:S(2)}, u32[]{:S(2)}) collective-permute-start(bf16[2,128,1024]{2,1,0:T(8,128)(2,1)S(1)} %slice_add_fusion), channel_id=1, source_target_pairs={{1,2},{2,1},{5,6},{6,5},{9,10},{10,9},{13,14},{14,13},{17,18},{18,... | collective-permute-start | bytes 1572872 | tf_op jit(solution)/shard_map/ppermute | solution.py:691
  139.1 15.1 %collective-permute-start.34 = (bf16[1,256,1024]{2,1,0:T(8,128)(2,1)}, bf16[1,256,1024]{2,1,0:T(8,128)(2,1)}, u32[]{:S(2)}, u32[]{:S(2)}) collective-permute-start(bf16[1,256,1024]{2,1,0:T(8,128)(2,1)} %get-tuple-element.122), channel_id=1, source_target_pairs={{0,1},{3,2},{4,5},{7,6},{8,9},{11,10},{12,13},{15,14},{16,17},{19,... | collective-permute-start | bytes 1572872 | tf_op jit(solution)/shard_map/ppermute | solution.py:691
  142.3 19.6 %collective-permute-start.36 = (bf16[1,256,1024]{2,1,0:T(8,128)(2,1)}, bf16[1,256,1024]{2,1,0:T(8,128)(2,1)S(1)}, u32[]{:S(2)}, u32[]{:S(2)}) collective-permute-start(bf16[1,256,1024]{2,1,0:T(8,128)(2,1)} %get-tuple-element.128), channel_id=1, source_target_pairs={{0,1},{3,2},{4,5},{7,6},{8,9},{11,10},{12,13},{15,14},{16,17},{19,... | collective-permute-start | bytes 1572872 | tf_op jit(solution)/shard_map/ppermute | solution.py:691
  144.8 22.2 %collective-permute-start.32 = (bf16[2,128,1024]{2,1,0:T(8,128)(2,1)S(1)}, bf16[2,128,1024]{2,1,0:T(8,128)(2,1)S(1)}, u32[]{:S(2)}, u32[]{:S(2)}) collective-permute-start(bf16[2,128,1024]{2,1,0:T(8,128)(2,1)S(1)} %slice_add_fusion.1.refs_0_), channel_id=1, source_target_pairs={{1,2},{2,1},{5,6},{6,5},{9,10},{10,9},{13,14},{14,13},{17,18},{18,... | collective-permute-start | bytes 1572872 | tf_op jit(solution)/shard_map/ppermute | solution.py:691
  155.4 23.2 %collective-permute-start.35 = (bf16[1,256,1024]{2,1,0:T(8,128)(2,1)S(1)}, bf16[1,256,1024]{2,1,0:T(8,128)(2,1)S(1)}, u32[]{:S(2)}, u32[]{:S(2)}) collective-permute-start(bf16[1,256,1024]{2,1,0:T(8,128)(2,1)S(1)} %add.17.refs_0_), channel_id=1, source_target_pairs={{1,2},{2,1},{5,6},{6,5},{9,10},{10,9},{13,14},{14,13},{17,18},{18,... | collective-permute-start | bytes 1572872 | tf_op jit(solution)/shard_map/ppermute | solution.py:691
  161.9 18.2 %collective-permute-start.37 = (bf16[1,256,1024]{2,1,0:T(8,128)(2,1)}, bf16[1,256,1024]{2,1,0:T(8,128)(2,1)}, u32[]{:S(2)}, u32[]{:S(2)}) collective-permute-start(bf16[1,256,1024]{2,1,0:T(8,128)(2,1)} %get-tuple-element.134.near_ref), channel_id=1, source_target_pairs={{0,1},{3,2},{4,5},{7,6},{8,9},{11,10},{12,13},{15,14},{16,17},{19,... | collective-permute-start | bytes 1572872 | tf_op jit(solution)/shard_map/ppermute | solution.py:691
  170.0 22.2 %collective-permute-start.33 = (bf16[1,256,1024]{2,1,0:T(8,128)(2,1)}, bf16[1,256,1024]{2,1,0:T(8,128)(2,1)S(1)}, u32[]{:S(2)}, u32[]{:S(2)}) collective-permute-start(bf16[1,256,1024]{2,1,0:T(8,128)(2,1)} %outer.1.refs_1_), channel_id=1, source_target_pairs={{1,0},{2,3},{5,4},{6,7},{9,8},{10,11},{13,12},{14,15},{17,16},{18,... | collective-permute-start | bytes 1572872 | tf_op jit(solution)/shard_map/ppermute | solution.py:691
  177.2 18.4 %collective-permute-start.38 = (bf16[1,256,1024]{2,1,0:T(8,128)(2,1)S(1)}, bf16[1,256,1024]{2,1,0:T(8,128)(2,1)}, u32[]{:S(2)}, u32[]{:S(2)}) collective-permute-start(bf16[1,256,1024]{2,1,0:T(8,128)(2,1)S(1)} %add.18), channel_id=1, source_target_pairs={{1,2},{2,1},{5,6},{6,5},{9,10},{10,9},{13,14},{14,13},{17,18},{18,... | collective-permute-start | bytes 1572872 | tf_op jit(solution)/shard_map/ppermute | solution.py:691
  178.8 16.7 %collective-permute-start.39 = (bf16[1,256,1024]{2,1,0:T(8,128)(2,1)S(1)}, bf16[1,256,1024]{2,1,0:T(8,128)(2,1)S(1)}, u32[]{:S(2)}, u32[]{:S(2)}) collective-permute-start(bf16[1,256,1024]{2,1,0:T(8,128)(2,1)S(1)} %add.19), channel_id=1, source_target_pairs={{1,0},{2,3},{5,4},{6,7},{9,8},{10,11},{13,12},{14,15},{17,16},{18,... | collective-permute-start | bytes 1572872 | tf_op jit(solution)/shard_map/ppermute | solution.py:691
  (51 other events, 361.9 us)

commit v10 on v9

--- a/solution.py
+++ b/solution.py
@@ -596,35 +596,38 @@
     )
 
 
-def adjoint_kernel(heads, blocks, first, carried, afters, ints_ref, *refs):
+def adjoint_kernel(heads, blocks, afters, ints_ref, *refs):
     refs = refs[afters:]
-    carry_refs, refs = refs[:carried], refs[carried:]
     dcums = [ref.at[j] for ref in refs[:-4] for j in range(ref.shape[0])]
     unit_ref, rows_ref, inv_ref, out_ref = refs[-4:]
     count, width = unit_ref.shape
     stacked = (len(dcums) * count, count)
     eye = (iota((count, count), 0) == iota((count, count), 1)).astype(F32)
-    base = ints_ref[0] * blocks + first
+    base = ints_ref[0] * blocks
     level, col = iota(stacked, 0), iota(stacked, 1)
     row = level % count
     mine = base + level // count
     alive = row[:, :1] <= mine[:, :1]
-    for h in range(heads):
-        units, rows, inverse = unit_ref[:, head(h)], rows_ref[:, head(h)], inv_ref[h]
-        inverse_t = nt_high(eye, inverse)
-        moved = jnp.concatenate([nt_high(rows, dcum[h]) for dcum in dcums], axis=0)
-        overlap = jnp.where(col <= mine, nt_high(moved, units), 0.0)
-        gamma = nn_high(overlap, inverse)
-        gamma = jnp.where((row < col) & (col <= mine), gamma, 0.0)
-        beta = jnp.concatenate([eye - inverse_t] * len(dcums), axis=0)
-        beta = jnp.where(col <= mine, beta, 0.0)
-        x_all = jnp.where(alive, moved - 2.0 * nn_high(gamma, units), 0.0)
-        turned = jnp.concatenate([units] * len(dcums), axis=0) - nn_high(beta, units)
-        turned = jnp.where(alive, turned, 0.0)
+    every = range(heads)
+    units = [unit_ref[:, head(h)] for h in every]
+    moved = [[nt_high(rows_ref[:, head(h)], dcum[h]) for dcum in dcums] for h in every]
+    moved = [jnp.concatenate(parts, axis=0) for parts in moved]
+    inverse_t = [nt_high(eye, inv_ref[h]) for h in every]
+    overlap = [jnp.where(col <= mine, nt_high(moved[h], units[h]), 0.0) for h in every]
+    beta = [jnp.concatenate([eye - inverse_t[h]] * len(dcums), axis=0) for h in every]
+    beta = [jnp.where(col <= mine, beta[h], 0.0) for h in every]
+    turned = [nn_high(beta[h], units[h]) for h in every]
+    gamma = [nn_high(overlap[h], inv_ref[h]) for h in every]
+    gamma = [jnp.where((row < col) & (col <= mine), gamma[h], 0.0) for h in every]
+    lifted = [nn_high(gamma[h], units[h]) for h in every]
+    for h in every:
+        x_all = jnp.where(alive, moved[h] - 2.0 * lifted[h], 0.0)
+        own = jnp.concatenate([units[h]] * len(dcums), axis=0)
+        own = jnp.where(alive, own - turned[h], 0.0)
         x_total, y_total = None, None
         for j, dcum in enumerate(dcums):
             here = slice(j * count, (j + 1) * count)
-            y_part = nn_high(turned[here], dcum[h])
+            y_part = nn_high(own[here], dcum[h])
             x_total = x_all[here] if j == 0 else x_total + x_all[here]
             y_total = y_part if j == 0 else y_total + y_part
         for total, lanes in (
@@ -632,25 +635,22 @@
             (y_total, slice(width + h * DH, width + (h + 1) * DH)),
         ):
             for c in range(count // blocks):
-                part = total[c * blocks : (c + 1) * blocks]
-                for ref in carry_refs:
-                    part = part + ref[c, :, lanes]
-                out_ref[c, :, lanes] = part
-
-
-def run_adjoint(ints, first, carry, afters, dcums, unit, rows, inverse, heads, blocks):
+                out_ref[c, :, lanes] = total[c * blocks : (c + 1) * blocks]
+
+
+def run_adjoint(ints, afters, dcums, unit, rows, inverse, heads, blocks):
     count, width = unit.shape
     return pl.pallas_call(
-        functools.partial(adjoint_kernel, heads, blocks, first, len(carry), len(afters)),
+        functools.partial(adjoint_kernel, heads, blocks, len(afters)),
         out_shape=jax.ShapeDtypeStruct((count // blocks, blocks, 2 * width), F32),
         in_specs=in_smem(1)
         + [pl.BlockSpec(memory_space=pl.ANY)] * len(afters)
-        + in_vmem(len(carry) + len(dcums) + 3),
+        + in_vmem(len(dcums) + 3),
         out_specs=pl.BlockSpec(memory_space=pltpu.VMEM),
         compiler_params=grant(60),
         cost_estimate=cost(0.2),
         name="adjoint",
-    )(ints, *afters, *carry, *dcums, unit, rows, inverse)
+    )(ints, *afters, *dcums, unit, rows, inverse)
 
 
 def house_kernel(heads, blocks, base_ref, got_ref, unit_ref, rows_ref, house_ref, out_ref):
@@ -801,13 +801,12 @@
 
 def line_scatter_apart(first, near, far, last, meanwhile, exchange, earlier):
     in_last, in_far = slide(last, INWARD), slide(far, INWARD)
-    near, in_far = lax.optimization_barrier((near, in_far))
-    in_near = slide(near, INWARD)
     in_last, first = lax.optimization_barrier((in_last, first))
     sum_last = last + in_last
     swap_last = slide(sum_last, MIDDLE)
     other = meanwhile(sum_last)
-    in_far, other = lax.optimization_barrier((in_far, other))
+    in_far, near, other = lax.optimization_barrier((in_far, near, other))
+    in_near = slide(near, INWARD)
     sum_far = far + in_far
     swap_far = slide(sum_far, MIDDLE)
     swap_last, *_ = lax.optimization_barrier((swap_last, earlier, sum_far))
@@ -911,8 +910,7 @@
         firsts, rest_1, dcum_1, *_ = project(1, split_off, [rest_0], parts_1, before)
         inward_0, inward_1 = slide(rest_0, INWARD), slide(rest_1, INWARD)
         house = (unit, rows, inverse, heads, blocks)
-        sums = run_adjoint(ints, 0, (), (), [dcum_0, dcum_1], *house)
-        far, last, dcum_2, *grads_2 = project(2, ((2,), (3,)), [rest_1, sums], parts_2)
+        far, last, dcum_2, *grads_2 = project(2, ((2,), (3,)), [rest_1], parts_2)
         swapped_0 = slide(rest_0[1:] + inward_0[1:], MIDDLE)
         inward_1, *_ = lax.optimization_barrier((inward_1, swapped_0, dcum_2))
         sum_1 = rest_1[1:] + inward_1[1:]
@@ -924,10 +922,10 @@
         outward = slide(outer, OUTWARD)
 
         def meanwhile(after):
-            return run_adjoint(ints, 2, (sums,), (after, outer), [dcum_2], *house)
+            return run_adjoint(ints, (after, outer), [dcum_0, dcum_1, dcum_2], *house)
 
         total_2, swapped_2, outward_2, got, outer_2 = line_scatter_apart(
-            first, near, far, last, meanwhile, share_sums, outer
+            first, near, far, last, meanwhile, share_sums, outward
         )
         outward, _ = lax.optimization_barrier((outward, outer_2))
         parts = (rest_0, inward_0, swapped_0, rest_1, inward_1, swapped_1)
@@ -948,7 +946,7 @@
             done = lax.psum_scatter(term, "head", scatter_dimension=0, tiled=False)
             share = lax.dynamic_update_slice(share, done, (j * BLK, 0))
 
-        sums = run_adjoint(ints, 0, (), (), dcums, unit, rows, inverse, heads, blocks)
+        sums = run_adjoint(ints, (), dcums, unit, rows, inverse, heads, blocks)
         got = share_sums(sums)
 
     house_grad = run_house(ints, got, unit, rows, house_dirs, heads, blocks)

time: 201 us -> 194 us (0.965)
  Pallas kernels: 97.9 us -> 92.2 us
    pallas_call x2 -> x1, Pallas kernels: 11.1 us -> 5.41 us  [run_adjoint(): pl.pallas_call(functools.partial(adjoint_kernel, heads, blocks, len(after...]
    ppermute x29, waiting for transfers between devices: 23.5 us -> 27.5 us  [hop(): return lax.ppermute(value, 'ctx', [(i, i ^ distance) for i in range(count)])]
    all_to_all x1, waiting for transfers between devices: 3.01 us -> 0.45 us  [share_sums(): return lax.all_to_all(sums, 'ctx', split_axis=0, concat_axis=0, tiled=True)]
  transfers between devices with their start and end apart: 41 -> 41, of which waited for: 10 -> 11; matrix products, arithmetic and copies ran while one was open for 3% -> 2% of each run, Pallas kernels for 41% -> 39%
where the time goes in v10:
time: 194 us; the launch traced here: 193 us
  Pallas kernels  92.2 us (48%)
  starting transfers between devices  52.3 us (27%)
  waiting for transfers between devices  33.2 us (17%)
  local copies, waits for them, and re-layouts  11.8 us (6%)
  other arithmetic  2.51 us (1%)
    pallas_call x3, Pallas kernels, run_project(): pl.pallas_call(functools.partial(project_kernel, heads, len(parts[0]), si...  32.8 us
    ppermute x29, waiting for transfers between devices, hop(): return lax.ppermute(value, 'ctx', [(i, i ^ distance) for i in range(count)])  27.5 us
    ppermute x29, starting transfers between devices, hop(): return lax.ppermute(value, 'ctx', [(i, i ^ distance) for i in range(count)])  25.1 us
    ppermute x11, starting transfers between devices, slide(): return lax.ppermute(value, 'head', pairs)  23.8 us
    pallas_call x1, Pallas kernels, run_attend(): pl.pallas_call(functools.partial(attend_kernel, heads, blocks, places, pi...  15.2 us
    unnamed x70, local copies, waits for them, and re-layouts  11.6 us
    pallas_call x3, Pallas kernels, run_merge(): pl.pallas_call(merge_kernel, grid=(size, cut), out_shape=[jax.ShapeDtypeS...  8.82 us
    pallas_call x1, Pallas kernels, run_project_more(): pl.pallas_call(functools.partial(project_more_kernel, groups, layout, len...  7.92 us
  transfers between devices with their start and end apart: 41, of which 11 were waited for; matrix products, arithmetic and copies ran while one was open for 2% of the time, Pallas kernels for 39%

profile of v10, /device:TPU:0, one launch (start us, length us, event | category | flops | bytes accessed | tf_op | source)
XLA Modules:
  0.0 193.1 jit_solution(2375700865156226639)
XLA Ops:
  0.6 3.0 %collective-permute-start.1 = (bf16[512,512]{1,0:T(8,128)(2,1)}, bf16[512,512]{1,0:T(8,128)(2,1)S(1)}, u32[]{:S(2)}, u32[]{:S(2)}) collective-permute-start(bf16[512,512]{1,0:T(8,128)(2,1)} %refs_20_.1), channel_id=1, source_target_pairs={{0,8},{4,12},{8,0},{12,4},{16,24},{20,28},{24,16},{28,20},{1,9},{5... | collective-permute-start | bytes 1572872 | tf_op jit(solution)/shard_map/ppermute | solution.py:687
  8.2 8.4 %collective-permute-done.1.refs_6_ = bf16[512,512]{1,0:T(8,128)(2,1)S(1)} collective-permute-done((bf16[512,512]{1,0:T(8,128)(2,1)}, bf16[512,512]{1,0:T(8,128)(2,1)S(1)}, u32[]{:S(2)}, u32[]{:S(2)}) %collective-permute-start.1) | collective-permute-done | bytes 524320 | tf_op jit(solution)/shard_map/ppermute | solution.py:687
  22.3 5.1 %collective-permute-done.refs_5_ = bf16[512,512]{1,0:T(8,128)(2,1)S(1)} collective-permute-done((bf16[512,512]{1,0:T(8,128)(2,1)}, bf16[512,512]{1,0:T(8,128)(2,1)S(1)}, u32[]{:S(2)}, u32[]{:S(2)}) %collective-permute-start) | collective-permute-done | bytes 524320 | tf_op jit(solution)/shard_map/ppermute | solution.py:687
  31.3 4.5 %house_chain.1 = (f32[32,512]{1,0:T(8,128)S(1)}, f32[32,512]{1,0:T(8,128)S(1)}, f32[4,32,32]{2,1,0:T(8,128)S(1)}, bf16[4,128,96]{2,1,0:T(8,128)(2,1)S(1)}, bf16[4,96,128]{2,1,0:T(8,128)(2,1)S(1)}) custom-call(s32[17]{0:T(128)S(1)} %pad_add_fusion.ints_ref.refs_0_.base_ref, f32[8,512]{1,0:T(8,128)S(1)} %pad_maximum_fusion.refs_0_, ...), custom_call_target="tpu_custom_call" | custom-call | flops 6899999744 | bytes 1048576 | tf_op jit(solution)/shard_map/house_chain/pallas_call | solution.py:119
  38.6 5.5 %rotate.1 = (bf16[512,512]{1,0:T(8,128)(2,1)S(1)}, bf16[512,512]{1,0:T(8,128)(2,1)S(1)}, bf16[4,4,128,128]{3,2,1,0:T(8,128)(2,1)S(1)}, bf16[8,4,256,128]{3,2,1,0:T(8,128)(2,1)S(1)}) custom-call(s32[17]{0:T(128)S(1)} %pad_add_fusion.ints_ref.refs_0_.base_ref, bf16[4,128,96]{2,1,0:T(8,128)(2,1)S(1)} %get-tuple-element.76.wide_ref, ...), custom_call_target="tpu_custom_call" | custom-call | flops 10350000128 | bytes 1048576 | tf_op jit(solution)/shard_map/rotate/pallas_call | solution.py:187
  46.9 15.2 %attend.1 = (bf16[512,512]{1,0:T(8,128)(2,1)}, f32[4,4,128,128]{3,2,1,0:T(8,128)}, f32[512,512]{1,0:T(8,128)}, f32[512,512]{1,0:T(8,128)}, bf16[1,4,128,1024]{3,...) custom-call(s32[17]{0:T(128)S(1)} %pad_add_fusion.ints_ref.refs_0_.b, ...), custom_call_target="tpu_custom_call" | custom-call | flops 17250000896 | bytes 1048576 | tf_op jit(solution)/shard_map/attend/pallas_call | solution.py:376
  62.3 2.8 %collective-permute-done.18.got_ref = bf16[1,4,128,1024]{3,2,1,0:T(8,128)(2,1)S(1)} collective-permute-done((bf16[1,4,128,1024]{3,2,1,0:T(8,128)(2,1)}, bf16[1,4,128,1024]{3,2,1,0:T(8,128)(2,1)S(1)}, u32[]{:S(2)}, u32[]{:S(2)}) %collective-permute-start.18) | collective-permute-done | bytes 1048608 | tf_op jit(solution)/shard_map/ppermute | solution.py:687
  66.2 2.3 %merge.3 = (bf16[1,128,1024]{2,1,0:T(8,128)(2,1)}, bf16[1,128,1024]{2,1,0:T(8,128)(2,1)}, bf16[1,128,1024]{2,1,0:T(8,128)(2,1)}) custom-call(bf16[1,4,128,1024]{3,2,1,0:T(8,128)(2,1)} %get-tuple-element.89.own_ref, bf16[1,4,128,1024]{3,2,1,0:T(8,128)(2,1)} %copy-done.22), custom_call_target="tpu_custom_call" | custom-call | flops 2300000000 | bytes 1048576 | tf_op jit(solution)/shard_map/merge/pallas_call | solution.py:405
  69.4 2.7 %collective-permute-start.22 = (bf16[1,128,1024]{2,1,0:T(8,128)(2,1)}, bf16[1,128,1024]{2,1,0:T(8,128)(2,1)}, u32[]{:S(2)}, u32[]{:S(2)}) collective-permute-start(bf16[1,128,1024]{2,1,0:T(8,128)(2,1)} %get-tuple-element.94), channel_id=1, source_target_pairs={{0,24},{4,28},{8,16},{12,20},{16,8},{20,12},{24,0},{28,4},{1,25},{... | collective-permute-start | bytes 786440 | tf_op jit(solution)/shard_map/ppermute | solution.py:687
  76.1 4.2 %merge.5 = (bf16[2,128,1024]{2,1,0:T(8,128)(2,1)}, bf16[2,128,1024]{2,1,0:T(8,128)(2,1)}, bf16[2,128,1024]{2,1,0:T(8,128)(2,1)}) custom-call(bf16[3,4,128,1024]{3,2,1,0:T(8,128)(2,1)} %get-tuple-element.85.own_ref, bf16[3,4,128,1024]{3,2,1,0:T(8,128)(2,1)} %copy-done.9, bf16[1,128,1024]{2,1,0:T(8,128)(2,1)} %get-tuple-element.104.refs_0_), custom_call_target="tpu_custom_call" | custom-call | flops 2300000000 | bytes 1048576 | tf_op jit(solution)/shard_map/merge/pallas_call | solution.py:405
  80.3 3.0 %collective-permute-done.21.refs_4_ = bf16[1,128,1024]{2,1,0:T(8,128)(2,1)S(1)} collective-permute-done((bf16[1,128,1024]{2,1,0:T(8,128)(2,1)}, bf16[1,128,1024]{2,1,0:T(8,128)(2,1)S(1)}, u32[]{:S(2)}, u32[]{:S(2)}) %collective-permute-start.21) | collective-permute-done | bytes 262176 | tf_op jit(solution)/shard_map/ppermute | solution.py:687
  86.8 10.5 %project.3 = (bf16[3,128,1024]{2,1,0:T(8,128)(2,1)}, f32[1,4,128,128]{3,2,1,0:T(8,128)}, bf16[128,512]{1,0:T(8,128)(2,1)}, bf16[128,512]{1,0:T(8,128)(2,1)}) custom-call(s32[1]{0:T(128)} %bitcast.1.flip_ref, bf16[2,128,1024]{2,1,0:T(8,128)(2,1)} %get-tuple-element.111.refs_0_, bf16[4,128,1024]{2,1,0:T(8,128)(2,1)} %bitcast.14, ...), custom_call_target="tpu_custom_call" | custom-call | flops 10350000128 | bytes 1048576 | tf_op jit(solution)/shard_map/project/pallas_call | solution.py:552
  97.3 3.7 %collective-permute-start.26 = (bf16[3,128,1024]{2,1,0:T(8,128)(2,1)}, bf16[3,128,1024]{2,1,0:T(8,128)(2,1)S(1)}, u32[]{:S(2)}, u32[]{:S(2)}) collective-permute-start(bf16[3,128,1024]{2,1,0:T(8,128)(2,1)} %get-tuple-element.99.refs_0_), channel_id=1, source_target_pairs={{0,1},{3,2},{4,5},{7,6},{8,9},{11,10},{12,13},{15,14},{16,17},{19,... | collective-permute-start | bytes 2359304 | tf_op jit(solution)/shard_map/ppermute | solution.py:691
  105.5 13.1 %project.4 = (bf16[1,256,1024]{2,1,0:T(8,128)(2,1)}, bf16[3,128,1024]{2,1,0:T(8,128)(2,1)}, f32[1,4,128,128]{3,2,1,0:T(8,128)}, bf16[128,512]{1,0:T(8,128)(2,1)}, bf16[128,512]{1,0:T(8,128)(2,1)}) custom-call(s32[1]{0:T(128)} %bitcast.1.flip_ref, bf16[3,128,1024]{2,1,0:T(8,128)(2,1)} %get-tuple-element.99.refs_0_, bf16[12,128,1024]{2,1,0:T(8,128)(2,1)} %bitcast.7, ...), custom_call_target="tpu_custom_call" | custom-call | flops 13799999488 | bytes 1048576 | tf_op jit(solution)/shard_map/project/pallas_call | solution.py:552
  122.4 4.0 %collective-permute-done.30.refs_4_.refs_9_ = bf16[2,128,1024]{2,1,0:T(8,128)(2,1)S(1)} collective-permute-done((bf16[2,128,1024]{2,1,0:T(8,128)(2,1)}, bf16[2,128,1024]{2,1,0:T(8,128)(2,1)S(1)}, u32[]{:S(2)}, u32[]{:S(2)}) %collective-permute-start.30) | collective-permute-done | bytes 524320 | tf_op jit(solution)/shard_map/ppermute | solution.py:687
  128.0 9.3 %project.5 = (bf16[1,256,1024]{2,1,0:T(8,128)(2,1)}, bf16[1,256,1024]{2,1,0:T(8,128)(2,1)}, f32[2,4,128,128]{3,2,1,0:T(8,128)}, bf16[256,512]{1,0:T(8,128)(2,1)}, bf16[256,512]{1,0:T(8,128)(2,1)}) custom-call(s32[1]{0:T(128)} %bitcast.1.flip_ref, bf16[3,128,1024]{2,1,0:T(8,128)(2,1)} %get-tuple-element.110.refs_0_.refs_3_, bf16[12,128,1024]{2,1,0:T(8,128)(2,1)} %bitcast.8, ...), custom_call_target="tpu_custom_call" | custom-call | flops 6899999744 | bytes 1048576 | tf_op jit(solution)/shard_map/project/pallas_call | solution.py:552
  142.2 7.9 %project_more.1 = (bf16[1,256,1024]{2,1,0:T(8,128)(2,1)}, bf16[1,256,1024]{2,1,0:T(8,128)(2,1)}) custom-call(s32[1]{0:T(128)} %bitcast.1.flip_ref, bf16[2,128,1024]{2,1,0:T(8,128)(2,1)} %copy-done.18, bf16[512,512]{1,0:T(8,128)(2,1)} %get-tuple-element.97.refs_8_.refs_6_.refs_11_.refs_13_.refs_1_, bf16[256,512]{1,0:T(8,128)(2,1)} %get-tuple-element.117.refs_2_, ...), custom_call_target="tpu_custom_call" | custom-call | flops 6899999744 | bytes 1048576 | tf_op jit(solution)/shard_map/project_more/pallas_call | solution.py:511
  157.1 5.4 %adjoint.1 = f32[8,4,1024]{2,1,0:T(4,128)} custom-call(s32[17]{0:T(128)} %copy-done.5, bf16[1,256,1024]{2,1,0:T(8,128)(2,1)} %copy-done.14, bf16[1,256,1024]{2,1,0:T(8,128)(2,1)} %outer.1.refs_1_, f32[1,4,128,128]{3,2,1,0:T(8,128)} %get-tuple-element.124.refs_2_, f32[1,4,128,128]{3,2,1,0:T(8,128)} %get-tuple-element.125.refs_3_, ...), custom_call_target="tpu_custom_call" | custom-call | flops 230000000 | bytes 1048576 | tf_op jit(solution)/shard_map/adjoint/pallas_call | solution.py:643
  162.5 8.4 %collective-permute-start.37 = (bf16[1,256,1024]{2,1,0:T(8,128)(2,1)}, bf16[1,256,1024]{2,1,0:T(8,128)(2,1)}, u32[]{:S(2)}, u32[]{:S(2)}) collective-permute-start(bf16[1,256,1024]{2,1,0:T(8,128)(2,1)} %get-tuple-element.132.near_ref), channel_id=1, source_target_pairs={{0,1},{3,2},{4,5},{7,6},{8,9},{11,10},{12,13},{15,14},{16,17},{19,... | collective-permute-start | bytes 1572872 | tf_op jit(solution)/shard_map/ppermute | solution.py:691
  173.4 3.8 %collective-permute-done.37.inward_ref = bf16[1,256,1024]{2,1,0:T(8,128)(2,1)} collective-permute-done((bf16[1,256,1024]{2,1,0:T(8,128)(2,1)}, bf16[1,256,1024]{2,1,0:T(8,128)(2,1)}, u32[]{:S(2)}, u32[]{:S(2)}) %collective-permute-start.37) | collective-permute-done | bytes 524320 | tf_op jit(solution)/shard_map/ppermute | solution.py:691
  177.1 3.4 %all-to-all-start = ((f32[8,4,1024]{2,1,0:T(4,128)}), f32[8,4,1024]{2,1,0:T(4,128)S(1)}, u32[]{:S(2)}, u32[]{:S(2)}) async-start(f32[8,4,1024]{2,1,0:T(4,128)} %adjoint.1), calls=%async_computation | async-start | bytes 262144 | tf_op jit(solution)/shard_map/all_to_all | solution.py:884
  180.5 2.5 %near_sum.1.refs_1_ = f32[256,1024]{1,0:T(8,128)} custom-call(s32[1]{0:T(128)} %bitcast.ends_ref, bf16[1,256,1024]{2,1,0:T(8,128)(2,1)} %get-tuple-element.120.first_ref, bf16[1,256,1024]{2,1,0:T(8,128)(2,1)} %get-tuple-element.132.near_ref, bf16[1,256,1024]{2,1,0:T(8,128)(2,1)} %collective-permute-done.37.inward_ref), custom_call_target="tpu_custom_call" | custom-call | flops 5750000128 | bytes 1048576 | tf_op jit(solution)/shard_map/near_sum/pallas_call | solution.py:706
  183.0 2.6 %first_band.1.refs_0_ = bf16[512,1024]{1,0:T(8,128)(2,1)} custom-call(s32[1]{0:T(128)} %bitcast.ends_ref, bf16[1,256,1024]{2,1,0:T(8,128)(2,1)} %get-tuple-element.109.first_ref, bf16[1,256,1024]{2,1,0:T(8,128)(2,1)} %collective-permute-done.33.outward_ref, bf16[3,128,1024]{2,1,0:T(8,128)(2,1)} %get-tuple-element.99.refs_0_, ...), custom_call_target="tpu_custom_call" | custom-call | flops 2300000000 | bytes 1048576 | tf_op jit(solution)/shard_map/first_band/pallas_call | solution.py:790
  186.6 2.6 %house_grad.1 = f32[4,512]{1,0:T(4,128)} custom-call(s32[17]{0:T(128)} %copy-done.5, f32[8,4,1024]{2,1,0:T(4,128)} %copy-done.21, f32[32,512]{1,0:T(8,128)} %copy-done.2, f32[32,512]{1,0:T(8,128)} %copy-done.3, f32[4,512]{1,0:T(4,128)} %house_ref.1), custom_call_target="tpu_custom_call" | custom-call | flops 2300000000 | bytes 1048576 | tf_op jit(solution)/shard_map/house_grad/pallas_call | solution.py:675
  (154 shorter events, 58.3 us)
Async XLA Ops:
  0.6 16.0 %collective-permute-start.1 = (bf16[512,512]{1,0:T(8,128)(2,1)}, bf16[512,512]{1,0:T(8,128)(2,1)S(1)}, u32[]{:S(2)}, u32[]{:S(2)}) collective-permute-start(bf16[512,512]{1,0:T(8,128)(2,1)} %refs_20_.1), channel_id=1, source_target_pairs={{0,8},{4,12},{8,0},{12,4},{16,24},{20,28},{24,16},{28,20},{1,9},{5... | collective-permute-start | bytes 1572872 | tf_op jit(solution)/shard_map/ppermute | solution.py:687
  3.6 15.1 %collective-permute-start.2 = (bf16[512,512]{1,0:T(8,128)(2,1)}, bf16[512,512]{1,0:T(8,128)(2,1)S(1)}, u32[]{:S(2)}, u32[]{:S(2)}) collective-permute-start(bf16[512,512]{1,0:T(8,128)(2,1)} %refs_14_.3), channel_id=1, source_target_pairs={{0,16},{4,20},{8,24},{12,28},{16,0},{20,4},{24,8},{28,12},{1,17},{... | collective-permute-start | bytes 1572872 | tf_op jit(solution)/shard_map/ppermute | solution.py:687
  5.2 22.2 %collective-permute-start = (bf16[512,512]{1,0:T(8,128)(2,1)}, bf16[512,512]{1,0:T(8,128)(2,1)S(1)}, u32[]{:S(2)}, u32[]{:S(2)}) collective-permute-start(bf16[512,512]{1,0:T(8,128)(2,1)} %refs_14_.3), channel_id=1, source_target_pairs={{0,8},{4,12},{8,0},{12,4},{16,24},{20,28},{24,16},{28,20},{1,9},{5... | collective-permute-start | bytes 1572872 | tf_op jit(solution)/shard_map/ppermute | solution.py:687
  5.7 23.4 %collective-permute-start.3 = (bf16[512,512]{1,0:T(8,128)(2,1)}, bf16[512,512]{1,0:T(8,128)(2,1)S(1)}, u32[]{:S(2)}, u32[]{:S(2)}) collective-permute-start(bf16[512,512]{1,0:T(8,128)(2,1)} %refs_20_.1), channel_id=1, source_target_pairs={{0,16},{4,20},{8,24},{12,28},{16,0},{20,4},{24,8},{28,12},{1,17},{... | collective-permute-start | bytes 1572872 | tf_op jit(solution)/shard_map/ppermute | solution.py:687
  27.4 16.8 %collective-permute-start.14 = (bf16[512,512]{1,0:T(8,128)(2,1)S(1)}, bf16[512,512]{1,0:T(8,128)(2,1)S(1)}, u32[]{:S(2)}, u32[]{:S(2)}) collective-permute-start(bf16[512,512]{1,0:T(8,128)(2,1)S(1)} %collective-permute-done.2.refs_9_), channel_id=1, source_target_pairs={{0,8},{4,12},{8,0},{12,4},{16,24},{20,28},{24,16},{28,20},{1,9},{5... | collective-permute-start | bytes 1572872 | tf_op jit(solution)/shard_map/ppermute | solution.py:687
  29.1 15.1 %collective-permute-start.15 = (bf16[512,512]{1,0:T(8,128)(2,1)S(1)}, bf16[512,512]{1,0:T(8,128)(2,1)S(1)}, u32[]{:S(2)}, u32[]{:S(2)}) collective-permute-start(bf16[512,512]{1,0:T(8,128)(2,1)S(1)} %collective-permute-done.1.refs_6_), channel_id=1, source_target_pairs={{0,16},{4,20},{8,24},{12,28},{16,0},{20,4},{24,8},{28,12},{1,17},{... | collective-permute-start | bytes 1572872 | tf_op jit(solution)/shard_map/ppermute | solution.py:687
  69.1 14.1 %collective-permute-start.21 = (bf16[1,128,1024]{2,1,0:T(8,128)(2,1)}, bf16[1,128,1024]{2,1,0:T(8,128)(2,1)S(1)}, u32[]{:S(2)}, u32[]{:S(2)}) collective-permute-start(bf16[1,128,1024]{2,1,0:T(8,128)(2,1)} %get-tuple-element.93), channel_id=1, source_target_pairs={{0,16},{4,20},{8,24},{12,28},{16,0},{20,4},{24,8},{28,12},{1,17},{... | collective-permute-start | bytes 786440 | tf_op jit(solution)/shard_map/ppermute | solution.py:687
  69.4 13.9 %collective-permute-start.22 = (bf16[1,128,1024]{2,1,0:T(8,128)(2,1)}, bf16[1,128,1024]{2,1,0:T(8,128)(2,1)}, u32[]{:S(2)}, u32[]{:S(2)}) collective-permute-start(bf16[1,128,1024]{2,1,0:T(8,128)(2,1)} %get-tuple-element.94), channel_id=1, source_target_pairs={{0,24},{4,28},{8,16},{12,20},{16,8},{20,12},{24,0},{28,4},{1,25},{... | collective-permute-start | bytes 786440 | tf_op jit(solution)/shard_map/ppermute | solution.py:687
  83.2 17.8 %collective-permute-start.23 = (bf16[1,128,1024]{2,1,0:T(8,128)(2,1)S(1)}, bf16[1,128,1024]{2,1,0:T(8,128)(2,1)S(1)}, u32[]{:S(2)}, u32[]{:S(2)}) collective-permute-start(bf16[1,128,1024]{2,1,0:T(8,128)(2,1)S(1)} %copy-done.32), channel_id=1, source_target_pairs={{0,8},{4,12},{8,0},{12,4},{16,24},{20,28},{24,16},{28,20},{1,9},{5... | collective-permute-start | bytes 786440 | tf_op jit(solution)/shard_map/ppermute | solution.py:687
  84.8 16.2 %collective-permute-start.24 = (bf16[1,128,1024]{2,1,0:T(8,128)(2,1)S(1)}, bf16[1,128,1024]{2,1,0:T(8,128)(2,1)S(1)}, u32[]{:S(2)}, u32[]{:S(2)}) collective-permute-start(bf16[1,128,1024]{2,1,0:T(8,128)(2,1)S(1)} %copy-done.30), channel_id=1, source_target_pairs={{0,16},{4,20},{8,24},{12,28},{16,0},{20,4},{24,8},{28,12},{1,17},{... | collective-permute-start | bytes 786440 | tf_op jit(solution)/shard_map/ppermute | solution.py:687
  85.3 15.7 %collective-permute-start.25 = (bf16[1,128,1024]{2,1,0:T(8,128)(2,1)S(1)}, bf16[1,128,1024]{2,1,0:T(8,128)(2,1)S(1)}, u32[]{:S(2)}, u32[]{:S(2)}) collective-permute-start(bf16[1,128,1024]{2,1,0:T(8,128)(2,1)S(1)} %copy-done.27), channel_id=1, source_target_pairs={{0,24},{4,28},{8,16},{12,20},{16,8},{20,12},{24,0},{28,4},{1,25},{... | collective-permute-start | bytes 786440 | tf_op jit(solution)/shard_map/ppermute | solution.py:687
  97.3 23.5 %collective-permute-start.26 = (bf16[3,128,1024]{2,1,0:T(8,128)(2,1)}, bf16[3,128,1024]{2,1,0:T(8,128)(2,1)S(1)}, u32[]{:S(2)}, u32[]{:S(2)}) collective-permute-start(bf16[3,128,1024]{2,1,0:T(8,128)(2,1)} %get-tuple-element.99.refs_0_), channel_id=1, source_target_pairs={{0,1},{3,2},{4,5},{7,6},{8,9},{11,10},{12,13},{15,14},{16,17},{19,... | collective-permute-start | bytes 2359304 | tf_op jit(solution)/shard_map/ppermute | solution.py:691
  101.8 20.6 %collective-permute-start.29 = (bf16[2,128,1024]{2,1,0:T(8,128)(2,1)}, bf16[2,128,1024]{2,1,0:T(8,128)(2,1)S(1)}, u32[]{:S(2)}, u32[]{:S(2)}) collective-permute-start(bf16[2,128,1024]{2,1,0:T(8,128)(2,1)} %get-tuple-element.111.refs_0_), channel_id=1, source_target_pairs={{0,8},{4,12},{8,0},{12,4},{16,24},{20,28},{24,16},{28,20},{1,9},{5... | collective-permute-start | bytes 1572872 | tf_op jit(solution)/shard_map/ppermute | solution.py:687
  103.3 23.1 %collective-permute-start.30 = (bf16[2,128,1024]{2,1,0:T(8,128)(2,1)}, bf16[2,128,1024]{2,1,0:T(8,128)(2,1)S(1)}, u32[]{:S(2)}, u32[]{:S(2)}) collective-permute-start(bf16[2,128,1024]{2,1,0:T(8,128)(2,1)} %get-tuple-element.112), channel_id=1, source_target_pairs={{0,16},{4,20},{8,24},{12,28},{16,0},{20,4},{24,8},{28,12},{1,17},{... | collective-permute-start | bytes 1572872 | tf_op jit(solution)/shard_map/ppermute | solution.py:687
  103.8 22.6 %collective-permute-start.31 = (bf16[2,128,1024]{2,1,0:T(8,128)(2,1)}, bf16[2,128,1024]{2,1,0:T(8,128)(2,1)S(1)}, u32[]{:S(2)}, u32[]{:S(2)}) collective-permute-start(bf16[2,128,1024]{2,1,0:T(8,128)(2,1)} %get-tuple-element.113), channel_id=1, source_target_pairs={{0,24},{4,28},{8,16},{12,20},{16,8},{20,12},{24,0},{28,4},{1,25},{... | collective-permute-start | bytes 1572872 | tf_op jit(solution)/shard_map/ppermute | solution.py:687
  118.6 21.7 %collective-permute-start.28 = (bf16[3,128,1024]{2,1,0:T(8,128)(2,1)}, bf16[3,128,1024]{2,1,0:T(8,128)(2,1)}, u32[]{:S(2)}, u32[]{:S(2)}) collective-permute-start(bf16[3,128,1024]{2,1,0:T(8,128)(2,1)} %get-tuple-element.110.refs_0_.refs_3_), channel_id=1, source_target_pairs={{0,1},{3,2},{4,5},{7,6},{8,9},{11,10},{12,13},{15,14},{16,17},{19,... | collective-permute-start | bytes 2359304 | tf_op jit(solution)/shard_map/ppermute | solution.py:691
  120.8 19.4 %collective-permute-start.27 = (bf16[2,128,1024]{2,1,0:T(8,128)(2,1)S(1)}, bf16[2,128,1024]{2,1,0:T(8,128)(2,1)}, u32[]{:S(2)}, u32[]{:S(2)}) collective-permute-start(bf16[2,128,1024]{2,1,0:T(8,128)(2,1)S(1)} %slice_add_fusion), channel_id=1, source_target_pairs={{1,2},{2,1},{5,6},{6,5},{9,10},{10,9},{13,14},{14,13},{17,18},{18,... | collective-permute-start | bytes 1572872 | tf_op jit(solution)/shard_map/ppermute | solution.py:691
  137.3 14.2 %collective-permute-start.34 = (bf16[1,256,1024]{2,1,0:T(8,128)(2,1)}, bf16[1,256,1024]{2,1,0:T(8,128)(2,1)S(1)}, u32[]{:S(2)}, u32[]{:S(2)}) collective-permute-start(bf16[1,256,1024]{2,1,0:T(8,128)(2,1)} %get-tuple-element.116), channel_id=1, source_target_pairs={{0,1},{3,2},{4,5},{7,6},{8,9},{11,10},{12,13},{15,14},{16,17},{19,... | collective-permute-start | bytes 1572872 | tf_op jit(solution)/shard_map/ppermute | solution.py:691
  138.9 23.6 %collective-permute-start.36 = (bf16[1,256,1024]{2,1,0:T(8,128)(2,1)}, bf16[1,256,1024]{2,1,0:T(8,128)(2,1)S(1)}, u32[]{:S(2)}, u32[]{:S(2)}) collective-permute-start(bf16[1,256,1024]{2,1,0:T(8,128)(2,1)} %get-tuple-element.122), channel_id=1, source_target_pairs={{0,1},{3,2},{4,5},{7,6},{8,9},{11,10},{12,13},{15,14},{16,17},{19,... | collective-permute-start | bytes 1572872 | tf_op jit(solution)/shard_map/ppermute | solution.py:691
  151.8 20.1 %collective-permute-start.35 = (bf16[1,256,1024]{2,1,0:T(8,128)(2,1)S(1)}, bf16[1,256,1024]{2,1,0:T(8,128)(2,1)S(1)}, u32[]{:S(2)}, u32[]{:S(2)}) collective-permute-start(bf16[1,256,1024]{2,1,0:T(8,128)(2,1)S(1)} %add.17.refs_0_), channel_id=1, source_target_pairs={{1,2},{2,1},{5,6},{6,5},{9,10},{10,9},{13,14},{14,13},{17,18},{18,... | collective-permute-start | bytes 1572872 | tf_op jit(solution)/shard_map/ppermute | solution.py:691
  155.4 16.4 %collective-permute-start.33 = (bf16[1,256,1024]{2,1,0:T(8,128)(2,1)}, bf16[1,256,1024]{2,1,0:T(8,128)(2,1)}, u32[]{:S(2)}, u32[]{:S(2)}) collective-permute-start(bf16[1,256,1024]{2,1,0:T(8,128)(2,1)} %outer.1.refs_1_), channel_id=1, source_target_pairs={{1,0},{2,3},{5,4},{6,7},{9,8},{10,11},{13,12},{14,15},{17,16},{18,... | collective-permute-start | bytes 1572872 | tf_op jit(solution)/shard_map/ppermute | solution.py:691
  162.5 14.6 %collective-permute-start.37 = (bf16[1,256,1024]{2,1,0:T(8,128)(2,1)}, bf16[1,256,1024]{2,1,0:T(8,128)(2,1)}, u32[]{:S(2)}, u32[]{:S(2)}) collective-permute-start(bf16[1,256,1024]{2,1,0:T(8,128)(2,1)} %get-tuple-element.132.near_ref), channel_id=1, source_target_pairs={{0,1},{3,2},{4,5},{7,6},{8,9},{11,10},{12,13},{15,14},{16,17},{19,... | collective-permute-start | bytes 1572872 | tf_op jit(solution)/shard_map/ppermute | solution.py:691
  171.1 18.1 %collective-permute-start.38 = (bf16[1,256,1024]{2,1,0:T(8,128)(2,1)S(1)}, bf16[1,256,1024]{2,1,0:T(8,128)(2,1)S(1)}, u32[]{:S(2)}, u32[]{:S(2)}) collective-permute-start(bf16[1,256,1024]{2,1,0:T(8,128)(2,1)S(1)} %add.18), channel_id=1, source_target_pairs={{1,2},{2,1},{5,6},{6,5},{9,10},{10,9},{13,14},{14,13},{17,18},{18,... | collective-permute-start | bytes 1572872 | tf_op jit(solution)/shard_map/ppermute | solution.py:691
  172.1 17.1 %collective-permute-start.39 = (bf16[1,256,1024]{2,1,0:T(8,128)(2,1)S(1)}, bf16[1,256,1024]{2,1,0:T(8,128)(2,1)S(1)}, u32[]{:S(2)}, u32[]{:S(2)}) collective-permute-start(bf16[1,256,1024]{2,1,0:T(8,128)(2,1)S(1)} %add.19), channel_id=1, source_target_pairs={{1,0},{2,3},{5,4},{6,7},{9,8},{10,11},{13,12},{14,15},{17,16},{18,... | collective-permute-start | bytes 1572872 | tf_op jit(solution)/shard_map/ppermute | solution.py:691
  (51 other events, 368.8 us)

commit v11 on v10

--- a/solution.py
+++ b/solution.py
@@ -696,50 +696,31 @@
 OUTWARD = [(1, 0), (2, 3)]
 
 
-def near_kernel(ends_ref, first_ref, near_ref, inward_ref, out_ref):
-    mine = jnp.where(ends_ref[0] > 0, first_ref[0], near_ref[0]).astype(F32)
-    out_ref[...] = mine + inward_ref[0].astype(F32)
-
-
-def run_near(ends, first, band, near, inward):
-    _, rows, width = near.shape
-    return pl.pallas_call(
-        near_kernel,
-        grid=(1,),
-        out_shape=jax.ShapeDtypeStruct((rows, width), F32),
+def last_band_kernel(ends_ref, share_ref, first_ref, near_ref, inward_ref, far_ref, *refs):
+    outward_ref, out_ref = refs
+    total = jnp.where(ends_ref[0] > 0, first_ref[0], near_ref[0]).astype(F32)
+    total = total + inward_ref[0].astype(F32)
+    total = total + (far_ref[0].astype(F32) + outward_ref[0].astype(F32))
+    out_ref[...] = total.astype(BF16)
+
+
+def run_last_band(share, *parts):
+    _, rows, width = parts[0].shape
+    tile = min(512, width)
+    band = share.shape[0] // rows - 1
+    return pl.pallas_call(
+        last_band_kernel,
+        grid=(width // tile,),
+        out_shape=jax.ShapeDtypeStruct(share.shape, BF16),
         in_specs=in_smem(1)
-        + [pl.BlockSpec((1, rows, width), lambda t: (0, band, 0))]
-        + [pl.BlockSpec((1, rows, width), lambda t: (0, 0, 0))] * 2,
-        out_specs=pl.BlockSpec((rows, width), lambda t: (0, 0)),
-        compiler_params=grant(60),
-        cost_estimate=cost(5),
-        name="near_sum",
-    )(ends, first, near, inward)
-
-
-def share_kernel(*refs):
-    total_ref, far_ref, outward_ref, out_ref = refs[-4:]
-    far = far_ref[0].astype(F32) + outward_ref[0].astype(F32)
-    out_ref[...] = (total_ref[...] + far).astype(BF16)
-
-
-def run_share(share, band, bands, total, far, outward):
-    rows, width = total.shape
-    tile = min(512, width)
-    part = pl.BlockSpec((1, rows, tile), lambda t: (0, 0, t))
-    given = [] if share is None else [share]
-    return pl.pallas_call(
-        share_kernel,
-        grid=(width // tile,),
-        out_shape=jax.ShapeDtypeStruct((bands * rows, width), BF16),
-        in_specs=[pl.BlockSpec(memory_space=pl.ANY)] * len(given)
-        + [pl.BlockSpec((rows, tile), lambda t: (0, t)), part, part],
+        + [pl.BlockSpec(memory_space=pl.ANY)]
+        + [pl.BlockSpec((1, rows, tile), lambda t: (0, 0, t))] * len(parts),
         out_specs=pl.BlockSpec((rows, tile), lambda t: (band, t)),
-        input_output_aliases={0: 0} if given else {},
+        input_output_aliases={1: 0},
         compiler_params=grant(60),
         cost_estimate=cost(2),
-        name="share",
-    )(*given, total, far, outward)
+        name="last_band",
+    )(line_ends(), share, *parts)
 
 
 def line_ends():
@@ -805,17 +786,15 @@
     sum_last = last + in_last
     swap_last = slide(sum_last, MIDDLE)
     other = meanwhile(sum_last)
-    in_far, near, other = lax.optimization_barrier((in_far, near, other))
-    in_near = slide(near, INWARD)
+    in_far, other = lax.optimization_barrier((in_far, other))
     sum_far = far + in_far
     swap_far = slide(sum_far, MIDDLE)
     swap_last, *_ = lax.optimization_barrier((swap_last, earlier, sum_far))
     outer = first + swap_last
     outward = slide(outer, OUTWARD)
-    other, in_near, _ = lax.optimization_barrier((other, in_near, outer))
-    other = exchange(other)
-    total = run_near(line_ends(), first, 0, near, in_near)
-    return total, swap_far, outward, other, outer
+    other, near, _ = lax.optimization_barrier((other, near, outer))
+    in_near = slide(near, INWARD)
+    return (first, near, in_near, swap_far, outward), exchange(other), outer
 
 
 def shards(
@@ -924,13 +903,13 @@
         def meanwhile(after):
             return run_adjoint(ints, (after, outer), [dcum_0, dcum_1, dcum_2], *house)
 
-        total_2, swapped_2, outward_2, got, outer_2 = line_scatter_apart(
+        last_parts, got, outer_2 = line_scatter_apart(
             first, near, far, last, meanwhile, share_sums, outward
         )
         outward, _ = lax.optimization_barrier((outward, outer_2))
         parts = (rest_0, inward_0, swapped_0, rest_1, inward_1, swapped_1)
         share = run_first_band(2, firsts, outward, *parts)
-        share = run_share(share, 1, 2, total_2, swapped_2, outward_2)
+        share = run_last_band(share, *last_parts)
     else:
         spots = (owners * blocks + offsets).reshape(-1)
         empty = jnp.zeros((ctx_count * blocks, BLK, 2 * width), BF16)

time: 194 us -> 190 us (0.979)
  starting transfers between devices: 52.3 us -> 47 us
  waiting for transfers between devices: 33.2 us -> 36.9 us
  Pallas kernels: 92.2 us -> 90.1 us
    ppermute x11, starting transfers between devices: 23.8 us -> 18.7 us  [slide(): return lax.ppermute(value, 'head', pairs)]
    all_to_all x1, waiting for transfers between devices: 0.45 us -> 2.89 us  [share_sums(): return lax.all_to_all(sums, 'ctx', split_axis=0, concat_axis=0, tiled=True)]
    pallas_call x2 -> x1, Pallas kernels: 4.74 us -> 2.5 us  [run_last_band(): pl.pallas_call(last_band_kernel, grid=(width // tile,), out_shape=jax.Sha...]
    unnamed x70 -> x72, local copies, waits for them, and re-layouts: 11.6 us -> 10.2 us
  transfers between devices with their start and end apart: 41 -> 41, of which waited for: 11 -> 11; matrix products, arithmetic and copies ran while one was open for 2% -> 2% of each run, Pallas kernels for 39% -> 38%
where the time goes in v11:
time: 190 us; the launch traced here: 188 us
  Pallas kernels  90.1 us (47%)
  starting transfers between devices  47 us (25%)
  waiting for transfers between devices  36.9 us (19%)
  local copies, waits for them, and re-layouts  10.4 us (5%)
  other arithmetic  2.7 us (1%)
    pallas_call x3, Pallas kernels, run_project(): pl.pallas_call(functools.partial(project_kernel, heads, len(parts[0]), si...  32.8 us
    ppermute x29, waiting for transfers between devices, hop(): return lax.ppermute(value, 'ctx', [(i, i ^ distance) for i in range(count)])  27.4 us
    ppermute x29, starting transfers between devices, hop(): return lax.ppermute(value, 'ctx', [(i, i ^ distance) for i in range(count)])  24.9 us
    ppermute x11, starting transfers between devices, slide(): return lax.ppermute(value, 'head', pairs)  18.7 us
    pallas_call x1, Pallas kernels, run_attend(): pl.pallas_call(functools.partial(attend_kernel, heads, blocks, places, pi...  15.2 us
    unnamed x72, local copies, waits for them, and re-layouts  10.2 us
    pallas_call x3, Pallas kernels, run_merge(): pl.pallas_call(merge_kernel, grid=(size, cut), out_shape=[jax.ShapeDtypeS...  8.86 us
    pallas_call x1, Pallas kernels, run_project_more(): pl.pallas_call(functools.partial(project_more_kernel, groups, layout, len...  7.93 us
  transfers between devices with their start and end apart: 41, of which 11 were waited for; matrix products, arithmetic and copies ran while one was open for 2% of the time, Pallas kernels for 38%

profile of v11, /device:TPU:0, one launch (start us, length us, event | category | flops | bytes accessed | tf_op | source)
XLA Modules:
  0.0 188.3 jit_solution(8785749211411788009)
XLA Ops:
  0.6 3.0 %collective-permute-start.1 = (bf16[512,512]{1,0:T(8,128)(2,1)}, bf16[512,512]{1,0:T(8,128)(2,1)S(1)}, u32[]{:S(2)}, u32[]{:S(2)}) collective-permute-start(bf16[512,512]{1,0:T(8,128)(2,1)} %refs_20_.1), channel_id=1, source_target_pairs={{0,8},{4,12},{8,0},{12,4},{16,24},{20,28},{24,16},{28,20},{1,9},{5... | collective-permute-start | bytes 1572872 | tf_op jit(solution)/shard_map/ppermute | solution.py:687
  8.2 8.4 %collective-permute-done.1.refs_6_ = bf16[512,512]{1,0:T(8,128)(2,1)S(1)} collective-permute-done((bf16[512,512]{1,0:T(8,128)(2,1)}, bf16[512,512]{1,0:T(8,128)(2,1)S(1)}, u32[]{:S(2)}, u32[]{:S(2)}) %collective-permute-start.1) | collective-permute-done | bytes 524320 | tf_op jit(solution)/shard_map/ppermute | solution.py:687
  22.3 5.1 %collective-permute-done.refs_5_ = bf16[512,512]{1,0:T(8,128)(2,1)S(1)} collective-permute-done((bf16[512,512]{1,0:T(8,128)(2,1)}, bf16[512,512]{1,0:T(8,128)(2,1)S(1)}, u32[]{:S(2)}, u32[]{:S(2)}) %collective-permute-start) | collective-permute-done | bytes 524320 | tf_op jit(solution)/shard_map/ppermute | solution.py:687
  31.3 4.5 %house_chain.1 = (f32[32,512]{1,0:T(8,128)S(1)}, f32[32,512]{1,0:T(8,128)S(1)}, f32[4,32,32]{2,1,0:T(8,128)S(1)}, bf16[4,128,96]{2,1,0:T(8,128)(2,1)S(1)}, bf16[4,96,128]{2,1,0:T(8,128)(2,1)S(1)}) custom-call(s32[17]{0:T(128)S(1)} %pad_add_fusion.ints_ref.refs_0_.base_ref, f32[8,512]{1,0:T(8,128)S(1)} %pad_maximum_fusion.refs_0_, ...), custom_call_target="tpu_custom_call" | custom-call | flops 6899999744 | bytes 1048576 | tf_op jit(solution)/shard_map/house_chain/pallas_call | solution.py:119
  38.6 5.5 %rotate.1 = (bf16[512,512]{1,0:T(8,128)(2,1)S(1)}, bf16[512,512]{1,0:T(8,128)(2,1)S(1)}, bf16[4,4,128,128]{3,2,1,0:T(8,128)(2,1)S(1)}, bf16[8,4,256,128]{3,2,1,0:T(8,128)(2,1)S(1)}) custom-call(s32[17]{0:T(128)S(1)} %pad_add_fusion.ints_ref.refs_0_.base_ref, bf16[4,128,96]{2,1,0:T(8,128)(2,1)S(1)} %get-tuple-element.75.wide_ref, ...), custom_call_target="tpu_custom_call" | custom-call | flops 10350000128 | bytes 1048576 | tf_op jit(solution)/shard_map/rotate/pallas_call | solution.py:187
  46.9 15.2 %attend.1 = (bf16[512,512]{1,0:T(8,128)(2,1)}, f32[4,4,128,128]{3,2,1,0:T(8,128)}, f32[512,512]{1,0:T(8,128)}, f32[512,512]{1,0:T(8,128)}, bf16[1,4,128,1024]{3,...) custom-call(s32[17]{0:T(128)S(1)} %pad_add_fusion.ints_ref.refs_0_.b, ...), custom_call_target="tpu_custom_call" | custom-call | flops 17250000896 | bytes 1048576 | tf_op jit(solution)/shard_map/attend/pallas_call | solution.py:376
  62.3 2.8 %collective-permute-done.18.got_ref = bf16[1,4,128,1024]{3,2,1,0:T(8,128)(2,1)S(1)} collective-permute-done((bf16[1,4,128,1024]{3,2,1,0:T(8,128)(2,1)}, bf16[1,4,128,1024]{3,2,1,0:T(8,128)(2,1)S(1)}, u32[]{:S(2)}, u32[]{:S(2)}) %collective-permute-start.18) | collective-permute-done | bytes 1048608 | tf_op jit(solution)/shard_map/ppermute | solution.py:687
  69.4 2.7 %collective-permute-start.22 = (bf16[1,128,1024]{2,1,0:T(8,128)(2,1)}, bf16[1,128,1024]{2,1,0:T(8,128)(2,1)}, u32[]{:S(2)}, u32[]{:S(2)}) collective-permute-start(bf16[1,128,1024]{2,1,0:T(8,128)(2,1)} %get-tuple-element.93), channel_id=1, source_target_pairs={{0,24},{4,28},{8,16},{12,20},{16,8},{20,12},{24,0},{28,4},{1,25},{... | collective-permute-start | bytes 786440 | tf_op jit(solution)/shard_map/ppermute | solution.py:687
  76.1 4.2 %merge.5 = (bf16[2,128,1024]{2,1,0:T(8,128)(2,1)}, bf16[2,128,1024]{2,1,0:T(8,128)(2,1)}, bf16[2,128,1024]{2,1,0:T(8,128)(2,1)}) custom-call(bf16[3,4,128,1024]{3,2,1,0:T(8,128)(2,1)} %get-tuple-element.84.own_ref, bf16[3,4,128,1024]{3,2,1,0:T(8,128)(2,1)} %copy-done.9, bf16[1,128,1024]{2,1,0:T(8,128)(2,1)} %get-tuple-element.103.refs_0_), custom_call_target="tpu_custom_call" | custom-call | flops 2300000000 | bytes 1048576 | tf_op jit(solution)/shard_map/merge/pallas_call | solution.py:405
  80.3 2.9 %collective-permute-done.21.refs_4_ = bf16[1,128,1024]{2,1,0:T(8,128)(2,1)S(1)} collective-permute-done((bf16[1,128,1024]{2,1,0:T(8,128)(2,1)}, bf16[1,128,1024]{2,1,0:T(8,128)(2,1)S(1)}, u32[]{:S(2)}, u32[]{:S(2)}) %collective-permute-start.21) | collective-permute-done | bytes 262176 | tf_op jit(solution)/shard_map/ppermute | solution.py:687
  86.8 10.4 %project.3 = (bf16[3,128,1024]{2,1,0:T(8,128)(2,1)}, f32[1,4,128,128]{3,2,1,0:T(8,128)}, bf16[128,512]{1,0:T(8,128)(2,1)}, bf16[128,512]{1,0:T(8,128)(2,1)}) custom-call(s32[1]{0:T(128)} %bitcast.1.flip_ref, bf16[2,128,1024]{2,1,0:T(8,128)(2,1)} %get-tuple-element.110.refs_0_, bf16[4,128,1024]{2,1,0:T(8,128)(2,1)} %bitcast.14, ...), custom_call_target="tpu_custom_call" | custom-call | flops 10350000128 | bytes 1048576 | tf_op jit(solution)/shard_map/project/pallas_call | solution.py:552
  97.2 3.8 %collective-permute-start.26 = (bf16[3,128,1024]{2,1,0:T(8,128)(2,1)}, bf16[3,128,1024]{2,1,0:T(8,128)(2,1)S(1)}, u32[]{:S(2)}, u32[]{:S(2)}) collective-permute-start(bf16[3,128,1024]{2,1,0:T(8,128)(2,1)} %get-tuple-element.98.refs_0_), channel_id=1, source_target_pairs={{0,1},{3,2},{4,5},{7,6},{8,9},{11,10},{12,13},{15,14},{16,17},{19,... | collective-permute-start | bytes 2359304 | tf_op jit(solution)/shard_map/ppermute | solution.py:691
  104.6 13.1 %project.4 = (bf16[1,256,1024]{2,1,0:T(8,128)(2,1)}, bf16[3,128,1024]{2,1,0:T(8,128)(2,1)}, f32[1,4,128,128]{3,2,1,0:T(8,128)}, bf16[128,512]{1,0:T(8,128)(2,1)}, bf16[128,512]{1,0:T(8,128)(2,1)}) custom-call(s32[1]{0:T(128)} %bitcast.1.flip_ref, bf16[3,128,1024]{2,1,0:T(8,128)(2,1)} %get-tuple-element.98.refs_0_, bf16[12,128,1024]{2,1,0:T(8,128)(2,1)} %bitcast.7, ...), custom_call_target="tpu_custom_call" | custom-call | flops 13799999488 | bytes 1048576 | tf_op jit(solution)/shard_map/project/pallas_call | solution.py:552
  121.8 3.9 %collective-permute-done.30.refs_4_.refs_9_ = bf16[2,128,1024]{2,1,0:T(8,128)(2,1)S(1)} collective-permute-done((bf16[2,128,1024]{2,1,0:T(8,128)(2,1)}, bf16[2,128,1024]{2,1,0:T(8,128)(2,1)S(1)}, u32[]{:S(2)}, u32[]{:S(2)}) %collective-permute-start.30) | collective-permute-done | bytes 524320 | tf_op jit(solution)/shard_map/ppermute | solution.py:687
  127.3 9.3 %project.5 = (bf16[1,256,1024]{2,1,0:T(8,128)(2,1)}, bf16[1,256,1024]{2,1,0:T(8,128)(2,1)}, f32[2,4,128,128]{3,2,1,0:T(8,128)}, bf16[256,512]{1,0:T(8,128)(2,1)}, bf16[256,512]{1,0:T(8,128)(2,1)}) custom-call(s32[1]{0:T(128)} %bitcast.1.flip_ref, bf16[3,128,1024]{2,1,0:T(8,128)(2,1)} %get-tuple-element.109.refs_0_.refs_3_, bf16[12,128,1024]{2,1,0:T(8,128)(2,1)} %bitcast.8, ...), custom_call_target="tpu_custom_call" | custom-call | flops 6899999744 | bytes 1048576 | tf_op jit(solution)/shard_map/project/pallas_call | solution.py:552
  142.3 7.9 %project_more.1 = (bf16[1,256,1024]{2,1,0:T(8,128)(2,1)}, bf16[1,256,1024]{2,1,0:T(8,128)(2,1)}) custom-call(s32[1]{0:T(128)} %bitcast.1.flip_ref, bf16[2,128,1024]{2,1,0:T(8,128)(2,1)} %copy-done.18, bf16[512,512]{1,0:T(8,128)(2,1)} %get-tuple-element.96.refs_8_.refs_6_.refs_11_.refs_13_.refs_1_, bf16[256,512]{1,0:T(8,128)(2,1)} %get-tuple-element.116.refs_2_, ...), custom_call_target="tpu_custom_call" | custom-call | flops 6899999744 | bytes 1048576 | tf_op jit(solution)/shard_map/project_more/pallas_call | solution.py:511
  155.6 5.4 %adjoint.1 = f32[8,4,1024]{2,1,0:T(4,128)} custom-call(s32[17]{0:T(128)} %copy-done.5, bf16[1,256,1024]{2,1,0:T(8,128)(2,1)} %copy-done.14, bf16[1,256,1024]{2,1,0:T(8,128)(2,1)} %outer.1.refs_1_, f32[1,4,128,128]{3,2,1,0:T(8,128)} %get-tuple-element.122.refs_2_, f32[1,4,128,128]{3,2,1,0:T(8,128)} %get-tuple-element.123.refs_3_, ...), custom_call_target="tpu_custom_call" | custom-call | flops 230000000 | bytes 1048576 | tf_op jit(solution)/shard_map/adjoint/pallas_call | solution.py:643
  161.9 6.0 %collective-permute-done.33.outward_ref = bf16[1,256,1024]{2,1,0:T(8,128)(2,1)} collective-permute-done((bf16[1,256,1024]{2,1,0:T(8,128)(2,1)}, bf16[1,256,1024]{2,1,0:T(8,128)(2,1)}, u32[]{:S(2)}, u32[]{:S(2)}) %collective-permute-start.33) | collective-permute-done | bytes 524320 | tf_op jit(solution)/shard_map/ppermute | solution.py:691
  168.1 3.3 %collective-permute-start.37 = (bf16[1,256,1024]{2,1,0:T(8,128)(2,1)S(1)}, bf16[1,256,1024]{2,1,0:T(8,128)(2,1)S(1)}, u32[]{:S(2)}, u32[]{:S(2)}) collective-permute-start(bf16[1,256,1024]{2,1,0:T(8,128)(2,1)S(1)} %copy-done.24), channel_id=1, source_target_pairs={{0,1},{3,2},{4,5},{7,6},{8,9},{11,10},{12,13},{15,14},{16,17},{19,... | collective-permute-start | bytes 1572872 | tf_op jit(solution)/shard_map/ppermute | solution.py:691
  172.7 3.4 %all-to-all-start = ((f32[8,4,1024]{2,1,0:T(4,128)}), f32[8,4,1024]{2,1,0:T(4,128)S(1)}, u32[]{:S(2)}, u32[]{:S(2)}) async-start(f32[8,4,1024]{2,1,0:T(4,128)} %adjoint.1), calls=%async_computation | async-start | bytes 262144 | tf_op jit(solution)/shard_map/all_to_all | solution.py:863
  176.1 2.6 %first_band.1.share_ref = bf16[512,1024]{1,0:T(8,128)(2,1)} custom-call(s32[1]{0:T(128)} %bitcast.ends_ref, bf16[1,256,1024]{2,1,0:T(8,128)(2,1)} %get-tuple-element.108.first_ref, bf16[1,256,1024]{2,1,0:T(8,128)(2,1)} %collective-permute-done.33.outward_ref, bf16[3,128,1024]{2,1,0:T(8,128)(2,1)} %get-tuple-element.98.refs_0_, ...), custom_call_target="tpu_custom_call" | custom-call | flops 2300000000 | bytes 1048576 | tf_op jit(solution)/shard_map/first_band/pallas_call | solution.py:771
  178.7 2.9 %all-to-all-done.got_ref = f32[8,4,1024]{2,1,0:T(4,128)S(1)} async-done(((f32[8,4,1024]{2,1,0:T(4,128)}), f32[8,4,1024]{2,1,0:T(4,128)S(1)}, u32[]{:S(2)}, u32[]{:S(2)}) %all-to-all-start) | async-done | bytes 131104 | tf_op jit(solution)/shard_map/all_to_all | solution.py:863
  182.2 2.6 %house_grad.1 = f32[4,512]{1,0:T(4,128)} custom-call(s32[17]{0:T(128)} %copy-done.5, f32[8,4,1024]{2,1,0:T(4,128)} %copy-done.21, f32[32,512]{1,0:T(8,128)} %copy-done.2, f32[32,512]{1,0:T(8,128)} %copy-done.3, f32[4,512]{1,0:T(4,128)} %house_ref.1), custom_call_target="tpu_custom_call" | custom-call | flops 2300000000 | bytes 1048576 | tf_op jit(solution)/shard_map/house_grad/pallas_call | solution.py:675
  185.8 2.5 %last_band.1 = bf16[512,1024]{1,0:T(8,128)(2,1)} custom-call(s32[1]{0:T(128)} %bitcast.ends_ref, bf16[512,1024]{1,0:T(8,128)(2,1)} %first_band.1.share_ref, bf16[1,256,1024]{2,1,0:T(8,128)(2,1)} %get-tuple-element.119.first_ref, bf16[1,256,1024]{2,1,0:T(8,128)(2,1)} %get-tuple-element.132.near_ref, ...), custom_call_target="tpu_custom_call", output_to_operand_aliasing={{}: (1, {})} | custom-call | flops 2300000000 | bytes 1048576 | tf_op jit(solution)/shard_map/last_band/pallas_call | solution.py:711
  (155 shorter events, 55.8 us)
Async XLA Ops:
  0.6 16.0 %collective-permute-start.1 = (bf16[512,512]{1,0:T(8,128)(2,1)}, bf16[512,512]{1,0:T(8,128)(2,1)S(1)}, u32[]{:S(2)}, u32[]{:S(2)}) collective-permute-start(bf16[512,512]{1,0:T(8,128)(2,1)} %refs_20_.1), channel_id=1, source_target_pairs={{0,8},{4,12},{8,0},{12,4},{16,24},{20,28},{24,16},{28,20},{1,9},{5... | collective-permute-start | bytes 1572872 | tf_op jit(solution)/shard_map/ppermute | solution.py:687
  3.6 15.1 %collective-permute-start.2 = (bf16[512,512]{1,0:T(8,128)(2,1)}, bf16[512,512]{1,0:T(8,128)(2,1)S(1)}, u32[]{:S(2)}, u32[]{:S(2)}) collective-permute-start(bf16[512,512]{1,0:T(8,128)(2,1)} %refs_14_.3), channel_id=1, source_target_pairs={{0,16},{4,20},{8,24},{12,28},{16,0},{20,4},{24,8},{28,12},{1,17},{... | collective-permute-start | bytes 1572872 | tf_op jit(solution)/shard_map/ppermute | solution.py:687
  5.2 22.2 %collective-permute-start = (bf16[512,512]{1,0:T(8,128)(2,1)}, bf16[512,512]{1,0:T(8,128)(2,1)S(1)}, u32[]{:S(2)}, u32[]{:S(2)}) collective-permute-start(bf16[512,512]{1,0:T(8,128)(2,1)} %refs_14_.3), channel_id=1, source_target_pairs={{0,8},{4,12},{8,0},{12,4},{16,24},{20,28},{24,16},{28,20},{1,9},{5... | collective-permute-start | bytes 1572872 | tf_op jit(solution)/shard_map/ppermute | solution.py:687
  5.7 23.4 %collective-permute-start.3 = (bf16[512,512]{1,0:T(8,128)(2,1)}, bf16[512,512]{1,0:T(8,128)(2,1)S(1)}, u32[]{:S(2)}, u32[]{:S(2)}) collective-permute-start(bf16[512,512]{1,0:T(8,128)(2,1)} %refs_20_.1), channel_id=1, source_target_pairs={{0,16},{4,20},{8,24},{12,28},{16,0},{20,4},{24,8},{28,12},{1,17},{... | collective-permute-start | bytes 1572872 | tf_op jit(solution)/shard_map/ppermute | solution.py:687
  18.7 11.9 %collective-permute-start.5 = (f32[8,512]{1,0:T(8,128)S(1)}, f32[8,512]{1,0:T(8,128)S(1)}, u32[]{:S(2)}, u32[]{:S(2)}) collective-permute-start(f32[8,512]{1,0:T(8,128)S(1)} %pad_maximum_fusion.refs_0_), channel_id=1, source_target_pairs={{0,8},{4,12},{8,0},{12,4},{16,24},{20,28},{24,16},{28,20},{1,9},{5... | collective-permute-start | bytes 49160 | tf_op jit(solution)/shard_map/ppermute | solution.py:687
  27.4 16.8 %collective-permute-start.14 = (bf16[512,512]{1,0:T(8,128)(2,1)S(1)}, bf16[512,512]{1,0:T(8,128)(2,1)S(1)}, u32[]{:S(2)}, u32[]{:S(2)}) collective-permute-start(bf16[512,512]{1,0:T(8,128)(2,1)S(1)} %collective-permute-done.2.refs_9_), channel_id=1, source_target_pairs={{0,8},{4,12},{8,0},{12,4},{16,24},{20,28},{24,16},{28,20},{1,9},{5... | collective-permute-start | bytes 1572872 | tf_op jit(solution)/shard_map/ppermute | solution.py:687
  29.1 15.1 %collective-permute-start.15 = (bf16[512,512]{1,0:T(8,128)(2,1)S(1)}, bf16[512,512]{1,0:T(8,128)(2,1)S(1)}, u32[]{:S(2)}, u32[]{:S(2)}) collective-permute-start(bf16[512,512]{1,0:T(8,128)(2,1)S(1)} %collective-permute-done.1.refs_6_), channel_id=1, source_target_pairs={{0,16},{4,20},{8,24},{12,28},{16,0},{20,4},{24,8},{28,12},{1,17},{... | collective-permute-start | bytes 1572872 | tf_op jit(solution)/shard_map/ppermute | solution.py:687
  69.1 14.1 %collective-permute-start.21 = (bf16[1,128,1024]{2,1,0:T(8,128)(2,1)}, bf16[1,128,1024]{2,1,0:T(8,128)(2,1)S(1)}, u32[]{:S(2)}, u32[]{:S(2)}) collective-permute-start(bf16[1,128,1024]{2,1,0:T(8,128)(2,1)} %get-tuple-element.92), channel_id=1, source_target_pairs={{0,16},{4,20},{8,24},{12,28},{16,0},{20,4},{24,8},{28,12},{1,17},{... | collective-permute-start | bytes 786440 | tf_op jit(solution)/shard_map/ppermute | solution.py:687
  69.4 13.9 %collective-permute-start.22 = (bf16[1,128,1024]{2,1,0:T(8,128)(2,1)}, bf16[1,128,1024]{2,1,0:T(8,128)(2,1)}, u32[]{:S(2)}, u32[]{:S(2)}) collective-permute-start(bf16[1,128,1024]{2,1,0:T(8,128)(2,1)} %get-tuple-element.93), channel_id=1, source_target_pairs={{0,24},{4,28},{8,16},{12,20},{16,8},{20,12},{24,0},{28,4},{1,25},{... | collective-permute-start | bytes 786440 | tf_op jit(solution)/shard_map/ppermute | solution.py:687
  83.2 17.8 %collective-permute-start.23 = (bf16[1,128,1024]{2,1,0:T(8,128)(2,1)S(1)}, bf16[1,128,1024]{2,1,0:T(8,128)(2,1)S(1)}, u32[]{:S(2)}, u32[]{:S(2)}) collective-permute-start(bf16[1,128,1024]{2,1,0:T(8,128)(2,1)S(1)} %copy-done.33), channel_id=1, source_target_pairs={{0,8},{4,12},{8,0},{12,4},{16,24},{20,28},{24,16},{28,20},{1,9},{5... | collective-permute-start | bytes 786440 | tf_op jit(solution)/shard_map/ppermute | solution.py:687
  84.8 16.2 %collective-permute-start.24 = (bf16[1,128,1024]{2,1,0:T(8,128)(2,1)S(1)}, bf16[1,128,1024]{2,1,0:T(8,128)(2,1)S(1)}, u32[]{:S(2)}, u32[]{:S(2)}) collective-permute-start(bf16[1,128,1024]{2,1,0:T(8,128)(2,1)S(1)} %copy-done.31), channel_id=1, source_target_pairs={{0,16},{4,20},{8,24},{12,28},{16,0},{20,4},{24,8},{28,12},{1,17},{... | collective-permute-start | bytes 786440 | tf_op jit(solution)/shard_map/ppermute | solution.py:687
  85.3 15.8 %collective-permute-start.25 = (bf16[1,128,1024]{2,1,0:T(8,128)(2,1)S(1)}, bf16[1,128,1024]{2,1,0:T(8,128)(2,1)S(1)}, u32[]{:S(2)}, u32[]{:S(2)}) collective-permute-start(bf16[1,128,1024]{2,1,0:T(8,128)(2,1)S(1)} %copy-done.28), channel_id=1, source_target_pairs={{0,24},{4,28},{8,16},{12,20},{16,8},{20,12},{24,0},{28,4},{1,25},{... | collective-permute-start | bytes 786440 | tf_op jit(solution)/shard_map/ppermute | solution.py:687
  97.2 22.7 %collective-permute-start.26 = (bf16[3,128,1024]{2,1,0:T(8,128)(2,1)}, bf16[3,128,1024]{2,1,0:T(8,128)(2,1)S(1)}, u32[]{:S(2)}, u32[]{:S(2)}) collective-permute-start(bf16[3,128,1024]{2,1,0:T(8,128)(2,1)} %get-tuple-element.98.refs_0_), channel_id=1, source_target_pairs={{0,1},{3,2},{4,5},{7,6},{8,9},{11,10},{12,13},{15,14},{16,17},{19,... | collective-permute-start | bytes 2359304 | tf_op jit(solution)/shard_map/ppermute | solution.py:691
  101.0 20.7 %collective-permute-start.29 = (bf16[2,128,1024]{2,1,0:T(8,128)(2,1)}, bf16[2,128,1024]{2,1,0:T(8,128)(2,1)S(1)}, u32[]{:S(2)}, u32[]{:S(2)}) collective-permute-start(bf16[2,128,1024]{2,1,0:T(8,128)(2,1)} %get-tuple-element.110.refs_0_), channel_id=1, source_target_pairs={{0,8},{4,12},{8,0},{12,4},{16,24},{20,28},{24,16},{28,20},{1,9},{5... | collective-permute-start | bytes 1572872 | tf_op jit(solution)/shard_map/ppermute | solution.py:687
  102.6 23.1 %collective-permute-start.30 = (bf16[2,128,1024]{2,1,0:T(8,128)(2,1)}, bf16[2,128,1024]{2,1,0:T(8,128)(2,1)S(1)}, u32[]{:S(2)}, u32[]{:S(2)}) collective-permute-start(bf16[2,128,1024]{2,1,0:T(8,128)(2,1)} %get-tuple-element.111), channel_id=1, source_target_pairs={{0,16},{4,20},{8,24},{12,28},{16,0},{20,4},{24,8},{28,12},{1,17},{... | collective-permute-start | bytes 1572872 | tf_op jit(solution)/shard_map/ppermute | solution.py:687
  103.1 22.6 %collective-permute-start.31 = (bf16[2,128,1024]{2,1,0:T(8,128)(2,1)}, bf16[2,128,1024]{2,1,0:T(8,128)(2,1)S(1)}, u32[]{:S(2)}, u32[]{:S(2)}) collective-permute-start(bf16[2,128,1024]{2,1,0:T(8,128)(2,1)} %get-tuple-element.112), channel_id=1, source_target_pairs={{0,24},{4,28},{8,16},{12,20},{16,8},{20,12},{24,0},{28,4},{1,25},{... | collective-permute-start | bytes 1572872 | tf_op jit(solution)/shard_map/ppermute | solution.py:687
  117.7 21.8 %collective-permute-start.28 = (bf16[3,128,1024]{2,1,0:T(8,128)(2,1)}, bf16[3,128,1024]{2,1,0:T(8,128)(2,1)}, u32[]{:S(2)}, u32[]{:S(2)}) collective-permute-start(bf16[3,128,1024]{2,1,0:T(8,128)(2,1)} %get-tuple-element.109.refs_0_.refs_3_), channel_id=1, source_target_pairs={{0,1},{3,2},{4,5},{7,6},{8,9},{11,10},{12,13},{15,14},{16,17},{19,... | collective-permute-start | bytes 2359304 | tf_op jit(solution)/shard_map/ppermute | solution.py:691
  120.9 18.6 %collective-permute-start.27 = (bf16[2,128,1024]{2,1,0:T(8,128)(2,1)S(1)}, bf16[2,128,1024]{2,1,0:T(8,128)(2,1)S(1)}, u32[]{:S(2)}, u32[]{:S(2)}) collective-permute-start(bf16[2,128,1024]{2,1,0:T(8,128)(2,1)S(1)} %slice_add_fusion), channel_id=1, source_target_pairs={{1,2},{2,1},{5,6},{6,5},{9,10},{10,9},{13,14},{14,13},{17,18},{18,... | collective-permute-start | bytes 1572872 | tf_op jit(solution)/shard_map/ppermute | solution.py:691
  136.6 14.2 %collective-permute-start.34 = (bf16[1,256,1024]{2,1,0:T(8,128)(2,1)}, bf16[1,256,1024]{2,1,0:T(8,128)(2,1)S(1)}, u32[]{:S(2)}, u32[]{:S(2)}) collective-permute-start(bf16[1,256,1024]{2,1,0:T(8,128)(2,1)} %get-tuple-element.115), channel_id=1, source_target_pairs={{0,1},{3,2},{4,5},{7,6},{8,9},{11,10},{12,13},{15,14},{16,17},{19,... | collective-permute-start | bytes 1572872 | tf_op jit(solution)/shard_map/ppermute | solution.py:691
  138.1 22.8 %collective-permute-start.36 = (bf16[1,256,1024]{2,1,0:T(8,128)(2,1)}, bf16[1,256,1024]{2,1,0:T(8,128)(2,1)S(1)}, u32[]{:S(2)}, u32[]{:S(2)}) collective-permute-start(bf16[1,256,1024]{2,1,0:T(8,128)(2,1)} %get-tuple-element.121), channel_id=1, source_target_pairs={{0,1},{3,2},{4,5},{7,6},{8,9},{11,10},{12,13},{15,14},{16,17},{19,... | collective-permute-start | bytes 1572872 | tf_op jit(solution)/shard_map/ppermute | solution.py:691
  153.9 14.0 %collective-permute-start.33 = (bf16[1,256,1024]{2,1,0:T(8,128)(2,1)}, bf16[1,256,1024]{2,1,0:T(8,128)(2,1)}, u32[]{:S(2)}, u32[]{:S(2)}) collective-permute-start(bf16[1,256,1024]{2,1,0:T(8,128)(2,1)} %outer.1.refs_1_), channel_id=1, source_target_pairs={{1,0},{2,3},{5,4},{6,7},{9,8},{10,11},{13,12},{14,15},{17,16},{18,... | collective-permute-start | bytes 1572872 | tf_op jit(solution)/shard_map/ppermute | solution.py:691
  161.2 23.6 %collective-permute-start.38 = (bf16[1,256,1024]{2,1,0:T(8,128)(2,1)S(1)}, bf16[1,256,1024]{2,1,0:T(8,128)(2,1)S(1)}, u32[]{:S(2)}, u32[]{:S(2)}) collective-permute-start(bf16[1,256,1024]{2,1,0:T(8,128)(2,1)S(1)} %add.18), channel_id=1, source_target_pairs={{1,2},{2,1},{5,6},{6,5},{9,10},{10,9},{13,14},{14,13},{17,18},{18,... | collective-permute-start | bytes 1572872 | tf_op jit(solution)/shard_map/ppermute | solution.py:691
  168.1 16.7 %collective-permute-start.37 = (bf16[1,256,1024]{2,1,0:T(8,128)(2,1)S(1)}, bf16[1,256,1024]{2,1,0:T(8,128)(2,1)S(1)}, u32[]{:S(2)}, u32[]{:S(2)}) collective-permute-start(bf16[1,256,1024]{2,1,0:T(8,128)(2,1)S(1)} %copy-done.24), channel_id=1, source_target_pairs={{0,1},{3,2},{4,5},{7,6},{8,9},{11,10},{12,13},{15,14},{16,17},{19,... | collective-permute-start | bytes 1572872 | tf_op jit(solution)/shard_map/ppermute | solution.py:691
  171.4 13.4 %collective-permute-start.39 = (bf16[1,256,1024]{2,1,0:T(8,128)(2,1)S(1)}, bf16[1,256,1024]{2,1,0:T(8,128)(2,1)}, u32[]{:S(2)}, u32[]{:S(2)}) collective-permute-start(bf16[1,256,1024]{2,1,0:T(8,128)(2,1)S(1)} %add.19), channel_id=1, source_target_pairs={{1,0},{2,3},{5,4},{6,7},{9,8},{10,11},{13,12},{14,15},{17,16},{18,... | collective-permute-start | bytes 1572872 | tf_op jit(solution)/shard_map/ppermute | solution.py:691
  (52 other events, 368.4 us)

commit v12 on v11

--- a/solution.py
+++ b/solution.py
@@ -647,7 +647,7 @@
         + [pl.BlockSpec(memory_space=pl.ANY)] * len(afters)
         + in_vmem(len(dcums) + 3),
         out_specs=pl.BlockSpec(memory_space=pltpu.VMEM),
-        compiler_params=grant(60),
+        compiler_params=grant(16),
         cost_estimate=cost(0.2),
         name="adjoint",
     )(ints, *afters, *dcums, unit, rows, inverse)
@@ -677,7 +677,7 @@
         out_shape=jax.ShapeDtypeStruct(house_dirs.shape, F32),
         in_specs=in_smem(1) + in_vmem(4),
         out_specs=pl.BlockSpec(memory_space=pltpu.VMEM),
-        compiler_params=grant(60),
+        compiler_params=grant(12),
         cost_estimate=cost(2),
         name="house_grad",
     )(ints, got, unit, rows, house_dirs)
@@ -717,7 +717,7 @@
         + [pl.BlockSpec((1, rows, tile), lambda t: (0, 0, t))] * len(parts),
         out_specs=pl.BlockSpec((rows, tile), lambda t: (band, t)),
         input_output_aliases={1: 0},
-        compiler_params=grant(60),
+        compiler_params=grant(12),
         cost_estimate=cost(2),
         name="last_band",
     )(line_ends(), share, *parts)
@@ -745,7 +745,7 @@
         out_shape=jax.ShapeDtypeStruct(firsts.shape, BF16),
         in_specs=[both, swapped, swapped],
         out_specs=both,
-        compiler_params=grant(60),
+        compiler_params=grant(12),
         cost_estimate=cost(2),
         name="outer",
     )(firsts, low, high)
@@ -774,7 +774,7 @@
         out_shape=jax.ShapeDtypeStruct((bands * height, width), BF16),
         in_specs=in_smem(1) + [both] * 2 + [part] * len(parts),
         out_specs=pl.BlockSpec((height, tile), lambda t: (0, t)),
-        compiler_params=grant(60),
+        compiler_params=grant(12),
         cost_estimate=cost(2),
         name="first_band",
     )(line_ends(), firsts, outward, *parts)
@@ -789,12 +789,14 @@
     in_far, other = lax.optimization_barrier((in_far, other))
     sum_far = far + in_far
     swap_far = slide(sum_far, MIDDLE)
+    other, _ = lax.optimization_barrier((other, sum_far))
+    other = exchange(other)
     swap_last, *_ = lax.optimization_barrier((swap_last, earlier, sum_far))
     outer = first + swap_last
     outward = slide(outer, OUTWARD)
-    other, near, _ = lax.optimization_barrier((other, near, outer))
+    near, _ = lax.optimization_barrier((near, outer))
     in_near = slide(near, INWARD)
-    return (first, near, in_near, swap_far, outward), exchange(other), outer
+    return (first, near, in_near, swap_far, outward), other, outer
 
 
 def shards(

time: 190 us -> 196 us (1.032)
  starting transfers between devices: 47 us -> 54 us
  other arithmetic: 2.7 us -> 8.03 us
  Pallas kernels: 90.1 us -> 85.6 us
  local copies, waits for them, and re-layouts: 10.4 us -> 8.22 us
    ppermute x11, starting transfers between devices: 18.7 us -> 25.6 us  [slide(): return lax.ppermute(value, 'head', pairs)]
    ppermute x11, waiting for transfers between devices: 6.63 us -> 10.5 us  [slide(): return lax.ppermute(value, 'head', pairs)]
    all_to_all x1, waiting for transfers between devices: 2.89 us -> 0.01 us  [share_sums(): return lax.all_to_all(sums, 'ctx', split_axis=0, concat_axis=0, tiled=True)]
    unnamed x72, local copies, waits for them, and re-layouts: 10.2 us -> 8.06 us
    pallas_call x1, Pallas kernels: 2.16 us -> 0.13 us  [run_outer(): pl.pallas_call(outer_kernel, grid=(1,), out_shape=jax.ShapeDtypeStruct(fi...]
  transfers between devices with their start and end apart: 41 -> 41, of which waited for: 11 -> 11; matrix products, arithmetic and copies ran while one was open for 2% -> 5% of each run, Pallas kernels for 38% -> 35%
where the time goes in v12:
time: 196 us; the launch traced here: 195 us
  Pallas kernels  85.6 us (44%)
  starting transfers between devices  54 us (28%)
  waiting for transfers between devices  38.2 us (19%)
  local copies, waits for them, and re-layouts  8.22 us (4%)
  other arithmetic  8.03 us (4%)
    pallas_call x3, Pallas kernels, run_project(): pl.pallas_call(functools.partial(project_kernel, heads, len(parts[0]), si...  32.8 us
    ppermute x29, waiting for transfers between devices, hop(): return lax.ppermute(value, 'ctx', [(i, i ^ distance) for i in range(count)])  27.7 us
    ppermute x11, starting transfers between devices, slide(): return lax.ppermute(value, 'head', pairs)  25.6 us
    ppermute x29, starting transfers between devices, hop(): return lax.ppermute(value, 'ctx', [(i, i ^ distance) for i in range(count)])  25 us
    pallas_call x1, Pallas kernels, run_attend(): pl.pallas_call(functools.partial(attend_kernel, heads, blocks, places, pi...  14.8 us
    ppermute x11, waiting for transfers between devices, slide(): return lax.ppermute(value, 'head', pairs)  10.5 us
    pallas_call x3, Pallas kernels, run_merge(): pl.pallas_call(merge_kernel, grid=(size, cut), out_shape=[jax.ShapeDtypeS...  8.82 us
    unnamed x72, local copies, waits for them, and re-layouts  8.06 us
  transfers between devices with their start and end apart: 41, of which 11 were waited for; matrix products, arithmetic and copies ran while one was open for 5% of the time, Pallas kernels for 35%

profile of v12, /device:TPU:0, one launch (start us, length us, event | category | flops | bytes accessed | tf_op | source)
XLA Modules:
  0.0 195.1 jit_solution(2517915923893135978)
XLA Ops:
  0.6 3.0 %collective-permute-start.1 = (bf16[512,512]{1,0:T(8,128)(2,1)}, bf16[512,512]{1,0:T(8,128)(2,1)S(1)}, u32[]{:S(2)}, u32[]{:S(2)}) collective-permute-start(bf16[512,512]{1,0:T(8,128)(2,1)} %refs_20_.1), channel_id=1, source_target_pairs={{0,8},{4,12},{8,0},{12,4},{16,24},{20,28},{24,16},{28,20},{1,9},{5... | collective-permute-start | bytes 1572872 | tf_op jit(solution)/shard_map/ppermute | solution.py:687
  8.2 8.4 %collective-permute-done.1.refs_6_ = bf16[512,512]{1,0:T(8,128)(2,1)S(1)} collective-permute-done((bf16[512,512]{1,0:T(8,128)(2,1)}, bf16[512,512]{1,0:T(8,128)(2,1)S(1)}, u32[]{:S(2)}, u32[]{:S(2)}) %collective-permute-start.1) | collective-permute-done | bytes 524320 | tf_op jit(solution)/shard_map/ppermute | solution.py:687
  22.3 5.1 %collective-permute-done.refs_5_ = bf16[512,512]{1,0:T(8,128)(2,1)S(1)} collective-permute-done((bf16[512,512]{1,0:T(8,128)(2,1)}, bf16[512,512]{1,0:T(8,128)(2,1)S(1)}, u32[]{:S(2)}, u32[]{:S(2)}) %collective-permute-start) | collective-permute-done | bytes 524320 | tf_op jit(solution)/shard_map/ppermute | solution.py:687
  31.3 4.5 %house_chain.1 = (f32[32,512]{1,0:T(8,128)S(1)}, f32[32,512]{1,0:T(8,128)S(1)}, f32[4,32,32]{2,1,0:T(8,128)S(1)}, bf16[4,128,96]{2,1,0:T(8,128)(2,1)S(1)}, bf16[4,96,128]{2,1,0:T(8,128)(2,1)S(1)}) custom-call(s32[17]{0:T(128)S(1)} %pad_add_fusion.ints_ref.refs_0_.base_ref, f32[8,512]{1,0:T(8,128)S(1)} %pad_maximum_fusion.refs_0_, ...), custom_call_target="tpu_custom_call" | custom-call | flops 6899999744 | bytes 1048576 | tf_op jit(solution)/shard_map/house_chain/pallas_call | solution.py:119
  36.8 5.5 %rotate.1 = (bf16[512,512]{1,0:T(8,128)(2,1)S(1)}, bf16[512,512]{1,0:T(8,128)(2,1)S(1)}, bf16[4,4,128,128]{3,2,1,0:T(8,128)(2,1)S(1)}, bf16[8,4,256,128]{3,2,1,0:T(8,128)(2,1)S(1)}) custom-call(s32[17]{0:T(128)S(1)} %pad_add_fusion.ints_ref.refs_0_.base_ref, bf16[4,128,96]{2,1,0:T(8,128)(2,1)S(1)} %get-tuple-element.75.wide_ref, ...), custom_call_target="tpu_custom_call" | custom-call | flops 10350000128 | bytes 1048576 | tf_op jit(solution)/shard_map/rotate/pallas_call | solution.py:187
  45.1 14.8 %attend.1 = (bf16[512,512]{1,0:T(8,128)(2,1)}, f32[4,4,128,128]{3,2,1,0:T(8,128)}, f32[512,512]{1,0:T(8,128)}, f32[512,512]{1,0:T(8,128)}, bf16[1,4,128,1024]{3,...) custom-call(s32[17]{0:T(128)S(1)} %pad_add_fusion.ints_ref.refs_0_.b, ...), custom_call_target="tpu_custom_call" | custom-call | flops 17250000896 | bytes 1048576 | tf_op jit(solution)/shard_map/attend/pallas_call | solution.py:376
  60.1 2.7 %collective-permute-done.18.got_ref = bf16[1,4,128,1024]{3,2,1,0:T(8,128)(2,1)S(1)} collective-permute-done((bf16[1,4,128,1024]{3,2,1,0:T(8,128)(2,1)}, bf16[1,4,128,1024]{3,2,1,0:T(8,128)(2,1)S(1)}, u32[]{:S(2)}, u32[]{:S(2)}) %collective-permute-start.18) | collective-permute-done | bytes 1048608 | tf_op jit(solution)/shard_map/ppermute | solution.py:687
  64.0 2.3 %merge.3 = (bf16[1,128,1024]{2,1,0:T(8,128)(2,1)}, bf16[1,128,1024]{2,1,0:T(8,128)(2,1)}, bf16[1,128,1024]{2,1,0:T(8,128)(2,1)}) custom-call(bf16[1,4,128,1024]{3,2,1,0:T(8,128)(2,1)} %get-tuple-element.88.own_ref, bf16[1,4,128,1024]{3,2,1,0:T(8,128)(2,1)} %copy-done.27), custom_call_target="tpu_custom_call" | custom-call | flops 2300000000 | bytes 1048576 | tf_op jit(solution)/shard_map/merge/pallas_call | solution.py:405
  67.4 2.4 %collective-permute-start.22 = (bf16[1,128,1024]{2,1,0:T(8,128)(2,1)}, bf16[1,128,1024]{2,1,0:T(8,128)(2,1)}, u32[]{:S(2)}, u32[]{:S(2)}) collective-permute-start(bf16[1,128,1024]{2,1,0:T(8,128)(2,1)} %get-tuple-element.93), channel_id=1, source_target_pairs={{0,24},{4,28},{8,16},{12,20},{16,8},{20,12},{24,0},{28,4},{1,25},{... | collective-permute-start | bytes 786440 | tf_op jit(solution)/shard_map/ppermute | solution.py:687
  71.5 2.3 %merge.4 = (bf16[1,128,1024]{2,1,0:T(8,128)(2,1)}, bf16[1,128,1024]{2,1,0:T(8,128)(2,1)}, bf16[1,128,1024]{2,1,0:T(8,128)(2,1)}) custom-call(bf16[3,4,128,1024]{3,2,1,0:T(8,128)(2,1)} %get-tuple-element.84.own_ref, bf16[3,4,128,1024]{3,2,1,0:T(8,128)(2,1)} %copy-done.24, bf16[1,128,1024]{2,1,0:T(8,128)(2,1)} %get-tuple-element.89.refs_0_), custom_call_target="tpu_custom_call" | custom-call | flops 2300000000 | bytes 1048576 | tf_op jit(solution)/shard_map/merge/pallas_call | solution.py:405
  73.8 4.2 %merge.5 = (bf16[2,128,1024]{2,1,0:T(8,128)(2,1)}, bf16[2,128,1024]{2,1,0:T(8,128)(2,1)}, bf16[2,128,1024]{2,1,0:T(8,128)(2,1)}) custom-call(bf16[3,4,128,1024]{3,2,1,0:T(8,128)(2,1)} %get-tuple-element.84.own_ref, bf16[3,4,128,1024]{3,2,1,0:T(8,128)(2,1)} %copy-done.24, bf16[1,128,1024]{2,1,0:T(8,128)(2,1)} %get-tuple-element.103.refs_0_), custom_call_target="tpu_custom_call" | custom-call | flops 2300000000 | bytes 1048576 | tf_op jit(solution)/shard_map/merge/pallas_call | solution.py:405
  78.0 3.0 %collective-permute-done.21.refs_4_ = bf16[1,128,1024]{2,1,0:T(8,128)(2,1)} collective-permute-done((bf16[1,128,1024]{2,1,0:T(8,128)(2,1)}, bf16[1,128,1024]{2,1,0:T(8,128)(2,1)}, u32[]{:S(2)}, u32[]{:S(2)}) %collective-permute-start.21) | collective-permute-done | bytes 262176 | tf_op jit(solution)/shard_map/ppermute | solution.py:687
  84.5 10.4 %project.3 = (bf16[3,128,1024]{2,1,0:T(8,128)(2,1)}, f32[1,4,128,128]{3,2,1,0:T(8,128)}, bf16[128,512]{1,0:T(8,128)(2,1)}, bf16[128,512]{1,0:T(8,128)(2,1)}) custom-call(s32[1]{0:T(128)} %bitcast.1.flip_ref, bf16[2,128,1024]{2,1,0:T(8,128)(2,1)} %get-tuple-element.110.refs_0_, bf16[4,128,1024]{2,1,0:T(8,128)(2,1)} %bitcast.14, ...), custom_call_target="tpu_custom_call" | custom-call | flops 10350000128 | bytes 1048576 | tf_op jit(solution)/shard_map/project/pallas_call | solution.py:552
  95.0 3.8 %collective-permute-start.26 = (bf16[3,128,1024]{2,1,0:T(8,128)(2,1)}, bf16[3,128,1024]{2,1,0:T(8,128)(2,1)S(1)}, u32[]{:S(2)}, u32[]{:S(2)}) collective-permute-start(bf16[3,128,1024]{2,1,0:T(8,128)(2,1)} %get-tuple-element.98.refs_0_), channel_id=1, source_target_pairs={{0,1},{3,2},{4,5},{7,6},{8,9},{11,10},{12,13},{15,14},{16,17},{19,... | collective-permute-start | bytes 2359304 | tf_op jit(solution)/shard_map/ppermute | solution.py:691
  102.4 13.1 %project.4 = (bf16[1,256,1024]{2,1,0:T(8,128)(2,1)}, bf16[3,128,1024]{2,1,0:T(8,128)(2,1)}, f32[1,4,128,128]{3,2,1,0:T(8,128)}, bf16[128,512]{1,0:T(8,128)(2,1)}, bf16[128,512]{1,0:T(8,128)(2,1)}) custom-call(s32[1]{0:T(128)} %bitcast.1.flip_ref, bf16[3,128,1024]{2,1,0:T(8,128)(2,1)} %get-tuple-element.98.refs_0_, bf16[12,128,1024]{2,1,0:T(8,128)(2,1)} %bitcast.7, ...), custom_call_target="tpu_custom_call" | custom-call | flops 13799999488 | bytes 1048576 | tf_op jit(solution)/shard_map/project/pallas_call | solution.py:552
  119.5 4.1 %collective-permute-done.30.refs_4_.refs_9_ = bf16[2,128,1024]{2,1,0:T(8,128)(2,1)} collective-permute-done((bf16[2,128,1024]{2,1,0:T(8,128)(2,1)}, bf16[2,128,1024]{2,1,0:T(8,128)(2,1)}, u32[]{:S(2)}, u32[]{:S(2)}) %collective-permute-start.30) | collective-permute-done | bytes 524320 | tf_op jit(solution)/shard_map/ppermute | solution.py:687
  123.6 9.3 %project.5 = (bf16[1,256,1024]{2,1,0:T(8,128)(2,1)}, bf16[1,256,1024]{2,1,0:T(8,128)(2,1)}, f32[2,4,128,128]{3,2,1,0:T(8,128)}, bf16[256,512]{1,0:T(8,128)(2,1)}, bf16[256,512]{1,0:T(8,128)(2,1)}) custom-call(s32[1]{0:T(128)} %bitcast.1.flip_ref, bf16[3,128,1024]{2,1,0:T(8,128)(2,1)} %get-tuple-element.109.refs_0_.refs_3_, bf16[12,128,1024]{2,1,0:T(8,128)(2,1)} %bitcast.8, ...), custom_call_target="tpu_custom_call" | custom-call | flops 6899999744 | bytes 1048576 | tf_op jit(solution)/shard_map/project/pallas_call | solution.py:552
  132.9 2.3 %collective-permute-start.34 = (bf16[1,256,1024]{2,1,0:T(8,128)(2,1)}, bf16[1,256,1024]{2,1,0:T(8,128)(2,1)}, u32[]{:S(2)}, u32[]{:S(2)}) collective-permute-start(bf16[1,256,1024]{2,1,0:T(8,128)(2,1)} %get-tuple-element.115), channel_id=1, source_target_pairs={{0,1},{3,2},{4,5},{7,6},{8,9},{11,10},{12,13},{15,14},{16,17},{19,... | collective-permute-start | bytes 1572872 | tf_op jit(solution)/shard_map/ppermute | solution.py:691
  139.0 7.9 %project_more.1 = (bf16[1,256,1024]{2,1,0:T(8,128)(2,1)}, bf16[1,256,1024]{2,1,0:T(8,128)(2,1)}) custom-call(s32[1]{0:T(128)} %bitcast.1.flip_ref, bf16[2,128,1024]{2,1,0:T(8,128)(2,1)} %slice_add_fusion.1.refs_0_, bf16[512,512]{1,0:T(8,128)(2,1)} %get-tuple-element.96.refs_8_.refs_6_.refs_11_.refs_13_.refs_1_, bf16[256,512]{1,0:T(8,128)(2,1)} %get-tuple-element.116.refs_2_, ...), custom_call_target="tpu_custom_call" | custom-call | flops 6899999744 | bytes 1048576 | tf_op jit(solution)/shard_map/project_more/pallas_call | solution.py:511
  154.7 4.7 %adjoint.1 = f32[8,4,1024]{2,1,0:T(4,128)} custom-call(s32[17]{0:T(128)S(1)} %pad_add_fusion.ints_ref.refs_0_.base_ref, bf16[1,256,1024]{2,1,0:T(8,128)(2,1)S(1)} %add.17.refs_0_, bf16[1,256,1024]{2,1,0:T(8,128)(2,1)S(1)} %outer.1.refs_1_, f32[1,4,128,128]{3,2,1,0:T(8,128)S(1)} %copy-done.10, f32[1,4,128,128]{3,2,1,0:T(8,128)S(1)} %copy-done.11, ...), custom_call_target="tpu_custom_call" | custom-call | flops 230000000 | bytes 1048576 | tf_op jit(solution)/shard_map/adjoint/pallas_call | solution.py:643
  161.4 3.4 %all-to-all-start = ((f32[8,4,1024]{2,1,0:T(4,128)}), f32[8,4,1024]{2,1,0:T(4,128)S(1)}, u32[]{:S(2)}, u32[]{:S(2)}) async-start(f32[8,4,1024]{2,1,0:T(4,128)} %adjoint.1), calls=%async_computation | async-start | bytes 262144 | tf_op jit(solution)/shard_map/all_to_all | solution.py:865
  168.3 8.7 %collective-permute-start.37 = (bf16[1,256,1024]{2,1,0:T(8,128)(2,1)}, bf16[1,256,1024]{2,1,0:T(8,128)(2,1)}, u32[]{:S(2)}, u32[]{:S(2)}) collective-permute-start(bf16[1,256,1024]{2,1,0:T(8,128)(2,1)} %get-tuple-element.131.near_ref), channel_id=1, source_target_pairs={{0,1},{3,2},{4,5},{7,6},{8,9},{11,10},{12,13},{15,14},{16,17},{19,... | collective-permute-start | bytes 1572872 | tf_op jit(solution)/shard_map/ppermute | solution.py:691
  182.7 5.3 %collective-permute-done.37.inward_ref = bf16[1,256,1024]{2,1,0:T(8,128)(2,1)} collective-permute-done((bf16[1,256,1024]{2,1,0:T(8,128)(2,1)}, bf16[1,256,1024]{2,1,0:T(8,128)(2,1)}, u32[]{:S(2)}, u32[]{:S(2)}) %collective-permute-start.37) | collective-permute-done | bytes 524320 | tf_op jit(solution)/shard_map/ppermute | solution.py:691
  188.0 4.9 %collective-permute-done.39.refs_0_ = bf16[1,256,1024]{2,1,0:T(8,128)(2,1)} collective-permute-done((bf16[1,256,1024]{2,1,0:T(8,128)(2,1)}, bf16[1,256,1024]{2,1,0:T(8,128)(2,1)}, u32[]{:S(2)}, u32[]{:S(2)}) %collective-permute-start.39) | collective-permute-done | bytes 524320 | tf_op jit(solution)/shard_map/ppermute | solution.py:691
  (155 shorter events, 57.8 us)
Async XLA Ops:
  0.6 16.0 %collective-permute-start.1 = (bf16[512,512]{1,0:T(8,128)(2,1)}, bf16[512,512]{1,0:T(8,128)(2,1)S(1)}, u32[]{:S(2)}, u32[]{:S(2)}) collective-permute-start(bf16[512,512]{1,0:T(8,128)(2,1)} %refs_20_.1), channel_id=1, source_target_pairs={{0,8},{4,12},{8,0},{12,4},{16,24},{20,28},{24,16},{28,20},{1,9},{5... | collective-permute-start | bytes 1572872 | tf_op jit(solution)/shard_map/ppermute | solution.py:687
  3.6 15.1 %collective-permute-start.2 = (bf16[512,512]{1,0:T(8,128)(2,1)}, bf16[512,512]{1,0:T(8,128)(2,1)S(1)}, u32[]{:S(2)}, u32[]{:S(2)}) collective-permute-start(bf16[512,512]{1,0:T(8,128)(2,1)} %refs_14_.3), channel_id=1, source_target_pairs={{0,16},{4,20},{8,24},{12,28},{16,0},{20,4},{24,8},{28,12},{1,17},{... | collective-permute-start | bytes 1572872 | tf_op jit(solution)/shard_map/ppermute | solution.py:687
  5.2 22.2 %collective-permute-start = (bf16[512,512]{1,0:T(8,128)(2,1)}, bf16[512,512]{1,0:T(8,128)(2,1)S(1)}, u32[]{:S(2)}, u32[]{:S(2)}) collective-permute-start(bf16[512,512]{1,0:T(8,128)(2,1)} %refs_14_.3), channel_id=1, source_target_pairs={{0,8},{4,12},{8,0},{12,4},{16,24},{20,28},{24,16},{28,20},{1,9},{5... | collective-permute-start | bytes 1572872 | tf_op jit(solution)/shard_map/ppermute | solution.py:687
  5.7 23.4 %collective-permute-start.3 = (bf16[512,512]{1,0:T(8,128)(2,1)}, bf16[512,512]{1,0:T(8,128)(2,1)}, u32[]{:S(2)}, u32[]{:S(2)}) collective-permute-start(bf16[512,512]{1,0:T(8,128)(2,1)} %refs_20_.1), channel_id=1, source_target_pairs={{0,16},{4,20},{8,24},{12,28},{16,0},{20,4},{24,8},{28,12},{1,17},{... | collective-permute-start | bytes 1572872 | tf_op jit(solution)/shard_map/ppermute | solution.py:687
  27.4 15.0 %collective-permute-start.14 = (bf16[512,512]{1,0:T(8,128)(2,1)S(1)}, bf16[512,512]{1,0:T(8,128)(2,1)S(1)}, u32[]{:S(2)}, u32[]{:S(2)}) collective-permute-start(bf16[512,512]{1,0:T(8,128)(2,1)S(1)} %collective-permute-done.2.refs_9_), channel_id=1, source_target_pairs={{0,8},{4,12},{8,0},{12,4},{16,24},{20,28},{24,16},{28,20},{1,9},{5... | collective-permute-start | bytes 1572872 | tf_op jit(solution)/shard_map/ppermute | solution.py:687
  29.1 13.3 %collective-permute-start.15 = (bf16[512,512]{1,0:T(8,128)(2,1)S(1)}, bf16[512,512]{1,0:T(8,128)(2,1)S(1)}, u32[]{:S(2)}, u32[]{:S(2)}) collective-permute-start(bf16[512,512]{1,0:T(8,128)(2,1)S(1)} %collective-permute-done.1.refs_6_), channel_id=1, source_target_pairs={{0,16},{4,20},{8,24},{12,28},{16,0},{20,4},{24,8},{28,12},{1,17},{... | collective-permute-start | bytes 1572872 | tf_op jit(solution)/shard_map/ppermute | solution.py:687
  66.9 14.1 %collective-permute-start.21 = (bf16[1,128,1024]{2,1,0:T(8,128)(2,1)}, bf16[1,128,1024]{2,1,0:T(8,128)(2,1)}, u32[]{:S(2)}, u32[]{:S(2)}) collective-permute-start(bf16[1,128,1024]{2,1,0:T(8,128)(2,1)} %get-tuple-element.92), channel_id=1, source_target_pairs={{0,16},{4,20},{8,24},{12,28},{16,0},{20,4},{24,8},{28,12},{1,17},{... | collective-permute-start | bytes 786440 | tf_op jit(solution)/shard_map/ppermute | solution.py:687
  67.4 13.7 %collective-permute-start.22 = (bf16[1,128,1024]{2,1,0:T(8,128)(2,1)}, bf16[1,128,1024]{2,1,0:T(8,128)(2,1)}, u32[]{:S(2)}, u32[]{:S(2)}) collective-permute-start(bf16[1,128,1024]{2,1,0:T(8,128)(2,1)} %get-tuple-element.93), channel_id=1, source_target_pairs={{0,24},{4,28},{8,16},{12,20},{16,8},{20,12},{24,0},{28,4},{1,25},{... | collective-permute-start | bytes 786440 | tf_op jit(solution)/shard_map/ppermute | solution.py:687
  81.1 17.7 %collective-permute-start.23 = (bf16[1,128,1024]{2,1,0:T(8,128)(2,1)S(1)}, bf16[1,128,1024]{2,1,0:T(8,128)(2,1)S(1)}, u32[]{:S(2)}, u32[]{:S(2)}) collective-permute-start(bf16[1,128,1024]{2,1,0:T(8,128)(2,1)S(1)} %copy-done.33), channel_id=1, source_target_pairs={{0,8},{4,12},{8,0},{12,4},{16,24},{20,28},{24,16},{28,20},{1,9},{5... | collective-permute-start | bytes 786440 | tf_op jit(solution)/shard_map/ppermute | solution.py:687
  82.6 16.2 %collective-permute-start.24 = (bf16[1,128,1024]{2,1,0:T(8,128)(2,1)S(1)}, bf16[1,128,1024]{2,1,0:T(8,128)(2,1)S(1)}, u32[]{:S(2)}, u32[]{:S(2)}) collective-permute-start(bf16[1,128,1024]{2,1,0:T(8,128)(2,1)S(1)} %copy-done.31), channel_id=1, source_target_pairs={{0,16},{4,20},{8,24},{12,28},{16,0},{20,4},{24,8},{28,12},{1,17},{... | collective-permute-start | bytes 786440 | tf_op jit(solution)/shard_map/ppermute | solution.py:687
  83.1 15.7 %collective-permute-start.25 = (bf16[1,128,1024]{2,1,0:T(8,128)(2,1)S(1)}, bf16[1,128,1024]{2,1,0:T(8,128)(2,1)S(1)}, u32[]{:S(2)}, u32[]{:S(2)}) collective-permute-start(bf16[1,128,1024]{2,1,0:T(8,128)(2,1)S(1)} %copy-done.29), channel_id=1, source_target_pairs={{0,24},{4,28},{8,16},{12,20},{16,8},{20,12},{24,0},{28,4},{1,25},{... | collective-permute-start | bytes 786440 | tf_op jit(solution)/shard_map/ppermute | solution.py:687
  95.0 21.9 %collective-permute-start.26 = (bf16[3,128,1024]{2,1,0:T(8,128)(2,1)}, bf16[3,128,1024]{2,1,0:T(8,128)(2,1)S(1)}, u32[]{:S(2)}, u32[]{:S(2)}) collective-permute-start(bf16[3,128,1024]{2,1,0:T(8,128)(2,1)} %get-tuple-element.98.refs_0_), channel_id=1, source_target_pairs={{0,1},{3,2},{4,5},{7,6},{8,9},{11,10},{12,13},{15,14},{16,17},{19,... | collective-permute-start | bytes 2359304 | tf_op jit(solution)/shard_map/ppermute | solution.py:691
  98.8 20.6 %collective-permute-start.29 = (bf16[2,128,1024]{2,1,0:T(8,128)(2,1)}, bf16[2,128,1024]{2,1,0:T(8,128)(2,1)S(1)}, u32[]{:S(2)}, u32[]{:S(2)}) collective-permute-start(bf16[2,128,1024]{2,1,0:T(8,128)(2,1)} %get-tuple-element.110.refs_0_), channel_id=1, source_target_pairs={{0,8},{4,12},{8,0},{12,4},{16,24},{20,28},{24,16},{28,20},{1,9},{5... | collective-permute-start | bytes 1572872 | tf_op jit(solution)/shard_map/ppermute | solution.py:687
  100.4 23.2 %collective-permute-start.30 = (bf16[2,128,1024]{2,1,0:T(8,128)(2,1)}, bf16[2,128,1024]{2,1,0:T(8,128)(2,1)}, u32[]{:S(2)}, u32[]{:S(2)}) collective-permute-start(bf16[2,128,1024]{2,1,0:T(8,128)(2,1)} %get-tuple-element.111), channel_id=1, source_target_pairs={{0,16},{4,20},{8,24},{12,28},{16,0},{20,4},{24,8},{28,12},{1,17},{... | collective-permute-start | bytes 1572872 | tf_op jit(solution)/shard_map/ppermute | solution.py:687
  100.9 22.7 %collective-permute-start.31 = (bf16[2,128,1024]{2,1,0:T(8,128)(2,1)}, bf16[2,128,1024]{2,1,0:T(8,128)(2,1)}, u32[]{:S(2)}, u32[]{:S(2)}) collective-permute-start(bf16[2,128,1024]{2,1,0:T(8,128)(2,1)} %get-tuple-element.112), channel_id=1, source_target_pairs={{0,24},{4,28},{8,16},{12,20},{16,8},{20,12},{24,0},{28,4},{1,25},{... | collective-permute-start | bytes 1572872 | tf_op jit(solution)/shard_map/ppermute | solution.py:687
  115.5 21.8 %collective-permute-start.28 = (bf16[3,128,1024]{2,1,0:T(8,128)(2,1)}, bf16[3,128,1024]{2,1,0:T(8,128)(2,1)S(1)}, u32[]{:S(2)}, u32[]{:S(2)}) collective-permute-start(bf16[3,128,1024]{2,1,0:T(8,128)(2,1)} %get-tuple-element.109.refs_0_.refs_3_), channel_id=1, source_target_pairs={{0,1},{3,2},{4,5},{7,6},{8,9},{11,10},{12,13},{15,14},{16,17},{19,... | collective-permute-start | bytes 2359304 | tf_op jit(solution)/shard_map/ppermute | solution.py:691
  118.6 18.7 %collective-permute-start.27 = (bf16[2,128,1024]{2,1,0:T(8,128)(2,1)}, bf16[2,128,1024]{2,1,0:T(8,128)(2,1)S(1)}, u32[]{:S(2)}, u32[]{:S(2)}) collective-permute-start(bf16[2,128,1024]{2,1,0:T(8,128)(2,1)} %slice_add_fusion), channel_id=1, source_target_pairs={{1,2},{2,1},{5,6},{6,5},{9,10},{10,9},{13,14},{14,13},{17,18},{18,... | collective-permute-start | bytes 1572872 | tf_op jit(solution)/shard_map/ppermute | solution.py:691
  132.9 14.2 %collective-permute-start.34 = (bf16[1,256,1024]{2,1,0:T(8,128)(2,1)}, bf16[1,256,1024]{2,1,0:T(8,128)(2,1)}, u32[]{:S(2)}, u32[]{:S(2)}) collective-permute-start(bf16[1,256,1024]{2,1,0:T(8,128)(2,1)} %get-tuple-element.115), channel_id=1, source_target_pairs={{0,1},{3,2},{4,5},{7,6},{8,9},{11,10},{12,13},{15,14},{16,17},{19,... | collective-permute-start | bytes 1572872 | tf_op jit(solution)/shard_map/ppermute | solution.py:691
  135.2 24.2 %collective-permute-start.36 = (bf16[1,256,1024]{2,1,0:T(8,128)(2,1)}, bf16[1,256,1024]{2,1,0:T(8,128)(2,1)}, u32[]{:S(2)}, u32[]{:S(2)}) collective-permute-start(bf16[1,256,1024]{2,1,0:T(8,128)(2,1)} %get-tuple-element.121), channel_id=1, source_target_pairs={{0,1},{3,2},{4,5},{7,6},{8,9},{11,10},{12,13},{15,14},{16,17},{19,... | collective-permute-start | bytes 1572872 | tf_op jit(solution)/shard_map/ppermute | solution.py:691
  148.5 17.8 %collective-permute-start.35 = (bf16[1,256,1024]{2,1,0:T(8,128)(2,1)S(1)}, bf16[1,256,1024]{2,1,0:T(8,128)(2,1)}, u32[]{:S(2)}, u32[]{:S(2)}) collective-permute-start(bf16[1,256,1024]{2,1,0:T(8,128)(2,1)S(1)} %add.17.refs_0_), channel_id=1, source_target_pairs={{1,2},{2,1},{5,6},{6,5},{9,10},{10,9},{13,14},{14,13},{17,18},{18,... | collective-permute-start | bytes 1572872 | tf_op jit(solution)/shard_map/ppermute | solution.py:691
  161.4 16.9 %all-to-all-start = ((f32[8,4,1024]{2,1,0:T(4,128)}), f32[8,4,1024]{2,1,0:T(4,128)S(1)}, u32[]{:S(2)}, u32[]{:S(2)}) async-start(f32[8,4,1024]{2,1,0:T(4,128)} %adjoint.1), calls=%async_computation | async-start | bytes 262144 | tf_op jit(solution)/shard_map/all_to_all | solution.py:865
  164.8 17.8 %collective-permute-start.38 = (bf16[1,256,1024]{2,1,0:T(8,128)(2,1)}, bf16[1,256,1024]{2,1,0:T(8,128)(2,1)}, u32[]{:S(2)}, u32[]{:S(2)}) collective-permute-start(bf16[1,256,1024]{2,1,0:T(8,128)(2,1)} %add.18), channel_id=1, source_target_pairs={{1,2},{2,1},{5,6},{6,5},{9,10},{10,9},{13,14},{14,13},{17,18},{18,... | collective-permute-start | bytes 1572872 | tf_op jit(solution)/shard_map/ppermute | solution.py:691
  168.3 19.7 %collective-permute-start.37 = (bf16[1,256,1024]{2,1,0:T(8,128)(2,1)}, bf16[1,256,1024]{2,1,0:T(8,128)(2,1)}, u32[]{:S(2)}, u32[]{:S(2)}) collective-permute-start(bf16[1,256,1024]{2,1,0:T(8,128)(2,1)} %get-tuple-element.131.near_ref), channel_id=1, source_target_pairs={{0,1},{3,2},{4,5},{7,6},{8,9},{11,10},{12,13},{15,14},{16,17},{19,... | collective-permute-start | bytes 1572872 | tf_op jit(solution)/shard_map/ppermute | solution.py:691
  177.1 15.8 %collective-permute-start.39 = (bf16[1,256,1024]{2,1,0:T(8,128)(2,1)}, bf16[1,256,1024]{2,1,0:T(8,128)(2,1)}, u32[]{:S(2)}, u32[]{:S(2)}) collective-permute-start(bf16[1,256,1024]{2,1,0:T(8,128)(2,1)} %add.19), channel_id=1, source_target_pairs={{1,0},{2,3},{5,4},{6,7},{9,8},{10,11},{13,12},{14,15},{17,16},{18,... | collective-permute-start | bytes 1572872 | tf_op jit(solution)/shard_map/ppermute | solution.py:691
  (52 other events, 368.7 us)

commit v13 on v12

--- a/solution.py
+++ b/solution.py
@@ -789,14 +789,12 @@
     in_far, other = lax.optimization_barrier((in_far, other))
     sum_far = far + in_far
     swap_far = slide(sum_far, MIDDLE)
-    other, _ = lax.optimization_barrier((other, sum_far))
-    other = exchange(other)
     swap_last, *_ = lax.optimization_barrier((swap_last, earlier, sum_far))
     outer = first + swap_last
     outward = slide(outer, OUTWARD)
-    near, _ = lax.optimization_barrier((near, outer))
+    other, near, _ = lax.optimization_barrier((other, near, outer))
     in_near = slide(near, INWARD)
-    return (first, near, in_near, swap_far, outward), other, outer
+    return (first, near, in_near, swap_far, outward), exchange(other), outer
 
 
 def shards(

time: 196 us -> 188 us (0.959)
  waiting for transfers between devices: 38.2 us -> 31.6 us
  starting transfers between devices: 54 us -> 50.3 us
    ppermute x11, waiting for transfers between devices: 10.5 us -> 3.18 us  [slide(): return lax.ppermute(value, 'head', pairs)]
    ppermute x11, starting transfers between devices: 25.6 us -> 21.9 us  [slide(): return lax.ppermute(value, 'head', pairs)]
    unnamed x72 -> x66, local copies, waits for them, and re-layouts: 8.06 us -> 8.65 us
  transfers between devices with their start and end apart: 41 -> 41, of which waited for: 11 -> 10; matrix products, arithmetic and copies ran while one was open for 5% -> 5% of each run, Pallas kernels for 35% -> 37%
where the time goes in v13:
time: 188 us; the launch traced here: 186 us
  Pallas kernels  86.1 us (46%)
  starting transfers between devices  50.3 us (27%)
  waiting for transfers between devices  31.6 us (17%)
  local copies, waits for them, and re-layouts  8.82 us (5%)
  other arithmetic  8.12 us (4%)
    pallas_call x3, Pallas kernels, run_project(): pl.pallas_call(functools.partial(project_kernel, heads, len(parts[0]), si...  32.9 us
    ppermute x29, waiting for transfers between devices, hop(): return lax.ppermute(value, 'ctx', [(i, i ^ distance) for i in range(count)])  28.5 us
    ppermute x29, starting transfers between devices, hop(): return lax.ppermute(value, 'ctx', [(i, i ^ distance) for i in range(count)])  25 us
    ppermute x11, starting transfers between devices, slide(): return lax.ppermute(value, 'head', pairs)  21.9 us
    pallas_call x1, Pallas kernels, run_attend(): pl.pallas_call(functools.partial(attend_kernel, heads, blocks, places, pi...  15 us
    pallas_call x3, Pallas kernels, run_merge(): pl.pallas_call(merge_kernel, grid=(size, cut), out_shape=[jax.ShapeDtypeS...  8.91 us
    unnamed x66, local copies, waits for them, and re-layouts  8.65 us
    pallas_call x1, Pallas kernels, run_project_more(): pl.pallas_call(functools.partial(project_more_kernel, groups, layout, len...  7.91 us
  transfers between devices with their start and end apart: 41, of which 10 were waited for; matrix products, arithmetic and copies ran while one was open for 5% of the time, Pallas kernels for 37%

profile of v13, /device:TPU:0, one launch (start us, length us, event | category | flops | bytes accessed | tf_op | source)
XLA Modules:
  0.0 186.1 jit_solution(15836397318453018870)
XLA Ops:
  0.6 3.0 %collective-permute-start.1 = (bf16[512,512]{1,0:T(8,128)(2,1)}, bf16[512,512]{1,0:T(8,128)(2,1)S(1)}, u32[]{:S(2)}, u32[]{:S(2)}) collective-permute-start(bf16[512,512]{1,0:T(8,128)(2,1)} %refs_20_.1), channel_id=1, source_target_pairs={{0,8},{4,12},{8,0},{12,4},{16,24},{20,28},{24,16},{28,20},{1,9},{5... | collective-permute-start | bytes 1572872 | tf_op jit(solution)/shard_map/ppermute | solution.py:687
  8.2 8.4 %collective-permute-done.1.refs_6_ = bf16[512,512]{1,0:T(8,128)(2,1)S(1)} collective-permute-done((bf16[512,512]{1,0:T(8,128)(2,1)}, bf16[512,512]{1,0:T(8,128)(2,1)S(1)}, u32[]{:S(2)}, u32[]{:S(2)}) %collective-permute-start.1) | collective-permute-done | bytes 524320 | tf_op jit(solution)/shard_map/ppermute | solution.py:687
  22.3 5.1 %collective-permute-done.refs_5_ = bf16[512,512]{1,0:T(8,128)(2,1)S(1)} collective-permute-done((bf16[512,512]{1,0:T(8,128)(2,1)}, bf16[512,512]{1,0:T(8,128)(2,1)S(1)}, u32[]{:S(2)}, u32[]{:S(2)}) %collective-permute-start) | collective-permute-done | bytes 524320 | tf_op jit(solution)/shard_map/ppermute | solution.py:687
  31.3 4.5 %house_chain.1 = (f32[32,512]{1,0:T(8,128)S(1)}, f32[32,512]{1,0:T(8,128)S(1)}, f32[4,32,32]{2,1,0:T(8,128)S(1)}, bf16[4,128,96]{2,1,0:T(8,128)(2,1)S(1)}, bf16[4,96,128]{2,1,0:T(8,128)(2,1)S(1)}) custom-call(s32[17]{0:T(128)S(1)} %pad_add_fusion.ints_ref.refs_0_.base_ref, f32[8,512]{1,0:T(8,128)S(1)} %pad_maximum_fusion.refs_0_, ...), custom_call_target="tpu_custom_call" | custom-call | flops 6899999744 | bytes 1048576 | tf_op jit(solution)/shard_map/house_chain/pallas_call | solution.py:119
  36.8 5.5 %rotate.1 = (bf16[512,512]{1,0:T(8,128)(2,1)S(1)}, bf16[512,512]{1,0:T(8,128)(2,1)S(1)}, bf16[4,4,128,128]{3,2,1,0:T(8,128)(2,1)S(1)}, bf16[8,4,256,128]{3,2,1,0:T(8,128)(2,1)S(1)}) custom-call(s32[17]{0:T(128)S(1)} %pad_add_fusion.ints_ref.refs_0_.base_ref, bf16[4,128,96]{2,1,0:T(8,128)(2,1)S(1)} %get-tuple-element.75.wide_ref, ...), custom_call_target="tpu_custom_call" | custom-call | flops 10350000128 | bytes 1048576 | tf_op jit(solution)/shard_map/rotate/pallas_call | solution.py:187
  45.2 15.0 %attend.1 = (bf16[512,512]{1,0:T(8,128)(2,1)}, f32[4,4,128,128]{3,2,1,0:T(8,128)}, f32[512,512]{1,0:T(8,128)}, f32[512,512]{1,0:T(8,128)}, bf16[1,4,128,1024]{3,...) custom-call(s32[17]{0:T(128)S(1)} %pad_add_fusion.ints_ref.refs_0_.b, ...), custom_call_target="tpu_custom_call" | custom-call | flops 17250000896 | bytes 1048576 | tf_op jit(solution)/shard_map/attend/pallas_call | solution.py:376
  60.4 2.7 %collective-permute-done.18.got_ref = bf16[1,4,128,1024]{3,2,1,0:T(8,128)(2,1)S(1)} collective-permute-done((bf16[1,4,128,1024]{3,2,1,0:T(8,128)(2,1)}, bf16[1,4,128,1024]{3,2,1,0:T(8,128)(2,1)S(1)}, u32[]{:S(2)}, u32[]{:S(2)}) %collective-permute-start.18) | collective-permute-done | bytes 1048608 | tf_op jit(solution)/shard_map/ppermute | solution.py:687
  64.1 2.4 %merge.3 = (bf16[1,128,1024]{2,1,0:T(8,128)(2,1)}, bf16[1,128,1024]{2,1,0:T(8,128)(2,1)}, bf16[1,128,1024]{2,1,0:T(8,128)(2,1)}) custom-call(bf16[1,4,128,1024]{3,2,1,0:T(8,128)(2,1)} %get-tuple-element.88.own_ref, bf16[1,4,128,1024]{3,2,1,0:T(8,128)(2,1)} %copy-done.22), custom_call_target="tpu_custom_call" | custom-call | flops 2300000000 | bytes 1048576 | tf_op jit(solution)/shard_map/merge/pallas_call | solution.py:405
  67.6 2.4 %collective-permute-start.22 = (bf16[1,128,1024]{2,1,0:T(8,128)(2,1)}, bf16[1,128,1024]{2,1,0:T(8,128)(2,1)S(1)}, u32[]{:S(2)}, u32[]{:S(2)}) collective-permute-start(bf16[1,128,1024]{2,1,0:T(8,128)(2,1)} %get-tuple-element.93), channel_id=1, source_target_pairs={{0,24},{4,28},{8,16},{12,20},{16,8},{20,12},{24,0},{28,4},{1,25},{... | collective-permute-start | bytes 786440 | tf_op jit(solution)/shard_map/ppermute | solution.py:687
  70.0 2.3 %merge.4 = (bf16[1,128,1024]{2,1,0:T(8,128)(2,1)}, bf16[1,128,1024]{2,1,0:T(8,128)(2,1)}, bf16[1,128,1024]{2,1,0:T(8,128)(2,1)}) custom-call(bf16[3,4,128,1024]{3,2,1,0:T(8,128)(2,1)} %get-tuple-element.84.own_ref, bf16[3,4,128,1024]{3,2,1,0:T(8,128)(2,1)} %collective-permute-done.19.got_ref, bf16[1,128,1024]{2,1,0:T(8,128)(2,1)} %get-tuple-element.89.refs_0_), custom_call_target="tpu_custom_call" | custom-call | flops 2300000000 | bytes 1048576 | tf_op jit(solution)/shard_map/merge/pallas_call | solution.py:405
  72.3 4.2 %merge.5 = (bf16[2,128,1024]{2,1,0:T(8,128)(2,1)}, bf16[2,128,1024]{2,1,0:T(8,128)(2,1)}, bf16[2,128,1024]{2,1,0:T(8,128)(2,1)}) custom-call(bf16[3,4,128,1024]{3,2,1,0:T(8,128)(2,1)} %get-tuple-element.84.own_ref, bf16[3,4,128,1024]{3,2,1,0:T(8,128)(2,1)} %collective-permute-done.19.got_ref, bf16[1,128,1024]{2,1,0:T(8,128)(2,1)} %get-tuple-element.103.refs_0_), custom_call_target="tpu_custom_call" | custom-call | flops 2300000000 | bytes 1048576 | tf_op jit(solution)/shard_map/merge/pallas_call | solution.py:405
  76.5 4.5 %collective-permute-done.21.refs_4_ = bf16[1,128,1024]{2,1,0:T(8,128)(2,1)S(1)} collective-permute-done((bf16[1,128,1024]{2,1,0:T(8,128)(2,1)}, bf16[1,128,1024]{2,1,0:T(8,128)(2,1)S(1)}, u32[]{:S(2)}, u32[]{:S(2)}) %collective-permute-start.21) | collective-permute-done | bytes 262176 | tf_op jit(solution)/shard_map/ppermute | solution.py:687
  84.6 10.4 %project.3 = (bf16[3,128,1024]{2,1,0:T(8,128)(2,1)}, f32[1,4,128,128]{3,2,1,0:T(8,128)}, bf16[128,512]{1,0:T(8,128)(2,1)}, bf16[128,512]{1,0:T(8,128)(2,1)}) custom-call(s32[1]{0:T(128)} %bitcast.1.flip_ref, bf16[2,128,1024]{2,1,0:T(8,128)(2,1)} %get-tuple-element.110.refs_0_, bf16[4,128,1024]{2,1,0:T(8,128)(2,1)} %bitcast.11, ...), custom_call_target="tpu_custom_call" | custom-call | flops 10350000128 | bytes 1048576 | tf_op jit(solution)/shard_map/project/pallas_call | solution.py:552
  95.0 3.8 %collective-permute-start.26 = (bf16[3,128,1024]{2,1,0:T(8,128)(2,1)}, bf16[3,128,1024]{2,1,0:T(8,128)(2,1)S(1)}, u32[]{:S(2)}, u32[]{:S(2)}) collective-permute-start(bf16[3,128,1024]{2,1,0:T(8,128)(2,1)} %get-tuple-element.98.refs_0_), channel_id=1, source_target_pairs={{0,1},{3,2},{4,5},{7,6},{8,9},{11,10},{12,13},{15,14},{16,17},{19,... | collective-permute-start | bytes 2359304 | tf_op jit(solution)/shard_map/ppermute | solution.py:691
  102.4 13.2 %project.4 = (bf16[1,256,1024]{2,1,0:T(8,128)(2,1)}, bf16[3,128,1024]{2,1,0:T(8,128)(2,1)}, f32[1,4,128,128]{3,2,1,0:T(8,128)}, bf16[128,512]{1,0:T(8,128)(2,1)}, bf16[128,512]{1,0:T(8,128)(2,1)}) custom-call(s32[1]{0:T(128)} %bitcast.1.flip_ref, bf16[3,128,1024]{2,1,0:T(8,128)(2,1)} %get-tuple-element.98.refs_0_, bf16[12,128,1024]{2,1,0:T(8,128)(2,1)} %bitcast.7, ...), custom_call_target="tpu_custom_call" | custom-call | flops 13799999488 | bytes 1048576 | tf_op jit(solution)/shard_map/project/pallas_call | solution.py:552
  115.6 2.2 %collective-permute-start.28 = (bf16[3,128,1024]{2,1,0:T(8,128)(2,1)}, bf16[3,128,1024]{2,1,0:T(8,128)(2,1)}, u32[]{:S(2)}, u32[]{:S(2)}) collective-permute-start(bf16[3,128,1024]{2,1,0:T(8,128)(2,1)} %get-tuple-element.109.refs_0_.refs_3_), channel_id=1, source_target_pairs={{0,1},{3,2},{4,5},{7,6},{8,9},{11,10},{12,13},{15,14},{16,17},{19,... | collective-permute-start | bytes 2359304 | tf_op jit(solution)/shard_map/ppermute | solution.py:691
  122.9 9.3 %project.5 = (bf16[1,256,1024]{2,1,0:T(8,128)(2,1)}, bf16[1,256,1024]{2,1,0:T(8,128)(2,1)}, f32[2,4,128,128]{3,2,1,0:T(8,128)}, bf16[256,512]{1,0:T(8,128)(2,1)}, bf16[256,512]{1,0:T(8,128)(2,1)}) custom-call(s32[1]{0:T(128)} %bitcast.1.flip_ref, bf16[3,128,1024]{2,1,0:T(8,128)(2,1)} %get-tuple-element.109.refs_0_.refs_3_, bf16[12,128,1024]{2,1,0:T(8,128)(2,1)} %bitcast.8, ...), custom_call_target="tpu_custom_call" | custom-call | flops 6899999744 | bytes 1048576 | tf_op jit(solution)/shard_map/project/pallas_call | solution.py:552
  132.3 2.3 %collective-permute-start.34 = (bf16[1,256,1024]{2,1,0:T(8,128)(2,1)}, bf16[1,256,1024]{2,1,0:T(8,128)(2,1)}, u32[]{:S(2)}, u32[]{:S(2)}) collective-permute-start(bf16[1,256,1024]{2,1,0:T(8,128)(2,1)} %get-tuple-element.115), channel_id=1, source_target_pairs={{0,1},{3,2},{4,5},{7,6},{8,9},{11,10},{12,13},{15,14},{16,17},{19,... | collective-permute-start | bytes 1572872 | tf_op jit(solution)/shard_map/ppermute | solution.py:691
  139.5 7.9 %project_more.1 = (bf16[1,256,1024]{2,1,0:T(8,128)(2,1)}, bf16[1,256,1024]{2,1,0:T(8,128)(2,1)}) custom-call(s32[1]{0:T(128)} %bitcast.1.flip_ref, bf16[2,128,1024]{2,1,0:T(8,128)(2,1)} %slice_add_fusion.1.refs_0_, bf16[512,512]{1,0:T(8,128)(2,1)} %get-tuple-element.96.refs_8_.refs_6_.refs_11_.refs_13_.refs_1_, bf16[256,512]{1,0:T(8,128)(2,1)} %get-tuple-element.116.refs_2_, ...), custom_call_target="tpu_custom_call" | custom-call | flops 6899999744 | bytes 1048576 | tf_op jit(solution)/shard_map/project_more/pallas_call | solution.py:511
  152.6 4.7 %adjoint.1 = f32[8,4,1024]{2,1,0:T(4,128)} custom-call(s32[17]{0:T(128)S(1)} %pad_add_fusion.ints_ref.refs_0_.base_ref, bf16[1,256,1024]{2,1,0:T(8,128)(2,1)S(1)} %add.17.refs_0_, bf16[1,256,1024]{2,1,0:T(8,128)(2,1)S(1)} %outer.1.refs_1_, f32[1,4,128,128]{3,2,1,0:T(8,128)S(1)} %copy-done.6, f32[1,4,128,128]{3,2,1,0:T(8,128)S(1)} %copy-done.7, ...), custom_call_target="tpu_custom_call" | custom-call | flops 230000000 | bytes 1048576 | tf_op jit(solution)/shard_map/adjoint/pallas_call | solution.py:643
  160.9 3.2 %collective-permute-done.33.outward_ref = bf16[1,256,1024]{2,1,0:T(8,128)(2,1)S(1)} collective-permute-done((bf16[1,256,1024]{2,1,0:T(8,128)(2,1)S(1)}, bf16[1,256,1024]{2,1,0:T(8,128)(2,1)S(1)}, u32[]{:S(2)}, u32[]{:S(2)}) %collective-permute-start.33) | collective-permute-done | bytes 524320 | tf_op jit(solution)/shard_map/ppermute | solution.py:691
  165.8 4.8 %collective-permute-start.37 = (bf16[1,256,1024]{2,1,0:T(8,128)(2,1)}, bf16[1,256,1024]{2,1,0:T(8,128)(2,1)}, u32[]{:S(2)}, u32[]{:S(2)}) collective-permute-start(bf16[1,256,1024]{2,1,0:T(8,128)(2,1)} %get-tuple-element.132.near_ref), channel_id=1, source_target_pairs={{0,1},{3,2},{4,5},{7,6},{8,9},{11,10},{12,13},{15,14},{16,17},{19,... | collective-permute-start | bytes 1572872 | tf_op jit(solution)/shard_map/ppermute | solution.py:691
  171.9 3.4 %all-to-all-start = ((f32[8,4,1024]{2,1,0:T(4,128)}), f32[8,4,1024]{2,1,0:T(4,128)S(1)}, u32[]{:S(2)}, u32[]{:S(2)}) async-start(f32[8,4,1024]{2,1,0:T(4,128)} %adjoint.1), calls=%async_computation | async-start | bytes 262144 | tf_op jit(solution)/shard_map/all_to_all | solution.py:863
  183.7 2.4 %last_band.1 = bf16[512,1024]{1,0:T(8,128)(2,1)} custom-call(s32[1]{0:T(128)} %bitcast.ends_ref, bf16[512,1024]{1,0:T(8,128)(2,1)} %first_band.1.share_ref, bf16[1,256,1024]{2,1,0:T(8,128)(2,1)S(1)} %copy-done.3, bf16[1,256,1024]{2,1,0:T(8,128)(2,1)} %get-tuple-element.132.near_ref, ...), custom_call_target="tpu_custom_call", output_to_operand_aliasing={{}: (1, {})} | custom-call | flops 2300000000 | bytes 1048576 | tf_op jit(solution)/shard_map/last_band/pallas_call | solution.py:711
  (149 shorter events, 57.3 us)
Async XLA Ops:
  0.6 16.0 %collective-permute-start.1 = (bf16[512,512]{1,0:T(8,128)(2,1)}, bf16[512,512]{1,0:T(8,128)(2,1)S(1)}, u32[]{:S(2)}, u32[]{:S(2)}) collective-permute-start(bf16[512,512]{1,0:T(8,128)(2,1)} %refs_20_.1), channel_id=1, source_target_pairs={{0,8},{4,12},{8,0},{12,4},{16,24},{20,28},{24,16},{28,20},{1,9},{5... | collective-permute-start | bytes 1572872 | tf_op jit(solution)/shard_map/ppermute | solution.py:687
  3.6 15.1 %collective-permute-start.2 = (bf16[512,512]{1,0:T(8,128)(2,1)}, bf16[512,512]{1,0:T(8,128)(2,1)S(1)}, u32[]{:S(2)}, u32[]{:S(2)}) collective-permute-start(bf16[512,512]{1,0:T(8,128)(2,1)} %refs_14_.3), channel_id=1, source_target_pairs={{0,16},{4,20},{8,24},{12,28},{16,0},{20,4},{24,8},{28,12},{1,17},{... | collective-permute-start | bytes 1572872 | tf_op jit(solution)/shard_map/ppermute | solution.py:687
  5.2 22.2 %collective-permute-start = (bf16[512,512]{1,0:T(8,128)(2,1)}, bf16[512,512]{1,0:T(8,128)(2,1)S(1)}, u32[]{:S(2)}, u32[]{:S(2)}) collective-permute-start(bf16[512,512]{1,0:T(8,128)(2,1)} %refs_14_.3), channel_id=1, source_target_pairs={{0,8},{4,12},{8,0},{12,4},{16,24},{20,28},{24,16},{28,20},{1,9},{5... | collective-permute-start | bytes 1572872 | tf_op jit(solution)/shard_map/ppermute | solution.py:687
  5.7 23.4 %collective-permute-start.3 = (bf16[512,512]{1,0:T(8,128)(2,1)}, bf16[512,512]{1,0:T(8,128)(2,1)}, u32[]{:S(2)}, u32[]{:S(2)}) collective-permute-start(bf16[512,512]{1,0:T(8,128)(2,1)} %refs_20_.1), channel_id=1, source_target_pairs={{0,16},{4,20},{8,24},{12,28},{16,0},{20,4},{24,8},{28,12},{1,17},{... | collective-permute-start | bytes 1572872 | tf_op jit(solution)/shard_map/ppermute | solution.py:687
  27.4 15.0 %collective-permute-start.14 = (bf16[512,512]{1,0:T(8,128)(2,1)S(1)}, bf16[512,512]{1,0:T(8,128)(2,1)S(1)}, u32[]{:S(2)}, u32[]{:S(2)}) collective-permute-start(bf16[512,512]{1,0:T(8,128)(2,1)S(1)} %collective-permute-done.2.refs_9_), channel_id=1, source_target_pairs={{0,8},{4,12},{8,0},{12,4},{16,24},{20,28},{24,16},{28,20},{1,9},{5... | collective-permute-start | bytes 1572872 | tf_op jit(solution)/shard_map/ppermute | solution.py:687
  29.1 13.3 %collective-permute-start.15 = (bf16[512,512]{1,0:T(8,128)(2,1)S(1)}, bf16[512,512]{1,0:T(8,128)(2,1)S(1)}, u32[]{:S(2)}, u32[]{:S(2)}) collective-permute-start(bf16[512,512]{1,0:T(8,128)(2,1)S(1)} %collective-permute-done.1.refs_6_), channel_id=1, source_target_pairs={{0,16},{4,20},{8,24},{12,28},{16,0},{20,4},{24,8},{28,12},{1,17},{... | collective-permute-start | bytes 1572872 | tf_op jit(solution)/shard_map/ppermute | solution.py:687
  67.1 13.9 %collective-permute-start.21 = (bf16[1,128,1024]{2,1,0:T(8,128)(2,1)}, bf16[1,128,1024]{2,1,0:T(8,128)(2,1)S(1)}, u32[]{:S(2)}, u32[]{:S(2)}) collective-permute-start(bf16[1,128,1024]{2,1,0:T(8,128)(2,1)} %get-tuple-element.92), channel_id=1, source_target_pairs={{0,16},{4,20},{8,24},{12,28},{16,0},{20,4},{24,8},{28,12},{1,17},{... | collective-permute-start | bytes 786440 | tf_op jit(solution)/shard_map/ppermute | solution.py:687
  67.6 13.5 %collective-permute-start.22 = (bf16[1,128,1024]{2,1,0:T(8,128)(2,1)}, bf16[1,128,1024]{2,1,0:T(8,128)(2,1)S(1)}, u32[]{:S(2)}, u32[]{:S(2)}) collective-permute-start(bf16[1,128,1024]{2,1,0:T(8,128)(2,1)} %get-tuple-element.93), channel_id=1, source_target_pairs={{0,24},{4,28},{8,16},{12,20},{16,8},{20,12},{24,0},{28,4},{1,25},{... | collective-permute-start | bytes 786440 | tf_op jit(solution)/shard_map/ppermute | solution.py:687
  81.0 17.8 %collective-permute-start.23 = (bf16[1,128,1024]{2,1,0:T(8,128)(2,1)S(1)}, bf16[1,128,1024]{2,1,0:T(8,128)(2,1)S(1)}, u32[]{:S(2)}, u32[]{:S(2)}) collective-permute-start(bf16[1,128,1024]{2,1,0:T(8,128)(2,1)S(1)} %copy-done.30), channel_id=1, source_target_pairs={{0,8},{4,12},{8,0},{12,4},{16,24},{20,28},{24,16},{28,20},{1,9},{5... | collective-permute-start | bytes 786440 | tf_op jit(solution)/shard_map/ppermute | solution.py:687
  82.5 16.3 %collective-permute-start.24 = (bf16[1,128,1024]{2,1,0:T(8,128)(2,1)S(1)}, bf16[1,128,1024]{2,1,0:T(8,128)(2,1)S(1)}, u32[]{:S(2)}, u32[]{:S(2)}) collective-permute-start(bf16[1,128,1024]{2,1,0:T(8,128)(2,1)S(1)} %copy-done.27), channel_id=1, source_target_pairs={{0,16},{4,20},{8,24},{12,28},{16,0},{20,4},{24,8},{28,12},{1,17},{... | collective-permute-start | bytes 786440 | tf_op jit(solution)/shard_map/ppermute | solution.py:687
  83.0 15.9 %collective-permute-start.25 = (bf16[1,128,1024]{2,1,0:T(8,128)(2,1)S(1)}, bf16[1,128,1024]{2,1,0:T(8,128)(2,1)S(1)}, u32[]{:S(2)}, u32[]{:S(2)}) collective-permute-start(bf16[1,128,1024]{2,1,0:T(8,128)(2,1)S(1)} %copy-done.24), channel_id=1, source_target_pairs={{0,24},{4,28},{8,16},{12,20},{16,8},{20,12},{24,0},{28,4},{1,25},{... | collective-permute-start | bytes 786440 | tf_op jit(solution)/shard_map/ppermute | solution.py:687
  95.0 22.8 %collective-permute-start.26 = (bf16[3,128,1024]{2,1,0:T(8,128)(2,1)}, bf16[3,128,1024]{2,1,0:T(8,128)(2,1)S(1)}, u32[]{:S(2)}, u32[]{:S(2)}) collective-permute-start(bf16[3,128,1024]{2,1,0:T(8,128)(2,1)} %get-tuple-element.98.refs_0_), channel_id=1, source_target_pairs={{0,1},{3,2},{4,5},{7,6},{8,9},{11,10},{12,13},{15,14},{16,17},{19,... | collective-permute-start | bytes 2359304 | tf_op jit(solution)/shard_map/ppermute | solution.py:691
  98.9 20.6 %collective-permute-start.29 = (bf16[2,128,1024]{2,1,0:T(8,128)(2,1)}, bf16[2,128,1024]{2,1,0:T(8,128)(2,1)S(1)}, u32[]{:S(2)}, u32[]{:S(2)}) collective-permute-start(bf16[2,128,1024]{2,1,0:T(8,128)(2,1)} %get-tuple-element.110.refs_0_), channel_id=1, source_target_pairs={{0,8},{4,12},{8,0},{12,4},{16,24},{20,28},{24,16},{28,20},{1,9},{5... | collective-permute-start | bytes 1572872 | tf_op jit(solution)/shard_map/ppermute | solution.py:687
  100.3 21.2 %collective-permute-start.30 = (bf16[2,128,1024]{2,1,0:T(8,128)(2,1)}, bf16[2,128,1024]{2,1,0:T(8,128)(2,1)}, u32[]{:S(2)}, u32[]{:S(2)}) collective-permute-start(bf16[2,128,1024]{2,1,0:T(8,128)(2,1)} %get-tuple-element.111), channel_id=1, source_target_pairs={{0,16},{4,20},{8,24},{12,28},{16,0},{20,4},{24,8},{28,12},{1,17},{... | collective-permute-start | bytes 1572872 | tf_op jit(solution)/shard_map/ppermute | solution.py:687
  100.7 22.2 %collective-permute-start.31 = (bf16[2,128,1024]{2,1,0:T(8,128)(2,1)}, bf16[2,128,1024]{2,1,0:T(8,128)(2,1)}, u32[]{:S(2)}, u32[]{:S(2)}) collective-permute-start(bf16[2,128,1024]{2,1,0:T(8,128)(2,1)} %get-tuple-element.112), channel_id=1, source_target_pairs={{0,24},{4,28},{8,16},{12,20},{16,8},{20,12},{24,0},{28,4},{1,25},{... | collective-permute-start | bytes 1572872 | tf_op jit(solution)/shard_map/ppermute | solution.py:687
  115.6 21.1 %collective-permute-start.28 = (bf16[3,128,1024]{2,1,0:T(8,128)(2,1)}, bf16[3,128,1024]{2,1,0:T(8,128)(2,1)}, u32[]{:S(2)}, u32[]{:S(2)}) collective-permute-start(bf16[3,128,1024]{2,1,0:T(8,128)(2,1)} %get-tuple-element.109.refs_0_.refs_3_), channel_id=1, source_target_pairs={{0,1},{3,2},{4,5},{7,6},{8,9},{11,10},{12,13},{15,14},{16,17},{19,... | collective-permute-start | bytes 2359304 | tf_op jit(solution)/shard_map/ppermute | solution.py:691
  118.7 18.0 %collective-permute-start.27 = (bf16[2,128,1024]{2,1,0:T(8,128)(2,1)}, bf16[2,128,1024]{2,1,0:T(8,128)(2,1)S(1)}, u32[]{:S(2)}, u32[]{:S(2)}) collective-permute-start(bf16[2,128,1024]{2,1,0:T(8,128)(2,1)} %slice_add_fusion), channel_id=1, source_target_pairs={{1,2},{2,1},{5,6},{6,5},{9,10},{10,9},{13,14},{14,13},{17,18},{18,... | collective-permute-start | bytes 1572872 | tf_op jit(solution)/shard_map/ppermute | solution.py:691
  132.3 15.1 %collective-permute-start.34 = (bf16[1,256,1024]{2,1,0:T(8,128)(2,1)}, bf16[1,256,1024]{2,1,0:T(8,128)(2,1)}, u32[]{:S(2)}, u32[]{:S(2)}) collective-permute-start(bf16[1,256,1024]{2,1,0:T(8,128)(2,1)} %get-tuple-element.115), channel_id=1, source_target_pairs={{0,1},{3,2},{4,5},{7,6},{8,9},{11,10},{12,13},{15,14},{16,17},{19,... | collective-permute-start | bytes 1572872 | tf_op jit(solution)/shard_map/ppermute | solution.py:691
  134.6 22.8 %collective-permute-start.36 = (bf16[1,256,1024]{2,1,0:T(8,128)(2,1)}, bf16[1,256,1024]{2,1,0:T(8,128)(2,1)}, u32[]{:S(2)}, u32[]{:S(2)}) collective-permute-start(bf16[1,256,1024]{2,1,0:T(8,128)(2,1)} %get-tuple-element.121), channel_id=1, source_target_pairs={{0,1},{3,2},{4,5},{7,6},{8,9},{11,10},{12,13},{15,14},{16,17},{19,... | collective-permute-start | bytes 1572872 | tf_op jit(solution)/shard_map/ppermute | solution.py:691
  148.8 12.1 %collective-permute-start.35 = (bf16[1,256,1024]{2,1,0:T(8,128)(2,1)S(1)}, bf16[1,256,1024]{2,1,0:T(8,128)(2,1)S(1)}, u32[]{:S(2)}, u32[]{:S(2)}) collective-permute-start(bf16[1,256,1024]{2,1,0:T(8,128)(2,1)S(1)} %add.17.refs_0_), channel_id=1, source_target_pairs={{1,2},{2,1},{5,6},{6,5},{9,10},{10,9},{13,14},{14,13},{17,18},{18,... | collective-permute-start | bytes 1572872 | tf_op jit(solution)/shard_map/ppermute | solution.py:691
  150.9 13.1 %collective-permute-start.33 = (bf16[1,256,1024]{2,1,0:T(8,128)(2,1)S(1)}, bf16[1,256,1024]{2,1,0:T(8,128)(2,1)S(1)}, u32[]{:S(2)}, u32[]{:S(2)}) collective-permute-start(bf16[1,256,1024]{2,1,0:T(8,128)(2,1)S(1)} %outer.1.refs_1_), channel_id=1, source_target_pairs={{1,0},{2,3},{5,4},{6,7},{9,8},{10,11},{13,12},{14,15},{17,16},{18,... | collective-permute-start | bytes 1572872 | tf_op jit(solution)/shard_map/ppermute | solution.py:691
  159.4 24.2 %collective-permute-start.38 = (bf16[1,256,1024]{2,1,0:T(8,128)(2,1)}, bf16[1,256,1024]{2,1,0:T(8,128)(2,1)}, u32[]{:S(2)}, u32[]{:S(2)}) collective-permute-start(bf16[1,256,1024]{2,1,0:T(8,128)(2,1)} %add.18), channel_id=1, source_target_pairs={{1,2},{2,1},{5,6},{6,5},{9,10},{10,9},{13,14},{14,13},{17,18},{18,... | collective-permute-start | bytes 1572872 | tf_op jit(solution)/shard_map/ppermute | solution.py:691
  165.8 17.8 %collective-permute-start.37 = (bf16[1,256,1024]{2,1,0:T(8,128)(2,1)}, bf16[1,256,1024]{2,1,0:T(8,128)(2,1)}, u32[]{:S(2)}, u32[]{:S(2)}) collective-permute-start(bf16[1,256,1024]{2,1,0:T(8,128)(2,1)} %get-tuple-element.132.near_ref), channel_id=1, source_target_pairs={{0,1},{3,2},{4,5},{7,6},{8,9},{11,10},{12,13},{15,14},{16,17},{19,... | collective-permute-start | bytes 1572872 | tf_op jit(solution)/shard_map/ppermute | solution.py:691
  170.6 13.0 %collective-permute-start.39 = (bf16[1,256,1024]{2,1,0:T(8,128)(2,1)}, bf16[1,256,1024]{2,1,0:T(8,128)(2,1)}, u32[]{:S(2)}, u32[]{:S(2)}) collective-permute-start(bf16[1,256,1024]{2,1,0:T(8,128)(2,1)} %add.19), channel_id=1, source_target_pairs={{1,0},{2,3},{5,4},{6,7},{9,8},{10,11},{13,12},{14,15},{17,16},{18,... | collective-permute-start | bytes 1572872 | tf_op jit(solution)/shard_map/ppermute | solution.py:691
  (49 other events, 322.0 us)
